TPU v7x, 128 devices: a whole 4x4x4 slice. The times are simulated.
128 devices in a mesh: outer: 16 (over y, z_lo, core), inner: 8 (over z_hi, x).
Axes of the slice: x: 4, y: 4, z: 4 (z_hi: 2, z_lo: 2; z = z_hi * 2 + z_lo), core: 2. Of those that a mesh axis runs over, the one named last changes fastest.
Arguments:
- queries: bfloat16 [16384, 768], P(('outer', 'inner')), may hold values from -5.5 to 5.5
- keys: bfloat16 [16384, 128], P(('outer', 'inner')), may hold values from -5.5 to 5.5
- values: bfloat16 [16384, 128], P(('outer', 'inner')), may hold values from -6 to 6
- grad_out: bfloat16 [16384, 768], P(('outer', 'inner')), may hold values from -96 to 96
- span_slot: int32 [256], replicated, may hold values from 0 to 255, as said below
Outputs:
- grad_queries: bfloat16 [16384, 768], P(('outer', 'inner'))
- grad_keys: bfloat16 [16384, 128], P(('outer', 'inner'))
- grad_values: bfloat16 [16384, 128], P(('outer', 'inner'))
Inputs may be any that keep to these rules, and one draw needn't show every extreme that they name: `span_slot`: slots 2 d and 2 d + 1 hold spans c and 255 - c for some c below 128; every span is held once.
All inputs are finite; a program needn't handle non-finite values.
Results may differ from a plain program's by a relative error of at most 0.0074.
Values may be sent and summed in bfloat16 or wider, within the bound.
No kernel may reach another device: no remote copies, remote signals or barrier semaphores. Data moves between devices by JAX's collectives and lax.ppermute only.
A program may use at most 128 MiB of HBM per device.

v0:
```python
import math

import jax
import jax.numpy as jnp
from jax import lax
from jax.sharding import PartitionSpec as P

NEG_FILL = -1e30


def slot_positions(slots, span_len):
    offsets = jnp.arange(span_len, dtype=jnp.int32)
    return (slots[:, None] * span_len + offsets[None, :]).reshape(-1)


def grad_terms(q_rows, do_rows, k_blk, v_blk, live, lse, delta, scale):
    scores = jnp.dot(q_rows, k_blk.T, preferred_element_type=jnp.float32) * scale
    probs = jnp.where(live, jnp.exp(scores - lse[:, None]), 0.0)
    dprobs = jnp.dot(do_rows, v_blk.T, preferred_element_type=jnp.float32)
    dscores = (probs * (dprobs - delta[:, None]) * scale).astype(jnp.bfloat16)
    return (probs, dscores)


def local(queries, keys, values, grad_out, span_slot):
    tok_rows = keys.shape[0]
    span_len = tok_rows // 2
    head_dim = keys.shape[1]
    group = queries.shape[1] // head_dim
    scale = 1.0 / math.sqrt(head_dim)
    keys_all, values_all = (
        lax.all_gather(keys, ("outer", "inner"), axis=0, tiled=True),
        lax.all_gather(values, ("outer", "inner"), axis=0, tiled=True),
    )
    total_rows = keys_all.shape[0]
    key_pos = slot_positions(span_slot, span_len)
    linear = lax.axis_index(("outer", "inner"))
    own_slots = lax.dynamic_slice_in_dim(span_slot, 2 * linear, 2, 0)
    q_pos = jnp.repeat(slot_positions(own_slots, span_len), group)
    q_rows = queries.reshape(tok_rows * group, head_dim)
    do_rows = grad_out.reshape(tok_rows * group, head_dim)
    width = q_rows.shape[0]
    key_block = math.gcd(total_rows, 512)
    contract = (((0,), (0,)), ((), ()))

    def stats_step(index, carry):
        top, total, weighted = carry
        first = index * key_block
        k_blk = lax.dynamic_slice_in_dim(keys_all, first, key_block, 0)
        v_blk = lax.dynamic_slice_in_dim(values_all, first, key_block, 0)
        k_pos = lax.dynamic_slice_in_dim(key_pos, first, key_block, 0)
        live = q_pos[:, None] >= k_pos[None, :]
        scores = jnp.where(
            live, jnp.dot(q_rows, k_blk.T, preferred_element_type=jnp.float32) * scale, NEG_FILL
        )
        dprobs = jnp.dot(do_rows, v_blk.T, preferred_element_type=jnp.float32)
        new_top = jnp.maximum(top, jnp.max(scores, axis=1))
        shrink = jnp.exp(top - new_top)
        expo = jnp.where(live, jnp.exp(scores - new_top[:, None]), 0.0)
        return (
            new_top,
            total * shrink + jnp.sum(expo, axis=1),
            weighted * shrink + jnp.sum(expo * dprobs, axis=1),
        )

    start_stats = (
        jnp.full((width,), NEG_FILL, jnp.float32),
        jnp.zeros((width,), jnp.float32),
        jnp.zeros((width,), jnp.float32),
    )
    top, total, weighted = lax.fori_loop(0, total_rows // key_block, stats_step, start_stats)
    lse = top + jnp.log(total)
    delta = weighted / total

    def block_terms(first, size):
        k_blk = lax.dynamic_slice_in_dim(keys_all, first, size, 0)
        v_blk = lax.dynamic_slice_in_dim(values_all, first, size, 0)
        k_pos = lax.dynamic_slice_in_dim(key_pos, first, size, 0)
        live = q_pos[:, None] >= k_pos[None, :]
        probs, dscores = grad_terms(q_rows, do_rows, k_blk, v_blk, live, lse, delta, scale)
        dkey = lax.dot_general(dscores, q_rows, contract, preferred_element_type=jnp.float32)
        dval = lax.dot_general(
            probs.astype(jnp.bfloat16), do_rows, contract, preferred_element_type=jnp.float32
        )
        return (k_blk, dscores, jnp.concatenate([dkey, dval], axis=1))

    def joint_step(index, carry):
        acc, terms = carry
        first = index * key_block
        k_blk, dscores, piece = block_terms(first, key_block)
        acc = acc + jnp.dot(dscores, k_blk, preferred_element_type=jnp.float32)
        return (acc, lax.dynamic_update_slice_in_dim(terms, piece, first, 0))

    start_joint = (
        jnp.zeros((width, head_dim), jnp.float32),
        jnp.zeros((total_rows, 2 * head_dim), jnp.float32),
    )
    dq_acc, all_terms = lax.fori_loop(0, total_rows // key_block, joint_step, start_joint)
    summed = lax.psum_scatter(all_terms, ("outer", "inner"), scatter_dimension=0, tiled=True)
    grad_queries = dq_acc.astype(jnp.bfloat16).reshape(tok_rows, group * head_dim)
    grad_keys = summed[:, :head_dim].astype(jnp.bfloat16)
    grad_values = summed[:, head_dim:].astype(jnp.bfloat16)
    return (grad_queries, grad_keys, grad_values)


def solution(mesh):
    placed = (
        P(("outer", "inner"), None),
        P(("outer", "inner"), None),
        P(("outer", "inner"), None),
        P(("outer", "inner"), None),
        P(),
    )
    return jax.shard_map(
        local,
        mesh=mesh,
        in_specs=placed,
        out_specs=(
            P(("outer", "inner"), None),
            P(("outer", "inner"), None),
            P(("outer", "inner"), None),
        ),
        check_vma=False,
    )
```

profile of v0, /device:TPU:0, one launch (start us, length us, event | category | flops | bytes accessed | tf_op | source)
XLA Modules:
  0.0 1627.3 jit_solution(3825690210073952188)
XLA Ops:
  12.8 305.0 %all-gather.3.cloned.1.call-done = bf16[16384,128]{1,0:T(8,128)(2,1)} async-done(((bf16[128,128]{1,0:T(8,128)(2,1)}), bf16[16384,128]{1,0:T(8,128)(2,1)}) %all-gather.3.cloned.1.call-update) | async-done | bytes 4194320 | tf_op jit(solution)/shard_map/all_gather | solution.py:31
  317.7 309.4 %all-gather.5.cloned.1.call-done = bf16[16384,128]{1,0:T(8,128)(2,1)} async-done(((bf16[128,128]{1,0:T(8,128)(2,1)}), bf16[16384,128]{1,0:T(8,128)(2,1)}) %all-gather.5.cloned.1.call-update) | async-done | bytes 4194320 | tf_op jit(solution)/shard_map/all_gather | solution.py:32
  627.1 109.4 %while.34 = (s32[]{:T(128)}, f32[768]{0:T(1024)S(1)}, f32[768]{0:T(1024)S(1)}, f32[768]{0:T(1024)S(1)}, s32[16384]{0:T(1024)S(1)}, /*index=5*/bf16[16384,128]{1,...) while((s32[]{:T(128)}, f32[768]{0:T(1024)S(1)}, ...), condition=%wide.region_4.5_spmd.clone, body=%wide.region_0.4_spmd.clone.sunk | while | flops 206443776 | bytes 5458642 | solution.py:70
  632.1 1.4 fusion.58
  642.4 1.4 fusion.58
  652.6 1.4 fusion.58
  662.9 1.4 fusion.58
  673.2 1.4 fusion.58
  683.4 1.4 fusion.58
  693.7 1.4 fusion.58
  703.9 1.4 fusion.58
  714.2 1.4 fusion.58
  724.4 1.4 fusion.58
  734.7 1.4 fusion.58
  736.5 6.0 broadcast_in_dim.54.clone
  742.5 201.1 %while.35 = (s32[]{:T(128)}, f32[768,128]{1,0:T(8,128)S(1)}, f32[16384,256]{1,0:T(8,128)}, s32[16384]{0:T(1024)S(1)}, bf16[16384,128]{1,0:T(8,128)(2,1)}, /*inde...) while((s32[]{:T(128)}, f32[768,128]{1,0:T(8,128)S(1)}, ...), condition=%wide.region_6.7_spmd.clone, body=%wide.region_5.6_spmd.clone.sunk | while | flops 507183104 | bytes 12739297 | solution.py:97
  742.8 1.4 bitcast_select_fusion.2
  755.3 1.4 bitcast_select_fusion.2
  761.6 1.4 bitcast_select_fusion.2
  874.7 1.4 bitcast_select_fusion.2
  881.0 1.4 bitcast_select_fusion.2
  918.7 1.4 bitcast_select_fusion.2
  931.3 1.4 bitcast_select_fusion.2
  944.5 674.7 %reduce-scatter.2.cloned.1.call-done = f32[128,256]{1,0:T(8,128)} async-done(((f32[16384,256]{1,0:T(8,128)}), f32[128,256]{1,0:T(8,128)}) %reduce-scatter.2.cloned.1.call-update) | async-done | bytes 131088 | tf_op jit(solution)/shard_map/reduce_scatter | solution.py:98
  (645 shorter events, 288.8 us)
Async XLA Ops:
  7.2 310.6 %all-gather.3.cloned.1.call-start = ((), (), s32[]{:S(2)}) async-start(), calls=%async_computation.1 | async-start | bytes 4227072 | tf_op jit(solution)/shard_map/all_gather | solution.py:31
  7.9 619.2 %all-gather.5.cloned.1.call-start = ((), (), s32[]{:S(2)}) async-start(), calls=%async_computation.2 | async-start | bytes 4227072 | tf_op jit(solution)/shard_map/all_gather | solution.py:32
  8.6 1610.6 %reduce-scatter.2.cloned.1.call-start = ((), (), s32[]{:S(2)}) async-start(), calls=%async_computation.3 | async-start | bytes 16908288 | tf_op jit(solution)/shard_map/reduce_scatter | solution.py:98
Sparse Core Ops, SparseCore 0:
  9.7 307.9 all-gather.2
  319.4 307.6 all-gather.4
  943.7 675.4 reduce-scatter.1
where the time goes:
time: 1630 us
  waiting for transfers between devices  1290 us (79%)
  matrix products  242 us (15%)
  local copies, waits for them, and re-layouts  61.9 us (4%)
    reduce_scatter x1, waiting for transfers between devices, local(): lax.psum_scatter(all_terms, ('outer', 'inner'), scatter_dimension=0, tile...  675 us
    all_gather x1, waiting for transfers between devices, local(): lax.all_gather(values, ('outer', 'inner'), axis=0, tiled=True)  309 us
    all_gather x1, waiting for transfers between devices, local(): lax.all_gather(keys, ('outer', 'inner'), axis=0, tiled=True)  305 us
    dot_general x32, matrix products, stats_step(): dprobs = jnp.dot(do_rows, v_blk.T, preferred_element_type=jnp.float32)  44.8 us
    dot_general x32, matrix products, grad_terms(): jnp.dot(q_rows, k_blk.T, preferred_element_type=jnp.float32) * scale  44.7 us
    dot_general x32, matrix products, joint_step(): acc = acc + jnp.dot(dscores, k_blk, preferred_element_type=jnp.float32)  44.7 us
    dot_general x32, matrix products, stats_step(): jnp.dot(q_rows, k_blk.T, preferred_element_type=jnp.float32) * scale  41.5 us
    dot_general x32, matrix products, grad_terms(): dprobs = jnp.dot(do_rows, v_blk.T, preferred_element_type=jnp.float32)  40.8 us
  transfers between devices with their start and end apart: 3, of which 3 were waited for; matrix products, arithmetic and copies ran while one was open for 0% of the time, Pallas kernels for 0%

commit v1 on v0

v1 whole, which is shorter than its diff:
```python
import math

import jax
import jax.numpy as jnp
from jax import lax
from jax.experimental import pallas as pl
from jax.experimental.pallas import tpu as pltpu
from jax.sharding import Mesh, PartitionSpec as P

AXES = ("y", "zl", "core", "zh", "x")
NEG = -1e30
HD = 128
SCALE = 1.0 / math.sqrt(HD)
C2 = math.log2(math.e) * SCALE
SPAN = 64
HEADS = 6
ROWS = SPAN * HEADS
KB = 256
UNITS = 8
KEYS = 4096

NT = (((1,), (1,)), ((), ()))
NN = (((1,), (0,)), ((), ()))
TN = (((0,), (0,)), ((), ()))


def dot(a, b, dims):
    return lax.dot_general(a, b, dims, preferred_element_type=jnp.float32)


def load_sorted(meta, kvs, kv_s):
    for g, ref in enumerate(kvs):
        for s in range(32):
            r = pl.multiple_of(meta[g * 32 + s] * SPAN, SPAN)
            kv_s[pl.ds(r, SPAN), :] = ref[s // 2, (s % 2) * SPAN : (s % 2 + 1) * SPAN, :]


def load_rows(qds, q_s, do_s):
    for d, ref in enumerate(qds):
        for half in range(2):
            t = slice(half * SPAN, (half + 1) * SPAN)
            for h in range(HEADS):
                r = slice(h * SPAN, (h + 1) * SPAN)
                q_s[d * 2 + half, r, :] = ref[t, h * HD : (h + 1) * HD]
                do_s[d * 2 + half, r, :] = ref[t, (HEADS + h) * HD : (HEADS + h + 1) * HD]


def stats_kernel(meta, lim, qd0, qd1, qd2, qd3, kv0, kv1, out, q_s, do_s, kv_s):
    load_sorted(meta, (kv0, kv1), kv_s)
    load_rows((qd0, qd1, qd2, qd3), q_s, do_s)
    iota = lax.broadcasted_iota(jnp.int32, (KB, ROWS), 0)
    for u in range(UNITS):
        q = q_s[u]
        do = do_s[u]
        limit = lim[u : u + 1, :]

        def body(j, carry):
            m, l, d = carry
            k0 = pl.multiple_of(j * KB, KB)
            kv = kv_s[pl.ds(k0, KB), :]
            s = dot(kv[:, :HD], q, NT) * C2
            dp = dot(kv[:, HD:], do, NT)
            s = jnp.where(iota < limit - k0, s, NEG).reshape(KB // 8, 8, ROWS)
            mn = jnp.maximum(m, jnp.max(s, axis=0))
            a = jnp.exp2(m - mn)
            e = jnp.exp2(s - mn[None])
            l = l * a + jnp.sum(e, axis=0)
            d = d * a + jnp.sum(e * dp.reshape(KB // 8, 8, ROWS), axis=0)
            return mn, l, d

        zero = jnp.zeros((8, ROWS), jnp.float32)
        m, l, d = lax.fori_loop(0, meta[64 + u], body, (zero + NEG, zero, zero))
        live = jnp.where(m > 0.5 * NEG, 1.0, 0.0)
        top = jnp.max(m, axis=0, keepdims=True)
        a = jnp.exp2(m - top) * live
        ll = jnp.sum(l * a, axis=0, keepdims=True)
        dd = jnp.sum(d * a, axis=0, keepdims=True)
        safe = jnp.where(ll > 0, ll, 1.0)
        out[0, u : u + 1, :] = jnp.where(ll > 0, top + jnp.log2(safe), NEG)
        out[1, u : u + 1, :] = dd / safe


def grads_kernel(
    meta, lim, st0, st1, st2, st3, qd0, qd1, qd2, qd3, kv0, kv1, dq, dkv, q_s, do_s, kv_s, acc, dq_s
):
    load_sorted(meta, (kv0, kv1), kv_s)
    load_rows((qd0, qd1, qd2, qd3), q_s, do_s)
    acc[...] = jnp.zeros_like(acc)
    sts = (st0, st1, st2, st3)
    top = jnp.maximum(jnp.maximum(st0[0], st1[0]), jnp.maximum(st2[0], st3[0]))
    ws = [jnp.exp2(t[0] - top) for t in sts]
    total = ws[0] + ws[1] + ws[2] + ws[3]
    lse = top + jnp.log2(total)
    delta = (ws[0] * st0[1] + ws[1] * st1[1] + ws[2] * st2[1] + ws[3] * st3[1]) / total
    iota = lax.broadcasted_iota(jnp.int32, (KB, ROWS), 0)
    for u in range(UNITS):
        q = q_s[u]
        do = do_s[u]
        limit = lim[u : u + 1, :]
        lse_u = lse[u : u + 1]
        delta_u = delta[u : u + 1]
        dq_s[...] = jnp.zeros_like(dq_s)

        def body(j, carry):
            k0 = pl.multiple_of(j * KB, KB)
            kv = kv_s[pl.ds(k0, KB), :]
            k = kv[:, :HD]
            s = dot(k, q, NT)
            dp = dot(kv[:, HD:], do, NT)
            p = jnp.where(iota < limit - k0, jnp.exp2(s * C2 - lse_u), 0.0)
            ds = (p * (dp - delta_u)).astype(jnp.bfloat16)
            acc[pl.ds(k0, KB), :HD] += dot(ds, q, NN)
            acc[pl.ds(k0, KB), HD:] += dot(p.astype(jnp.bfloat16), do, NN)
            dq_s[...] += dot(ds, k, TN)
            return carry

        lax.fori_loop(0, meta[64 + u], body, 0)
        t = slice((u % 2) * SPAN, (u % 2 + 1) * SPAN)
        for h in range(HEADS):
            dq[u // 2, t, h * HD : (h + 1) * HD] = (
                dq_s[h * SPAN : (h + 1) * SPAN, :] * SCALE
            ).astype(jnp.bfloat16)
    for g in range(2):
        for s in range(32):
            r = pl.multiple_of(meta[g * 32 + s] * SPAN, SPAN)
            t = slice((s % 2) * SPAN, (s % 2 + 1) * SPAN)
            dkv[g, s // 2, t, :HD] = (acc[pl.ds(r, SPAN), :HD] * SCALE).astype(jnp.bfloat16)
            dkv[g, s // 2, t, HD:] = acc[pl.ds(r, SPAN), HD:].astype(jnp.bfloat16)


VM = pl.BlockSpec(memory_space=pltpu.VMEM)
SM = pl.BlockSpec(memory_space=pltpu.SMEM)
PARAMS = pltpu.CompilerParams(vmem_limit_bytes=48 * 2**20)
COPIES = [
    pltpu.VMEM((UNITS, ROWS, HD), jnp.bfloat16),
    pltpu.VMEM((UNITS, ROWS, HD), jnp.bfloat16),
    pltpu.VMEM((KEYS, 2 * HD), jnp.bfloat16),
]


def stats(meta, lim, qds, kvs):
    return pl.pallas_call(
        stats_kernel,
        out_shape=jax.ShapeDtypeStruct((2, UNITS, ROWS), jnp.float32),
        in_specs=[SM] + [VM] * 7,
        out_specs=VM,
        scratch_shapes=COPIES,
        compiler_params=PARAMS,
        name="stats",
    )(meta, lim, *qds, *kvs)


def grads(meta, lim, sts, qds, kvs):
    return pl.pallas_call(
        grads_kernel,
        out_shape=(
            jax.ShapeDtypeStruct((4, 2 * SPAN, HEADS * HD), jnp.bfloat16),
            jax.ShapeDtypeStruct((2, 16, 2 * SPAN, 2 * HD), jnp.bfloat16),
        ),
        in_specs=[SM] + [VM] * 11,
        out_specs=(VM, VM),
        scratch_shapes=COPIES
        + [pltpu.VMEM((KEYS, 2 * HD), jnp.float32), pltpu.VMEM((ROWS, HD), jnp.float32)],
        compiler_params=PARAMS,
        name="grads",
    )(meta, lim, *sts, *qds, *kvs)


def x_shift(a, step):
    return lax.ppermute(a, "x", [(i, (i + step) % 4) for i in range(4)])


def core_swap(a):
    return lax.ppermute(a, "core", [(0, 1), (1, 0)])


def local(queries, keys, values, grad_out, span_slot):
    y, zl, core, zh, x = (lax.axis_index(a) for a in AXES)
    qd = jnp.concatenate([queries, grad_out], axis=1)
    qds = [qd] + [x_shift(qd, r) for r in (1, 2, 3)]
    kv = jnp.concatenate([keys, values], axis=1)
    mine = lax.all_to_all(
        jnp.broadcast_to(kv[None], (16,) + kv.shape), ("y", "zl", "zh"), 0, 0, tiled=True
    )
    kvs = [mine, core_swap(mine)]

    grid = span_slot.reshape(4, 2, 2, 2, 4, 2)
    at_x = lax.dynamic_index_in_dim(grid, x, 4, keepdims=False)
    key_spans = jnp.concatenate(
        [
            lax.dynamic_index_in_dim(at_x, c, 2, keepdims=False).reshape(32)
            for c in (core, 1 - core)
        ]
    )
    ring = grid[y, zl, core, zh]
    query_spans = jnp.concatenate([ring[(x - r) % 4] for r in range(4)])
    rank = jnp.sum((key_spans[None, :] < key_spans[:, None]).astype(jnp.int32), axis=1)
    below = jnp.sum((key_spans[None, :] < query_spans[:, None]).astype(jnp.int32), axis=1)
    own = jnp.any(key_spans[None, :] == query_spans[:, None], axis=1)
    token = jnp.tile(jnp.arange(SPAN, dtype=jnp.int32), HEADS)
    lim = below[:, None] * SPAN + jnp.where(own[:, None], token[None, :] + 1, 0)
    tiles = (below * SPAN + jnp.where(own, SPAN, 0) + KB - 1) // KB
    meta = jnp.concatenate([rank, tiles]).astype(jnp.int32)

    part = stats(meta, lim, qds, kvs)
    def turned(r):
        got = x_shift(part, r)
        return jnp.roll(got, 2 * r, axis=1)

    sts = [part] + [turned(r) for r in (1, 2, 3)]
    dq, dkv = grads(meta, lim, sts, qds, kvs)

    pair = (dkv[0].astype(jnp.float32) + core_swap(dkv[1]).astype(jnp.float32)).astype(jnp.bfloat16)
    parts = lax.all_to_all(pair, ("y", "zl", "zh"), 0, 0, tiled=True)
    summed = jnp.sum(parts.astype(jnp.float32), axis=0)
    total = dq[0].astype(jnp.float32)
    for r in (1, 2, 3):
        total = total + x_shift(dq[r], 4 - r).astype(jnp.float32)
    return (
        total.astype(jnp.bfloat16),
        summed[:, :HD].astype(jnp.bfloat16),
        summed[:, HD:].astype(jnp.bfloat16),
    )


def solution(mesh):
    fine = Mesh(mesh.devices.reshape(4, 2, 2, 2, 4), AXES)
    rows = P(AXES, None)
    return jax.shard_map(
        local,
        mesh=fine,
        in_specs=(rows, rows, rows, rows, P()),
        out_specs=(rows, rows, rows),
        check_vma=False,
    )
```

time: 1630 us -> 137 us (0.08)
  waiting for transfers between devices: 1290 us -> 38.7 us
  matrix products: 242 us -> 0 us
  Pallas kernels: 0 us -> 64.1 us
  local copies, waits for them, and re-layouts: 61.9 us -> 4.64 us
  starting transfers between devices: 0.11 us -> 25.1 us
    reduce_scatter x1 -> x0, waiting for transfers between devices: 675 us -> none  [local(): lax.psum_scatter(all_terms, ('outer', 'inner'), scatter_dimension=0, tile...]
    all_gather x2 -> x0, waiting for transfers between devices: 614 us -> none  [the longest x1 309 us: local(): lax.all_gather(values, ('outer', 'inner'), axis=0, tiled=True)]
    dot_general x224 -> x0, matrix products: 242 us -> none  [the longest x32 44.8 us: stats_step(): dprobs = jnp.dot(do_rows, v_blk.T, preferred_element_type=jnp.float32)]
    pallas_call x0 -> x2, Pallas kernels: none -> 64.1 us  [the longest x1 42 us: grads(): pl.pallas_call(grads_kernel, out_shape=(jax.ShapeDtypeStruct((4, 2 * SPAN...]
    dynamic_update_slice x64 -> x0, local copies, waits for them, and re-layouts: 33.2 us -> none  [joint_step(): return (acc, lax.dynamic_update_slice_in_dim(terms, piece, first, 0))]
    ppermute x0 -> x11, waiting for transfers between devices: none -> 21.5 us  [the longest x9 18.9 us: x_shift(): return lax.ppermute(a, 'x', [(i, (i + step) % 4) for i in range(4)])]
    all_to_all x0 -> x2, waiting for transfers between devices: none -> 17.2 us  [the longest x1 13.1 us: local(): lax.all_to_all(jnp.broadcast_to(kv[None], (16,) + kv.shape), ('y', 'zl',...]
  transfers between devices with their start and end apart: 3 -> 13, of which waited for: 3 -> 10; matrix products, arithmetic and copies ran while one was open for 0% -> 2% of each run, Pallas kernels for 0% -> 0%
where the time goes in v1:
time: 137 us
  Pallas kernels  64.1 us (47%)
  waiting for transfers between devices  38.7 us (28%)
  starting transfers between devices  25.1 us (18%)
  local copies, waits for them, and re-layouts  4.64 us (3%)
  other arithmetic  3.97 us (3%)
    pallas_call x1, Pallas kernels, grads(): pl.pallas_call(grads_kernel, out_shape=(jax.ShapeDtypeStruct((4, 2 * SPAN...  42 us
    pallas_call x1, Pallas kernels, stats(): pl.pallas_call(stats_kernel, out_shape=jax.ShapeDtypeStruct((2, UNITS, RO...  22.1 us
    ppermute x9, waiting for transfers between devices, x_shift(): return lax.ppermute(a, 'x', [(i, (i + step) % 4) for i in range(4)])  18.9 us
    all_to_all x1, waiting for transfers between devices, local(): lax.all_to_all(jnp.broadcast_to(kv[None], (16,) + kv.shape), ('y', 'zl',...  13.1 us
    ppermute x9, starting transfers between devices, x_shift(): return lax.ppermute(a, 'x', [(i, (i + step) % 4) for i in range(4)])  10.3 us
    all_to_all x1, starting transfers between devices, local(): lax.all_to_all(jnp.broadcast_to(kv[None], (16,) + kv.shape), ('y', 'zl',...  8.13 us
    all_to_all x1, starting transfers between devices, local(): parts = lax.all_to_all(pair, ('y', 'zl', 'zh'), 0, 0, tiled=True)  6.64 us
    all_to_all x1, waiting for transfers between devices, local(): parts = lax.all_to_all(pair, ('y', 'zl', 'zh'), 0, 0, tiled=True)  4.12 us
  transfers between devices with their start and end apart: 13, of which 10 were waited for; matrix products, arithmetic and copies ran while one was open for 2% of the time, Pallas kernels for 0%

profile of v1, /device:TPU:0, one launch (start us, length us, event | category | flops | bytes accessed | tf_op | source)
XLA Modules:
  0.0 137.3 jit_solution(8725042507036933233)
XLA Ops:
  0.7 0.8 pad_maximum_fusion
  1.5 1.1 broadcast_in_dim.44
  2.6 8.1 %all-to-all-start = ((bf16[16,128,256]{2,1,0:T(8,128)(2,1)}), bf16[16,128,256]{2,1,0:T(8,128)(2,1)S(1)}, u32[]{:S(2)}, u32[]{:S(2)}) async-start(bf16[16,128,256]{2,1,0:T(8,128)(2,1)} %broadcast_in_dim.44), calls=%async_computation | async-start | bytes 2097152 | tf_op jit(solution)/shard_map/all_to_all | solution.py:182
  10.8 2.8 %collective-permute-start.2 = (bf16[128,1536]{1,0:T(8,128)(2,1)S(1)}, bf16[128,1536]{1,0:T(8,128)(2,1)S(1)}, u32[]{:S(2)}, u32[]{:S(2)}) collective-permute-start(bf16[128,1536]{1,0:T(8,128)(2,1)S(1)} %constant_dynamic-update-slice_fusion.qd0), channel_id=1, source_target_pairs={{0,3},{1,0},{2,1},{3,2},{4,7},{5,4},{6,5},{7,6},{8,11},{9,8},{10,9... | collective-permute-start | bytes 1179656 | tf_op jit(solution)/shard_map/ppermute | solution.py:170
  13.6 0.8 collective-permute-start.1
  14.4 0.9 collective-permute-start
  15.8 13.1 %all-to-all-done.kv0 = bf16[16,128,256]{2,1,0:T(8,128)(2,1)S(1)} async-done(((bf16[16,128,256]{2,1,0:T(8,128)(2,1)}), bf16[16,128,256]{2,1,0:T(8,128)(2,1)S(1)}, u32[]{:S(2)}, u32[]{:S(2)}) %all-to-all-start) | async-done | bytes 1048608 | tf_op jit(solution)/shard_map/all_to_all | solution.py:182
  30.2 3.8 %collective-permute-done.qd1 = bf16[128,1536]{1,0:T(8,128)(2,1)} collective-permute-done((bf16[128,1536]{1,0:T(8,128)(2,1)S(1)}, bf16[128,1536]{1,0:T(8,128)(2,1)}, u32[]{:S(2)}, u32[]{:S(2)}) %collective-permute-start) | collective-permute-done | bytes 393248 | tf_op jit(solution)/shard_map/ppermute | solution.py:170
  33.9 22.1 %stats.1.st0 = f32[2,8,384]{2,1,0:T(8,128)S(1)} custom-call(s32[72]{0:T(128)S(1)} %pad_add_fusion.2.meta, s32[8,384]{1,0:T(8,128)S(1)} %select_add_fusion.lim, bf16[128,1536]{1,0:T(8,128)(2,1)S(1)} %constant_dynamic-update-slice_fusion.qd0, bf16[128,1536]{1,0:T(8,128)(2,1)} %collective-permute-done.qd1, bf16[128,1536]{1,0:T(8,128)(2,1)S(1)} %collective-permute-done.1.qd2, ...), custom_call_target="tpu_custom_call" | custom-call | tf_op jit(solution)/shard_map/stats/pallas_call | solution.py:142
  56.7 0.8 collective-permute-start.5
  58.1 1.8 %collective-permute-done.6 = f32[2,8,384]{2,1,0:T(8,128)S(1)} collective-permute-done((f32[2,8,384]{2,1,0:T(8,128)S(1)}, f32[2,8,384]{2,1,0:T(8,128)S(1)}, u32[]{:S(2)}, u32[]{:S(2)}) %collective-permute-start.6) | collective-permute-done | bytes 24608 | tf_op jit(solution)/shard_map/ppermute | solution.py:170
  60.0 2.1 %collective-permute-done.5 = f32[2,8,384]{2,1,0:T(8,128)S(1)} collective-permute-done((f32[2,8,384]{2,1,0:T(8,128)S(1)}, f32[2,8,384]{2,1,0:T(8,128)S(1)}, u32[]{:S(2)}, u32[]{:S(2)}) %collective-permute-start.5) | collective-permute-done | bytes 24608 | tf_op jit(solution)/shard_map/ppermute | solution.py:170
  62.6 42.0 %grads.1 = (bf16[4,128,768]{2,1,0:T(8,128)(2,1)S(1)}, bf16[2,16,128,256]{3,2,1,0:T(8,128)(2,1)}) custom-call(s32[72]{0:T(128)S(1)} %pad_add_fusion.2.meta, s32[8,384]{1,0:T(8,128)S(1)} %select_add_fusion.lim, f32[2,8,384]{2,1,0:T(8,128)S(1)} %stats.1.st0, f32[2,8,384]{2,1,0:T(8,128)S(1)} %pad_maximum_fusion.1.st1, f32[2,8,384]{2,1,0:T(8,128)S(1)} %pad_maximum_fusion.2.st2, ...), custom_call_target="tpu_custom_call" | custom-call | tf_op jit(solution)/shard_map/grads/pallas_call | solution.py:154
  104.7 0.9 copy-done
  105.5 1.4 %slice_bitcast_fusion = bf16[16,128,256]{2,1,0:T(8,128)(2,1)S(1)} fusion(bf16[2,16,128,256]{3,2,1,0:T(8,128)(2,1)} %get-tuple-element.6), kind=kLoop, calls=%fused_computation.2 | loop fusion | bytes 2097152 | tf_op jit(solution)/shard_map/squeeze | solution.py:213
  107.1 2.6 %collective-permute-done.10 = bf16[16,128,256]{2,1,0:T(8,128)(2,1)S(1)} collective-permute-done((bf16[16,128,256]{2,1,0:T(8,128)(2,1)S(1)}, bf16[16,128,256]{2,1,0:T(8,128)(2,1)S(1)}, u32[]{:S(2)}, u32[]{:S(2)}) %collective-permute-start.10) | collective-permute-done | bytes 1048608 | tf_op jit(solution)/shard_map/ppermute | solution.py:174
  109.7 1.3 fusion
  111.0 6.6 %all-to-all-start.1 = ((bf16[16,128,256]{2,1,0:T(8,128)(2,1)}), bf16[16,128,256]{2,1,0:T(8,128)(2,1)S(1)}, u32[]{:S(2)}, u32[]{:S(2)}) async-start(bf16[16,128,256]{2,1,0:T(8,128)(2,1)} %fusion), calls=%async_computation.1 | async-start | bytes 2097152 | tf_op jit(solution)/shard_map/all_to_all | solution.py:214
  117.8 2.1 %collective-permute-start.7 = (bf16[128,768]{1,0:T(8,128)(2,1)S(1)}, bf16[128,768]{1,0:T(8,128)(2,1)S(1)}, u32[]{:S(2)}, u32[]{:S(2)}) collective-permute-start(bf16[128,768]{1,0:T(8,128)(2,1)S(1)} %get-tuple-element.9), channel_id=1, source_target_pairs={{0,3},{1,0},{2,1},{3,2},{4,7},{5,4},{6,5},{7,6},{8,11},{9,8},{10,9... | collective-permute-start | bytes 589832 | tf_op jit(solution)/shard_map/ppermute | solution.py:170
  119.8 1.5 %collective-permute-start.8 = (bf16[128,768]{1,0:T(8,128)(2,1)S(1)}, bf16[128,768]{1,0:T(8,128)(2,1)S(1)}, u32[]{:S(2)}, u32[]{:S(2)}) collective-permute-start(bf16[128,768]{1,0:T(8,128)(2,1)S(1)} %get-tuple-element.11), channel_id=1, source_target_pairs={{0,2},{1,3},{2,0},{3,1},{4,6},{5,7},{6,4},{7,5},{8,10},{9,11},{10,... | collective-permute-start | bytes 589832 | tf_op jit(solution)/shard_map/ppermute | solution.py:170
  121.4 6.9 %collective-permute-done.7 = bf16[128,768]{1,0:T(8,128)(2,1)S(1)} collective-permute-done((bf16[128,768]{1,0:T(8,128)(2,1)S(1)}, bf16[128,768]{1,0:T(8,128)(2,1)S(1)}, u32[]{:S(2)}, u32[]{:S(2)}) %collective-permute-start.7) | collective-permute-done | bytes 196640 | tf_op jit(solution)/shard_map/ppermute | solution.py:170
  128.3 3.4 %collective-permute-done.9 = bf16[128,768]{1,0:T(8,128)(2,1)S(1)} collective-permute-done((bf16[128,768]{1,0:T(8,128)(2,1)S(1)}, bf16[128,768]{1,0:T(8,128)(2,1)S(1)}, u32[]{:S(2)}, u32[]{:S(2)}) %collective-permute-start.9) | collective-permute-done | bytes 196640 | tf_op jit(solution)/shard_map/ppermute | solution.py:170
  131.7 0.8 fusion.3
  132.4 4.1 %all-to-all-done.1 = bf16[16,128,256]{2,1,0:T(8,128)(2,1)S(1)} async-done(((bf16[16,128,256]{2,1,0:T(8,128)(2,1)}), bf16[16,128,256]{2,1,0:T(8,128)(2,1)S(1)}, u32[]{:S(2)}, u32[]{:S(2)}) %all-to-all-start.1) | async-done | bytes 1048608 | tf_op jit(solution)/shard_map/all_to_all | solution.py:214
  (48 shorter events, 4.6 us)
Async XLA Ops:
  0.6 10.1 %copy-start.3 = (bf16[128,768]{1,0:T(8,128)(2,1)S(1)}, bf16[128,768]{1,0:T(8,128)(2,1)}, u32[]{:S(2)}) copy-start(bf16[128,768]{1,0:T(8,128)(2,1)} %param.5) | copy-start | bytes 589828
  0.6 10.1 %copy-start.4 = (bf16[128,768]{1,0:T(8,128)(2,1)S(1)}, bf16[128,768]{1,0:T(8,128)(2,1)}, u32[]{:S(2)}) copy-start(bf16[128,768]{1,0:T(8,128)(2,1)} %param.8) | copy-start | bytes 589828
  1.5 13.8 %copy-start.5 = (s32[256]{0:T(256)S(1)}, s32[256]{0:T(256)}, u32[]{:S(2)}) copy-start(s32[256]{0:T(256)} %param.9) | copy-start | bytes 3076
  2.6 26.3 %all-to-all-start = ((bf16[16,128,256]{2,1,0:T(8,128)(2,1)}), bf16[16,128,256]{2,1,0:T(8,128)(2,1)S(1)}, u32[]{:S(2)}, u32[]{:S(2)}) async-start(bf16[16,128,256]{2,1,0:T(8,128)(2,1)} %broadcast_in_dim.44), calls=%async_computation | async-start | bytes 2097152 | tf_op jit(solution)/shard_map/all_to_all | solution.py:182
  10.8 19.4 %collective-permute-start.2 = (bf16[128,1536]{1,0:T(8,128)(2,1)S(1)}, bf16[128,1536]{1,0:T(8,128)(2,1)S(1)}, u32[]{:S(2)}, u32[]{:S(2)}) collective-permute-start(bf16[128,1536]{1,0:T(8,128)(2,1)S(1)} %constant_dynamic-update-slice_fusion.qd0), channel_id=1, source_target_pairs={{0,3},{1,0},{2,1},{3,2},{4,7},{5,4},{6,5},{7,6},{8,11},{9,8},{10,9... | collective-permute-start | bytes 1179656 | tf_op jit(solution)/shard_map/ppermute | solution.py:170
  13.6 16.6 %collective-permute-start.1 = (bf16[128,1536]{1,0:T(8,128)(2,1)S(1)}, bf16[128,1536]{1,0:T(8,128)(2,1)S(1)}, u32[]{:S(2)}, u32[]{:S(2)}) collective-permute-start(bf16[128,1536]{1,0:T(8,128)(2,1)S(1)} %constant_dynamic-update-slice_fusion.qd0), channel_id=1, source_target_pairs={{0,2},{1,3},{2,0},{3,1},{4,6},{5,7},{6,4},{7,5},{8,10},{9,11},{10,... | collective-permute-start | bytes 1179656 | tf_op jit(solution)/shard_map/ppermute | solution.py:170
  14.4 19.5 %collective-permute-start = (bf16[128,1536]{1,0:T(8,128)(2,1)S(1)}, bf16[128,1536]{1,0:T(8,128)(2,1)}, u32[]{:S(2)}, u32[]{:S(2)}) collective-permute-start(bf16[128,1536]{1,0:T(8,128)(2,1)S(1)} %constant_dynamic-update-slice_fusion.qd0), channel_id=1, source_target_pairs={{0,1},{1,2},{2,3},{3,0},{4,5},{5,6},{6,7},{7,4},{8,9},{9,10},{10,1... | collective-permute-start | bytes 1179656 | tf_op jit(solution)/shard_map/ppermute | solution.py:170
  28.9 5.1 %collective-permute-start.3 = (bf16[16,128,256]{2,1,0:T(8,128)(2,1)S(1)}, bf16[16,128,256]{2,1,0:T(8,128)(2,1)S(1)}, u32[]{:S(2)}, u32[]{:S(2)}) collective-permute-start(bf16[16,128,256]{2,1,0:T(8,128)(2,1)S(1)} %all-to-all-done.kv0), channel_id=1, source_target_pairs={{0,8},{8,0},{1,9},{9,1},{2,10},{10,2},{3,11},{11,3},{4,12},{12,4},... | collective-permute-start | bytes 3145736 | tf_op jit(solution)/shard_map/ppermute | solution.py:174
  56.0 3.9 %collective-permute-start.6 = (f32[2,8,384]{2,1,0:T(8,128)S(1)}, f32[2,8,384]{2,1,0:T(8,128)S(1)}, u32[]{:S(2)}, u32[]{:S(2)}) collective-permute-start(f32[2,8,384]{2,1,0:T(8,128)S(1)} %stats.1.st0), channel_id=1, source_target_pairs={{0,3},{1,0},{2,1},{3,2},{4,7},{5,4},{6,5},{7,6},{8,11},{9,8},{10,9... | collective-permute-start | bytes 73736 | tf_op jit(solution)/shard_map/ppermute | solution.py:170
  56.7 5.4 %collective-permute-start.5 = (f32[2,8,384]{2,1,0:T(8,128)S(1)}, f32[2,8,384]{2,1,0:T(8,128)S(1)}, u32[]{:S(2)}, u32[]{:S(2)}) collective-permute-start(f32[2,8,384]{2,1,0:T(8,128)S(1)} %stats.1.st0), channel_id=1, source_target_pairs={{0,2},{1,3},{2,0},{3,1},{4,6},{5,7},{6,4},{7,5},{8,10},{9,11},{10,... | collective-permute-start | bytes 73736 | tf_op jit(solution)/shard_map/ppermute | solution.py:170
  57.5 5.1 %collective-permute-start.4 = (f32[2,8,384]{2,1,0:T(8,128)S(1)}, f32[2,8,384]{2,1,0:T(8,128)S(1)}, u32[]{:S(2)}, u32[]{:S(2)}) collective-permute-start(f32[2,8,384]{2,1,0:T(8,128)S(1)} %stats.1.st0), channel_id=1, source_target_pairs={{0,1},{1,2},{2,3},{3,0},{4,5},{5,6},{6,7},{7,4},{8,9},{9,10},{10,1... | collective-permute-start | bytes 73736 | tf_op jit(solution)/shard_map/ppermute | solution.py:170
  104.6 0.9 copy-start
  105.5 4.2 %copy-start.2 = (bf16[2,16,128,256]{3,2,1,0:T(8,128)(2,1)S(1)}, bf16[2,16,128,256]{3,2,1,0:T(8,128)(2,1)}, u32[]{:S(2)}) copy-start(bf16[2,16,128,256]{3,2,1,0:T(8,128)(2,1)} %get-tuple-element.6) | copy-start | bytes 6291460
  107.0 10.7 %copy-start.1 = (bf16[4,128,768]{2,1,0:T(8,128)(2,1)S(1)}, bf16[4,128,768]{2,1,0:T(8,128)(2,1)}, u32[]{:S(2)}) copy-start(bf16[4,128,768]{2,1,0:T(8,128)(2,1)} %copy-done) | copy-start | bytes 2359300
  107.0 2.7 %collective-permute-start.10 = (bf16[16,128,256]{2,1,0:T(8,128)(2,1)S(1)}, bf16[16,128,256]{2,1,0:T(8,128)(2,1)S(1)}, u32[]{:S(2)}, u32[]{:S(2)}) collective-permute-start(bf16[16,128,256]{2,1,0:T(8,128)(2,1)S(1)} %slice_bitcast_fusion), channel_id=1, source_target_pairs={{0,8},{8,0},{1,9},{9,1},{2,10},{10,2},{3,11},{11,3},{4,12},{12,4},... | collective-permute-start | bytes 3145736 | tf_op jit(solution)/shard_map/ppermute | solution.py:174
  111.0 25.5 %all-to-all-start.1 = ((bf16[16,128,256]{2,1,0:T(8,128)(2,1)}), bf16[16,128,256]{2,1,0:T(8,128)(2,1)S(1)}, u32[]{:S(2)}, u32[]{:S(2)}) async-start(bf16[16,128,256]{2,1,0:T(8,128)(2,1)} %fusion), calls=%async_computation.1 | async-start | bytes 2097152 | tf_op jit(solution)/shard_map/all_to_all | solution.py:214
  117.8 10.5 %collective-permute-start.7 = (bf16[128,768]{1,0:T(8,128)(2,1)S(1)}, bf16[128,768]{1,0:T(8,128)(2,1)S(1)}, u32[]{:S(2)}, u32[]{:S(2)}) collective-permute-start(bf16[128,768]{1,0:T(8,128)(2,1)S(1)} %get-tuple-element.9), channel_id=1, source_target_pairs={{0,3},{1,0},{2,1},{3,2},{4,7},{5,4},{6,5},{7,6},{8,11},{9,8},{10,9... | collective-permute-start | bytes 589832 | tf_op jit(solution)/shard_map/ppermute | solution.py:170
  119.8 11.8 %collective-permute-start.9 = (bf16[128,768]{1,0:T(8,128)(2,1)S(1)}, bf16[128,768]{1,0:T(8,128)(2,1)S(1)}, u32[]{:S(2)}, u32[]{:S(2)}) collective-permute-start(bf16[128,768]{1,0:T(8,128)(2,1)S(1)} %get-tuple-element.10), channel_id=1, source_target_pairs={{0,1},{1,2},{2,3},{3,0},{4,5},{5,6},{6,7},{7,4},{8,9},{9,10},{10,1... | collective-permute-start | bytes 589832 | tf_op jit(solution)/shard_map/ppermute | solution.py:170
  119.8 11.8 %collective-permute-start.8 = (bf16[128,768]{1,0:T(8,128)(2,1)S(1)}, bf16[128,768]{1,0:T(8,128)(2,1)S(1)}, u32[]{:S(2)}, u32[]{:S(2)}) collective-permute-start(bf16[128,768]{1,0:T(8,128)(2,1)S(1)} %get-tuple-element.11), channel_id=1, source_target_pairs={{0,2},{1,3},{2,0},{3,1},{4,6},{5,7},{6,4},{7,5},{8,10},{9,11},{10,... | collective-permute-start | bytes 589832 | tf_op jit(solution)/shard_map/ppermute | solution.py:170

commit v2 on v1

v2 whole, which is shorter than its diff:
```python
import math

import jax
import jax.numpy as jnp
from jax import lax
from jax.experimental import pallas as pl
from jax.experimental.pallas import tpu as pltpu
from jax.sharding import Mesh, PartitionSpec as P

AXES = ("y", "zl", "core", "zh", "x")
NEG = -1e30
HD = 128
SCALE = 1.0 / math.sqrt(HD)
C2 = math.log2(math.e) * SCALE
SPAN = 64
HEADS = 6
WIDE = HEADS * HD
KEYS = 4096
KB = 256
R = 256
GROUPS = 12
UNROLL = 8
LIST = 136
IN, OUT, UNIT, COUNT = 0, 64, 128, 136
GROUP, BLOCK = 137, 137 + LIST

NT = (((1,), (1,)), ((), ()))
NN = (((1,), (0,)), ((), ()))
TN = (((0,), (0,)), ((), ()))


def dot(a, b, dims):
    return lax.dot_general(a, b, dims, preferred_element_type=jnp.float32)


def aligned(i, n):
    return pl.multiple_of(i * n, n)


def tree(op, xs):
    acc = list(xs[:4])
    for i, x in enumerate(xs[4:]):
        acc[i % 4] = op(acc[i % 4], x)
    return op(op(acc[0], acc[1]), op(acc[2], acc[3]))


def load_sorted(meta, kvs, kv_s):
    s = 0
    for ref in kvs:
        for e in range(ref.shape[0]):
            for half in range(2):
                r = aligned(meta[IN + s], SPAN)
                kv_s[pl.ds(r, SPAN), :] = ref[e, half * SPAN : (half + 1) * SPAN, :]
                s += 1


def row_of(place, h):
    odd = place % 2
    inner = odd * 512 + h * SPAN if h < 4 else R + odd * 128 + (h - 4) * SPAN
    return pl.multiple_of((place // 2) * 768 + inner, SPAN)


def load_rows(meta, qs, dos, q_s, do_s):
    for d in range(4):
        for half in range(2):
            place = meta[UNIT + 2 * d + half]
            t = slice(half * SPAN, (half + 1) * SPAN)
            for h in range(HEADS):
                r = row_of(place, h)
                for (ref, first), dst in ((qs[d], q_s), (dos[d], do_s)):
                    dst[pl.ds(r, SPAN), :] = ref[t, first + h * HD : first + (h + 1) * HD]
    q_s[GROUPS * R :, :] = jnp.zeros((R, HD), q_s.dtype)
    do_s[GROUPS * R :, :] = jnp.zeros((R, HD), do_s.dtype)


def products(meta, t, q_s, do_s, kv_s, s_b, dp_b):
    r, k = aligned(meta[GROUP + t], R), aligned(meta[BLOCK + t], KB)
    s_b[...] = dot(kv_s[pl.ds(k, KB), :HD], q_s[pl.ds(r, R), :], NT)
    dp_b[...] = dot(kv_s[pl.ds(k, KB), HD:], do_s[pl.ds(r, R), :], NT)


def operands(refs):
    qd0, qd1, q2, do2, qd3 = refs[:5]
    qs = ((qd0, 0), (qd1, 0), (q2, 0), (qd3, 0))
    dos = ((qd0, WIDE), (qd1, WIDE), (do2, 0), (qd3, WIDE))
    return qs, dos, refs[5:13]


def stats_kernel(meta, lim, *refs):
    qs, dos, kvs = operands(refs)
    out, q_s, do_s, kv_s, s0, s1, dp0, dp1, m_s, l_s, d_s = refs[13:]
    load_sorted(meta, kvs, kv_s)
    load_rows(meta, qs, dos, q_s, do_s)
    m_s[...] = jnp.full_like(m_s, NEG)
    l_s[...] = jnp.zeros_like(l_s)
    d_s[...] = jnp.zeros_like(d_s)
    iota = lax.broadcasted_iota(jnp.int32, (KB, R), 0)

    def online(t, s_b, dp_b):
        g = meta[GROUP + t]
        limit = lim[pl.ds(g, 1), :] - meta[BLOCK + t] * KB
        rows = [slice(8 * i, 8 * i + 8) for i in range(KB // 8)]
        s = [jnp.where(iota[r] < limit, s_b[r, :] * C2, NEG) for r in rows]
        m = m_s[g]
        top = jnp.maximum(m, tree(jnp.maximum, s))
        a = jnp.exp2(m - top)
        e = [jnp.exp2(x - top) for x in s]
        m_s[g] = top
        l_s[g] = l_s[g] * a + tree(jnp.add, e)
        d_s[g] = d_s[g] * a + tree(jnp.add, [x * dp_b[r, :] for r, x in zip(rows, e)])

    ss, dps = (s0, s1), (dp0, dp1)
    products(meta, 0, q_s, do_s, kv_s, s0, dp0)

    def body(i, carry):
        for v in range(UNROLL):
            t = i * UNROLL + v
            products(meta, t + 1, q_s, do_s, kv_s, ss[(v + 1) % 2], dps[(v + 1) % 2])
            online(t, ss[v % 2], dps[v % 2])
        return carry

    lax.fori_loop(0, (meta[COUNT] + UNROLL - 1) // UNROLL, body, 0)
    for g in range(GROUPS):
        m = m_s[g]
        live = jnp.where(m > 0.5 * NEG, 1.0, 0.0)
        top = jnp.max(m, axis=0, keepdims=True)
        a = jnp.exp2(m - top) * live
        ll = jnp.sum(l_s[g] * a, axis=0, keepdims=True)
        dd = jnp.sum(d_s[g] * a, axis=0, keepdims=True)
        safe = jnp.where(ll > 0, ll, 1.0)
        out[0, g : g + 1, :] = jnp.where(ll > 0, top + jnp.log2(safe), NEG)
        out[1, g : g + 1, :] = dd / safe
    out[:, GROUPS:, :] = jnp.zeros((2, 16 - GROUPS, R), jnp.float32)


def grads_kernel(meta, lim, st0, st1, st2, st3, *refs):
    qs, dos, kvs = operands(refs)
    dqs, dkvs = refs[13:17], refs[17:19]
    q_s, do_s, kv_s, s0, s1, dp0, dp1, acc, dq_s, p0, p1, ds0, ds1, lse, delta = refs[19:]
    load_sorted(meta, kvs, kv_s)
    load_rows(meta, qs, dos, q_s, do_s)
    acc[...] = jnp.zeros_like(acc)
    dq_s[...] = jnp.zeros_like(dq_s)
    sts = (st0, st1, st2, st3)
    top = jnp.maximum(jnp.maximum(st0[0], st1[0]), jnp.maximum(st2[0], st3[0]))
    ws = [jnp.exp2(t[0] - top) for t in sts]
    total = ws[0] + ws[1] + ws[2] + ws[3]
    lse[...] = top + jnp.log2(total)
    delta[...] = sum(w * t[1] for w, t in zip(ws, sts)) / total
    iota = lax.broadcasted_iota(jnp.int32, (KB, R), 0)

    def weights(t, s_b, dp_b, p_b, ds_b):
        g = meta[GROUP + t]
        limit = lim[pl.ds(g, 1), :] - meta[BLOCK + t] * KB
        p = jnp.where(iota < limit, jnp.exp2(s_b[...] * C2 - lse[pl.ds(g, 1), :]), 0.0)
        p_b[...] = p.astype(jnp.bfloat16)
        ds_b[...] = (p * (dp_b[...] - delta[pl.ds(g, 1), :])).astype(jnp.bfloat16)

    def sums(t, p_b, ds_b):
        r, k = aligned(meta[GROUP + t], R), aligned(meta[BLOCK + t], KB)
        dk = dot(ds_b[...], q_s[pl.ds(r, R), :], NN)
        dv = dot(p_b[...], do_s[pl.ds(r, R), :], NN)
        dq = dot(ds_b[...], kv_s[pl.ds(k, KB), :HD], TN)
        acc[pl.ds(k, KB), :HD] += dk
        acc[pl.ds(k, KB), HD:] += dv
        dq_s[pl.ds(r, R), :] += dq

    ss, dps, ps, dss = (s0, s1), (dp0, dp1), (p0, p1), (ds0, ds1)
    products(meta, 0, q_s, do_s, kv_s, s0, dp0)
    products(meta, 1, q_s, do_s, kv_s, s1, dp1)
    weights(0, s0, dp0, p0, ds0)

    def body(i, carry):
        for v in range(UNROLL):
            t, a, b = i * UNROLL + v, v % 2, 1 - v % 2
            products(meta, t + 2, q_s, do_s, kv_s, ss[a], dps[a])
            weights(t + 1, ss[b], dps[b], ps[b], dss[b])
            sums(t, ps[a], dss[a])
        return carry

    lax.fori_loop(0, (meta[COUNT] + UNROLL - 1) // UNROLL, body, 0)
    for d in range(4):
        for half in range(2):
            place = meta[UNIT + 2 * d + half]
            t = slice(half * SPAN, (half + 1) * SPAN)
            for h in range(HEADS):
                got = dq_s[pl.ds(row_of(place, h), SPAN), :] * SCALE
                dqs[d][t, h * HD : (h + 1) * HD] = got.astype(dqs[d].dtype)
    for c in range(2):
        for s in range(32):
            r = aligned(meta[OUT + c * 32 + s], SPAN)
            t = slice((s % 2) * SPAN, (s % 2 + 1) * SPAN)
            dkvs[c][s // 2, t, :HD] = (acc[pl.ds(r, SPAN), :HD] * SCALE).astype(jnp.bfloat16)
            dkvs[c][s // 2, t, HD:] = acc[pl.ds(r, SPAN), HD:].astype(jnp.bfloat16)


VM = pl.BlockSpec(memory_space=pltpu.VMEM)
SM = pl.BlockSpec(memory_space=pltpu.SMEM)
PARAMS = pltpu.CompilerParams(vmem_limit_bytes=48 * 2**20)
COPIES = [
    pltpu.VMEM(((GROUPS + 1) * R, HD), jnp.bfloat16),
    pltpu.VMEM(((GROUPS + 1) * R, HD), jnp.bfloat16),
    pltpu.VMEM((KEYS, 2 * HD), jnp.bfloat16),
] + [pltpu.VMEM((KB, R), jnp.float32)] * 4


def stats(meta, lim, arrays):
    return pl.pallas_call(
        stats_kernel,
        out_shape=jax.ShapeDtypeStruct((2, 16, R), jnp.float32),
        in_specs=[SM] + [VM] * 14,
        out_specs=VM,
        scratch_shapes=COPIES + [pltpu.VMEM((GROUPS + 1, 8, R), jnp.float32)] * 3,
        compiler_params=PARAMS,
        name="stats",
    )(meta, lim, *arrays)


def grads(meta, lim, sts, arrays):
    dq = [jax.ShapeDtypeStruct((2 * SPAN, WIDE), t) for t in (jnp.float32,) + (jnp.bfloat16,) * 3]
    dkv = [jax.ShapeDtypeStruct((16, 2 * SPAN, 2 * HD), jnp.bfloat16)] * 2
    return pl.pallas_call(
        grads_kernel,
        out_shape=dq + dkv,
        in_specs=[SM] + [VM] * 18,
        out_specs=[VM] * 6,
        scratch_shapes=COPIES
        + [
            pltpu.VMEM((KEYS, 2 * HD), jnp.float32),
            pltpu.VMEM(((GROUPS + 1) * R, HD), jnp.float32),
        ]
        + [pltpu.VMEM((KB, R), jnp.bfloat16)] * 4
        + [pltpu.VMEM((16, R), jnp.float32)] * 2,
        compiler_params=PARAMS,
        name="grads",
    )(meta, lim, *sts, *arrays)


def shift(a, axis, step):
    if axis == "z":
        at = lambda z: (z % 2) * 2 + z // 2
        return lax.ppermute(a, ("zl", "zh"), [(at(i), at((i + step) % 4)) for i in range(4)])
    return lax.ppermute(a, axis, [(i, (i + step) % 4) for i in range(4)])


def core_swap(a):
    return lax.ppermute(a, "core", [(0, 1), (1, 0)])


def plan(span_slot):
    i32 = jnp.int32
    y, zl, core, zh, x = (lax.axis_index(a) for a in AXES)
    z = 2 * zh + zl
    grid = span_slot.reshape(4, 2, 2, 2, 4, 2)
    own_x = jnp.transpose(lax.dynamic_index_in_dim(grid, x, 4, keepdims=False), (2, 0, 3, 1, 4))
    own_x = own_x.reshape(2, 4, 4, 2)
    own_x = jnp.where(core == 0, own_x, own_x[::-1])
    by_z = jnp.stack([lax.dynamic_index_in_dim(own_x, (z - r) % 4, 2, keepdims=False) for r in range(4)], 1)
    by_yz = jnp.stack([lax.dynamic_index_in_dim(by_z, (y - r) % 4, 2, keepdims=False) for r in range(4)], 2)
    arrived = by_yz.reshape(64)
    owners = jnp.transpose(own_x.reshape(2, 4, 2, 2, 2), (0, 1, 3, 2, 4)).reshape(64)
    ring = grid[y, zl, core, zh]
    queries = jnp.concatenate([ring[(x - r) % 4] for r in range(4)])

    def rank(a, among):
        return jnp.sum((among[None, :] < a[:, None]).astype(i32), axis=1)

    place = rank(queries, queries)
    hit = (place[None, :] == jnp.arange(8)[:, None]).astype(i32)
    spans = jnp.sum(hit * queries[None, :], axis=1)
    below = rank(spans, owners)
    own = jnp.any(owners[None, :] == spans[:, None], axis=1).astype(i32)
    token = jnp.tile(jnp.arange(SPAN, dtype=i32), 2)
    seen = below[:, None] * SPAN + own[:, None] * (token[None, :] + 1)
    a, b = seen[0::2], seen[1::2]
    lim = jnp.stack([a, a, a, b, b, b], axis=1).reshape(GROUPS, R)
    lim = jnp.concatenate([lim, jnp.zeros((4, R), i32)])
    tiles = ((below + own) * SPAN + KB - 1) // KB
    each = jnp.stack([tiles[0::2], tiles[1::2], tiles[1::2]], axis=1).reshape(GROUPS)
    end = jnp.sum(jnp.tril(jnp.ones((GROUPS, GROUPS), i32)) * each[None, :], axis=1)
    t = jnp.arange(LIST, dtype=i32)
    past = (t[:, None] >= end[None, :]).astype(i32)
    group = jnp.sum(past, axis=1)
    block = jnp.where(group < GROUPS, t - jnp.sum(past * each[None, :], axis=1), 0)
    meta = [rank(arrived, owners), rank(owners, owners), place, end[-1:], group, block]
    return jnp.concatenate(meta).astype(i32), lim


def local(queries, keys, values, grad_out, span_slot):
    meta, lim = plan(span_slot)
    qd0 = jnp.concatenate([queries, grad_out], axis=1)
    qd1, qd3 = shift(qd0, "x", 1), shift(qd0, "x", 3)
    q2, do2 = shift(qd3[:, :WIDE], "x", 3), shift(qd1[:, WIDE:], "x", 1)
    kv = jnp.concatenate([keys, values], axis=1)[None]
    kv = jnp.concatenate([kv] + [shift(kv, "y", r) for r in (1, 2, 3)], axis=0)
    kvs = [kv] + [shift(kv, "z", r) for r in (1, 2, 3)]
    arrays = [qd0, qd1, q2, do2, qd3] + kvs + [core_swap(a) for a in kvs]

    part = stats(meta, lim, arrays)
    sts = [part] + [shift(part, "x", r) for r in (1, 2, 3)]
    dq0, dq1, dq2, dq3, dkv, dkv_other = grads(meta, lim, sts, arrays)

    pair = (dkv.astype(jnp.float32) + core_swap(dkv_other).astype(jnp.float32)).astype(jnp.bfloat16)
    parts = lax.all_to_all(pair, ("y", "zl", "zh"), 0, 0, tiled=True)
    summed = jnp.sum(parts.astype(jnp.float32), axis=0)
    for r, part in ((1, dq1), (2, dq2), (3, dq3)):
        dq0 = dq0 + shift(part, "x", 4 - r).astype(jnp.float32)
    return (
        dq0.astype(jnp.bfloat16),
        summed[:, :HD].astype(jnp.bfloat16),
        summed[:, HD:].astype(jnp.bfloat16),
    )


def solution(mesh):
    fine = Mesh(mesh.devices.reshape(4, 2, 2, 2, 4), AXES)
    rows = P(AXES, None)
    return jax.shard_map(
        local,
        mesh=fine,
        in_specs=(rows, rows, rows, rows, P()),
        out_specs=(rows, rows, rows),
        check_vma=False,
    )
```

time: 137 us -> 125 us (0.912)
  Pallas kernels: 64.1 us -> 39.7 us
  local copies, waits for them, and re-layouts: 4.64 us -> 9.5 us
  starting transfers between devices: 25.1 us -> 28.3 us
  waiting for transfers between devices: 38.7 us -> 41.4 us
    pallas_call x2, Pallas kernels: 64.1 us -> 39.7 us  [the longest x1 25.4 us: grads(): pl.pallas_call(grads_kernel, out_shape=dq + dkv, in_specs=[SM] + [VM] * 1...]
    ppermute x9 -> x16, waiting for transfers between devices: 18.9 us -> 34.6 us  [the longest x13 23 us: shift(): return lax.ppermute(a, axis, [(i, (i + step) % 4) for i in range(4)])]
    all_to_all x1 -> x0, waiting for transfers between devices: 13.1 us -> none  [local(): lax.all_to_all(jnp.broadcast_to(kv[None], (16,) + kv.shape), ('y', 'zl',...]
    ppermute x9 -> x16, starting transfers between devices: 10.3 us -> 21 us  [the longest x13 15.6 us: shift(): return lax.ppermute(a, axis, [(i, (i + step) % 4) for i in range(4)])]
    all_to_all x1 -> x0, starting transfers between devices: 8.13 us -> none  [local(): lax.all_to_all(jnp.broadcast_to(kv[None], (16,) + kv.shape), ('y', 'zl',...]
    unnamed x13 -> x19, local copies, waits for them, and re-layouts: 0.92 us -> 3.76 us
    slice x4 -> x7, local copies, waits for them, and re-layouts: 0.02 us -> 2.18 us  [the longest x2 1.38 us: local(): q2, do2 = (shift(qd3[:, :WIDE], 'x', 3), shift(qd1[:, WIDE:], 'x', 1))]
    concatenate x1 -> x3, local copies, waits for them, and re-layouts: 0.02 us -> 1.68 us  [the longest x1 0.94 us: local(): qd0 = jnp.concatenate([queries, grad_out], axis=1)]
  transfers between devices with their start and end apart: 13 -> 22, of which waited for: 10 -> 13; matrix products, arithmetic and copies ran while one was open for 2% -> 7% of each run, Pallas kernels for 0% -> 0%
where the time goes in v2:
time: 125 us; the launch traced here: 124 us
  waiting for transfers between devices  41.4 us (33%)
  Pallas kernels  39.7 us (32%)
  starting transfers between devices  28.3 us (23%)
  local copies, waits for them, and re-layouts  9.5 us (8%)
  other arithmetic  4.41 us (4%)
    pallas_call x1, Pallas kernels, grads(): pl.pallas_call(grads_kernel, out_shape=dq + dkv, in_specs=[SM] + [VM] * 1...  25.4 us
    ppermute x13, waiting for transfers between devices, shift(): return lax.ppermute(a, axis, [(i, (i + step) % 4) for i in range(4)])  23 us
    ppermute x13, starting transfers between devices, shift(): return lax.ppermute(a, axis, [(i, (i + step) % 4) for i in range(4)])  15.6 us
    pallas_call x1, Pallas kernels, stats(): pl.pallas_call(stats_kernel, out_shape=jax.ShapeDtypeStruct((2, 16, R), j...  14.2 us
    ppermute x3, waiting for transfers between devices, shift(): lax.ppermute(a, ('zl', 'zh'), [(at(i), at((i + step) % 4)) for i in range...  11.6 us
    all_to_all x1, starting transfers between devices, local(): parts = lax.all_to_all(pair, ('y', 'zl', 'zh'), 0, 0, tiled=True)  6.79 us
    ppermute x3, starting transfers between devices, shift(): lax.ppermute(a, ('zl', 'zh'), [(at(i), at((i + step) % 4)) for i in range...  5.36 us
    all_to_all x1, waiting for transfers between devices, local(): parts = lax.all_to_all(pair, ('y', 'zl', 'zh'), 0, 0, tiled=True)  3.93 us
  transfers between devices with their start and end apart: 22, of which 13 were waited for; matrix products, arithmetic and copies ran while one was open for 7% of the time, Pallas kernels for 0%

profile of v2, /device:TPU:0, one launch (start us, length us, event | category | flops | bytes accessed | tf_op | source)
XLA Modules:
  0.0 124.2 jit_solution(5268375560365794634)
XLA Ops:
  1.4 3.2 %collective-permute-start.6 = (bf16[1,128,256]{2,1,0:T(8,128)(2,1)S(1)}, bf16[1,128,256]{2,1,0:T(8,128)(2,1)S(1)}, u32[]{:S(2)}, u32[]{:S(2)}) collective-permute-start(bf16[1,128,256]{2,1,0:T(8,128)(2,1)S(1)} %maximum_bitcast_fusion), channel_id=1, source_target_pairs={{0,96},{32,0},{64,32},{96,64},{1,97},{33,1},{65,33},{97,65},{2,98}... | collective-permute-start | bytes 196616 | tf_op jit(solution)/shard_map/ppermute | solution.py:243
  5.2 1.0 collective-permute-start.4
  8.1 2.8 %collective-permute-start.1 = (bf16[128,1536]{1,0:T(8,128)(2,1)S(1)}, bf16[128,1536]{1,0:T(8,128)(2,1)S(1)}, u32[]{:S(2)}, u32[]{:S(2)}) collective-permute-start(bf16[128,1536]{1,0:T(8,128)(2,1)S(1)} %constant_dynamic-update-slice_fusion.refs_0_), channel_id=1, source_target_pairs={{0,3},{1,0},{2,1},{3,2},{4,7},{5,4},{6,5},{7,6},{8,11},{9,8},{10,9... | collective-permute-start | bytes 1179656 | tf_op jit(solution)/shard_map/ppermute | solution.py:243
  12.6 4.1 %collective-permute-start.9 = (bf16[4,128,256]{2,1,0:T(8,128)(2,1)S(1)}, bf16[4,128,256]{2,1,0:T(8,128)(2,1)S(1)}, u32[]{:S(2)}, u32[]{:S(2)}) collective-permute-start(bf16[4,128,256]{2,1,0:T(8,128)(2,1)S(1)} %pad_maximum_fusion.refs_5_), channel_id=1, source_target_pairs={{0,20},{16,0},{4,16},{20,4},{1,21},{17,1},{5,17},{21,5},{2,22},{18... | collective-permute-start | bytes 786440 | tf_op jit(solution)/shard_map/ppermute | solution.py:242
  17.2 1.2 %collective-permute-start.7 = (bf16[4,128,256]{2,1,0:T(8,128)(2,1)S(1)}, bf16[4,128,256]{2,1,0:T(8,128)(2,1)S(1)}, u32[]{:S(2)}, u32[]{:S(2)}) collective-permute-start(bf16[4,128,256]{2,1,0:T(8,128)(2,1)S(1)} %pad_maximum_fusion.refs_5_), channel_id=1, source_target_pairs={{0,16},{16,4},{4,20},{20,0},{1,17},{17,5},{5,21},{21,1},{2,18},{18... | collective-permute-start | bytes 786440 | tf_op jit(solution)/shard_map/ppermute | solution.py:242
  18.6 8.2 %collective-permute-done.9.refs_8_ = bf16[4,128,256]{2,1,0:T(8,128)(2,1)S(1)} collective-permute-done((bf16[4,128,256]{2,1,0:T(8,128)(2,1)S(1)}, bf16[4,128,256]{2,1,0:T(8,128)(2,1)S(1)}, u32[]{:S(2)}, u32[]{:S(2)}) %collective-permute-start.9) | collective-permute-done | bytes 262176 | tf_op jit(solution)/shard_map/ppermute | solution.py:242
  28.0 2.8 %collective-permute-done.7.refs_6_ = bf16[4,128,256]{2,1,0:T(8,128)(2,1)S(1)} collective-permute-done((bf16[4,128,256]{2,1,0:T(8,128)(2,1)S(1)}, bf16[4,128,256]{2,1,0:T(8,128)(2,1)S(1)}, u32[]{:S(2)}, u32[]{:S(2)}) %collective-permute-start.7) | collective-permute-done | bytes 262176 | tf_op jit(solution)/shard_map/ppermute | solution.py:242
  32.7 3.0 %collective-permute-start.2 = (bf16[128,768]{1,0:T(8,128)(2,1)}, bf16[128,768]{1,0:T(8,128)(2,1)S(1)}, u32[]{:S(2)}, u32[]{:S(2)}) collective-permute-start(bf16[128,768]{1,0:T(8,128)(2,1)} %slice.39), channel_id=1, source_target_pairs={{0,3},{1,0},{2,1},{3,2},{4,7},{5,4},{6,5},{7,6},{8,11},{9,8},{10,9... | collective-permute-start | bytes 589832 | tf_op jit(solution)/shard_map/ppermute | solution.py:243
  37.1 3.2 %collective-permute-done.2.refs_2_ = bf16[128,768]{1,0:T(8,128)(2,1)S(1)} collective-permute-done((bf16[128,768]{1,0:T(8,128)(2,1)}, bf16[128,768]{1,0:T(8,128)(2,1)S(1)}, u32[]{:S(2)}, u32[]{:S(2)}) %collective-permute-start.2) | collective-permute-done | bytes 196640 | tf_op jit(solution)/shard_map/ppermute | solution.py:243
  40.3 4.1 %collective-permute-done.3.refs_3_ = bf16[128,768]{1,0:T(8,128)(2,1)} collective-permute-done((bf16[128,768]{1,0:T(8,128)(2,1)}, bf16[128,768]{1,0:T(8,128)(2,1)}, u32[]{:S(2)}, u32[]{:S(2)}) %collective-permute-start.3) | collective-permute-done | bytes 196640 | tf_op jit(solution)/shard_map/ppermute | solution.py:243
  44.4 14.2 %stats.1.st0 = f32[2,16,256]{2,1,0:T(8,128)S(1)} custom-call(s32[409]{0:T(512)S(1)} %concatenate.19.meta, s32[16,256]{1,0:T(8,128)S(1)} %concatenate.20.lim, bf16[128,1536]{1,0:T(8,128)(2,1)S(1)} %constant_dynamic-update-slice_fusion.refs_0_, bf16[128,1536]{1,0:T(8,128)(2,1)S(1)} %collective-permute-done.refs_1_, ...), custom_call_target="tpu_custom_call" | custom-call | tf_op jit(solution)/shard_map/stats/pallas_call | solution.py:208
  58.8 1.1 collective-permute-start.15
  60.8 1.9 %collective-permute-done.16.st3 = f32[2,16,256]{2,1,0:T(8,128)S(1)} collective-permute-done((f32[2,16,256]{2,1,0:T(8,128)S(1)}, f32[2,16,256]{2,1,0:T(8,128)S(1)}, u32[]{:S(2)}, u32[]{:S(2)}) %collective-permute-start.16) | collective-permute-done | bytes 32800 | tf_op jit(solution)/shard_map/ppermute | solution.py:243
  62.7 1.8 %collective-permute-done.15.st2 = f32[2,16,256]{2,1,0:T(8,128)S(1)} collective-permute-done((f32[2,16,256]{2,1,0:T(8,128)S(1)}, f32[2,16,256]{2,1,0:T(8,128)S(1)}, u32[]{:S(2)}, u32[]{:S(2)}) %collective-permute-start.15) | collective-permute-done | bytes 32800 | tf_op jit(solution)/shard_map/ppermute | solution.py:243
  65.4 25.4 %grads.1 = (f32[128,768]{1,0:T(8,128)S(1)}, bf16[128,768]{1,0:T(8,128)(2,1)S(1)}, bf16[128,768]{1,0:T(8,128)(2,1)S(1)}, bf16[128,768]{1,0:T(8,128)(2,1)S(1)}, bf...) custom-call(s32[409]{0:T(512)S(1)} %concatenate.19.meta, s32[16,256]{1,0:T(8,128)S(1)} %concatenate.20.lim, ...), custom_call_target="tpu_custom_call" | custom-call | tf_op jit(solution)/shard_map/grads/pallas_call | solution.py:222
  93.6 2.9 %collective-permute-done.20 = bf16[16,128,256]{2,1,0:T(8,128)(2,1)S(1)} collective-permute-done((bf16[16,128,256]{2,1,0:T(8,128)(2,1)}, bf16[16,128,256]{2,1,0:T(8,128)(2,1)S(1)}, u32[]{:S(2)}, u32[]{:S(2)}) %collective-permute-start.20) | collective-permute-done | bytes 1048608 | tf_op jit(solution)/shard_map/ppermute | solution.py:247
  96.5 1.3 %add_convert_fusion = bf16[16,128,256]{2,1,0:T(8,128)(2,1)} fusion(bf16[16,128,256]{2,1,0:T(8,128)(2,1)S(1)} %collective-permute-done.20, bf16[16,128,256]{2,1,0:T(8,128)(2,1)S(1)} %get-tuple-element.13), kind=kLoop, calls=%fused_computation | loop fusion | flops 2097152 | bytes 3145728 | tf_op jit(solution)/shard_map/convert_element_type | solution.py:303
  97.8 6.8 %all-to-all-start = ((bf16[16,128,256]{2,1,0:T(8,128)(2,1)}), bf16[16,128,256]{2,1,0:T(8,128)(2,1)S(1)}, u32[]{:S(2)}, u32[]{:S(2)}) async-start(bf16[16,128,256]{2,1,0:T(8,128)(2,1)} %add_convert_fusion), calls=%async_computation | async-start | bytes 2097152 | tf_op jit(solution)/shard_map/all_to_all | solution.py:304
  104.6 2.0 %collective-permute-start.17 = (bf16[128,768]{1,0:T(8,128)(2,1)S(1)}, bf16[128,768]{1,0:T(8,128)(2,1)S(1)}, u32[]{:S(2)}, u32[]{:S(2)}) collective-permute-start(bf16[128,768]{1,0:T(8,128)(2,1)S(1)} %copy-done.7), channel_id=1, source_target_pairs={{0,3},{1,0},{2,1},{3,2},{4,7},{5,4},{6,5},{7,6},{8,11},{9,8},{10,9... | collective-permute-start | bytes 589832 | tf_op jit(solution)/shard_map/ppermute | solution.py:243
  106.7 1.0 collective-permute-start.18
  107.6 7.5 %collective-permute-done.17 = bf16[128,768]{1,0:T(8,128)(2,1)S(1)} collective-permute-done((bf16[128,768]{1,0:T(8,128)(2,1)S(1)}, bf16[128,768]{1,0:T(8,128)(2,1)S(1)}, u32[]{:S(2)}, u32[]{:S(2)}) %collective-permute-start.17) | collective-permute-done | bytes 196640 | tf_op jit(solution)/shard_map/ppermute | solution.py:243
  115.1 1.0 collective-permute-done.18
  116.0 2.7 %collective-permute-done.19 = bf16[128,768]{1,0:T(8,128)(2,1)S(1)} collective-permute-done((bf16[128,768]{1,0:T(8,128)(2,1)S(1)}, bf16[128,768]{1,0:T(8,128)(2,1)S(1)}, u32[]{:S(2)}, u32[]{:S(2)}) %collective-permute-start.19) | collective-permute-done | bytes 196640 | tf_op jit(solution)/shard_map/ppermute | solution.py:243
  119.5 3.9 %all-to-all-done = bf16[16,128,256]{2,1,0:T(8,128)(2,1)S(1)} async-done(((bf16[16,128,256]{2,1,0:T(8,128)(2,1)}), bf16[16,128,256]{2,1,0:T(8,128)(2,1)S(1)}, u32[]{:S(2)}, u32[]{:S(2)}) %all-to-all-start) | async-done | bytes 1048608 | tf_op jit(solution)/shard_map/all_to_all | solution.py:304
  (89 shorter events, 16.3 us)
Async XLA Ops:
  0.6 10.3 %copy-start.8 = (s32[256]{0:T(256)S(1)}, s32[256]{0:T(256)}, u32[]{:S(2)}) copy-start(s32[256]{0:T(256)} %param.9) | copy-start | bytes 3076
  1.4 11.1 %collective-permute-start.6 = (bf16[1,128,256]{2,1,0:T(8,128)(2,1)S(1)}, bf16[1,128,256]{2,1,0:T(8,128)(2,1)S(1)}, u32[]{:S(2)}, u32[]{:S(2)}) collective-permute-start(bf16[1,128,256]{2,1,0:T(8,128)(2,1)S(1)} %maximum_bitcast_fusion), channel_id=1, source_target_pairs={{0,96},{32,0},{64,32},{96,64},{1,97},{33,1},{65,33},{97,65},{2,98}... | collective-permute-start | bytes 196616 | tf_op jit(solution)/shard_map/ppermute | solution.py:243
  4.6 7.9 %collective-permute-start.5 = (bf16[1,128,256]{2,1,0:T(8,128)(2,1)S(1)}, bf16[1,128,256]{2,1,0:T(8,128)(2,1)S(1)}, u32[]{:S(2)}, u32[]{:S(2)}) collective-permute-start(bf16[1,128,256]{2,1,0:T(8,128)(2,1)S(1)} %maximum_bitcast_fusion), channel_id=1, source_target_pairs={{0,64},{32,96},{64,0},{96,32},{1,65},{33,97},{65,1},{97,33},{2,66}... | collective-permute-start | bytes 196616 | tf_op jit(solution)/shard_map/ppermute | solution.py:243
  5.2 7.3 %collective-permute-start.4 = (bf16[1,128,256]{2,1,0:T(8,128)(2,1)S(1)}, bf16[1,128,256]{2,1,0:T(8,128)(2,1)S(1)}, u32[]{:S(2)}, u32[]{:S(2)}) collective-permute-start(bf16[1,128,256]{2,1,0:T(8,128)(2,1)S(1)} %maximum_bitcast_fusion), channel_id=1, source_target_pairs={{0,32},{32,64},{64,96},{96,0},{1,33},{33,65},{65,97},{97,1},{2,34}... | collective-permute-start | bytes 196616 | tf_op jit(solution)/shard_map/ppermute | solution.py:243
  8.1 22.7 %collective-permute-start.1 = (bf16[128,1536]{1,0:T(8,128)(2,1)S(1)}, bf16[128,1536]{1,0:T(8,128)(2,1)S(1)}, u32[]{:S(2)}, u32[]{:S(2)}) collective-permute-start(bf16[128,1536]{1,0:T(8,128)(2,1)S(1)} %constant_dynamic-update-slice_fusion.refs_0_), channel_id=1, source_target_pairs={{0,3},{1,0},{2,1},{3,2},{4,7},{5,4},{6,5},{7,6},{8,11},{9,8},{10,9... | collective-permute-start | bytes 1179656 | tf_op jit(solution)/shard_map/ppermute | solution.py:243
  10.9 21.8 %collective-permute-start = (bf16[128,1536]{1,0:T(8,128)(2,1)S(1)}, bf16[128,1536]{1,0:T(8,128)(2,1)S(1)}, u32[]{:S(2)}, u32[]{:S(2)}) collective-permute-start(bf16[128,1536]{1,0:T(8,128)(2,1)S(1)} %constant_dynamic-update-slice_fusion.refs_0_), channel_id=1, source_target_pairs={{0,1},{1,2},{2,3},{3,0},{4,5},{5,6},{6,7},{7,4},{8,9},{9,10},{10,1... | collective-permute-start | bytes 1179656 | tf_op jit(solution)/shard_map/ppermute | solution.py:243
  12.6 14.2 %collective-permute-start.9 = (bf16[4,128,256]{2,1,0:T(8,128)(2,1)S(1)}, bf16[4,128,256]{2,1,0:T(8,128)(2,1)S(1)}, u32[]{:S(2)}, u32[]{:S(2)}) collective-permute-start(bf16[4,128,256]{2,1,0:T(8,128)(2,1)S(1)} %pad_maximum_fusion.refs_5_), channel_id=1, source_target_pairs={{0,20},{16,0},{4,16},{20,4},{1,21},{17,1},{5,17},{21,5},{2,22},{18... | collective-permute-start | bytes 786440 | tf_op jit(solution)/shard_map/ppermute | solution.py:242
  17.2 10.8 %collective-permute-start.8 = (bf16[4,128,256]{2,1,0:T(8,128)(2,1)S(1)}, bf16[4,128,256]{2,1,0:T(8,128)(2,1)S(1)}, u32[]{:S(2)}, u32[]{:S(2)}) collective-permute-start(bf16[4,128,256]{2,1,0:T(8,128)(2,1)S(1)} %pad_maximum_fusion.refs_5_), channel_id=1, source_target_pairs={{0,4},{16,20},{4,0},{20,16},{1,5},{17,21},{5,1},{21,17},{2,6},{18,... | collective-permute-start | bytes 786440 | tf_op jit(solution)/shard_map/ppermute | solution.py:242
  17.2 13.5 %collective-permute-start.7 = (bf16[4,128,256]{2,1,0:T(8,128)(2,1)S(1)}, bf16[4,128,256]{2,1,0:T(8,128)(2,1)S(1)}, u32[]{:S(2)}, u32[]{:S(2)}) collective-permute-start(bf16[4,128,256]{2,1,0:T(8,128)(2,1)S(1)} %pad_maximum_fusion.refs_5_), channel_id=1, source_target_pairs={{0,16},{16,4},{4,20},{20,0},{1,17},{17,5},{5,21},{21,1},{2,18},{18... | collective-permute-start | bytes 786440 | tf_op jit(solution)/shard_map/ppermute | solution.py:242
  26.8 9.6 %collective-permute-start.10 = (bf16[4,128,256]{2,1,0:T(8,128)(2,1)S(1)}, bf16[4,128,256]{2,1,0:T(8,128)(2,1)S(1)}, u32[]{:S(2)}, u32[]{:S(2)}) collective-permute-start(bf16[4,128,256]{2,1,0:T(8,128)(2,1)S(1)} %pad_maximum_fusion.refs_5_), channel_id=1, source_target_pairs={{0,8},{8,0},{1,9},{9,1},{2,10},{10,2},{3,11},{11,3},{4,12},{12,4},... | collective-permute-start | bytes 786440 | tf_op jit(solution)/shard_map/ppermute | solution.py:247
  28.0 9.2 %collective-permute-start.13 = (bf16[4,128,256]{2,1,0:T(8,128)(2,1)S(1)}, bf16[4,128,256]{2,1,0:T(8,128)(2,1)S(1)}, u32[]{:S(2)}, u32[]{:S(2)}) collective-permute-start(bf16[4,128,256]{2,1,0:T(8,128)(2,1)S(1)} %collective-permute-done.9.refs_8_), channel_id=1, source_target_pairs={{0,8},{8,0},{1,9},{9,1},{2,10},{10,2},{3,11},{11,3},{4,12},{12,4},... | collective-permute-start | bytes 786440 | tf_op jit(solution)/shard_map/ppermute | solution.py:247
  30.8 6.4 %collective-permute-start.12 = (bf16[4,128,256]{2,1,0:T(8,128)(2,1)S(1)}, bf16[4,128,256]{2,1,0:T(8,128)(2,1)S(1)}, u32[]{:S(2)}, u32[]{:S(2)}) collective-permute-start(bf16[4,128,256]{2,1,0:T(8,128)(2,1)S(1)} %collective-permute-done.8.refs_7_), channel_id=1, source_target_pairs={{0,8},{8,0},{1,9},{9,1},{2,10},{10,2},{3,11},{11,3},{4,12},{12,4},... | collective-permute-start | bytes 786440 | tf_op jit(solution)/shard_map/ppermute | solution.py:247
  30.8 6.4 %collective-permute-start.11 = (bf16[4,128,256]{2,1,0:T(8,128)(2,1)S(1)}, bf16[4,128,256]{2,1,0:T(8,128)(2,1)S(1)}, u32[]{:S(2)}, u32[]{:S(2)}) collective-permute-start(bf16[4,128,256]{2,1,0:T(8,128)(2,1)S(1)} %collective-permute-done.7.refs_6_), channel_id=1, source_target_pairs={{0,8},{8,0},{1,9},{9,1},{2,10},{10,2},{3,11},{11,3},{4,12},{12,4},... | collective-permute-start | bytes 786440 | tf_op jit(solution)/shard_map/ppermute | solution.py:247
  32.7 7.6 %collective-permute-start.2 = (bf16[128,768]{1,0:T(8,128)(2,1)}, bf16[128,768]{1,0:T(8,128)(2,1)S(1)}, u32[]{:S(2)}, u32[]{:S(2)}) collective-permute-start(bf16[128,768]{1,0:T(8,128)(2,1)} %slice.39), channel_id=1, source_target_pairs={{0,3},{1,0},{2,1},{3,2},{4,7},{5,4},{6,5},{7,6},{8,11},{9,8},{10,9... | collective-permute-start | bytes 589832 | tf_op jit(solution)/shard_map/ppermute | solution.py:243
  36.4 8.1 %collective-permute-start.3 = (bf16[128,768]{1,0:T(8,128)(2,1)}, bf16[128,768]{1,0:T(8,128)(2,1)}, u32[]{:S(2)}, u32[]{:S(2)}) collective-permute-start(bf16[128,768]{1,0:T(8,128)(2,1)} %slice.40), channel_id=1, source_target_pairs={{0,1},{1,2},{2,3},{3,0},{4,5},{5,6},{6,7},{7,4},{8,9},{9,10},{10,1... | collective-permute-start | bytes 589832 | tf_op jit(solution)/shard_map/ppermute | solution.py:243
  58.7 4.0 %collective-permute-start.16 = (f32[2,16,256]{2,1,0:T(8,128)S(1)}, f32[2,16,256]{2,1,0:T(8,128)S(1)}, u32[]{:S(2)}, u32[]{:S(2)}) collective-permute-start(f32[2,16,256]{2,1,0:T(8,128)S(1)} %stats.1.st0), channel_id=1, source_target_pairs={{0,3},{1,0},{2,1},{3,2},{4,7},{5,4},{6,5},{7,6},{8,11},{9,8},{10,9... | collective-permute-start | bytes 98312 | tf_op jit(solution)/shard_map/ppermute | solution.py:243
  58.8 5.7 %collective-permute-start.15 = (f32[2,16,256]{2,1,0:T(8,128)S(1)}, f32[2,16,256]{2,1,0:T(8,128)S(1)}, u32[]{:S(2)}, u32[]{:S(2)}) collective-permute-start(f32[2,16,256]{2,1,0:T(8,128)S(1)} %stats.1.st0), channel_id=1, source_target_pairs={{0,2},{1,3},{2,0},{3,1},{4,6},{5,7},{6,4},{7,5},{8,10},{9,11},{10,... | collective-permute-start | bytes 98312 | tf_op jit(solution)/shard_map/ppermute | solution.py:243
  59.9 5.5 %collective-permute-start.14 = (f32[2,16,256]{2,1,0:T(8,128)S(1)}, f32[2,16,256]{2,1,0:T(8,128)S(1)}, u32[]{:S(2)}, u32[]{:S(2)}) collective-permute-start(f32[2,16,256]{2,1,0:T(8,128)S(1)} %stats.1.st0), channel_id=1, source_target_pairs={{0,1},{1,2},{2,3},{3,0},{4,5},{5,6},{6,7},{7,4},{8,9},{9,10},{10,1... | collective-permute-start | bytes 98312 | tf_op jit(solution)/shard_map/ppermute | solution.py:243
  93.6 2.9 %collective-permute-start.20 = (bf16[16,128,256]{2,1,0:T(8,128)(2,1)}, bf16[16,128,256]{2,1,0:T(8,128)(2,1)S(1)}, u32[]{:S(2)}, u32[]{:S(2)}) collective-permute-start(bf16[16,128,256]{2,1,0:T(8,128)(2,1)} %get-tuple-element.14), channel_id=1, source_target_pairs={{0,8},{8,0},{1,9},{9,1},{2,10},{10,2},{3,11},{11,3},{4,12},{12,4},... | collective-permute-start | bytes 3145736 | tf_op jit(solution)/shard_map/ppermute | solution.py:247
  97.8 21.0 %copy-start.1 = (f32[128,768]{1,0:T(8,128)S(1)}, f32[128,768]{1,0:T(8,128)}, u32[]{:S(2)}) copy-start(f32[128,768]{1,0:T(8,128)} %copy-done) | copy-start | bytes 1179652
  97.8 25.7 %all-to-all-start = ((bf16[16,128,256]{2,1,0:T(8,128)(2,1)}), bf16[16,128,256]{2,1,0:T(8,128)(2,1)S(1)}, u32[]{:S(2)}, u32[]{:S(2)}) async-start(bf16[16,128,256]{2,1,0:T(8,128)(2,1)} %add_convert_fusion), calls=%async_computation | async-start | bytes 2097152 | tf_op jit(solution)/shard_map/all_to_all | solution.py:304
  104.6 10.5 %collective-permute-start.17 = (bf16[128,768]{1,0:T(8,128)(2,1)S(1)}, bf16[128,768]{1,0:T(8,128)(2,1)S(1)}, u32[]{:S(2)}, u32[]{:S(2)}) collective-permute-start(bf16[128,768]{1,0:T(8,128)(2,1)S(1)} %copy-done.7), channel_id=1, source_target_pairs={{0,3},{1,0},{2,1},{3,2},{4,7},{5,4},{6,5},{7,6},{8,11},{9,8},{10,9... | collective-permute-start | bytes 589832 | tf_op jit(solution)/shard_map/ppermute | solution.py:243
  106.7 9.4 %collective-permute-start.18 = (bf16[128,768]{1,0:T(8,128)(2,1)S(1)}, bf16[128,768]{1,0:T(8,128)(2,1)S(1)}, u32[]{:S(2)}, u32[]{:S(2)}) collective-permute-start(bf16[128,768]{1,0:T(8,128)(2,1)S(1)} %copy-done.5), channel_id=1, source_target_pairs={{0,2},{1,3},{2,0},{3,1},{4,6},{5,7},{6,4},{7,5},{8,10},{9,11},{10,... | collective-permute-start | bytes 589832 | tf_op jit(solution)/shard_map/ppermute | solution.py:243
  107.6 11.1 %collective-permute-start.19 = (bf16[128,768]{1,0:T(8,128)(2,1)S(1)}, bf16[128,768]{1,0:T(8,128)(2,1)S(1)}, u32[]{:S(2)}, u32[]{:S(2)}) collective-permute-start(bf16[128,768]{1,0:T(8,128)(2,1)S(1)} %copy-done.3), channel_id=1, source_target_pairs={{0,1},{1,2},{2,3},{3,0},{4,5},{5,6},{6,7},{7,4},{8,9},{9,10},{10,1... | collective-permute-start | bytes 589832 | tf_op jit(solution)/shard_map/ppermute | solution.py:243
  (7 other events, 28.3 us)

commit v3 on v2

--- a/solution.py
+++ b/solution.py
@@ -2,12 +2,15 @@
 
 import jax
 import jax.numpy as jnp
+import numpy as np
 from jax import lax
 from jax.experimental import pallas as pl
 from jax.experimental.pallas import tpu as pltpu
 from jax.sharding import Mesh, PartitionSpec as P
 
 AXES = ("y", "zl", "core", "zh", "x")
+SIZES = (4, 2, 2, 2, 4)
+STEPS = (0, 1, 3, 2)
 NEG = -1e30
 HD = 128
 SCALE = 1.0 / math.sqrt(HD)
@@ -21,8 +24,8 @@
 GROUPS = 12
 UNROLL = 8
 LIST = 136
-IN, OUT, UNIT, COUNT = 0, 64, 128, 136
-GROUP, BLOCK = 137, 137 + LIST
+IN, UNIT, COUNT = 0, 64, 72
+GROUP, BLOCK = 73, 73 + LIST
 
 NT = (((1,), (1,)), ((), ()))
 NN = (((1,), (0,)), ((), ()))
@@ -60,15 +63,15 @@
     return pl.multiple_of((place // 2) * 768 + inner, SPAN)
 
 
-def load_rows(meta, qs, dos, q_s, do_s):
-    for d in range(4):
+def load_rows(meta, qds, q_s, do_s):
+    for d, ref in enumerate(qds):
         for half in range(2):
             place = meta[UNIT + 2 * d + half]
             t = slice(half * SPAN, (half + 1) * SPAN)
             for h in range(HEADS):
                 r = row_of(place, h)
-                for (ref, first), dst in ((qs[d], q_s), (dos[d], do_s)):
-                    dst[pl.ds(r, SPAN), :] = ref[t, first + h * HD : first + (h + 1) * HD]
+                q_s[pl.ds(r, SPAN), :] = ref[t, h * HD : (h + 1) * HD]
+                do_s[pl.ds(r, SPAN), :] = ref[t, WIDE + h * HD : WIDE + (h + 1) * HD]
     q_s[GROUPS * R :, :] = jnp.zeros((R, HD), q_s.dtype)
     do_s[GROUPS * R :, :] = jnp.zeros((R, HD), do_s.dtype)
 
@@ -79,18 +82,11 @@
     dp_b[...] = dot(kv_s[pl.ds(k, KB), HD:], do_s[pl.ds(r, R), :], NT)
 
 
-def operands(refs):
-    qd0, qd1, q2, do2, qd3 = refs[:5]
-    qs = ((qd0, 0), (qd1, 0), (q2, 0), (qd3, 0))
-    dos = ((qd0, WIDE), (qd1, WIDE), (do2, 0), (qd3, WIDE))
-    return qs, dos, refs[5:13]
-
-
 def stats_kernel(meta, lim, *refs):
-    qs, dos, kvs = operands(refs)
-    out, q_s, do_s, kv_s, s0, s1, dp0, dp1, m_s, l_s, d_s = refs[13:]
+    qds, kvs = refs[:4], refs[4:12]
+    out, q_s, do_s, kv_s, s0, s1, dp0, dp1, m_s, l_s, d_s = refs[12:]
     load_sorted(meta, kvs, kv_s)
-    load_rows(meta, qs, dos, q_s, do_s)
+    load_rows(meta, qds, q_s, do_s)
     m_s[...] = jnp.full_like(m_s, NEG)
     l_s[...] = jnp.zeros_like(l_s)
     d_s[...] = jnp.zeros_like(d_s)
@@ -134,11 +130,11 @@
 
 
 def grads_kernel(meta, lim, st0, st1, st2, st3, *refs):
-    qs, dos, kvs = operands(refs)
-    dqs, dkvs = refs[13:17], refs[17:19]
-    q_s, do_s, kv_s, s0, s1, dp0, dp1, acc, dq_s, p0, p1, ds0, ds1, lse, delta = refs[19:]
+    qds, kvs = refs[:4], refs[4:12]
+    dqs, dkvs, dkv_other = refs[12:16], refs[16:20], refs[20]
+    q_s, do_s, kv_s, s0, s1, dp0, dp1, acc, dq_s, p0, p1, ds0, ds1, lse, delta = refs[21:]
     load_sorted(meta, kvs, kv_s)
-    load_rows(meta, qs, dos, q_s, do_s)
+    load_rows(meta, qds, q_s, do_s)
     acc[...] = jnp.zeros_like(acc)
     dq_s[...] = jnp.zeros_like(dq_s)
     sts = (st0, st1, st2, st3)
@@ -186,12 +182,13 @@
             for h in range(HEADS):
                 got = dq_s[pl.ds(row_of(place, h), SPAN), :] * SCALE
                 dqs[d][t, h * HD : (h + 1) * HD] = got.astype(dqs[d].dtype)
-    for c in range(2):
-        for s in range(32):
-            r = aligned(meta[OUT + c * 32 + s], SPAN)
-            t = slice((s % 2) * SPAN, (s % 2 + 1) * SPAN)
-            dkvs[c][s // 2, t, :HD] = (acc[pl.ds(r, SPAN), :HD] * SCALE).astype(jnp.bfloat16)
-            dkvs[c][s // 2, t, HD:] = acc[pl.ds(r, SPAN), HD:].astype(jnp.bfloat16)
+    for s in range(64):
+        r = aligned(meta[IN + s], SPAN)
+        t = slice((s % 2) * SPAN, (s % 2 + 1) * SPAN)
+        e = (s // 2) % 4
+        ref = dkvs[s // 8] if s < 32 else dkv_other.at[s // 8 - 4]
+        ref[e, t, :HD] = (acc[pl.ds(r, SPAN), :HD] * SCALE).astype(jnp.bfloat16)
+        ref[e, t, HD:] = acc[pl.ds(r, SPAN), HD:].astype(jnp.bfloat16)
 
 
 VM = pl.BlockSpec(memory_space=pltpu.VMEM)
@@ -208,7 +205,7 @@
     return pl.pallas_call(
         stats_kernel,
         out_shape=jax.ShapeDtypeStruct((2, 16, R), jnp.float32),
-        in_specs=[SM] + [VM] * 14,
+        in_specs=[SM] + [VM] * 13,
         out_specs=VM,
         scratch_shapes=COPIES + [pltpu.VMEM((GROUPS + 1, 8, R), jnp.float32)] * 3,
         compiler_params=PARAMS,
@@ -218,12 +215,13 @@
 
 def grads(meta, lim, sts, arrays):
     dq = [jax.ShapeDtypeStruct((2 * SPAN, WIDE), t) for t in (jnp.float32,) + (jnp.bfloat16,) * 3]
-    dkv = [jax.ShapeDtypeStruct((16, 2 * SPAN, 2 * HD), jnp.bfloat16)] * 2
+    dkv = [jax.ShapeDtypeStruct((4, 2 * SPAN, 2 * HD), jnp.bfloat16)] * 4
+    dkv += [jax.ShapeDtypeStruct((4, 4, 2 * SPAN, 2 * HD), jnp.bfloat16)]
     return pl.pallas_call(
         grads_kernel,
         out_shape=dq + dkv,
-        in_specs=[SM] + [VM] * 18,
-        out_specs=[VM] * 6,
+        in_specs=[SM] + [VM] * 17,
+        out_specs=[VM] * 9,
         scratch_shapes=COPIES
         + [
             pltpu.VMEM((KEYS, 2 * HD), jnp.float32),
@@ -236,31 +234,44 @@
     )(meta, lim, *sts, *arrays)
 
 
-def shift(a, axis, step):
-    if axis == "z":
-        at = lambda z: (z % 2) * 2 + z // 2
-        return lax.ppermute(a, ("zl", "zh"), [(at(i), at((i + step) % 4)) for i in range(4)])
-    return lax.ppermute(a, axis, [(i, (i + step) % 4) for i in range(4)])
+def permute(a, move):
+    pairs = []
+    for i in range(128):
+        y, zl, core, zh, x = (int(c) for c in np.unravel_index(i, SIZES))
+        y, z, core, x = (c % n for c, n in zip(move(y, 2 * zh + zl, core, x), (4, 4, 2, 4)))
+        pairs.append((i, int(np.ravel_multi_index((y, z % 2, core, z // 2, x), SIZES))))
+    return lax.ppermute(a, AXES, pairs)
+
+
+def x_shift(a, step):
+    return permute(a, lambda y, z, core, x: (y, z, core, x + step))
+
+
+def first_shift(a, step):
+    return permute(a, lambda y, z, core, x: (y, z + step, core, x) if core else (y + step, z, core, x))
+
+
+def second_shift(a, step):
+    return permute(a, lambda y, z, core, x: (y + step, z, core, x) if core else (y, z + step, core, x))
 
 
 def core_swap(a):
-    return lax.ppermute(a, "core", [(0, 1), (1, 0)])
+    return permute(a, lambda y, z, core, x: (y, z, 1 - core, x))
 
 
 def plan(span_slot):
     i32 = jnp.int32
     y, zl, core, zh, x = (lax.axis_index(a) for a in AXES)
     z = 2 * zh + zl
-    grid = span_slot.reshape(4, 2, 2, 2, 4, 2)
+    grid = span_slot.reshape(*SIZES, 2)
     own_x = jnp.transpose(lax.dynamic_index_in_dim(grid, x, 4, keepdims=False), (2, 0, 3, 1, 4))
     own_x = own_x.reshape(2, 4, 4, 2)
-    own_x = jnp.where(core == 0, own_x, own_x[::-1])
-    by_z = jnp.stack([lax.dynamic_index_in_dim(own_x, (z - r) % 4, 2, keepdims=False) for r in range(4)], 1)
-    by_yz = jnp.stack([lax.dynamic_index_in_dim(by_z, (y - r) % 4, 2, keepdims=False) for r in range(4)], 2)
-    arrived = by_yz.reshape(64)
-    owners = jnp.transpose(own_x.reshape(2, 4, 2, 2, 2), (0, 1, 3, 2, 4)).reshape(64)
+    by_y = jnp.stack([lax.dynamic_index_in_dim(own_x, (y - r) % 4, 1, keepdims=False) for r in STEPS], 1)
+    by_yz = jnp.stack([lax.dynamic_index_in_dim(by_y, (z - r) % 4, 2, keepdims=False) for r in STEPS], 2)
+    of_core = jnp.stack([jnp.transpose(by_yz[0], (1, 0, 2)), by_yz[1]])
+    arrived = jnp.where(core == 0, of_core, of_core[::-1]).reshape(64)
     ring = grid[y, zl, core, zh]
-    queries = jnp.concatenate([ring[(x - r) % 4] for r in range(4)])
+    queries = jnp.concatenate([ring[(x - r) % 4] for r in STEPS])
 
     def rank(a, among):
         return jnp.sum((among[None, :] < a[:, None]).astype(i32), axis=1)
@@ -268,8 +279,8 @@
     place = rank(queries, queries)
     hit = (place[None, :] == jnp.arange(8)[:, None]).astype(i32)
     spans = jnp.sum(hit * queries[None, :], axis=1)
-    below = rank(spans, owners)
-    own = jnp.any(owners[None, :] == spans[:, None], axis=1).astype(i32)
+    below = rank(spans, arrived)
+    own = jnp.any(arrived[None, :] == spans[:, None], axis=1).astype(i32)
     token = jnp.tile(jnp.arange(SPAN, dtype=i32), 2)
     seen = below[:, None] * SPAN + own[:, None] * (token[None, :] + 1)
     a, b = seen[0::2], seen[1::2]
@@ -282,31 +293,39 @@
     past = (t[:, None] >= end[None, :]).astype(i32)
     group = jnp.sum(past, axis=1)
     block = jnp.where(group < GROUPS, t - jnp.sum(past * each[None, :], axis=1), 0)
-    meta = [rank(arrived, owners), rank(owners, owners), place, end[-1:], group, block]
+    meta = [rank(arrived, arrived), place, end[-1:], group, block]
     return jnp.concatenate(meta).astype(i32), lim
 
 
 def local(queries, keys, values, grad_out, span_slot):
     meta, lim = plan(span_slot)
-    qd0 = jnp.concatenate([queries, grad_out], axis=1)
-    qd1, qd3 = shift(qd0, "x", 1), shift(qd0, "x", 3)
-    q2, do2 = shift(qd3[:, :WIDE], "x", 3), shift(qd1[:, WIDE:], "x", 1)
     kv = jnp.concatenate([keys, values], axis=1)[None]
-    kv = jnp.concatenate([kv] + [shift(kv, "y", r) for r in (1, 2, 3)], axis=0)
-    kvs = [kv] + [shift(kv, "z", r) for r in (1, 2, 3)]
-    arrays = [qd0, qd1, q2, do2, qd3] + kvs + [core_swap(a) for a in kvs]
+    kv = jnp.concatenate([kv] + [first_shift(kv, r) for r in STEPS[1:]], axis=0)
+    kvs = [kv] + [second_shift(kv, r) for r in STEPS[1:]]
+    qd = jnp.concatenate([queries, grad_out], axis=1)
+    qds = [qd] + [x_shift(qd, r) for r in STEPS[1:]]
+    kvs[1], meta, lim = lax.optimization_barrier((kvs[1], meta, lim))
+    arrays = qds + kvs + [core_swap(a) for a in kvs]
 
     part = stats(meta, lim, arrays)
-    sts = [part] + [shift(part, "x", r) for r in (1, 2, 3)]
-    dq0, dq1, dq2, dq3, dkv, dkv_other = grads(meta, lim, sts, arrays)
-
-    pair = (dkv.astype(jnp.float32) + core_swap(dkv_other).astype(jnp.float32)).astype(jnp.bfloat16)
-    parts = lax.all_to_all(pair, ("y", "zl", "zh"), 0, 0, tiled=True)
-    summed = jnp.sum(parts.astype(jnp.float32), axis=0)
-    for r, part in ((1, dq1), (2, dq2), (3, dq3)):
-        dq0 = dq0 + shift(part, "x", 4 - r).astype(jnp.float32)
+    sts = [part] + [x_shift(part, r) for r in (1, 2, 3)]
+    dqs_dkv = grads(meta, lim, sts, arrays)
+    dqs, dkv, dkv_other = dqs_dkv[:4], dqs_dkv[4:8], dqs_dkv[8]
+
+    def total(*parts):
+        out = parts[0].astype(jnp.float32)
+        for part in parts[1:]:
+            out = out + part.astype(jnp.float32)
+        return out
+
+    dq = total(dqs[0], *[x_shift(a, -r) for r, a in zip(STEPS[1:], dqs[1:])])
+    other = core_swap(dkv_other)
+    pairs = [total(a, other[i]).astype(jnp.bfloat16) for i, a in enumerate(dkv)]
+    some = total(pairs[0], *[second_shift(a, -r) for r, a in zip(STEPS[1:], pairs[1:])])
+    sent = [first_shift(some[i].astype(jnp.bfloat16), -r) for i, r in ((1, 1), (2, 3), (3, 2))]
+    summed = total(some[0], *sent)
     return (
-        dq0.astype(jnp.bfloat16),
+        dq.astype(jnp.bfloat16),
         summed[:, :HD].astype(jnp.bfloat16),
         summed[:, HD:].astype(jnp.bfloat16),
     )

time: 125 us -> 108 us (0.86)
  waiting for transfers between devices: 41.4 us -> 26.1 us
  starting transfers between devices: 28.3 us -> 33 us
  local copies, waits for them, and re-layouts: 9.5 us -> 4.93 us
    ppermute x21 -> x26, starting transfers between devices: 21.5 us -> 33 us  [permute(): return lax.ppermute(a, AXES, pairs)]
    ppermute x21 -> x26, waiting for transfers between devices: 37.5 us -> 26.1 us  [permute(): return lax.ppermute(a, AXES, pairs)]
    all_to_all x1 -> x0, starting transfers between devices: 6.79 us -> none  [local(): parts = lax.all_to_all(pair, ('y', 'zl', 'zh'), 0, 0, tiled=True)]
    all_to_all x1 -> x0, waiting for transfers between devices: 3.93 us -> none  [local(): parts = lax.all_to_all(pair, ('y', 'zl', 'zh'), 0, 0, tiled=True)]
    unnamed x19 -> x5, local copies, waits for them, and re-layouts: 3.76 us -> 1.62 us
    slice x3 -> x2, local copies, waits for them, and re-layouts: 1.96 us -> 0.58 us  [the longest x1 0.58 us: plan(): meta = [rank(arrived, arrived), place, end[-1:], group, block]]
  transfers between devices with their start and end apart: 22 -> 26, of which waited for: 13 -> 16; matrix products, arithmetic and copies ran while one was open for 7% -> 6% of each run, Pallas kernels for 0% -> 0%
where the time goes in v3:
time: 108 us; the launch traced here: 107 us
  Pallas kernels  38.8 us (36%)
  starting transfers between devices  33 us (31%)
  waiting for transfers between devices  26.1 us (24%)
  local copies, waits for them, and re-layouts  4.93 us (5%)
  other arithmetic  3.36 us (3%)
    ppermute x26, starting transfers between devices, permute(): return lax.ppermute(a, AXES, pairs)  33 us
    ppermute x26, waiting for transfers between devices, permute(): return lax.ppermute(a, AXES, pairs)  26.1 us
    pallas_call x1, Pallas kernels, grads(): pl.pallas_call(grads_kernel, out_shape=dq + dkv, in_specs=[SM] + [VM] * 1...  24.9 us
    pallas_call x1, Pallas kernels, stats(): pl.pallas_call(stats_kernel, out_shape=jax.ShapeDtypeStruct((2, 16, R), j...  13.9 us
  transfers between devices with their start and end apart: 26, of which 16 were waited for; matrix products, arithmetic and copies ran while one was open for 6% of the time, Pallas kernels for 0%

profile of v3, /device:TPU:0, one launch (start us, length us, event | category | flops | bytes accessed | tf_op | source)
XLA Modules:
  0.0 107.0 jit_solution(18012477915990579869)
XLA Ops:
  1.4 3.4 %collective-permute-start.2 = (bf16[1,128,256]{2,1,0:T(8,128)(2,1)S(1)}, bf16[1,128,256]{2,1,0:T(8,128)(2,1)S(1)}, u32[]{:S(2)}, u32[]{:S(2)}) collective-permute-start(bf16[1,128,256]{2,1,0:T(8,128)(2,1)S(1)} %maximum_bitcast_fusion), channel_id=1, source_target_pairs={{0,64},{1,65},{2,66},{3,67},{4,68},{5,69},{6,70},{7,71},{8,12},{9,... | collective-permute-start | bytes 196616 | tf_op jit(solution)/shard_map/ppermute | solution.py:243
  4.8 1.1 collective-permute-start.1
  5.8 1.0 collective-permute-start
  7.8 3.1 %collective-permute-start.6 = (bf16[128,1536]{1,0:T(8,128)(2,1)S(1)}, bf16[128,1536]{1,0:T(8,128)(2,1)S(1)}, u32[]{:S(2)}, u32[]{:S(2)}) collective-permute-start(bf16[128,1536]{1,0:T(8,128)(2,1)S(1)} %constant_dynamic-update-slice_fusion.refs_0_), channel_id=1, source_target_pairs={{0,2},{1,3},{2,0},{3,1},{4,6},{5,7},{6,4},{7,5},{8,10},{9,11},{10,... | collective-permute-start | bytes 1179656 | tf_op jit(solution)/shard_map/ppermute | solution.py:243
  10.9 1.1 %collective-permute-start.5 = (bf16[128,1536]{1,0:T(8,128)(2,1)S(1)}, bf16[128,1536]{1,0:T(8,128)(2,1)S(1)}, u32[]{:S(2)}, u32[]{:S(2)}) collective-permute-start(bf16[128,1536]{1,0:T(8,128)(2,1)S(1)} %constant_dynamic-update-slice_fusion.refs_0_), channel_id=1, source_target_pairs={{0,3},{1,0},{2,1},{3,2},{4,7},{5,4},{6,5},{7,6},{8,11},{9,8},{10,9... | collective-permute-start | bytes 1179656 | tf_op jit(solution)/shard_map/ppermute | solution.py:243
  15.9 2.0 %collective-permute-start.3 = (bf16[4,128,256]{2,1,0:T(8,128)(2,1)S(1)}, bf16[4,128,256]{2,1,0:T(8,128)(2,1)S(1)}, u32[]{:S(2)}, u32[]{:S(2)}) collective-permute-start(bf16[4,128,256]{2,1,0:T(8,128)(2,1)S(1)} %pad_maximum_fusion.refs_4_), channel_id=1, source_target_pairs={{0,16},{1,17},{2,18},{3,19},{4,20},{5,21},{6,22},{7,23},{8,40},{9,... | collective-permute-start | bytes 786440 | tf_op jit(solution)/shard_map/ppermute | solution.py:243
  18.3 3.7 %collective-permute-start.8 = (bf16[4,128,256]{2,1,0:T(8,128)(2,1)S(1)}, bf16[4,128,256]{2,1,0:T(8,128)(2,1)S(1)}, u32[]{:S(2)}, u32[]{:S(2)}) collective-permute-start(bf16[4,128,256]{2,1,0:T(8,128)(2,1)S(1)} %pad_maximum_fusion.refs_4_), channel_id=1, source_target_pairs={{0,4},{1,5},{2,6},{3,7},{4,0},{5,1},{6,2},{7,3},{8,72},{9,73},{10,... | collective-permute-start | bytes 786440 | tf_op jit(solution)/shard_map/ppermute | solution.py:243
  22.0 2.4 %collective-permute-done.3.refs_5_ = bf16[4,128,256]{2,1,0:T(8,128)(2,1)S(1)} collective-permute-done((bf16[4,128,256]{2,1,0:T(8,128)(2,1)S(1)}, bf16[4,128,256]{2,1,0:T(8,128)(2,1)S(1)}, u32[]{:S(2)}, u32[]{:S(2)}) %collective-permute-start.3) | collective-permute-done | bytes 262176 | tf_op jit(solution)/shard_map/ppermute | solution.py:243
  24.4 2.0 %collective-permute-start.7 = (bf16[4,128,256]{2,1,0:T(8,128)(2,1)S(1)}, bf16[4,128,256]{2,1,0:T(8,128)(2,1)S(1)}, u32[]{:S(2)}, u32[]{:S(2)}) collective-permute-start(bf16[4,128,256]{2,1,0:T(8,128)(2,1)S(1)} %pad_maximum_fusion.refs_4_), channel_id=1, source_target_pairs={{0,20},{1,21},{2,22},{3,23},{4,16},{5,17},{6,18},{7,19},{8,104},{9... | collective-permute-start | bytes 786440 | tf_op jit(solution)/shard_map/ppermute | solution.py:243
  28.6 2.1 %collective-permute-done.7.refs_6_ = bf16[4,128,256]{2,1,0:T(8,128)(2,1)S(1)} collective-permute-done((bf16[4,128,256]{2,1,0:T(8,128)(2,1)S(1)}, bf16[4,128,256]{2,1,0:T(8,128)(2,1)S(1)}, u32[]{:S(2)}, u32[]{:S(2)}) %collective-permute-start.7) | collective-permute-done | bytes 262176 | tf_op jit(solution)/shard_map/ppermute | solution.py:243
  31.3 1.0 collective-permute-done.11.refs_10_
  32.6 13.9 %stats.1.st0 = f32[2,16,256]{2,1,0:T(8,128)S(1)} custom-call(s32[345]{0:T(512)S(1)} %concatenate.21.meta, s32[16,256]{1,0:T(8,128)S(1)} %concatenate.22.lim, bf16[128,1536]{1,0:T(8,128)(2,1)S(1)} %constant_dynamic-update-slice_fusion.refs_0_, bf16[128,1536]{1,0:T(8,128)(2,1)S(1)} %collective-permute-done.4.refs_1_, ...), custom_call_target="tpu_custom_call" | custom-call | tf_op jit(solution)/shard_map/stats/pallas_call | solution.py:205
  46.5 3.4 %collective-permute-start.15 = (f32[2,16,256]{2,1,0:T(8,128)S(1)}, f32[2,16,256]{2,1,0:T(8,128)S(1)}, u32[]{:S(2)}, u32[]{:S(2)}) collective-permute-start(f32[2,16,256]{2,1,0:T(8,128)S(1)} %stats.1.st0), channel_id=1, source_target_pairs={{0,3},{1,0},{2,1},{3,2},{4,7},{5,4},{6,5},{7,6},{8,11},{9,8},{10,9... | collective-permute-start | bytes 98312 | tf_op jit(solution)/shard_map/ppermute | solution.py:243
  51.5 3.9 %collective-permute-done.14.st2 = f32[2,16,256]{2,1,0:T(8,128)S(1)} collective-permute-done((f32[2,16,256]{2,1,0:T(8,128)S(1)}, f32[2,16,256]{2,1,0:T(8,128)S(1)}, u32[]{:S(2)}, u32[]{:S(2)}) %collective-permute-start.14) | collective-permute-done | bytes 32800 | tf_op jit(solution)/shard_map/ppermute | solution.py:243
  55.7 24.9 %grads.1 = (f32[128,768]{1,0:T(8,128)S(1)}, bf16[128,768]{1,0:T(8,128)(2,1)S(1)}, bf16[128,768]{1,0:T(8,128)(2,1)S(1)}, bf16[128,768]{1,0:T(8,128)(2,1)S(1)}, bf...) custom-call(s32[345]{0:T(512)S(1)} %concatenate.21.meta, ...), custom_call_target="tpu_custom_call" | custom-call | tf_op jit(solution)/shard_map/grads/pallas_call | solution.py:220
  80.6 2.9 %collective-permute-done.19 = bf16[4,4,128,256]{3,2,1,0:T(8,128)(2,1)S(1)} collective-permute-done((bf16[4,4,128,256]{3,2,1,0:T(8,128)(2,1)}, bf16[4,4,128,256]{3,2,1,0:T(8,128)(2,1)S(1)}, u32[]{:S(2)}, u32[]{:S(2)}) %collective-permute-start.19) | collective-permute-done | bytes 1048608 | tf_op jit(solution)/shard_map/ppermute | solution.py:243
  83.7 3.5 %collective-permute-start.20 = (bf16[4,128,256]{2,1,0:T(8,128)(2,1)S(1)}, bf16[4,128,256]{2,1,0:T(8,128)(2,1)S(1)}, u32[]{:S(2)}, u32[]{:S(2)}) collective-permute-start(bf16[4,128,256]{2,1,0:T(8,128)(2,1)S(1)} %get-tuple-element.31), channel_id=1, source_target_pairs={{0,20},{1,21},{2,22},{3,23},{4,16},{5,17},{6,18},{7,19},{8,104},{9... | collective-permute-start | bytes 786440 | tf_op jit(solution)/shard_map/ppermute | solution.py:243
  87.1 1.3 %collective-permute-start.21 = (bf16[4,128,256]{2,1,0:T(8,128)(2,1)S(1)}, bf16[4,128,256]{2,1,0:T(8,128)(2,1)S(1)}, u32[]{:S(2)}, u32[]{:S(2)}) collective-permute-start(bf16[4,128,256]{2,1,0:T(8,128)(2,1)S(1)} %get-tuple-element.33), channel_id=1, source_target_pairs={{0,16},{1,17},{2,18},{3,19},{4,20},{5,21},{6,22},{7,23},{8,40},{9,... | collective-permute-start | bytes 786440 | tf_op jit(solution)/shard_map/ppermute | solution.py:243
  89.3 1.1 %collective-permute-start.17 = (bf16[128,768]{1,0:T(8,128)(2,1)S(1)}, bf16[128,768]{1,0:T(8,128)(2,1)S(1)}, u32[]{:S(2)}, u32[]{:S(2)}) collective-permute-start(bf16[128,768]{1,0:T(8,128)(2,1)S(1)} %get-tuple-element.20), channel_id=1, source_target_pairs={{0,1},{1,2},{2,3},{3,0},{4,5},{5,6},{6,7},{7,4},{8,9},{9,10},{10,1... | collective-permute-start | bytes 589832 | tf_op jit(solution)/shard_map/ppermute | solution.py:243
  90.4 3.4 %collective-permute-done.20 = bf16[4,128,256]{2,1,0:T(8,128)(2,1)S(1)} collective-permute-done((bf16[4,128,256]{2,1,0:T(8,128)(2,1)S(1)}, bf16[4,128,256]{2,1,0:T(8,128)(2,1)S(1)}, u32[]{:S(2)}, u32[]{:S(2)}) %collective-permute-start.20) | collective-permute-done | bytes 262176 | tf_op jit(solution)/shard_map/ppermute | solution.py:243
  93.8 1.3 %collective-permute-done.22 = bf16[4,128,256]{2,1,0:T(8,128)(2,1)S(1)} collective-permute-done((bf16[4,128,256]{2,1,0:T(8,128)(2,1)S(1)}, bf16[4,128,256]{2,1,0:T(8,128)(2,1)S(1)}, u32[]{:S(2)}, u32[]{:S(2)}) %collective-permute-start.22) | collective-permute-done | bytes 262176 | tf_op jit(solution)/shard_map/ppermute | solution.py:243
  95.1 2.4 %collective-permute-done.21 = bf16[4,128,256]{2,1,0:T(8,128)(2,1)S(1)} collective-permute-done((bf16[4,128,256]{2,1,0:T(8,128)(2,1)S(1)}, bf16[4,128,256]{2,1,0:T(8,128)(2,1)S(1)}, u32[]{:S(2)}, u32[]{:S(2)}) %collective-permute-start.21) | collective-permute-done | bytes 262176 | tf_op jit(solution)/shard_map/ppermute | solution.py:243
  97.7 2.2 %collective-permute-start.23 = (bf16[128,256]{1,0:T(8,128)(2,1)S(1)}, bf16[128,256]{1,0:T(8,128)(2,1)S(1)}, u32[]{:S(2)}, u32[]{:S(2)}) collective-permute-start(bf16[128,256]{1,0:T(8,128)(2,1)S(1)} %get-tuple-element.34), channel_id=1, source_target_pairs={{0,96},{1,97},{2,98},{3,99},{4,100},{5,101},{6,102},{7,103},{8,28}... | collective-permute-start | bytes 196616 | tf_op jit(solution)/shard_map/ppermute | solution.py:243
  102.4 3.3 %collective-permute-done.25 = bf16[128,256]{1,0:T(8,128)(2,1)S(1)} collective-permute-done((bf16[128,256]{1,0:T(8,128)(2,1)S(1)}, bf16[128,256]{1,0:T(8,128)(2,1)S(1)}, u32[]{:S(2)}, u32[]{:S(2)}) %collective-permute-start.25) | collective-permute-done | bytes 65568 | tf_op jit(solution)/shard_map/ppermute | solution.py:243
  (85 shorter events, 16.0 us)
Async XLA Ops:
  1.4 13.4 %collective-permute-start.2 = (bf16[1,128,256]{2,1,0:T(8,128)(2,1)S(1)}, bf16[1,128,256]{2,1,0:T(8,128)(2,1)S(1)}, u32[]{:S(2)}, u32[]{:S(2)}) collective-permute-start(bf16[1,128,256]{2,1,0:T(8,128)(2,1)S(1)} %maximum_bitcast_fusion), channel_id=1, source_target_pairs={{0,64},{1,65},{2,66},{3,67},{4,68},{5,69},{6,70},{7,71},{8,12},{9,... | collective-permute-start | bytes 196616 | tf_op jit(solution)/shard_map/ppermute | solution.py:243
  4.8 11.0 %collective-permute-start.1 = (bf16[1,128,256]{2,1,0:T(8,128)(2,1)S(1)}, bf16[1,128,256]{2,1,0:T(8,128)(2,1)S(1)}, u32[]{:S(2)}, u32[]{:S(2)}) collective-permute-start(bf16[1,128,256]{2,1,0:T(8,128)(2,1)S(1)} %maximum_bitcast_fusion), channel_id=1, source_target_pairs={{0,96},{1,97},{2,98},{3,99},{4,100},{5,101},{6,102},{7,103},{8,28}... | collective-permute-start | bytes 196616 | tf_op jit(solution)/shard_map/ppermute | solution.py:243
  5.8 9.9 %collective-permute-start = (bf16[1,128,256]{2,1,0:T(8,128)(2,1)S(1)}, bf16[1,128,256]{2,1,0:T(8,128)(2,1)S(1)}, u32[]{:S(2)}, u32[]{:S(2)}) collective-permute-start(bf16[1,128,256]{2,1,0:T(8,128)(2,1)S(1)} %maximum_bitcast_fusion), channel_id=1, source_target_pairs={{0,32},{1,33},{2,34},{3,35},{4,36},{5,37},{6,38},{7,39},{8,24},{9,... | collective-permute-start | bytes 196616 | tf_op jit(solution)/shard_map/ppermute | solution.py:243
  7.8 22.9 %collective-permute-start.6 = (bf16[128,1536]{1,0:T(8,128)(2,1)S(1)}, bf16[128,1536]{1,0:T(8,128)(2,1)S(1)}, u32[]{:S(2)}, u32[]{:S(2)}) collective-permute-start(bf16[128,1536]{1,0:T(8,128)(2,1)S(1)} %constant_dynamic-update-slice_fusion.refs_0_), channel_id=1, source_target_pairs={{0,2},{1,3},{2,0},{3,1},{4,6},{5,7},{6,4},{7,5},{8,10},{9,11},{10,... | collective-permute-start | bytes 1179656 | tf_op jit(solution)/shard_map/ppermute | solution.py:243
  10.9 20.4 %collective-permute-start.5 = (bf16[128,1536]{1,0:T(8,128)(2,1)S(1)}, bf16[128,1536]{1,0:T(8,128)(2,1)S(1)}, u32[]{:S(2)}, u32[]{:S(2)}) collective-permute-start(bf16[128,1536]{1,0:T(8,128)(2,1)S(1)} %constant_dynamic-update-slice_fusion.refs_0_), channel_id=1, source_target_pairs={{0,3},{1,0},{2,1},{3,2},{4,7},{5,4},{6,5},{7,6},{8,11},{9,8},{10,9... | collective-permute-start | bytes 1179656 | tf_op jit(solution)/shard_map/ppermute | solution.py:243
  14.9 16.4 %collective-permute-start.4 = (bf16[128,1536]{1,0:T(8,128)(2,1)S(1)}, bf16[128,1536]{1,0:T(8,128)(2,1)S(1)}, u32[]{:S(2)}, u32[]{:S(2)}) collective-permute-start(bf16[128,1536]{1,0:T(8,128)(2,1)S(1)} %constant_dynamic-update-slice_fusion.refs_0_), channel_id=1, source_target_pairs={{0,1},{1,2},{2,3},{3,0},{4,5},{5,6},{6,7},{7,4},{8,9},{9,10},{10,1... | collective-permute-start | bytes 1179656 | tf_op jit(solution)/shard_map/ppermute | solution.py:243
  15.8 2.5 %collective-permute-start.9 = (bf16[4,128,256]{2,1,0:T(8,128)(2,1)S(1)}, bf16[4,128,256]{2,1,0:T(8,128)(2,1)S(1)}, u32[]{:S(2)}, u32[]{:S(2)}) collective-permute-start(bf16[4,128,256]{2,1,0:T(8,128)(2,1)S(1)} %pad_maximum_fusion.refs_4_), channel_id=1, source_target_pairs={{0,8},{1,9},{2,10},{3,11},{4,12},{5,13},{6,14},{7,15},{8,0},{9,1},... | collective-permute-start | bytes 786440 | tf_op jit(solution)/shard_map/ppermute | solution.py:243
  15.9 8.5 %collective-permute-start.3 = (bf16[4,128,256]{2,1,0:T(8,128)(2,1)S(1)}, bf16[4,128,256]{2,1,0:T(8,128)(2,1)S(1)}, u32[]{:S(2)}, u32[]{:S(2)}) collective-permute-start(bf16[4,128,256]{2,1,0:T(8,128)(2,1)S(1)} %pad_maximum_fusion.refs_4_), channel_id=1, source_target_pairs={{0,16},{1,17},{2,18},{3,19},{4,20},{5,21},{6,22},{7,23},{8,40},{9,... | collective-permute-start | bytes 786440 | tf_op jit(solution)/shard_map/ppermute | solution.py:243
  18.3 10.3 %collective-permute-start.8 = (bf16[4,128,256]{2,1,0:T(8,128)(2,1)S(1)}, bf16[4,128,256]{2,1,0:T(8,128)(2,1)S(1)}, u32[]{:S(2)}, u32[]{:S(2)}) collective-permute-start(bf16[4,128,256]{2,1,0:T(8,128)(2,1)S(1)} %pad_maximum_fusion.refs_4_), channel_id=1, source_target_pairs={{0,4},{1,5},{2,6},{3,7},{4,0},{5,1},{6,2},{7,3},{8,72},{9,73},{10,... | collective-permute-start | bytes 786440 | tf_op jit(solution)/shard_map/ppermute | solution.py:243
  24.4 6.4 %collective-permute-start.7 = (bf16[4,128,256]{2,1,0:T(8,128)(2,1)S(1)}, bf16[4,128,256]{2,1,0:T(8,128)(2,1)S(1)}, u32[]{:S(2)}, u32[]{:S(2)}) collective-permute-start(bf16[4,128,256]{2,1,0:T(8,128)(2,1)S(1)} %pad_maximum_fusion.refs_4_), channel_id=1, source_target_pairs={{0,20},{1,21},{2,22},{3,23},{4,16},{5,17},{6,18},{7,19},{8,104},{9... | collective-permute-start | bytes 786440 | tf_op jit(solution)/shard_map/ppermute | solution.py:243
  28.6 2.6 %collective-permute-start.12 = (bf16[4,128,256]{2,1,0:T(8,128)(2,1)S(1)}, bf16[4,128,256]{2,1,0:T(8,128)(2,1)S(1)}, u32[]{:S(2)}, u32[]{:S(2)}) collective-permute-start(bf16[4,128,256]{2,1,0:T(8,128)(2,1)S(1)} %collective-permute-done.8.refs_7_), channel_id=1, source_target_pairs={{0,8},{1,9},{2,10},{3,11},{4,12},{5,13},{6,14},{7,15},{8,0},{9,1},... | collective-permute-start | bytes 786440 | tf_op jit(solution)/shard_map/ppermute | solution.py:243
  46.5 5.0 %collective-permute-start.15 = (f32[2,16,256]{2,1,0:T(8,128)S(1)}, f32[2,16,256]{2,1,0:T(8,128)S(1)}, u32[]{:S(2)}, u32[]{:S(2)}) collective-permute-start(f32[2,16,256]{2,1,0:T(8,128)S(1)} %stats.1.st0), channel_id=1, source_target_pairs={{0,3},{1,0},{2,1},{3,2},{4,7},{5,4},{6,5},{7,6},{8,11},{9,8},{10,9... | collective-permute-start | bytes 98312 | tf_op jit(solution)/shard_map/ppermute | solution.py:243
  49.9 5.5 %collective-permute-start.14 = (f32[2,16,256]{2,1,0:T(8,128)S(1)}, f32[2,16,256]{2,1,0:T(8,128)S(1)}, u32[]{:S(2)}, u32[]{:S(2)}) collective-permute-start(f32[2,16,256]{2,1,0:T(8,128)S(1)} %stats.1.st0), channel_id=1, source_target_pairs={{0,2},{1,3},{2,0},{3,1},{4,6},{5,7},{6,4},{7,5},{8,10},{9,11},{10,... | collective-permute-start | bytes 98312 | tf_op jit(solution)/shard_map/ppermute | solution.py:243
  50.2 5.5 %collective-permute-start.13 = (f32[2,16,256]{2,1,0:T(8,128)S(1)}, f32[2,16,256]{2,1,0:T(8,128)S(1)}, u32[]{:S(2)}, u32[]{:S(2)}) collective-permute-start(f32[2,16,256]{2,1,0:T(8,128)S(1)} %stats.1.st0), channel_id=1, source_target_pairs={{0,1},{1,2},{2,3},{3,0},{4,5},{5,6},{6,7},{7,4},{8,9},{9,10},{10,1... | collective-permute-start | bytes 98312 | tf_op jit(solution)/shard_map/ppermute | solution.py:243
  80.6 2.9 %collective-permute-start.19 = (bf16[4,4,128,256]{3,2,1,0:T(8,128)(2,1)}, bf16[4,4,128,256]{3,2,1,0:T(8,128)(2,1)S(1)}, u32[]{:S(2)}, u32[]{:S(2)}) collective-permute-start(bf16[4,4,128,256]{3,2,1,0:T(8,128)(2,1)} %get-tuple-element.23), channel_id=1, source_target_pairs={{0,8},{1,9},{2,10},{3,11},{4,12},{5,13},{6,14},{7,15},{8,0},{9,1},... | collective-permute-start | bytes 3145736 | tf_op jit(solution)/shard_map/ppermute | solution.py:243
  83.7 10.2 %collective-permute-start.20 = (bf16[4,128,256]{2,1,0:T(8,128)(2,1)S(1)}, bf16[4,128,256]{2,1,0:T(8,128)(2,1)S(1)}, u32[]{:S(2)}, u32[]{:S(2)}) collective-permute-start(bf16[4,128,256]{2,1,0:T(8,128)(2,1)S(1)} %get-tuple-element.31), channel_id=1, source_target_pairs={{0,20},{1,21},{2,22},{3,23},{4,16},{5,17},{6,18},{7,19},{8,104},{9... | collective-permute-start | bytes 786440 | tf_op jit(solution)/shard_map/ppermute | solution.py:243
  87.1 8.0 %collective-permute-start.22 = (bf16[4,128,256]{2,1,0:T(8,128)(2,1)S(1)}, bf16[4,128,256]{2,1,0:T(8,128)(2,1)S(1)}, u32[]{:S(2)}, u32[]{:S(2)}) collective-permute-start(bf16[4,128,256]{2,1,0:T(8,128)(2,1)S(1)} %get-tuple-element.32), channel_id=1, source_target_pairs={{0,4},{1,5},{2,6},{3,7},{4,0},{5,1},{6,2},{7,3},{8,72},{9,73},{10,... | collective-permute-start | bytes 786440 | tf_op jit(solution)/shard_map/ppermute | solution.py:243
  87.1 10.4 %collective-permute-start.21 = (bf16[4,128,256]{2,1,0:T(8,128)(2,1)S(1)}, bf16[4,128,256]{2,1,0:T(8,128)(2,1)S(1)}, u32[]{:S(2)}, u32[]{:S(2)}) collective-permute-start(bf16[4,128,256]{2,1,0:T(8,128)(2,1)S(1)} %get-tuple-element.33), channel_id=1, source_target_pairs={{0,16},{1,17},{2,18},{3,19},{4,20},{5,21},{6,22},{7,23},{8,40},{9,... | collective-permute-start | bytes 786440 | tf_op jit(solution)/shard_map/ppermute | solution.py:243
  88.4 12.1 %collective-permute-start.16 = (bf16[128,768]{1,0:T(8,128)(2,1)S(1)}, bf16[128,768]{1,0:T(8,128)(2,1)S(1)}, u32[]{:S(2)}, u32[]{:S(2)}) collective-permute-start(bf16[128,768]{1,0:T(8,128)(2,1)S(1)} %get-tuple-element.19), channel_id=1, source_target_pairs={{0,3},{1,0},{2,1},{3,2},{4,7},{5,4},{6,5},{7,6},{8,11},{9,8},{10,9... | collective-permute-start | bytes 589832 | tf_op jit(solution)/shard_map/ppermute | solution.py:243
  89.3 11.5 %collective-permute-start.17 = (bf16[128,768]{1,0:T(8,128)(2,1)S(1)}, bf16[128,768]{1,0:T(8,128)(2,1)S(1)}, u32[]{:S(2)}, u32[]{:S(2)}) collective-permute-start(bf16[128,768]{1,0:T(8,128)(2,1)S(1)} %get-tuple-element.20), channel_id=1, source_target_pairs={{0,1},{1,2},{2,3},{3,0},{4,5},{5,6},{6,7},{7,4},{8,9},{9,10},{10,1... | collective-permute-start | bytes 589832 | tf_op jit(solution)/shard_map/ppermute | solution.py:243
  93.8 7.2 %collective-permute-start.18 = (bf16[128,768]{1,0:T(8,128)(2,1)S(1)}, bf16[128,768]{1,0:T(8,128)(2,1)S(1)}, u32[]{:S(2)}, u32[]{:S(2)}) collective-permute-start(bf16[128,768]{1,0:T(8,128)(2,1)S(1)} %get-tuple-element.21), channel_id=1, source_target_pairs={{0,2},{1,3},{2,0},{3,1},{4,6},{5,7},{6,4},{7,5},{8,10},{9,11},{10,... | collective-permute-start | bytes 589832 | tf_op jit(solution)/shard_map/ppermute | solution.py:243
  97.7 4.7 %collective-permute-start.23 = (bf16[128,256]{1,0:T(8,128)(2,1)S(1)}, bf16[128,256]{1,0:T(8,128)(2,1)S(1)}, u32[]{:S(2)}, u32[]{:S(2)}) collective-permute-start(bf16[128,256]{1,0:T(8,128)(2,1)S(1)} %get-tuple-element.34), channel_id=1, source_target_pairs={{0,96},{1,97},{2,98},{3,99},{4,100},{5,101},{6,102},{7,103},{8,28}... | collective-permute-start | bytes 196616 | tf_op jit(solution)/shard_map/ppermute | solution.py:243
  99.9 5.8 %collective-permute-start.25 = (bf16[128,256]{1,0:T(8,128)(2,1)S(1)}, bf16[128,256]{1,0:T(8,128)(2,1)S(1)}, u32[]{:S(2)}, u32[]{:S(2)}) collective-permute-start(bf16[128,256]{1,0:T(8,128)(2,1)S(1)} %get-tuple-element.35), channel_id=1, source_target_pairs={{0,64},{1,65},{2,66},{3,67},{4,68},{5,69},{6,70},{7,71},{8,12},{9,... | collective-permute-start | bytes 196616 | tf_op jit(solution)/shard_map/ppermute | solution.py:243
  100.5 5.9 %collective-permute-start.24 = (bf16[128,256]{1,0:T(8,128)(2,1)S(1)}, bf16[128,256]{1,0:T(8,128)(2,1)S(1)}, u32[]{:S(2)}, u32[]{:S(2)}) collective-permute-start(bf16[128,256]{1,0:T(8,128)(2,1)S(1)} %get-tuple-element.36), channel_id=1, source_target_pairs={{0,32},{1,33},{2,34},{3,35},{4,36},{5,37},{6,38},{7,39},{8,24},{9,... | collective-permute-start | bytes 196616 | tf_op jit(solution)/shard_map/ppermute | solution.py:243
  (4 other events, 10.5 us)

commit v4 on v3

--- a/solution.py
+++ b/solution.py
@@ -47,14 +47,34 @@
     return op(op(acc[0], acc[1]), op(acc[2], acc[3]))
 
 
+def merged(lse, delta, lse_b, delta_b):
+    top = jnp.maximum(lse, lse_b)
+    w, w_b = jnp.exp2(lse - top), jnp.exp2(lse_b - top)
+    total = w + w_b
+    return top + jnp.log2(total), (w * delta + w_b * delta_b) / total
+
+
+def tiles_loop(count, step):
+    def many(i, carry):
+        for v in range(UNROLL):
+            step(i * UNROLL + v, v)
+        return carry
+
+    def few(i, carry):
+        for v in range(2):
+            step(i * 2 + v, v)
+        return carry
+
+    bodies = count // UNROLL
+    lax.fori_loop(0, bodies, many, 0)
+    lax.fori_loop(bodies * (UNROLL // 2), (count + 1) // 2, few, 0)
+
+
 def load_sorted(meta, kvs, kv_s):
-    s = 0
-    for ref in kvs:
-        for e in range(ref.shape[0]):
-            for half in range(2):
-                r = aligned(meta[IN + s], SPAN)
-                kv_s[pl.ds(r, SPAN), :] = ref[e, half * SPAN : (half + 1) * SPAN, :]
-                s += 1
+    for s in range(64):
+        r = aligned(meta[IN + s], SPAN)
+        t = slice((s % 2) * SPAN, (s % 2 + 1) * SPAN)
+        kv_s[pl.ds(r, SPAN), :] = kvs[s // 16][(s // 4) % 4, (s // 2) % 2, t, :]
 
 
 def row_of(place, h):
@@ -83,8 +103,8 @@
 
 
 def stats_kernel(meta, lim, *refs):
-    qds, kvs = refs[:4], refs[4:12]
-    out, q_s, do_s, kv_s, s0, s1, dp0, dp1, m_s, l_s, d_s = refs[12:]
+    qds, kvs = refs[:4], refs[4:8]
+    out, q_s, do_s, kv_s, s0, s1, dp0, dp1, m_s, l_s, d_s = refs[8:]
     load_sorted(meta, kvs, kv_s)
     load_rows(meta, qds, q_s, do_s)
     m_s[...] = jnp.full_like(m_s, NEG)
@@ -108,14 +128,11 @@
     ss, dps = (s0, s1), (dp0, dp1)
     products(meta, 0, q_s, do_s, kv_s, s0, dp0)
 
-    def body(i, carry):
-        for v in range(UNROLL):
-            t = i * UNROLL + v
-            products(meta, t + 1, q_s, do_s, kv_s, ss[(v + 1) % 2], dps[(v + 1) % 2])
-            online(t, ss[v % 2], dps[v % 2])
-        return carry
-
-    lax.fori_loop(0, (meta[COUNT] + UNROLL - 1) // UNROLL, body, 0)
+    def step(t, v):
+        products(meta, t + 1, q_s, do_s, kv_s, ss[(v + 1) % 2], dps[(v + 1) % 2])
+        online(t, ss[v % 2], dps[v % 2])
+
+    tiles_loop(meta[COUNT], step)
     for g in range(GROUPS):
         m = m_s[g]
         live = jnp.where(m > 0.5 * NEG, 1.0, 0.0)
@@ -129,20 +146,15 @@
     out[:, GROUPS:, :] = jnp.zeros((2, 16 - GROUPS, R), jnp.float32)
 
 
-def grads_kernel(meta, lim, st0, st1, st2, st3, *refs):
-    qds, kvs = refs[:4], refs[4:12]
-    dqs, dkvs, dkv_other = refs[12:16], refs[16:20], refs[20]
-    q_s, do_s, kv_s, s0, s1, dp0, dp1, acc, dq_s, p0, p1, ds0, ds1, lse, delta = refs[21:]
+def grads_kernel(meta, lim, st0, st1, *refs):
+    qds, kvs = refs[:4], refs[4:8]
+    dqs, dkvs, dkv_other = refs[8:12], refs[12:16], refs[16]
+    q_s, do_s, kv_s, s0, s1, dp0, dp1, acc, dq_s, p0, p1, ds0, ds1, lse, delta = refs[17:]
     load_sorted(meta, kvs, kv_s)
     load_rows(meta, qds, q_s, do_s)
     acc[...] = jnp.zeros_like(acc)
     dq_s[...] = jnp.zeros_like(dq_s)
-    sts = (st0, st1, st2, st3)
-    top = jnp.maximum(jnp.maximum(st0[0], st1[0]), jnp.maximum(st2[0], st3[0]))
-    ws = [jnp.exp2(t[0] - top) for t in sts]
-    total = ws[0] + ws[1] + ws[2] + ws[3]
-    lse[...] = top + jnp.log2(total)
-    delta[...] = sum(w * t[1] for w, t in zip(ws, sts)) / total
+    lse[...], delta[...] = merged(st0[0], st0[1], st1[0], st1[1])
     iota = lax.broadcasted_iota(jnp.int32, (KB, R), 0)
 
     def weights(t, s_b, dp_b, p_b, ds_b):
@@ -166,15 +178,13 @@
     products(meta, 1, q_s, do_s, kv_s, s1, dp1)
     weights(0, s0, dp0, p0, ds0)
 
-    def body(i, carry):
-        for v in range(UNROLL):
-            t, a, b = i * UNROLL + v, v % 2, 1 - v % 2
-            products(meta, t + 2, q_s, do_s, kv_s, ss[a], dps[a])
-            weights(t + 1, ss[b], dps[b], ps[b], dss[b])
-            sums(t, ps[a], dss[a])
-        return carry
-
-    lax.fori_loop(0, (meta[COUNT] + UNROLL - 1) // UNROLL, body, 0)
+    def step(t, v):
+        a, b = v % 2, 1 - v % 2
+        products(meta, t + 2, q_s, do_s, kv_s, ss[a], dps[a])
+        weights(t + 1, ss[b], dps[b], ps[b], dss[b])
+        sums(t, ps[a], dss[a])
+
+    tiles_loop(meta[COUNT], step)
     for d in range(4):
         for half in range(2):
             place = meta[UNIT + 2 * d + half]
@@ -185,8 +195,8 @@
     for s in range(64):
         r = aligned(meta[IN + s], SPAN)
         t = slice((s % 2) * SPAN, (s % 2 + 1) * SPAN)
-        e = (s // 2) % 4
-        ref = dkvs[s // 8] if s < 32 else dkv_other.at[s // 8 - 4]
+        second, first = s // 16, (s // 4) % 4
+        ref, e = (dkv_other.at[first], second) if (s // 2) % 2 else (dkvs[second], first)
         ref[e, t, :HD] = (acc[pl.ds(r, SPAN), :HD] * SCALE).astype(jnp.bfloat16)
         ref[e, t, HD:] = acc[pl.ds(r, SPAN), HD:].astype(jnp.bfloat16)
 
@@ -201,11 +211,44 @@
 ] + [pltpu.VMEM((KB, R), jnp.float32)] * 4
 
 
+def pack_kernel(q, do, k, v, qd, kv, sem):
+    copies = [
+        pltpu.make_async_copy(a, b, sem.at[i])
+        for i, (a, b) in enumerate(
+            (
+                (q, qd.at[:, :WIDE]),
+                (do, qd.at[:, WIDE:]),
+                (k, kv.at[:, :HD]),
+                (v, kv.at[:, HD:]),
+            )
+        )
+    ]
+    for c in copies:
+        c.start()
+    for c in copies:
+        c.wait()
+
+
+def pack(queries, grad_out, keys, values):
+    return pl.pallas_call(
+        pack_kernel,
+        out_shape=(
+            jax.ShapeDtypeStruct((2 * SPAN, 2 * WIDE), jnp.bfloat16),
+            jax.ShapeDtypeStruct((2 * SPAN, 2 * HD), jnp.bfloat16),
+        ),
+        in_specs=[pl.BlockSpec(memory_space=pltpu.HBM)] * 4,
+        out_specs=(VM, VM),
+        scratch_shapes=[pltpu.SemaphoreType.DMA((4,))],
+        compiler_params=pltpu.CompilerParams(vmem_limit_bytes=60 * 2**20),
+        name="pack",
+    )(queries, grad_out, keys, values)
+
+
 def stats(meta, lim, arrays):
     return pl.pallas_call(
         stats_kernel,
         out_shape=jax.ShapeDtypeStruct((2, 16, R), jnp.float32),
-        in_specs=[SM] + [VM] * 13,
+        in_specs=[SM] + [VM] * 9,
         out_specs=VM,
         scratch_shapes=COPIES + [pltpu.VMEM((GROUPS + 1, 8, R), jnp.float32)] * 3,
         compiler_params=PARAMS,
@@ -220,7 +263,7 @@
     return pl.pallas_call(
         grads_kernel,
         out_shape=dq + dkv,
-        in_specs=[SM] + [VM] * 17,
+        in_specs=[SM] + [VM] * 11,
         out_specs=[VM] * 9,
         scratch_shapes=COPIES
         + [
@@ -268,8 +311,8 @@
     own_x = own_x.reshape(2, 4, 4, 2)
     by_y = jnp.stack([lax.dynamic_index_in_dim(own_x, (y - r) % 4, 1, keepdims=False) for r in STEPS], 1)
     by_yz = jnp.stack([lax.dynamic_index_in_dim(by_y, (z - r) % 4, 2, keepdims=False) for r in STEPS], 2)
-    of_core = jnp.stack([jnp.transpose(by_yz[0], (1, 0, 2)), by_yz[1]])
-    arrived = jnp.where(core == 0, of_core, of_core[::-1]).reshape(64)
+    mine = jnp.where(core == 0, jnp.transpose(by_yz, (2, 1, 0, 3)), jnp.transpose(by_yz[::-1], (1, 2, 0, 3)))
+    arrived = mine.reshape(64)
     ring = grid[y, zl, core, zh]
     queries = jnp.concatenate([ring[(x - r) % 4] for r in STEPS])
 
@@ -299,18 +342,19 @@
 
 def local(queries, keys, values, grad_out, span_slot):
     meta, lim = plan(span_slot)
-    kv = jnp.concatenate([keys, values], axis=1)[None]
+    qd, kv = pack(queries, grad_out, keys, values)
+    qds = [qd] + [x_shift(qd, r) for r in STEPS[1:]]
+    kv = jnp.stack([kv, core_swap(kv)])[None]
     kv = jnp.concatenate([kv] + [first_shift(kv, r) for r in STEPS[1:]], axis=0)
     kvs = [kv] + [second_shift(kv, r) for r in STEPS[1:]]
-    qd = jnp.concatenate([queries, grad_out], axis=1)
-    qds = [qd] + [x_shift(qd, r) for r in STEPS[1:]]
-    kvs[1], meta, lim = lax.optimization_barrier((kvs[1], meta, lim))
-    arrays = qds + kvs + [core_swap(a) for a in kvs]
+    arrays = qds + kvs
 
     part = stats(meta, lim, arrays)
-    sts = [part] + [x_shift(part, r) for r in (1, 2, 3)]
-    dqs_dkv = grads(meta, lim, sts, arrays)
-    dqs, dkv, dkv_other = dqs_dkv[:4], dqs_dkv[4:8], dqs_dkv[8]
+    got = permute(part, lambda y, z, core, x: (y, z, core, x ^ 1))
+    part = jnp.stack(merged(part[0], part[1], got[0], got[1]))
+    got = permute(part, lambda y, z, core, x: (y, z, core, x ^ 2))
+    results = grads(meta, lim, (part, got), arrays)
+    dqs, dkv, dkv_other = results[:4], results[4:8], results[8]
 
     def total(*parts):
         out = parts[0].astype(jnp.float32)

time: 108 us -> 112 us (1.037)
  waiting for transfers between devices: 26.1 us -> 29.6 us
  Pallas kernels: 38.8 us -> 40.6 us
  starting transfers between devices: 33 us -> 34.3 us
    ppermute x26 -> x22, waiting for transfers between devices: 26.1 us -> 29.6 us  [permute(): return lax.ppermute(a, AXES, pairs)]
    pallas_call x0 -> x1, Pallas kernels: none -> 1.82 us  [pack(): pl.pallas_call(pack_kernel, out_shape=(jax.ShapeDtypeStruct((2 * SPAN, 2...]
    ppermute x26 -> x22, starting transfers between devices: 33 us -> 34.3 us  [permute(): return lax.ppermute(a, AXES, pairs)]
  transfers between devices with their start and end apart: 26 -> 22, of which waited for: 16 -> 12; matrix products, arithmetic and copies ran while one was open for 6% -> 4% of each run, Pallas kernels for 0% -> 0%
where the time goes in v4:
time: 112 us
  Pallas kernels  40.6 us (36%)
  starting transfers between devices  34.3 us (31%)
  waiting for transfers between devices  29.6 us (26%)
  local copies, waits for them, and re-layouts  3.99 us (4%)
  other arithmetic  2.64 us (2%)
    ppermute x22, starting transfers between devices, permute(): return lax.ppermute(a, AXES, pairs)  34.3 us
    ppermute x22, waiting for transfers between devices, permute(): return lax.ppermute(a, AXES, pairs)  29.6 us
    pallas_call x1, Pallas kernels, grads(): pl.pallas_call(grads_kernel, out_shape=dq + dkv, in_specs=[SM] + [VM] * 1...  24.6 us
    pallas_call x1, Pallas kernels, stats(): pl.pallas_call(stats_kernel, out_shape=jax.ShapeDtypeStruct((2, 16, R), j...  14.2 us
  transfers between devices with their start and end apart: 22, of which 12 were waited for; matrix products, arithmetic and copies ran while one was open for 4% of the time, Pallas kernels for 0%

profile of v4, /device:TPU:0, one launch (start us, length us, event | category | flops | bytes accessed | tf_op | source)
XLA Modules:
  0.0 112.0 jit_solution(14141948563961906282)
XLA Ops:
  0.6 1.8 %pack.1 = (bf16[128,1536]{1,0:T(8,128)(2,1)}, bf16[128,256]{1,0:T(8,128)(2,1)}) custom-call(bf16[128,768]{1,0:T(8,128)(2,1)} %q.1, bf16[128,768]{1,0:T(8,128)(2,1)} %do.1, bf16[128,128]{1,0:T(8,128)(2,1)} %k.1, bf16[128,128]{1,0:T(8,128)(2,1)} %v.1), custom_call_target="tpu_custom_call" | custom-call | tf_op jit(solution)/shard_map/pack/pallas_call | solution.py:233
  2.5 3.2 %collective-permute-start.2 = (bf16[128,1536]{1,0:T(8,128)(2,1)}, bf16[128,1536]{1,0:T(8,128)(2,1)S(1)}, u32[]{:S(2)}, u32[]{:S(2)}) collective-permute-start(bf16[128,1536]{1,0:T(8,128)(2,1)} %get-tuple-element.14.refs_0_), channel_id=1, source_target_pairs={{0,2},{1,3},{2,0},{3,1},{4,6},{5,7},{6,4},{7,5},{8,10},{9,11},{10,... | collective-permute-start | bytes 1179656 | tf_op jit(solution)/shard_map/ppermute | solution.py:286
  9.8 3.3 %collective-permute-start.6 = (bf16[1,2,128,256]{3,2,1,0:T(8,128)(2,1)S(1)}, bf16[1,2,128,256]{3,2,1,0:T(8,128)(2,1)S(1)}, u32[]{:S(2)}, u32[]{:S(2)}) collective-permute-start(bf16[1,2,128,256]{3,2,1,0:T(8,128)(2,1)S(1)} %maximum_bitcast_fusion), channel_id=1, source_target_pairs={{0,64},{1,65},{2,66},{3,67},{4,68},{5,69},{6,70},{7,71},{8,12},{9,... | collective-permute-start | bytes 393224 | tf_op jit(solution)/shard_map/ppermute | solution.py:286
  16.3 1.7 %collective-permute-done.5 = bf16[1,2,128,256]{3,2,1,0:T(8,128)(2,1)S(1)} collective-permute-done((bf16[1,2,128,256]{3,2,1,0:T(8,128)(2,1)S(1)}, bf16[1,2,128,256]{3,2,1,0:T(8,128)(2,1)S(1)}, u32[]{:S(2)}, u32[]{:S(2)}) %collective-permute-start.5) | collective-permute-done | bytes 131104 | tf_op jit(solution)/shard_map/ppermute | solution.py:286
  18.1 2.2 %collective-permute-done.4 = bf16[1,2,128,256]{3,2,1,0:T(8,128)(2,1)S(1)} collective-permute-done((bf16[1,2,128,256]{3,2,1,0:T(8,128)(2,1)S(1)}, bf16[1,2,128,256]{3,2,1,0:T(8,128)(2,1)S(1)}, u32[]{:S(2)}, u32[]{:S(2)}) %collective-permute-start.4) | collective-permute-done | bytes 131104 | tf_op jit(solution)/shard_map/ppermute | solution.py:286
  20.3 4.0 %collective-permute-start.9 = (bf16[4,2,128,256]{3,2,1,0:T(8,128)(2,1)S(1)}, bf16[4,2,128,256]{3,2,1,0:T(8,128)(2,1)S(1)}, u32[]{:S(2)}, u32[]{:S(2)}) collective-permute-start(bf16[4,2,128,256]{3,2,1,0:T(8,128)(2,1)S(1)} %pad_maximum_fusion.refs_4_), channel_id=1, source_target_pairs={{0,4},{1,5},{2,6},{3,7},{4,0},{5,1},{6,2},{7,3},{8,72},{9,73},{10,... | collective-permute-start | bytes 1572872 | tf_op jit(solution)/shard_map/ppermute | solution.py:286
  25.0 1.3 %collective-permute-start.7 = (bf16[4,2,128,256]{3,2,1,0:T(8,128)(2,1)S(1)}, bf16[4,2,128,256]{3,2,1,0:T(8,128)(2,1)S(1)}, u32[]{:S(2)}, u32[]{:S(2)}) collective-permute-start(bf16[4,2,128,256]{3,2,1,0:T(8,128)(2,1)S(1)} %pad_maximum_fusion.refs_4_), channel_id=1, source_target_pairs={{0,16},{1,17},{2,18},{3,19},{4,20},{5,21},{6,22},{7,23},{8,40},{9,... | collective-permute-start | bytes 1572872 | tf_op jit(solution)/shard_map/ppermute | solution.py:286
  29.1 7.4 %collective-permute-done.refs_1_ = bf16[128,1536]{1,0:T(8,128)(2,1)} collective-permute-done((bf16[128,1536]{1,0:T(8,128)(2,1)S(1)}, bf16[128,1536]{1,0:T(8,128)(2,1)}, u32[]{:S(2)}, u32[]{:S(2)}) %collective-permute-start) | collective-permute-done | bytes 393248 | tf_op jit(solution)/shard_map/ppermute | solution.py:286
  36.5 1.6 %collective-permute-done.8.refs_6_ = bf16[4,2,128,256]{3,2,1,0:T(8,128)(2,1)S(1)} collective-permute-done((bf16[4,2,128,256]{3,2,1,0:T(8,128)(2,1)S(1)}, bf16[4,2,128,256]{3,2,1,0:T(8,128)(2,1)S(1)}, u32[]{:S(2)}, u32[]{:S(2)}) %collective-permute-start.8) | collective-permute-done | bytes 524320 | tf_op jit(solution)/shard_map/ppermute | solution.py:286
  38.1 14.2 %stats.1 = f32[2,16,256]{2,1,0:T(8,128)S(1)} custom-call(s32[345]{0:T(512)S(1)} %concatenate.13.meta, s32[16,256]{1,0:T(8,128)S(1)} %concatenate.14.lim, bf16[128,1536]{1,0:T(8,128)(2,1)S(1)} %copy-done, bf16[128,1536]{1,0:T(8,128)(2,1)} %collective-permute-done.refs_1_, bf16[128,1536]{1,0:T(8,128)(2,1)S(1)} %collective-permute-done.1.refs_2_, ...), custom_call_target="tpu_custom_call" | custom-call | tf_op jit(solution)/shard_map/stats/pallas_call | solution.py:248
  53.7 2.7 %collective-permute-done.10 = f32[2,16,256]{2,1,0:T(8,128)S(1)} collective-permute-done((f32[2,16,256]{2,1,0:T(8,128)S(1)}, f32[2,16,256]{2,1,0:T(8,128)S(1)}, u32[]{:S(2)}, u32[]{:S(2)}) %collective-permute-start.10) | collective-permute-done | bytes 32800 | tf_op jit(solution)/shard_map/ppermute | solution.py:286
  56.4 1.6 %collective-permute-start.11 = (f32[2,16,256]{2,1,0:T(8,128)S(1)}, f32[2,16,256]{2,1,0:T(8,128)S(1)}, u32[]{:S(2)}, u32[]{:S(2)}) collective-permute-start(f32[2,16,256]{2,1,0:T(8,128)S(1)} %pad_maximum_fusion.1.st0), channel_id=1, source_target_pairs={{0,2},{1,3},{2,0},{3,1},{4,6},{5,7},{6,4},{7,5},{8,10},{9,11},{10,... | collective-permute-start | bytes 98312 | tf_op jit(solution)/shard_map/ppermute | solution.py:286
  58.0 3.9 %collective-permute-done.11.st1 = f32[2,16,256]{2,1,0:T(8,128)S(1)} collective-permute-done((f32[2,16,256]{2,1,0:T(8,128)S(1)}, f32[2,16,256]{2,1,0:T(8,128)S(1)}, u32[]{:S(2)}, u32[]{:S(2)}) %collective-permute-start.11) | collective-permute-done | bytes 32800 | tf_op jit(solution)/shard_map/ppermute | solution.py:286
  61.9 24.6 %grads.1 = (f32[128,768]{1,0:T(8,128)S(1)}, bf16[128,768]{1,0:T(8,128)(2,1)S(1)}, bf16[128,768]{1,0:T(8,128)(2,1)S(1)}, bf16[128,768]{1,0:T(8,128)(2,1)S(1)}, bf...) custom-call(s32[345]{0:T(512)S(1)} %concatenate.13.meta, ...), custom_call_target="tpu_custom_call" | custom-call | tf_op jit(solution)/shard_map/grads/pallas_call | solution.py:263
  86.5 2.9 %collective-permute-done.15 = bf16[4,4,128,256]{3,2,1,0:T(8,128)(2,1)S(1)} collective-permute-done((bf16[4,4,128,256]{3,2,1,0:T(8,128)(2,1)}, bf16[4,4,128,256]{3,2,1,0:T(8,128)(2,1)S(1)}, u32[]{:S(2)}, u32[]{:S(2)}) %collective-permute-start.15) | collective-permute-done | bytes 1048608 | tf_op jit(solution)/shard_map/ppermute | solution.py:286
  89.6 2.0 %collective-permute-start.16 = (bf16[4,128,256]{2,1,0:T(8,128)(2,1)S(1)}, bf16[4,128,256]{2,1,0:T(8,128)(2,1)S(1)}, u32[]{:S(2)}, u32[]{:S(2)}) collective-permute-start(bf16[4,128,256]{2,1,0:T(8,128)(2,1)S(1)} %get-tuple-element.29), channel_id=1, source_target_pairs={{0,20},{1,21},{2,22},{3,23},{4,16},{5,17},{6,18},{7,19},{8,104},{9... | collective-permute-start | bytes 786440 | tf_op jit(solution)/shard_map/ppermute | solution.py:286
  91.6 1.6 %collective-permute-start.18 = (bf16[4,128,256]{2,1,0:T(8,128)(2,1)S(1)}, bf16[4,128,256]{2,1,0:T(8,128)(2,1)S(1)}, u32[]{:S(2)}, u32[]{:S(2)}) collective-permute-start(bf16[4,128,256]{2,1,0:T(8,128)(2,1)S(1)} %get-tuple-element.30), channel_id=1, source_target_pairs={{0,4},{1,5},{2,6},{3,7},{4,0},{5,1},{6,2},{7,3},{8,72},{9,73},{10,... | collective-permute-start | bytes 786440 | tf_op jit(solution)/shard_map/ppermute | solution.py:286
  93.2 1.3 %collective-permute-start.17 = (bf16[4,128,256]{2,1,0:T(8,128)(2,1)S(1)}, bf16[4,128,256]{2,1,0:T(8,128)(2,1)S(1)}, u32[]{:S(2)}, u32[]{:S(2)}) collective-permute-start(bf16[4,128,256]{2,1,0:T(8,128)(2,1)S(1)} %get-tuple-element.31), channel_id=1, source_target_pairs={{0,16},{1,17},{2,18},{3,19},{4,20},{5,21},{6,22},{7,23},{8,40},{9,... | collective-permute-start | bytes 786440 | tf_op jit(solution)/shard_map/ppermute | solution.py:286
  94.6 2.0 %collective-permute-start.13 = (bf16[128,768]{1,0:T(8,128)(2,1)S(1)}, bf16[128,768]{1,0:T(8,128)(2,1)S(1)}, u32[]{:S(2)}, u32[]{:S(2)}) collective-permute-start(bf16[128,768]{1,0:T(8,128)(2,1)S(1)} %get-tuple-element.18), channel_id=1, source_target_pairs={{0,1},{1,2},{2,3},{3,0},{4,5},{5,6},{6,7},{7,4},{8,9},{9,10},{10,1... | collective-permute-start | bytes 589832 | tf_op jit(solution)/shard_map/ppermute | solution.py:286
  96.6 4.5 %collective-permute-start.14 = (bf16[128,768]{1,0:T(8,128)(2,1)S(1)}, bf16[128,768]{1,0:T(8,128)(2,1)S(1)}, u32[]{:S(2)}, u32[]{:S(2)}) collective-permute-start(bf16[128,768]{1,0:T(8,128)(2,1)S(1)} %get-tuple-element.19), channel_id=1, source_target_pairs={{0,2},{1,3},{2,0},{3,1},{4,6},{5,7},{6,4},{7,5},{8,10},{9,11},{10,... | collective-permute-start | bytes 589832 | tf_op jit(solution)/shard_map/ppermute | solution.py:286
  102.5 1.6 %collective-permute-start.19 = (bf16[128,256]{1,0:T(8,128)(2,1)S(1)}, bf16[128,256]{1,0:T(8,128)(2,1)S(1)}, u32[]{:S(2)}, u32[]{:S(2)}) collective-permute-start(bf16[128,256]{1,0:T(8,128)(2,1)S(1)} %get-tuple-element.32), channel_id=1, source_target_pairs={{0,96},{1,97},{2,98},{3,99},{4,100},{5,101},{6,102},{7,103},{8,28}... | collective-permute-start | bytes 196616 | tf_op jit(solution)/shard_map/ppermute | solution.py:286
  104.1 1.8 %collective-permute-start.21 = (bf16[128,256]{1,0:T(8,128)(2,1)S(1)}, bf16[128,256]{1,0:T(8,128)(2,1)S(1)}, u32[]{:S(2)}, u32[]{:S(2)}) collective-permute-start(bf16[128,256]{1,0:T(8,128)(2,1)S(1)} %get-tuple-element.33), channel_id=1, source_target_pairs={{0,64},{1,65},{2,66},{3,67},{4,68},{5,69},{6,70},{7,71},{8,12},{9,... | collective-permute-start | bytes 196616 | tf_op jit(solution)/shard_map/ppermute | solution.py:286
  106.9 3.0 %collective-permute-done.21 = bf16[128,256]{1,0:T(8,128)(2,1)S(1)} collective-permute-done((bf16[128,256]{1,0:T(8,128)(2,1)S(1)}, bf16[128,256]{1,0:T(8,128)(2,1)S(1)}, u32[]{:S(2)}, u32[]{:S(2)}) %collective-permute-start.21) | collective-permute-done | bytes 65568 | tf_op jit(solution)/shard_map/ppermute | solution.py:286
  109.8 1.5 %collective-permute-done.20 = bf16[128,256]{1,0:T(8,128)(2,1)S(1)} collective-permute-done((bf16[128,256]{1,0:T(8,128)(2,1)S(1)}, bf16[128,256]{1,0:T(8,128)(2,1)S(1)}, u32[]{:S(2)}, u32[]{:S(2)}) %collective-permute-start.20) | collective-permute-done | bytes 65568 | tf_op jit(solution)/shard_map/ppermute | solution.py:286
  (77 shorter events, 15.4 us)
Async XLA Ops:
  2.5 24.1 %collective-permute-start.2 = (bf16[128,1536]{1,0:T(8,128)(2,1)}, bf16[128,1536]{1,0:T(8,128)(2,1)S(1)}, u32[]{:S(2)}, u32[]{:S(2)}) collective-permute-start(bf16[128,1536]{1,0:T(8,128)(2,1)} %get-tuple-element.14.refs_0_), channel_id=1, source_target_pairs={{0,2},{1,3},{2,0},{3,1},{4,6},{5,7},{6,4},{7,5},{8,10},{9,11},{10,... | collective-permute-start | bytes 1179656 | tf_op jit(solution)/shard_map/ppermute | solution.py:286
  5.6 23.5 %collective-permute-start.1 = (bf16[128,1536]{1,0:T(8,128)(2,1)}, bf16[128,1536]{1,0:T(8,128)(2,1)S(1)}, u32[]{:S(2)}, u32[]{:S(2)}) collective-permute-start(bf16[128,1536]{1,0:T(8,128)(2,1)} %get-tuple-element.14.refs_0_), channel_id=1, source_target_pairs={{0,3},{1,0},{2,1},{3,2},{4,7},{5,4},{6,5},{7,6},{8,11},{9,8},{10,9... | collective-permute-start | bytes 1179656 | tf_op jit(solution)/shard_map/ppermute | solution.py:286
  6.8 3.0 %collective-permute-start.3 = (bf16[128,256]{1,0:T(8,128)(2,1)}, bf16[128,256]{1,0:T(8,128)(2,1)S(1)}, u32[]{:S(2)}, u32[]{:S(2)}) collective-permute-start(bf16[128,256]{1,0:T(8,128)(2,1)} %get-tuple-element.15), channel_id=1, source_target_pairs={{0,8},{1,9},{2,10},{3,11},{4,12},{5,13},{6,14},{7,15},{8,0},{9,1},... | collective-permute-start | bytes 196616 | tf_op jit(solution)/shard_map/ppermute | solution.py:286
  8.5 1.3 %copy-start.1 = (bf16[128,256]{1,0:T(8,128)(2,1)S(1)}, bf16[128,256]{1,0:T(8,128)(2,1)}, u32[]{:S(2)}) copy-start(bf16[128,256]{1,0:T(8,128)(2,1)} %get-tuple-element.15) | copy-start | bytes 196612
  9.8 6.6 %collective-permute-start.6 = (bf16[1,2,128,256]{3,2,1,0:T(8,128)(2,1)S(1)}, bf16[1,2,128,256]{3,2,1,0:T(8,128)(2,1)S(1)}, u32[]{:S(2)}, u32[]{:S(2)}) collective-permute-start(bf16[1,2,128,256]{3,2,1,0:T(8,128)(2,1)S(1)} %maximum_bitcast_fusion), channel_id=1, source_target_pairs={{0,64},{1,65},{2,66},{3,67},{4,68},{5,69},{6,70},{7,71},{8,12},{9,... | collective-permute-start | bytes 393224 | tf_op jit(solution)/shard_map/ppermute | solution.py:286
  13.0 5.0 %collective-permute-start.5 = (bf16[1,2,128,256]{3,2,1,0:T(8,128)(2,1)S(1)}, bf16[1,2,128,256]{3,2,1,0:T(8,128)(2,1)S(1)}, u32[]{:S(2)}, u32[]{:S(2)}) collective-permute-start(bf16[1,2,128,256]{3,2,1,0:T(8,128)(2,1)S(1)} %maximum_bitcast_fusion), channel_id=1, source_target_pairs={{0,96},{1,97},{2,98},{3,99},{4,100},{5,101},{6,102},{7,103},{8,28}... | collective-permute-start | bytes 393224 | tf_op jit(solution)/shard_map/ppermute | solution.py:286
  14.1 6.2 %collective-permute-start.4 = (bf16[1,2,128,256]{3,2,1,0:T(8,128)(2,1)S(1)}, bf16[1,2,128,256]{3,2,1,0:T(8,128)(2,1)S(1)}, u32[]{:S(2)}, u32[]{:S(2)}) collective-permute-start(bf16[1,2,128,256]{3,2,1,0:T(8,128)(2,1)S(1)} %maximum_bitcast_fusion), channel_id=1, source_target_pairs={{0,32},{1,33},{2,34},{3,35},{4,36},{5,37},{6,38},{7,39},{8,24},{9,... | collective-permute-start | bytes 393224 | tf_op jit(solution)/shard_map/ppermute | solution.py:286
  15.1 11.4 %copy-start = (bf16[128,1536]{1,0:T(8,128)(2,1)S(1)}, bf16[128,1536]{1,0:T(8,128)(2,1)}, u32[]{:S(2)}) copy-start(bf16[128,1536]{1,0:T(8,128)(2,1)} %get-tuple-element.14.refs_0_) | copy-start | bytes 1179652
  20.3 16.2 %collective-permute-start.9 = (bf16[4,2,128,256]{3,2,1,0:T(8,128)(2,1)S(1)}, bf16[4,2,128,256]{3,2,1,0:T(8,128)(2,1)S(1)}, u32[]{:S(2)}, u32[]{:S(2)}) collective-permute-start(bf16[4,2,128,256]{3,2,1,0:T(8,128)(2,1)S(1)} %pad_maximum_fusion.refs_4_), channel_id=1, source_target_pairs={{0,4},{1,5},{2,6},{3,7},{4,0},{5,1},{6,2},{7,3},{8,72},{9,73},{10,... | collective-permute-start | bytes 1572872 | tf_op jit(solution)/shard_map/ppermute | solution.py:286
  24.3 13.8 %collective-permute-start.8 = (bf16[4,2,128,256]{3,2,1,0:T(8,128)(2,1)S(1)}, bf16[4,2,128,256]{3,2,1,0:T(8,128)(2,1)S(1)}, u32[]{:S(2)}, u32[]{:S(2)}) collective-permute-start(bf16[4,2,128,256]{3,2,1,0:T(8,128)(2,1)S(1)} %pad_maximum_fusion.refs_4_), channel_id=1, source_target_pairs={{0,20},{1,21},{2,22},{3,23},{4,16},{5,17},{6,18},{7,19},{8,104},{9... | collective-permute-start | bytes 1572872 | tf_op jit(solution)/shard_map/ppermute | solution.py:286
  25.0 13.1 %collective-permute-start.7 = (bf16[4,2,128,256]{3,2,1,0:T(8,128)(2,1)S(1)}, bf16[4,2,128,256]{3,2,1,0:T(8,128)(2,1)S(1)}, u32[]{:S(2)}, u32[]{:S(2)}) collective-permute-start(bf16[4,2,128,256]{3,2,1,0:T(8,128)(2,1)S(1)} %pad_maximum_fusion.refs_4_), channel_id=1, source_target_pairs={{0,16},{1,17},{2,18},{3,19},{4,20},{5,21},{6,22},{7,23},{8,40},{9,... | collective-permute-start | bytes 1572872 | tf_op jit(solution)/shard_map/ppermute | solution.py:286
  26.5 10.0 %collective-permute-start = (bf16[128,1536]{1,0:T(8,128)(2,1)S(1)}, bf16[128,1536]{1,0:T(8,128)(2,1)}, u32[]{:S(2)}, u32[]{:S(2)}) collective-permute-start(bf16[128,1536]{1,0:T(8,128)(2,1)S(1)} %copy-done), channel_id=1, source_target_pairs={{0,1},{1,2},{2,3},{3,0},{4,5},{5,6},{6,7},{7,4},{8,9},{9,10},{10,1... | collective-permute-start | bytes 1179656 | tf_op jit(solution)/shard_map/ppermute | solution.py:286
  52.4 4.0 %collective-permute-start.10 = (f32[2,16,256]{2,1,0:T(8,128)S(1)}, f32[2,16,256]{2,1,0:T(8,128)S(1)}, u32[]{:S(2)}, u32[]{:S(2)}) collective-permute-start(f32[2,16,256]{2,1,0:T(8,128)S(1)} %stats.1), channel_id=1, source_target_pairs={{0,1},{1,0},{2,3},{3,2},{4,5},{5,4},{6,7},{7,6},{8,9},{9,8},{10,11... | collective-permute-start | bytes 98312 | tf_op jit(solution)/shard_map/ppermute | solution.py:286
  56.4 5.5 %collective-permute-start.11 = (f32[2,16,256]{2,1,0:T(8,128)S(1)}, f32[2,16,256]{2,1,0:T(8,128)S(1)}, u32[]{:S(2)}, u32[]{:S(2)}) collective-permute-start(f32[2,16,256]{2,1,0:T(8,128)S(1)} %pad_maximum_fusion.1.st0), channel_id=1, source_target_pairs={{0,2},{1,3},{2,0},{3,1},{4,6},{5,7},{6,4},{7,5},{8,10},{9,11},{10,... | collective-permute-start | bytes 98312 | tf_op jit(solution)/shard_map/ppermute | solution.py:286
  86.5 2.9 %collective-permute-start.15 = (bf16[4,4,128,256]{3,2,1,0:T(8,128)(2,1)}, bf16[4,4,128,256]{3,2,1,0:T(8,128)(2,1)S(1)}, u32[]{:S(2)}, u32[]{:S(2)}) collective-permute-start(bf16[4,4,128,256]{3,2,1,0:T(8,128)(2,1)} %get-tuple-element.21), channel_id=1, source_target_pairs={{0,8},{1,9},{2,10},{3,11},{4,12},{5,13},{6,14},{7,15},{8,0},{9,1},... | collective-permute-start | bytes 3145736 | tf_op jit(solution)/shard_map/ppermute | solution.py:286
  89.6 7.0 %collective-permute-start.16 = (bf16[4,128,256]{2,1,0:T(8,128)(2,1)S(1)}, bf16[4,128,256]{2,1,0:T(8,128)(2,1)S(1)}, u32[]{:S(2)}, u32[]{:S(2)}) collective-permute-start(bf16[4,128,256]{2,1,0:T(8,128)(2,1)S(1)} %get-tuple-element.29), channel_id=1, source_target_pairs={{0,20},{1,21},{2,22},{3,23},{4,16},{5,17},{6,18},{7,19},{8,104},{9... | collective-permute-start | bytes 786440 | tf_op jit(solution)/shard_map/ppermute | solution.py:286
  91.6 9.5 %collective-permute-start.18 = (bf16[4,128,256]{2,1,0:T(8,128)(2,1)S(1)}, bf16[4,128,256]{2,1,0:T(8,128)(2,1)S(1)}, u32[]{:S(2)}, u32[]{:S(2)}) collective-permute-start(bf16[4,128,256]{2,1,0:T(8,128)(2,1)S(1)} %get-tuple-element.30), channel_id=1, source_target_pairs={{0,4},{1,5},{2,6},{3,7},{4,0},{5,1},{6,2},{7,3},{8,72},{9,73},{10,... | collective-permute-start | bytes 786440 | tf_op jit(solution)/shard_map/ppermute | solution.py:286
  93.2 9.1 %collective-permute-start.17 = (bf16[4,128,256]{2,1,0:T(8,128)(2,1)S(1)}, bf16[4,128,256]{2,1,0:T(8,128)(2,1)S(1)}, u32[]{:S(2)}, u32[]{:S(2)}) collective-permute-start(bf16[4,128,256]{2,1,0:T(8,128)(2,1)S(1)} %get-tuple-element.31), channel_id=1, source_target_pairs={{0,16},{1,17},{2,18},{3,19},{4,20},{5,21},{6,22},{7,23},{8,40},{9,... | collective-permute-start | bytes 786440 | tf_op jit(solution)/shard_map/ppermute | solution.py:286
  94.6 11.3 %collective-permute-start.12 = (bf16[128,768]{1,0:T(8,128)(2,1)S(1)}, bf16[128,768]{1,0:T(8,128)(2,1)S(1)}, u32[]{:S(2)}, u32[]{:S(2)}) collective-permute-start(bf16[128,768]{1,0:T(8,128)(2,1)S(1)} %get-tuple-element.17), channel_id=1, source_target_pairs={{0,3},{1,0},{2,1},{3,2},{4,7},{5,4},{6,5},{7,6},{8,11},{9,8},{10,9... | collective-permute-start | bytes 589832 | tf_op jit(solution)/shard_map/ppermute | solution.py:286
  94.6 11.3 %collective-permute-start.13 = (bf16[128,768]{1,0:T(8,128)(2,1)S(1)}, bf16[128,768]{1,0:T(8,128)(2,1)S(1)}, u32[]{:S(2)}, u32[]{:S(2)}) collective-permute-start(bf16[128,768]{1,0:T(8,128)(2,1)S(1)} %get-tuple-element.18), channel_id=1, source_target_pairs={{0,1},{1,2},{2,3},{3,0},{4,5},{5,6},{6,7},{7,4},{8,9},{9,10},{10,1... | collective-permute-start | bytes 589832 | tf_op jit(solution)/shard_map/ppermute | solution.py:286
  96.6 9.5 %collective-permute-start.14 = (bf16[128,768]{1,0:T(8,128)(2,1)S(1)}, bf16[128,768]{1,0:T(8,128)(2,1)S(1)}, u32[]{:S(2)}, u32[]{:S(2)}) collective-permute-start(bf16[128,768]{1,0:T(8,128)(2,1)S(1)} %get-tuple-element.19), channel_id=1, source_target_pairs={{0,2},{1,3},{2,0},{3,1},{4,6},{5,7},{6,4},{7,5},{8,10},{9,11},{10,... | collective-permute-start | bytes 589832 | tf_op jit(solution)/shard_map/ppermute | solution.py:286
  102.5 4.4 %collective-permute-start.19 = (bf16[128,256]{1,0:T(8,128)(2,1)S(1)}, bf16[128,256]{1,0:T(8,128)(2,1)S(1)}, u32[]{:S(2)}, u32[]{:S(2)}) collective-permute-start(bf16[128,256]{1,0:T(8,128)(2,1)S(1)} %get-tuple-element.32), channel_id=1, source_target_pairs={{0,96},{1,97},{2,98},{3,99},{4,100},{5,101},{6,102},{7,103},{8,28}... | collective-permute-start | bytes 196616 | tf_op jit(solution)/shard_map/ppermute | solution.py:286
  104.1 5.8 %collective-permute-start.21 = (bf16[128,256]{1,0:T(8,128)(2,1)S(1)}, bf16[128,256]{1,0:T(8,128)(2,1)S(1)}, u32[]{:S(2)}, u32[]{:S(2)}) collective-permute-start(bf16[128,256]{1,0:T(8,128)(2,1)S(1)} %get-tuple-element.33), channel_id=1, source_target_pairs={{0,64},{1,65},{2,66},{3,67},{4,68},{5,69},{6,70},{7,71},{8,12},{9,... | collective-permute-start | bytes 196616 | tf_op jit(solution)/shard_map/ppermute | solution.py:286
  105.9 5.5 %collective-permute-start.20 = (bf16[128,256]{1,0:T(8,128)(2,1)S(1)}, bf16[128,256]{1,0:T(8,128)(2,1)S(1)}, u32[]{:S(2)}, u32[]{:S(2)}) collective-permute-start(bf16[128,256]{1,0:T(8,128)(2,1)S(1)} %get-tuple-element.34), channel_id=1, source_target_pairs={{0,32},{1,33},{2,34},{3,35},{4,36},{5,37},{6,38},{7,39},{8,24},{9,... | collective-permute-start | bytes 196616 | tf_op jit(solution)/shard_map/ppermute | solution.py:286
  (1 other events, 0.7 us)

commit v5 on v4

--- a/solution.py
+++ b/solution.py
@@ -1,3 +1,4 @@
+import functools
 import math
 
 import jax
@@ -24,8 +25,16 @@
 GROUPS = 12
 UNROLL = 8
 LIST = 136
-IN, UNIT, COUNT = 0, 64, 72
-GROUP, BLOCK = 73, 73 + LIST
+IN = 0
+ALL, NEAR, FAR = range(3)
+UNIT, CANON, COUNT, GROUP = 0, 8, 16, 17
+BLOCK = GROUP + LIST
+SIZE = BLOCK + LIST
+
+
+def of(which):
+    return 64 + which * SIZE
+
 
 NT = (((1,), (1,)), ((), ()))
 NN = (((1,), (0,)), ((), ()))
@@ -74,7 +83,7 @@
     for s in range(64):
         r = aligned(meta[IN + s], SPAN)
         t = slice((s % 2) * SPAN, (s % 2 + 1) * SPAN)
-        kv_s[pl.ds(r, SPAN), :] = kvs[s // 16][(s // 4) % 4, (s // 2) % 2, t, :]
+        kv_s[pl.ds(r, SPAN), :] = kvs[s // 8][(s // 2) % 4, t, :]
 
 
 def row_of(place, h):
@@ -83,38 +92,46 @@
     return pl.multiple_of((place // 2) * 768 + inner, SPAN)
 
 
-def load_rows(meta, qds, q_s, do_s):
+def load_rows(meta, base, qds, q_s, do_s, first=0):
     for d, ref in enumerate(qds):
         for half in range(2):
-            place = meta[UNIT + 2 * d + half]
+            place = meta[base + UNIT + 2 * (first + d) + half]
             t = slice(half * SPAN, (half + 1) * SPAN)
             for h in range(HEADS):
                 r = row_of(place, h)
                 q_s[pl.ds(r, SPAN), :] = ref[t, h * HD : (h + 1) * HD]
                 do_s[pl.ds(r, SPAN), :] = ref[t, WIDE + h * HD : WIDE + (h + 1) * HD]
-    q_s[GROUPS * R :, :] = jnp.zeros((R, HD), q_s.dtype)
-    do_s[GROUPS * R :, :] = jnp.zeros((R, HD), do_s.dtype)
-
-
-def products(meta, t, q_s, do_s, kv_s, s_b, dp_b):
-    r, k = aligned(meta[GROUP + t], R), aligned(meta[BLOCK + t], KB)
+    rows = 3 * R * len(qds)
+    q_s[rows : rows + R, :] = jnp.zeros((R, HD), q_s.dtype)
+    do_s[rows : rows + R, :] = jnp.zeros((R, HD), do_s.dtype)
+
+
+def products(meta, base, t, q_s, do_s, kv_s, s_b, dp_b):
+    r, k = aligned(meta[base + GROUP + t], R), aligned(meta[base + BLOCK + t], KB)
     s_b[...] = dot(kv_s[pl.ds(k, KB), :HD], q_s[pl.ds(r, R), :], NT)
     dp_b[...] = dot(kv_s[pl.ds(k, KB), HD:], do_s[pl.ds(r, R), :], NT)
 
 
-def stats_kernel(meta, lim, *refs):
-    qds, kvs = refs[:4], refs[4:8]
-    out, q_s, do_s, kv_s, s0, s1, dp0, dp1, m_s, l_s, d_s = refs[8:]
+HALVES = ((0, 1), (2, 5), (3, 4))
+
+
+def stats_kernel(which, devices, meta, lim, *refs):
+    qds, kvs = refs[:devices], refs[devices : devices + 8]
+    rest = refs[devices + 8 :]
+    if which == FAR:
+        before, rest = rest[0], rest[1:]
+    out, q_s, do_s, kv_s, s0, s1, dp0, dp1, m_s, l_s, d_s = rest
+    base, groups = of(which), 3 * devices
     load_sorted(meta, kvs, kv_s)
-    load_rows(meta, qds, q_s, do_s)
+    load_rows(meta, base, qds, q_s, do_s, first=3 if which == FAR else 0)
     m_s[...] = jnp.full_like(m_s, NEG)
     l_s[...] = jnp.zeros_like(l_s)
     d_s[...] = jnp.zeros_like(d_s)
     iota = lax.broadcasted_iota(jnp.int32, (KB, R), 0)
 
     def online(t, s_b, dp_b):
-        g = meta[GROUP + t]
-        limit = lim[pl.ds(g, 1), :] - meta[BLOCK + t] * KB
+        g = meta[base + GROUP + t]
+        limit = lim[which, pl.ds(g, 1), :] - meta[base + BLOCK + t] * KB
         rows = [slice(8 * i, 8 * i + 8) for i in range(KB // 8)]
         s = [jnp.where(iota[r] < limit, s_b[r, :] * C2, NEG) for r in rows]
         m = m_s[g]
@@ -126,14 +143,15 @@
         d_s[g] = d_s[g] * a + tree(jnp.add, [x * dp_b[r, :] for r, x in zip(rows, e)])
 
     ss, dps = (s0, s1), (dp0, dp1)
-    products(meta, 0, q_s, do_s, kv_s, s0, dp0)
+    products(meta, base, 0, q_s, do_s, kv_s, s0, dp0)
 
     def step(t, v):
-        products(meta, t + 1, q_s, do_s, kv_s, ss[(v + 1) % 2], dps[(v + 1) % 2])
+        products(meta, base, t + 1, q_s, do_s, kv_s, ss[(v + 1) % 2], dps[(v + 1) % 2])
         online(t, ss[v % 2], dps[v % 2])
 
-    tiles_loop(meta[COUNT], step)
-    for g in range(GROUPS):
+    tiles_loop(meta[base + COUNT], step)
+    out[...] = before[...] if which == FAR else jnp.zeros_like(out)
+    for g in range(groups):
         m = m_s[g]
         live = jnp.where(m > 0.5 * NEG, 1.0, 0.0)
         top = jnp.max(m, axis=0, keepdims=True)
@@ -141,31 +159,44 @@
         ll = jnp.sum(l_s[g] * a, axis=0, keepdims=True)
         dd = jnp.sum(d_s[g] * a, axis=0, keepdims=True)
         safe = jnp.where(ll > 0, ll, 1.0)
-        out[0, g : g + 1, :] = jnp.where(ll > 0, top + jnp.log2(safe), NEG)
-        out[1, g : g + 1, :] = dd / safe
-    out[:, GROUPS:, :] = jnp.zeros((2, 16 - GROUPS, R), jnp.float32)
+        lse = jnp.where(ll > 0, top + jnp.log2(safe), NEG)
+        for half in range(2):
+            place, pair = divmod(HALVES[g % 3][half], 3)
+            row = meta[base + CANON + g // 3 * 2 + place] * 3 + pair
+            at = slice(half * 128, half * 128 + 128)
+            out[0, pl.ds(row, 1), :] = lse[:, at]
+            out[1, pl.ds(row, 1), :] = (dd / safe)[:, at]
 
 
 def grads_kernel(meta, lim, st0, st1, *refs):
-    qds, kvs = refs[:4], refs[4:8]
-    dqs, dkvs, dkv_other = refs[8:12], refs[12:16], refs[16]
-    q_s, do_s, kv_s, s0, s1, dp0, dp1, acc, dq_s, p0, p1, ds0, ds1, lse, delta = refs[17:]
+    qds, kvs = refs[:4], refs[4:12]
+    dqs, dkvs, dkv_other = refs[12:16], refs[16:20], refs[20]
+    q_s, do_s, kv_s, s0, s1, dp0, dp1, acc, dq_s, p0, p1, ds0, ds1, lse, delta = refs[21:]
     load_sorted(meta, kvs, kv_s)
-    load_rows(meta, qds, q_s, do_s)
+    base = of(ALL)
+    load_rows(meta, base, qds, q_s, do_s)
     acc[...] = jnp.zeros_like(acc)
     dq_s[...] = jnp.zeros_like(dq_s)
-    lse[...], delta[...] = merged(st0[0], st0[1], st1[0], st1[1])
+    all_lse, all_delta = merged(st0[0], st0[1], st1[0], st1[1])
+    lse[...] = jnp.zeros_like(lse)
+    delta[...] = jnp.zeros_like(delta)
+    for g in range(GROUPS):
+        for half in range(2):
+            row = g // 3 * 6 + HALVES[g % 3][half]
+            at = slice(half * 128, half * 128 + 128)
+            lse[g : g + 1, at] = all_lse[row : row + 1]
+            delta[g : g + 1, at] = all_delta[row : row + 1]
     iota = lax.broadcasted_iota(jnp.int32, (KB, R), 0)
 
     def weights(t, s_b, dp_b, p_b, ds_b):
-        g = meta[GROUP + t]
-        limit = lim[pl.ds(g, 1), :] - meta[BLOCK + t] * KB
+        g = meta[base + GROUP + t]
+        limit = lim[ALL, pl.ds(g, 1), :] - meta[base + BLOCK + t] * KB
         p = jnp.where(iota < limit, jnp.exp2(s_b[...] * C2 - lse[pl.ds(g, 1), :]), 0.0)
         p_b[...] = p.astype(jnp.bfloat16)
         ds_b[...] = (p * (dp_b[...] - delta[pl.ds(g, 1), :])).astype(jnp.bfloat16)
 
     def sums(t, p_b, ds_b):
-        r, k = aligned(meta[GROUP + t], R), aligned(meta[BLOCK + t], KB)
+        r, k = aligned(meta[base + GROUP + t], R), aligned(meta[base + BLOCK + t], KB)
         dk = dot(ds_b[...], q_s[pl.ds(r, R), :], NN)
         dv = dot(p_b[...], do_s[pl.ds(r, R), :], NN)
         dq = dot(ds_b[...], kv_s[pl.ds(k, KB), :HD], TN)
@@ -174,20 +205,20 @@
         dq_s[pl.ds(r, R), :] += dq
 
     ss, dps, ps, dss = (s0, s1), (dp0, dp1), (p0, p1), (ds0, ds1)
-    products(meta, 0, q_s, do_s, kv_s, s0, dp0)
-    products(meta, 1, q_s, do_s, kv_s, s1, dp1)
+    products(meta, base, 0, q_s, do_s, kv_s, s0, dp0)
+    products(meta, base, 1, q_s, do_s, kv_s, s1, dp1)
     weights(0, s0, dp0, p0, ds0)
 
     def step(t, v):
         a, b = v % 2, 1 - v % 2
-        products(meta, t + 2, q_s, do_s, kv_s, ss[a], dps[a])
+        products(meta, base, t + 2, q_s, do_s, kv_s, ss[a], dps[a])
         weights(t + 1, ss[b], dps[b], ps[b], dss[b])
         sums(t, ps[a], dss[a])
 
-    tiles_loop(meta[COUNT], step)
+    tiles_loop(meta[base + COUNT], step)
     for d in range(4):
         for half in range(2):
-            place = meta[UNIT + 2 * d + half]
+            place = meta[base + UNIT + 2 * d + half]
             t = slice(half * SPAN, (half + 1) * SPAN)
             for h in range(HEADS):
                 got = dq_s[pl.ds(row_of(place, h), SPAN), :] * SCALE
@@ -195,8 +226,8 @@
     for s in range(64):
         r = aligned(meta[IN + s], SPAN)
         t = slice((s % 2) * SPAN, (s % 2 + 1) * SPAN)
-        second, first = s // 16, (s // 4) % 4
-        ref, e = (dkv_other.at[first], second) if (s // 2) % 2 else (dkvs[second], first)
+        e = (s // 2) % 4
+        ref = dkvs[s // 8] if s < 32 else dkv_other.at[s // 8 - 4]
         ref[e, t, :HD] = (acc[pl.ds(r, SPAN), :HD] * SCALE).astype(jnp.bfloat16)
         ref[e, t, HD:] = acc[pl.ds(r, SPAN), HD:].astype(jnp.bfloat16)
 
@@ -211,49 +242,18 @@
 ] + [pltpu.VMEM((KB, R), jnp.float32)] * 4
 
 
-def pack_kernel(q, do, k, v, qd, kv, sem):
-    copies = [
-        pltpu.make_async_copy(a, b, sem.at[i])
-        for i, (a, b) in enumerate(
-            (
-                (q, qd.at[:, :WIDE]),
-                (do, qd.at[:, WIDE:]),
-                (k, kv.at[:, :HD]),
-                (v, kv.at[:, HD:]),
-            )
-        )
-    ]
-    for c in copies:
-        c.start()
-    for c in copies:
-        c.wait()
-
-
-def pack(queries, grad_out, keys, values):
+def stats(which, meta, lim, qds, kvs, *before):
+    n = len(qds)
     return pl.pallas_call(
-        pack_kernel,
-        out_shape=(
-            jax.ShapeDtypeStruct((2 * SPAN, 2 * WIDE), jnp.bfloat16),
-            jax.ShapeDtypeStruct((2 * SPAN, 2 * HD), jnp.bfloat16),
-        ),
-        in_specs=[pl.BlockSpec(memory_space=pltpu.HBM)] * 4,
-        out_specs=(VM, VM),
-        scratch_shapes=[pltpu.SemaphoreType.DMA((4,))],
-        compiler_params=pltpu.CompilerParams(vmem_limit_bytes=60 * 2**20),
-        name="pack",
-    )(queries, grad_out, keys, values)
-
-
-def stats(meta, lim, arrays):
-    return pl.pallas_call(
-        stats_kernel,
-        out_shape=jax.ShapeDtypeStruct((2, 16, R), jnp.float32),
-        in_specs=[SM] + [VM] * 9,
+        functools.partial(stats_kernel, which, n),
+        out_shape=jax.ShapeDtypeStruct((2, 24, 128), jnp.float32),
+        in_specs=[SM] + [VM] * (1 + n + 8 + len(before)),
         out_specs=VM,
-        scratch_shapes=COPIES + [pltpu.VMEM((GROUPS + 1, 8, R), jnp.float32)] * 3,
+        scratch_shapes=COPIES + [pltpu.VMEM((3 * n + 1, 8, R), jnp.float32)] * 3,
         compiler_params=PARAMS,
-        name="stats",
-    )(meta, lim, *arrays)
+        cost_estimate=pl.CostEstimate(flops=n * 1_600_000_000, bytes_accessed=4_000_000, transcendentals=0),
+        name="stats_near" if which == NEAR else "stats_far",
+    )(meta, lim, *qds, *kvs, *before)
 
 
 def grads(meta, lim, sts, arrays):
@@ -263,7 +263,7 @@
     return pl.pallas_call(
         grads_kernel,
         out_shape=dq + dkv,
-        in_specs=[SM] + [VM] * 11,
+        in_specs=[SM] + [VM] * 15,
         out_specs=[VM] * 9,
         scratch_shapes=COPIES
         + [
@@ -311,8 +311,8 @@
     own_x = own_x.reshape(2, 4, 4, 2)
     by_y = jnp.stack([lax.dynamic_index_in_dim(own_x, (y - r) % 4, 1, keepdims=False) for r in STEPS], 1)
     by_yz = jnp.stack([lax.dynamic_index_in_dim(by_y, (z - r) % 4, 2, keepdims=False) for r in STEPS], 2)
-    mine = jnp.where(core == 0, jnp.transpose(by_yz, (2, 1, 0, 3)), jnp.transpose(by_yz[::-1], (1, 2, 0, 3)))
-    arrived = mine.reshape(64)
+    of_core = jnp.stack([jnp.transpose(by_yz[0], (1, 0, 2)), by_yz[1]])
+    arrived = jnp.where(core == 0, of_core, of_core[::-1]).reshape(64)
     ring = grid[y, zl, core, zh]
     queries = jnp.concatenate([ring[(x - r) % 4] for r in STEPS])
 
@@ -320,36 +320,50 @@
         return jnp.sum((among[None, :] < a[:, None]).astype(i32), axis=1)
 
     place = rank(queries, queries)
-    hit = (place[None, :] == jnp.arange(8)[:, None]).astype(i32)
+    eight = jnp.arange(8, dtype=i32)
+    hit = (place[None, :] == eight[:, None]).astype(i32)
     spans = jnp.sum(hit * queries[None, :], axis=1)
     below = rank(spans, arrived)
     own = jnp.any(arrived[None, :] == spans[:, None], axis=1).astype(i32)
+    far = jnp.sum(hit[:, 6:], axis=1)
+    before = jnp.sum(jnp.tril(jnp.ones((8, 8), i32), -1) * far[None, :], axis=1)
+    order = jnp.stack([eight, jnp.where(far == 0, eight - before, 9), jnp.where(far == 1, before, 9)])
+    taken = (order[:, None, :] == eight[None, :, None]).astype(i32)
+    canon = jnp.sum(taken * eight, axis=2)
+    units = jnp.sum(order[:, None, :] * hit.T[None], axis=2)
     token = jnp.tile(jnp.arange(SPAN, dtype=i32), 2)
     seen = below[:, None] * SPAN + own[:, None] * (token[None, :] + 1)
-    a, b = seen[0::2], seen[1::2]
-    lim = jnp.stack([a, a, a, b, b, b], axis=1).reshape(GROUPS, R)
-    lim = jnp.concatenate([lim, jnp.zeros((4, R), i32)])
+    seen = jnp.sum(taken[:, :, :, None] * seen[None, None], axis=2)
+    a, b = seen[:, 0::2], seen[:, 1::2]
+    lim = jnp.stack([a, a, a, b, b, b], axis=2).reshape(3, GROUPS, R)
+    lim = jnp.concatenate([lim, jnp.zeros((3, 4, R), i32)], axis=1)
     tiles = ((below + own) * SPAN + KB - 1) // KB
-    each = jnp.stack([tiles[0::2], tiles[1::2], tiles[1::2]], axis=1).reshape(GROUPS)
-    end = jnp.sum(jnp.tril(jnp.ones((GROUPS, GROUPS), i32)) * each[None, :], axis=1)
+    tiles = jnp.sum(taken * tiles, axis=2)
+    each = jnp.stack([tiles[:, 0::2], tiles[:, 1::2], tiles[:, 1::2]], axis=2).reshape(3, GROUPS)
+    end = jnp.sum(jnp.tril(jnp.ones((GROUPS, GROUPS), i32)) * each[:, None, :], axis=2)
     t = jnp.arange(LIST, dtype=i32)
-    past = (t[:, None] >= end[None, :]).astype(i32)
-    group = jnp.sum(past, axis=1)
-    block = jnp.where(group < GROUPS, t - jnp.sum(past * each[None, :], axis=1), 0)
-    meta = [rank(arrived, arrived), place, end[-1:], group, block]
-    return jnp.concatenate(meta).astype(i32), lim
+    past = (t[None, :, None] >= end[:, None, :]).astype(i32)
+    group = jnp.minimum(jnp.sum(past, axis=2), jnp.array([[12], [9], [3]], i32))
+    block = jnp.where(t[None] < end[:, -1:], t[None] - jnp.sum(past * each[:, None, :], axis=2), 0)
+    lists = jnp.concatenate([units, canon, end[:, -1:], group, block], axis=1)
+    return jnp.concatenate([rank(arrived, arrived), lists.reshape(-1)]).astype(i32), lim
 
 
 def local(queries, keys, values, grad_out, span_slot):
-    meta, lim = plan(span_slot)
-    qd, kv = pack(queries, grad_out, keys, values)
-    qds = [qd] + [x_shift(qd, r) for r in STEPS[1:]]
-    kv = jnp.stack([kv, core_swap(kv)])[None]
+    kv = jnp.concatenate([keys, values], axis=1)[None]
     kv = jnp.concatenate([kv] + [first_shift(kv, r) for r in STEPS[1:]], axis=0)
     kvs = [kv] + [second_shift(kv, r) for r in STEPS[1:]]
-    arrays = qds + kvs
-
-    part = stats(meta, lim, arrays)
+    qd = jnp.concatenate([queries, grad_out], axis=1)
+    near = [qd, x_shift(qd, 1), x_shift(qd, 3)]
+    near[1], near[2], later = lax.optimization_barrier((near[1], near[2], qd))
+    far = x_shift(later, 2)
+    kvs[0], kvs[1], span_slot = lax.optimization_barrier((kvs[0], kvs[1], span_slot))
+    meta, lim = plan(span_slot)
+    kvs = kvs + [core_swap(a) for a in kvs]
+    arrays = near + [far] + kvs
+
+    part = stats(NEAR, meta, lim, near, kvs)
+    part = stats(FAR, meta, lim, [far], kvs, part)
     got = permute(part, lambda y, z, core, x: (y, z, core, x ^ 1))
     part = jnp.stack(merged(part[0], part[1], got[0], got[1]))
     got = permute(part, lambda y, z, core, x: (y, z, core, x ^ 2))

time: 112 us -> 103 us (0.920)
  waiting for transfers between devices: 29.6 us -> 24 us
  starting transfers between devices: 34.3 us -> 29.6 us
  other arithmetic: 2.64 us -> 4.35 us
    ppermute x22 -> x25, waiting for transfers between devices: 29.6 us -> 24 us  [permute(): return lax.ppermute(a, AXES, pairs)]
    ppermute x22 -> x25, starting transfers between devices: 34.3 us -> 29.6 us  [permute(): return lax.ppermute(a, AXES, pairs)]
  transfers between devices with their start and end apart: 22 -> 25, of which waited for: 12 -> 13; matrix products, arithmetic and copies ran while one was open for 4% -> 6% of each run, Pallas kernels for 0% -> 11%
where the time goes in v5:
time: 103 us
  Pallas kernels  40.8 us (40%)
  starting transfers between devices  29.6 us (29%)
  waiting for transfers between devices  24 us (23%)
  other arithmetic  4.35 us (4%)
  local copies, waits for them, and re-layouts  3.36 us (3%)
    ppermute x25, starting transfers between devices, permute(): return lax.ppermute(a, AXES, pairs)  29.6 us
    pallas_call x1, Pallas kernels, grads(): pl.pallas_call(grads_kernel, out_shape=dq + dkv, in_specs=[SM] + [VM] * 1...  24.4 us
    ppermute x25, waiting for transfers between devices, permute(): return lax.ppermute(a, AXES, pairs)  24 us
    pallas_call x2, Pallas kernels, stats(): pl.pallas_call(functools.partial(stats_kernel, which, n), out_shape=jax.S...  16.4 us
  transfers between devices with their start and end apart: 25, of which 13 were waited for; matrix products, arithmetic and copies ran while one was open for 6% of the time, Pallas kernels for 11%

profile of v5, /device:TPU:0, one launch (start us, length us, event | category | flops | bytes accessed | tf_op | source)
XLA Modules:
  0.0 103.1 jit_solution(17418904951943027987)
XLA Ops:
  1.4 3.4 %collective-permute-start.2 = (bf16[1,128,256]{2,1,0:T(8,128)(2,1)S(1)}, bf16[1,128,256]{2,1,0:T(8,128)(2,1)S(1)}, u32[]{:S(2)}, u32[]{:S(2)}) collective-permute-start(bf16[1,128,256]{2,1,0:T(8,128)(2,1)S(1)} %maximum_bitcast_fusion), channel_id=1, source_target_pairs={{0,64},{1,65},{2,66},{3,67},{4,68},{5,69},{6,70},{7,71},{8,12},{9,... | collective-permute-start | bytes 196616 | tf_op jit(solution)/shard_map/ppermute | solution.py:286
  4.8 1.1 %collective-permute-start.1 = (bf16[1,128,256]{2,1,0:T(8,128)(2,1)S(1)}, bf16[1,128,256]{2,1,0:T(8,128)(2,1)S(1)}, u32[]{:S(2)}, u32[]{:S(2)}) collective-permute-start(bf16[1,128,256]{2,1,0:T(8,128)(2,1)S(1)} %maximum_bitcast_fusion), channel_id=1, source_target_pairs={{0,96},{1,97},{2,98},{3,99},{4,100},{5,101},{6,102},{7,103},{8,28}... | collective-permute-start | bytes 196616 | tf_op jit(solution)/shard_map/ppermute | solution.py:286
  7.8 2.8 %collective-permute-start.5 = (bf16[128,1536]{1,0:T(8,128)(2,1)S(1)}, bf16[128,1536]{1,0:T(8,128)(2,1)S(1)}, u32[]{:S(2)}, u32[]{:S(2)}) collective-permute-start(bf16[128,1536]{1,0:T(8,128)(2,1)S(1)} %constant_dynamic-update-slice_fusion.6.refs_0_), channel_id=1, source_target_pairs={{0,3},{1,0},{2,1},{3,2},{4,7},{5,4},{6,5},{7,6},{8,11},{9,8},{10,9... | collective-permute-start | bytes 1179656 | tf_op jit(solution)/shard_map/ppermute | solution.py:286
  11.3 2.0 %collective-permute-start.3 = (bf16[4,128,256]{2,1,0:T(8,128)(2,1)S(1)}, bf16[4,128,256]{2,1,0:T(8,128)(2,1)S(1)}, u32[]{:S(2)}, u32[]{:S(2)}) collective-permute-start(bf16[4,128,256]{2,1,0:T(8,128)(2,1)S(1)} %pad_maximum_fusion.refs_3_.refs_1_.refs_4_), channel_id=1, source_target_pairs={{0,16},{1,17},{2,18},{3,19},{4,20},{5,21},{6,22},{7,23},{8,40},{9,... | collective-permute-start | bytes 786440 | tf_op jit(solution)/shard_map/ppermute | solution.py:286
  13.4 3.7 %collective-permute-start.8 = (bf16[4,128,256]{2,1,0:T(8,128)(2,1)S(1)}, bf16[4,128,256]{2,1,0:T(8,128)(2,1)S(1)}, u32[]{:S(2)}, u32[]{:S(2)}) collective-permute-start(bf16[4,128,256]{2,1,0:T(8,128)(2,1)S(1)} %pad_maximum_fusion.refs_3_.refs_1_.refs_4_), channel_id=1, source_target_pairs={{0,4},{1,5},{2,6},{3,7},{4,0},{5,1},{6,2},{7,3},{8,72},{9,73},{10,... | collective-permute-start | bytes 786440 | tf_op jit(solution)/shard_map/ppermute | solution.py:286
  17.1 1.0 collective-permute-start.7
  18.1 1.7 %collective-permute-done.3.refs_4_.refs_2_.refs_5_ = bf16[4,128,256]{2,1,0:T(8,128)(2,1)S(1)} collective-permute-done((bf16[4,128,256]{2,1,0:T(8,128)(2,1)S(1)}, bf16[4,128,256]{2,1,0:T(8,128)(2,1)S(1)}, u32[]{:S(2)}, u32[]{:S(2)}) %collective-permute-start.3) | collective-permute-done | bytes 262176 | tf_op jit(solution)/shard_map/ppermute | solution.py:286
  25.2 3.5 %collective-permute-start.6 = (bf16[128,1536]{1,0:T(8,128)(2,1)S(1)}, bf16[128,1536]{1,0:T(8,128)(2,1)S(1)}, u32[]{:S(2)}, u32[]{:S(2)}) collective-permute-start(bf16[128,1536]{1,0:T(8,128)(2,1)S(1)} %constant_dynamic-update-slice_fusion.6.refs_0_), channel_id=1, source_target_pairs={{0,2},{1,3},{2,0},{3,1},{4,6},{5,7},{6,4},{7,5},{8,10},{9,11},{10,... | collective-permute-start | bytes 1179656 | tf_op jit(solution)/shard_map/ppermute | solution.py:286
  28.7 11.2 %stats_near.1.refs_9_ = f32[2,24,128]{2,1,0:T(8,128)S(1)} custom-call(s32[931]{0:T(1024)S(1)} %pad_add_fusion.4.meta, s32[3,16,256]{2,1,0:T(8,128)S(1)} %concatenate.26.lim, bf16[128,1536]{1,0:T(8,128)(2,1)S(1)} %constant_dynamic-update-slice_fusion.6.refs_0_, bf16[128,1536]{1,0:T(8,128)(2,1)S(1)} %collective-permute-done.4.refs_1_, ...), custom_call_target="tpu_custom_call" | custom-call | flops 4800000000 | bytes 4000000 | tf_op jit(solution)/shard_map/stats_near/pallas_call | solution.py:247
  39.9 5.2 %stats_far.1 = f32[2,24,128]{2,1,0:T(8,128)S(1)} custom-call(s32[931]{0:T(1024)S(1)} %pad_add_fusion.4.meta, s32[3,16,256]{2,1,0:T(8,128)S(1)} %concatenate.26.lim, bf16[128,1536]{1,0:T(8,128)(2,1)S(1)} %collective-permute-done.6.refs_0_.refs_3_, bf16[4,128,256]{2,1,0:T(8,128)(2,1)S(1)} %pad_maximum_fusion.refs_3_.refs_1_.refs_4_, ...), custom_call_target="tpu_custom_call" | custom-call | flops 1600000000 | bytes 4000000 | tf_op jit(solution)/shard_map/stats_far/pallas_call | solution.py:247
  45.4 3.7 %collective-permute-done.13 = f32[2,24,128]{2,1,0:T(8,128)S(1)} collective-permute-done((f32[2,24,128]{2,1,0:T(8,128)S(1)}, f32[2,24,128]{2,1,0:T(8,128)S(1)}, u32[]{:S(2)}, u32[]{:S(2)}) %collective-permute-start.13) | collective-permute-done | bytes 24608 | tf_op jit(solution)/shard_map/ppermute | solution.py:286
  49.1 1.5 %collective-permute-start.14 = (f32[2,24,128]{2,1,0:T(8,128)S(1)}, f32[2,24,128]{2,1,0:T(8,128)S(1)}, u32[]{:S(2)}, u32[]{:S(2)}) collective-permute-start(f32[2,24,128]{2,1,0:T(8,128)S(1)} %pad_maximum_fusion.1.st0), channel_id=1, source_target_pairs={{0,2},{1,3},{2,0},{3,1},{4,6},{5,7},{6,4},{7,5},{8,10},{9,11},{10,... | collective-permute-start | bytes 73736 | tf_op jit(solution)/shard_map/ppermute | solution.py:286
  50.6 3.9 %collective-permute-done.14.st1 = f32[2,24,128]{2,1,0:T(8,128)S(1)} collective-permute-done((f32[2,24,128]{2,1,0:T(8,128)S(1)}, f32[2,24,128]{2,1,0:T(8,128)S(1)}, u32[]{:S(2)}, u32[]{:S(2)}) %collective-permute-start.14) | collective-permute-done | bytes 24608 | tf_op jit(solution)/shard_map/ppermute | solution.py:286
  54.5 24.4 %grads.1 = (f32[128,768]{1,0:T(8,128)S(1)}, bf16[128,768]{1,0:T(8,128)(2,1)S(1)}, bf16[128,768]{1,0:T(8,128)(2,1)S(1)}, bf16[128,768]{1,0:T(8,128)(2,1)S(1)}, bf...) custom-call(s32[931]{0:T(1024)S(1)} %pad_add_fusion.4.meta, ...), custom_call_target="tpu_custom_call" | custom-call | tf_op jit(solution)/shard_map/grads/pallas_call | solution.py:263
  78.9 2.9 %collective-permute-done.18 = bf16[4,4,128,256]{3,2,1,0:T(8,128)(2,1)S(1)} collective-permute-done((bf16[4,4,128,256]{3,2,1,0:T(8,128)(2,1)}, bf16[4,4,128,256]{3,2,1,0:T(8,128)(2,1)S(1)}, u32[]{:S(2)}, u32[]{:S(2)}) %collective-permute-start.18) | collective-permute-done | bytes 1048608 | tf_op jit(solution)/shard_map/ppermute | solution.py:286
  82.0 2.6 %collective-permute-start.19 = (bf16[4,128,256]{2,1,0:T(8,128)(2,1)S(1)}, bf16[4,128,256]{2,1,0:T(8,128)(2,1)S(1)}, u32[]{:S(2)}, u32[]{:S(2)}) collective-permute-start(bf16[4,128,256]{2,1,0:T(8,128)(2,1)S(1)} %get-tuple-element.40), channel_id=1, source_target_pairs={{0,20},{1,21},{2,22},{3,23},{4,16},{5,17},{6,18},{7,19},{8,104},{9... | collective-permute-start | bytes 786440 | tf_op jit(solution)/shard_map/ppermute | solution.py:286
  84.6 1.2 %collective-permute-start.21 = (bf16[4,128,256]{2,1,0:T(8,128)(2,1)S(1)}, bf16[4,128,256]{2,1,0:T(8,128)(2,1)S(1)}, u32[]{:S(2)}, u32[]{:S(2)}) collective-permute-start(bf16[4,128,256]{2,1,0:T(8,128)(2,1)S(1)} %get-tuple-element.41), channel_id=1, source_target_pairs={{0,4},{1,5},{2,6},{3,7},{4,0},{5,1},{6,2},{7,3},{8,72},{9,73},{10,... | collective-permute-start | bytes 786440 | tf_op jit(solution)/shard_map/ppermute | solution.py:286
  86.6 1.2 %collective-permute-start.16 = (bf16[128,768]{1,0:T(8,128)(2,1)S(1)}, bf16[128,768]{1,0:T(8,128)(2,1)S(1)}, u32[]{:S(2)}, u32[]{:S(2)}) collective-permute-start(bf16[128,768]{1,0:T(8,128)(2,1)S(1)} %get-tuple-element.26), channel_id=1, source_target_pairs={{0,1},{1,2},{2,3},{3,0},{4,5},{5,6},{6,7},{7,4},{8,9},{9,10},{10,1... | collective-permute-start | bytes 589832 | tf_op jit(solution)/shard_map/ppermute | solution.py:286
  87.8 3.5 %collective-permute-done.19 = bf16[4,128,256]{2,1,0:T(8,128)(2,1)S(1)} collective-permute-done((bf16[4,128,256]{2,1,0:T(8,128)(2,1)S(1)}, bf16[4,128,256]{2,1,0:T(8,128)(2,1)S(1)}, u32[]{:S(2)}, u32[]{:S(2)}) %collective-permute-start.19) | collective-permute-done | bytes 262176 | tf_op jit(solution)/shard_map/ppermute | solution.py:286
  91.3 1.0 collective-permute-start.17
  92.5 2.7 %collective-permute-done.20 = bf16[4,128,256]{2,1,0:T(8,128)(2,1)S(1)} collective-permute-done((bf16[4,128,256]{2,1,0:T(8,128)(2,1)S(1)}, bf16[4,128,256]{2,1,0:T(8,128)(2,1)S(1)}, u32[]{:S(2)}, u32[]{:S(2)}) %collective-permute-start.20) | collective-permute-done | bytes 262176 | tf_op jit(solution)/shard_map/ppermute | solution.py:286
  96.2 1.3 %collective-permute-start.23 = (bf16[128,256]{1,0:T(8,128)(2,1)S(1)}, bf16[128,256]{1,0:T(8,128)(2,1)S(1)}, u32[]{:S(2)}, u32[]{:S(2)}) collective-permute-start(bf16[128,256]{1,0:T(8,128)(2,1)S(1)} %get-tuple-element.45), channel_id=1, source_target_pairs={{0,32},{1,33},{2,34},{3,35},{4,36},{5,37},{6,38},{7,39},{8,24},{9,... | collective-permute-start | bytes 196616 | tf_op jit(solution)/shard_map/ppermute | solution.py:286
  99.8 1.6 %collective-permute-done.24 = bf16[128,256]{1,0:T(8,128)(2,1)S(1)} collective-permute-done((bf16[128,256]{1,0:T(8,128)(2,1)S(1)}, bf16[128,256]{1,0:T(8,128)(2,1)S(1)}, u32[]{:S(2)}, u32[]{:S(2)}) %collective-permute-start.24) | collective-permute-done | bytes 65568 | tf_op jit(solution)/shard_map/ppermute | solution.py:286
  101.4 1.1 %collective-permute-done.23 = bf16[128,256]{1,0:T(8,128)(2,1)S(1)} collective-permute-done((bf16[128,256]{1,0:T(8,128)(2,1)S(1)}, bf16[128,256]{1,0:T(8,128)(2,1)S(1)}, u32[]{:S(2)}, u32[]{:S(2)}) %collective-permute-start.23) | collective-permute-done | bytes 65568 | tf_op jit(solution)/shard_map/ppermute | solution.py:286
  (107 shorter events, 14.2 us)
Async XLA Ops:
  1.4 9.2 %collective-permute-start.2 = (bf16[1,128,256]{2,1,0:T(8,128)(2,1)S(1)}, bf16[1,128,256]{2,1,0:T(8,128)(2,1)S(1)}, u32[]{:S(2)}, u32[]{:S(2)}) collective-permute-start(bf16[1,128,256]{2,1,0:T(8,128)(2,1)S(1)} %maximum_bitcast_fusion), channel_id=1, source_target_pairs={{0,64},{1,65},{2,66},{3,67},{4,68},{5,69},{6,70},{7,71},{8,12},{9,... | collective-permute-start | bytes 196616 | tf_op jit(solution)/shard_map/ppermute | solution.py:286
  4.8 5.8 %collective-permute-start.1 = (bf16[1,128,256]{2,1,0:T(8,128)(2,1)S(1)}, bf16[1,128,256]{2,1,0:T(8,128)(2,1)S(1)}, u32[]{:S(2)}, u32[]{:S(2)}) collective-permute-start(bf16[1,128,256]{2,1,0:T(8,128)(2,1)S(1)} %maximum_bitcast_fusion), channel_id=1, source_target_pairs={{0,96},{1,97},{2,98},{3,99},{4,100},{5,101},{6,102},{7,103},{8,28}... | collective-permute-start | bytes 196616 | tf_op jit(solution)/shard_map/ppermute | solution.py:286
  5.8 5.5 %collective-permute-start = (bf16[1,128,256]{2,1,0:T(8,128)(2,1)S(1)}, bf16[1,128,256]{2,1,0:T(8,128)(2,1)S(1)}, u32[]{:S(2)}, u32[]{:S(2)}) collective-permute-start(bf16[1,128,256]{2,1,0:T(8,128)(2,1)S(1)} %maximum_bitcast_fusion), channel_id=1, source_target_pairs={{0,32},{1,33},{2,34},{3,35},{4,36},{5,37},{6,38},{7,39},{8,24},{9,... | collective-permute-start | bytes 196616 | tf_op jit(solution)/shard_map/ppermute | solution.py:286
  7.8 16.8 %collective-permute-start.5 = (bf16[128,1536]{1,0:T(8,128)(2,1)S(1)}, bf16[128,1536]{1,0:T(8,128)(2,1)S(1)}, u32[]{:S(2)}, u32[]{:S(2)}) collective-permute-start(bf16[128,1536]{1,0:T(8,128)(2,1)S(1)} %constant_dynamic-update-slice_fusion.6.refs_0_), channel_id=1, source_target_pairs={{0,3},{1,0},{2,1},{3,2},{4,7},{5,4},{6,5},{7,6},{8,11},{9,8},{10,9... | collective-permute-start | bytes 1179656 | tf_op jit(solution)/shard_map/ppermute | solution.py:286
  10.6 14.6 %collective-permute-start.4 = (bf16[128,1536]{1,0:T(8,128)(2,1)S(1)}, bf16[128,1536]{1,0:T(8,128)(2,1)S(1)}, u32[]{:S(2)}, u32[]{:S(2)}) collective-permute-start(bf16[128,1536]{1,0:T(8,128)(2,1)S(1)} %constant_dynamic-update-slice_fusion.6.refs_0_), channel_id=1, source_target_pairs={{0,1},{1,2},{2,3},{3,0},{4,5},{5,6},{6,7},{7,4},{8,9},{9,10},{10,1... | collective-permute-start | bytes 1179656 | tf_op jit(solution)/shard_map/ppermute | solution.py:286
  11.3 8.5 %collective-permute-start.3 = (bf16[4,128,256]{2,1,0:T(8,128)(2,1)S(1)}, bf16[4,128,256]{2,1,0:T(8,128)(2,1)S(1)}, u32[]{:S(2)}, u32[]{:S(2)}) collective-permute-start(bf16[4,128,256]{2,1,0:T(8,128)(2,1)S(1)} %pad_maximum_fusion.refs_3_.refs_1_.refs_4_), channel_id=1, source_target_pairs={{0,16},{1,17},{2,18},{3,19},{4,20},{5,21},{6,22},{7,23},{8,40},{9,... | collective-permute-start | bytes 786440 | tf_op jit(solution)/shard_map/ppermute | solution.py:286
  13.4 10.6 %collective-permute-start.8 = (bf16[4,128,256]{2,1,0:T(8,128)(2,1)S(1)}, bf16[4,128,256]{2,1,0:T(8,128)(2,1)S(1)}, u32[]{:S(2)}, u32[]{:S(2)}) collective-permute-start(bf16[4,128,256]{2,1,0:T(8,128)(2,1)S(1)} %pad_maximum_fusion.refs_3_.refs_1_.refs_4_), channel_id=1, source_target_pairs={{0,4},{1,5},{2,6},{3,7},{4,0},{5,1},{6,2},{7,3},{8,72},{9,73},{10,... | collective-permute-start | bytes 786440 | tf_op jit(solution)/shard_map/ppermute | solution.py:286
  17.1 7.0 %collective-permute-start.7 = (bf16[4,128,256]{2,1,0:T(8,128)(2,1)S(1)}, bf16[4,128,256]{2,1,0:T(8,128)(2,1)S(1)}, u32[]{:S(2)}, u32[]{:S(2)}) collective-permute-start(bf16[4,128,256]{2,1,0:T(8,128)(2,1)S(1)} %pad_maximum_fusion.refs_3_.refs_1_.refs_4_), channel_id=1, source_target_pairs={{0,20},{1,21},{2,22},{3,23},{4,16},{5,17},{6,18},{7,19},{8,104},{9... | collective-permute-start | bytes 786440 | tf_op jit(solution)/shard_map/ppermute | solution.py:286
  23.3 5.4 %collective-permute-start.9 = (bf16[4,128,256]{2,1,0:T(8,128)(2,1)S(1)}, bf16[4,128,256]{2,1,0:T(8,128)(2,1)S(1)}, u32[]{:S(2)}, u32[]{:S(2)}) collective-permute-start(bf16[4,128,256]{2,1,0:T(8,128)(2,1)S(1)} %pad_maximum_fusion.refs_3_.refs_1_.refs_4_), channel_id=1, source_target_pairs={{0,8},{1,9},{2,10},{3,11},{4,12},{5,13},{6,14},{7,15},{8,0},{9,1},... | collective-permute-start | bytes 786440 | tf_op jit(solution)/shard_map/ppermute | solution.py:286
  24.1 4.6 %collective-permute-start.10 = (bf16[4,128,256]{2,1,0:T(8,128)(2,1)S(1)}, bf16[4,128,256]{2,1,0:T(8,128)(2,1)S(1)}, u32[]{:S(2)}, u32[]{:S(2)}) collective-permute-start(bf16[4,128,256]{2,1,0:T(8,128)(2,1)S(1)} %collective-permute-done.3.refs_4_.refs_2_.refs_5_), channel_id=1, source_target_pairs={{0,8},{1,9},{2,10},{3,11},{4,12},{5,13},{6,14},{7,15},{8,0},{9,1},... | collective-permute-start | bytes 786440 | tf_op jit(solution)/shard_map/ppermute | solution.py:286
  24.1 4.6 %collective-permute-start.12 = (bf16[4,128,256]{2,1,0:T(8,128)(2,1)S(1)}, bf16[4,128,256]{2,1,0:T(8,128)(2,1)S(1)}, u32[]{:S(2)}, u32[]{:S(2)}) collective-permute-start(bf16[4,128,256]{2,1,0:T(8,128)(2,1)S(1)} %collective-permute-done.8.refs_6_.refs_4_.refs_7_), channel_id=1, source_target_pairs={{0,8},{1,9},{2,10},{3,11},{4,12},{5,13},{6,14},{7,15},{8,0},{9,1},... | collective-permute-start | bytes 786440 | tf_op jit(solution)/shard_map/ppermute | solution.py:286
  24.6 4.1 %collective-permute-start.11 = (bf16[4,128,256]{2,1,0:T(8,128)(2,1)S(1)}, bf16[4,128,256]{2,1,0:T(8,128)(2,1)S(1)}, u32[]{:S(2)}, u32[]{:S(2)}) collective-permute-start(bf16[4,128,256]{2,1,0:T(8,128)(2,1)S(1)} %collective-permute-done.7.refs_5_.refs_3_.refs_6_), channel_id=1, source_target_pairs={{0,8},{1,9},{2,10},{3,11},{4,12},{5,13},{6,14},{7,15},{8,0},{9,1},... | collective-permute-start | bytes 786440 | tf_op jit(solution)/shard_map/ppermute | solution.py:286
  25.2 14.7 %collective-permute-start.6 = (bf16[128,1536]{1,0:T(8,128)(2,1)S(1)}, bf16[128,1536]{1,0:T(8,128)(2,1)S(1)}, u32[]{:S(2)}, u32[]{:S(2)}) collective-permute-start(bf16[128,1536]{1,0:T(8,128)(2,1)S(1)} %constant_dynamic-update-slice_fusion.6.refs_0_), channel_id=1, source_target_pairs={{0,2},{1,3},{2,0},{3,1},{4,6},{5,7},{6,4},{7,5},{8,10},{9,11},{10,... | collective-permute-start | bytes 1179656 | tf_op jit(solution)/shard_map/ppermute | solution.py:286
  45.2 3.9 %collective-permute-start.13 = (f32[2,24,128]{2,1,0:T(8,128)S(1)}, f32[2,24,128]{2,1,0:T(8,128)S(1)}, u32[]{:S(2)}, u32[]{:S(2)}) collective-permute-start(f32[2,24,128]{2,1,0:T(8,128)S(1)} %stats_far.1), channel_id=1, source_target_pairs={{0,1},{1,0},{2,3},{3,2},{4,5},{5,4},{6,7},{7,6},{8,9},{9,8},{10,11... | collective-permute-start | bytes 73736 | tf_op jit(solution)/shard_map/ppermute | solution.py:286
  49.1 5.4 %collective-permute-start.14 = (f32[2,24,128]{2,1,0:T(8,128)S(1)}, f32[2,24,128]{2,1,0:T(8,128)S(1)}, u32[]{:S(2)}, u32[]{:S(2)}) collective-permute-start(f32[2,24,128]{2,1,0:T(8,128)S(1)} %pad_maximum_fusion.1.st0), channel_id=1, source_target_pairs={{0,2},{1,3},{2,0},{3,1},{4,6},{5,7},{6,4},{7,5},{8,10},{9,11},{10,... | collective-permute-start | bytes 73736 | tf_op jit(solution)/shard_map/ppermute | solution.py:286
  82.0 9.3 %collective-permute-start.19 = (bf16[4,128,256]{2,1,0:T(8,128)(2,1)S(1)}, bf16[4,128,256]{2,1,0:T(8,128)(2,1)S(1)}, u32[]{:S(2)}, u32[]{:S(2)}) collective-permute-start(bf16[4,128,256]{2,1,0:T(8,128)(2,1)S(1)} %get-tuple-element.40), channel_id=1, source_target_pairs={{0,20},{1,21},{2,22},{3,23},{4,16},{5,17},{6,18},{7,19},{8,104},{9... | collective-permute-start | bytes 786440 | tf_op jit(solution)/shard_map/ppermute | solution.py:286
  84.6 8.0 %collective-permute-start.21 = (bf16[4,128,256]{2,1,0:T(8,128)(2,1)S(1)}, bf16[4,128,256]{2,1,0:T(8,128)(2,1)S(1)}, u32[]{:S(2)}, u32[]{:S(2)}) collective-permute-start(bf16[4,128,256]{2,1,0:T(8,128)(2,1)S(1)} %get-tuple-element.41), channel_id=1, source_target_pairs={{0,4},{1,5},{2,6},{3,7},{4,0},{5,1},{6,2},{7,3},{8,72},{9,73},{10,... | collective-permute-start | bytes 786440 | tf_op jit(solution)/shard_map/ppermute | solution.py:286
  85.8 9.5 %collective-permute-start.20 = (bf16[4,128,256]{2,1,0:T(8,128)(2,1)S(1)}, bf16[4,128,256]{2,1,0:T(8,128)(2,1)S(1)}, u32[]{:S(2)}, u32[]{:S(2)}) collective-permute-start(bf16[4,128,256]{2,1,0:T(8,128)(2,1)S(1)} %get-tuple-element.42), channel_id=1, source_target_pairs={{0,16},{1,17},{2,18},{3,19},{4,20},{5,21},{6,22},{7,23},{8,40},{9,... | collective-permute-start | bytes 786440 | tf_op jit(solution)/shard_map/ppermute | solution.py:286
  85.8 10.5 %collective-permute-start.15 = (bf16[128,768]{1,0:T(8,128)(2,1)S(1)}, bf16[128,768]{1,0:T(8,128)(2,1)S(1)}, u32[]{:S(2)}, u32[]{:S(2)}) collective-permute-start(bf16[128,768]{1,0:T(8,128)(2,1)S(1)} %get-tuple-element.25), channel_id=1, source_target_pairs={{0,3},{1,0},{2,1},{3,2},{4,7},{5,4},{6,5},{7,6},{8,11},{9,8},{10,9... | collective-permute-start | bytes 589832 | tf_op jit(solution)/shard_map/ppermute | solution.py:286
  86.6 11.0 %collective-permute-start.16 = (bf16[128,768]{1,0:T(8,128)(2,1)S(1)}, bf16[128,768]{1,0:T(8,128)(2,1)S(1)}, u32[]{:S(2)}, u32[]{:S(2)}) collective-permute-start(bf16[128,768]{1,0:T(8,128)(2,1)S(1)} %get-tuple-element.26), channel_id=1, source_target_pairs={{0,1},{1,2},{2,3},{3,0},{4,5},{5,6},{6,7},{7,4},{8,9},{9,10},{10,1... | collective-permute-start | bytes 589832 | tf_op jit(solution)/shard_map/ppermute | solution.py:286
  91.3 7.2 %collective-permute-start.17 = (bf16[128,768]{1,0:T(8,128)(2,1)S(1)}, bf16[128,768]{1,0:T(8,128)(2,1)S(1)}, u32[]{:S(2)}, u32[]{:S(2)}) collective-permute-start(bf16[128,768]{1,0:T(8,128)(2,1)S(1)} %get-tuple-element.27), channel_id=1, source_target_pairs={{0,2},{1,3},{2,0},{3,1},{4,6},{5,7},{6,4},{7,5},{8,10},{9,11},{10,... | collective-permute-start | bytes 589832 | tf_op jit(solution)/shard_map/ppermute | solution.py:286
  95.4 4.3 %collective-permute-start.22 = (bf16[128,256]{1,0:T(8,128)(2,1)S(1)}, bf16[128,256]{1,0:T(8,128)(2,1)S(1)}, u32[]{:S(2)}, u32[]{:S(2)}) collective-permute-start(bf16[128,256]{1,0:T(8,128)(2,1)S(1)} %get-tuple-element.43), channel_id=1, source_target_pairs={{0,96},{1,97},{2,98},{3,99},{4,100},{5,101},{6,102},{7,103},{8,28}... | collective-permute-start | bytes 196616 | tf_op jit(solution)/shard_map/ppermute | solution.py:286
  95.6 5.8 %collective-permute-start.24 = (bf16[128,256]{1,0:T(8,128)(2,1)S(1)}, bf16[128,256]{1,0:T(8,128)(2,1)S(1)}, u32[]{:S(2)}, u32[]{:S(2)}) collective-permute-start(bf16[128,256]{1,0:T(8,128)(2,1)S(1)} %get-tuple-element.44), channel_id=1, source_target_pairs={{0,64},{1,65},{2,66},{3,67},{4,68},{5,69},{6,70},{7,71},{8,12},{9,... | collective-permute-start | bytes 196616 | tf_op jit(solution)/shard_map/ppermute | solution.py:286
  96.2 6.2 %collective-permute-start.23 = (bf16[128,256]{1,0:T(8,128)(2,1)S(1)}, bf16[128,256]{1,0:T(8,128)(2,1)S(1)}, u32[]{:S(2)}, u32[]{:S(2)}) collective-permute-start(bf16[128,256]{1,0:T(8,128)(2,1)S(1)} %get-tuple-element.45), channel_id=1, source_target_pairs={{0,32},{1,33},{2,34},{3,35},{4,36},{5,37},{6,38},{7,39},{8,24},{9,... | collective-permute-start | bytes 196616 | tf_op jit(solution)/shard_map/ppermute | solution.py:286
  (4 other events, 16.8 us)

commit v6 on v5

--- a/solution.py
+++ b/solution.py
@@ -19,21 +19,24 @@
 SPAN = 64
 HEADS = 6
 WIDE = HEADS * HD
-KEYS = 4096
+KEYS = 2048
 KB = 256
 R = 256
-GROUPS = 12
+UNITS = 16
+GROUPS = 24
 UNROLL = 8
 LIST = 136
 IN = 0
-ALL, NEAR, FAR = range(3)
-UNIT, CANON, COUNT, GROUP = 0, 8, 16, 17
+ALL, NEAR, OTHER, FAR = range(4)
+IDS = (tuple(range(8)), (0, 1, 2), (4, 5, 6), (3, 7))
+NAMES = ("", "stats_near", "stats_other", "stats_far")
+UNIT, CANON, COUNT, GROUP = 0, UNITS, 2 * UNITS, 2 * UNITS + 1
 BLOCK = GROUP + LIST
 SIZE = BLOCK + LIST
 
 
 def of(which):
-    return 64 + which * SIZE
+    return 32 + which * SIZE
 
 
 NT = (((1,), (1,)), ((), ()))
@@ -80,7 +83,7 @@
 
 
 def load_sorted(meta, kvs, kv_s):
-    for s in range(64):
+    for s in range(32):
         r = aligned(meta[IN + s], SPAN)
         t = slice((s % 2) * SPAN, (s % 2 + 1) * SPAN)
         kv_s[pl.ds(r, SPAN), :] = kvs[s // 8][(s // 2) % 4, t, :]
@@ -92,10 +95,10 @@
     return pl.multiple_of((place // 2) * 768 + inner, SPAN)
 
 
-def load_rows(meta, base, qds, q_s, do_s, first=0):
-    for d, ref in enumerate(qds):
+def load_rows(meta, base, ids, qds, q_s, do_s):
+    for d, ref in zip(ids, qds):
         for half in range(2):
-            place = meta[base + UNIT + 2 * (first + d) + half]
+            place = meta[base + UNIT + 2 * d + half]
             t = slice(half * SPAN, (half + 1) * SPAN)
             for h in range(HEADS):
                 r = row_of(place, h)
@@ -115,15 +118,17 @@
 HALVES = ((0, 1), (2, 5), (3, 4))
 
 
-def stats_kernel(which, devices, meta, lim, *refs):
-    qds, kvs = refs[:devices], refs[devices : devices + 8]
-    rest = refs[devices + 8 :]
-    if which == FAR:
+def stats_kernel(which, meta, lim, *refs):
+    ids = IDS[which]
+    devices = len(ids)
+    qds, kvs = refs[:devices], refs[devices : devices + 4]
+    rest = refs[devices + 4 :]
+    if which != NEAR:
         before, rest = rest[0], rest[1:]
     out, q_s, do_s, kv_s, s0, s1, dp0, dp1, m_s, l_s, d_s = rest
     base, groups = of(which), 3 * devices
     load_sorted(meta, kvs, kv_s)
-    load_rows(meta, base, qds, q_s, do_s, first=3 if which == FAR else 0)
+    load_rows(meta, base, ids, qds, q_s, do_s)
     m_s[...] = jnp.full_like(m_s, NEG)
     l_s[...] = jnp.zeros_like(l_s)
     d_s[...] = jnp.zeros_like(d_s)
@@ -150,7 +155,7 @@
         online(t, ss[v % 2], dps[v % 2])
 
     tiles_loop(meta[base + COUNT], step)
-    out[...] = before[...] if which == FAR else jnp.zeros_like(out)
+    out[...] = before[...] if which != NEAR else jnp.zeros_like(out)
     for g in range(groups):
         m = m_s[g]
         live = jnp.where(m > 0.5 * NEG, 1.0, 0.0)
@@ -169,12 +174,12 @@
 
 
 def grads_kernel(meta, lim, st0, st1, *refs):
-    qds, kvs = refs[:4], refs[4:12]
-    dqs, dkvs, dkv_other = refs[12:16], refs[16:20], refs[20]
+    qds, kvs = refs[:8], refs[8:12]
+    dqs, dq_other, dkvs = refs[12:16], refs[16], refs[17:21]
     q_s, do_s, kv_s, s0, s1, dp0, dp1, acc, dq_s, p0, p1, ds0, ds1, lse, delta = refs[21:]
     load_sorted(meta, kvs, kv_s)
     base = of(ALL)
-    load_rows(meta, base, qds, q_s, do_s)
+    load_rows(meta, base, IDS[ALL], qds, q_s, do_s)
     acc[...] = jnp.zeros_like(acc)
     dq_s[...] = jnp.zeros_like(dq_s)
     all_lse, all_delta = merged(st0[0], st0[1], st1[0], st1[1])
@@ -216,18 +221,18 @@
         sums(t, ps[a], dss[a])
 
     tiles_loop(meta[base + COUNT], step)
-    for d in range(4):
+    for d in range(8):
+        ref = dqs[d] if d < 4 else dq_other.at[d - 4]
         for half in range(2):
             place = meta[base + UNIT + 2 * d + half]
             t = slice(half * SPAN, (half + 1) * SPAN)
             for h in range(HEADS):
                 got = dq_s[pl.ds(row_of(place, h), SPAN), :] * SCALE
-                dqs[d][t, h * HD : (h + 1) * HD] = got.astype(dqs[d].dtype)
-    for s in range(64):
+                ref[t, h * HD : (h + 1) * HD] = got.astype(ref.dtype)
+    for s in range(32):
         r = aligned(meta[IN + s], SPAN)
         t = slice((s % 2) * SPAN, (s % 2 + 1) * SPAN)
-        e = (s // 2) % 4
-        ref = dkvs[s // 8] if s < 32 else dkv_other.at[s // 8 - 4]
+        ref, e = dkvs[s // 8], (s // 2) % 4
         ref[e, t, :HD] = (acc[pl.ds(r, SPAN), :HD] * SCALE).astype(jnp.bfloat16)
         ref[e, t, HD:] = acc[pl.ds(r, SPAN), HD:].astype(jnp.bfloat16)
 
@@ -243,23 +248,23 @@
 
 
 def stats(which, meta, lim, qds, kvs, *before):
-    n = len(qds)
+    n = len(IDS[which])
     return pl.pallas_call(
-        functools.partial(stats_kernel, which, n),
-        out_shape=jax.ShapeDtypeStruct((2, 24, 128), jnp.float32),
-        in_specs=[SM] + [VM] * (1 + n + 8 + len(before)),
+        functools.partial(stats_kernel, which),
+        out_shape=jax.ShapeDtypeStruct((2, 3 * UNITS, 128), jnp.float32),
+        in_specs=[SM] + [VM] * (1 + n + 4 + len(before)),
         out_specs=VM,
         scratch_shapes=COPIES + [pltpu.VMEM((3 * n + 1, 8, R), jnp.float32)] * 3,
         compiler_params=PARAMS,
-        cost_estimate=pl.CostEstimate(flops=n * 1_600_000_000, bytes_accessed=4_000_000, transcendentals=0),
-        name="stats_near" if which == NEAR else "stats_far",
+        cost_estimate=pl.CostEstimate(flops=n * 800_000_000, bytes_accessed=4_000_000, transcendentals=0),
+        name=NAMES[which],
     )(meta, lim, *qds, *kvs, *before)
 
 
-def grads(meta, lim, sts, arrays):
-    dq = [jax.ShapeDtypeStruct((2 * SPAN, WIDE), t) for t in (jnp.float32,) + (jnp.bfloat16,) * 3]
+def grads(meta, lim, sts, qds, kvs):
+    dq = [jax.ShapeDtypeStruct((2 * SPAN, WIDE), jnp.float32)] * 4
+    dq += [jax.ShapeDtypeStruct((4, 2 * SPAN, WIDE), jnp.bfloat16)]
     dkv = [jax.ShapeDtypeStruct((4, 2 * SPAN, 2 * HD), jnp.bfloat16)] * 4
-    dkv += [jax.ShapeDtypeStruct((4, 4, 2 * SPAN, 2 * HD), jnp.bfloat16)]
     return pl.pallas_call(
         grads_kernel,
         out_shape=dq + dkv,
@@ -271,10 +276,10 @@
             pltpu.VMEM(((GROUPS + 1) * R, HD), jnp.float32),
         ]
         + [pltpu.VMEM((KB, R), jnp.bfloat16)] * 4
-        + [pltpu.VMEM((16, R), jnp.float32)] * 2,
+        + [pltpu.VMEM((32, R), jnp.float32)] * 2,
         compiler_params=PARAMS,
         name="grads",
-    )(meta, lim, *sts, *arrays)
+    )(meta, lim, *sts, *qds, *kvs)
 
 
 def permute(a, move):
@@ -306,44 +311,49 @@
     i32 = jnp.int32
     y, zl, core, zh, x = (lax.axis_index(a) for a in AXES)
     z = 2 * zh + zl
-    grid = span_slot.reshape(*SIZES, 2)
-    own_x = jnp.transpose(lax.dynamic_index_in_dim(grid, x, 4, keepdims=False), (2, 0, 3, 1, 4))
-    own_x = own_x.reshape(2, 4, 4, 2)
-    by_y = jnp.stack([lax.dynamic_index_in_dim(own_x, (y - r) % 4, 1, keepdims=False) for r in STEPS], 1)
-    by_yz = jnp.stack([lax.dynamic_index_in_dim(by_y, (z - r) % 4, 2, keepdims=False) for r in STEPS], 2)
-    of_core = jnp.stack([jnp.transpose(by_yz[0], (1, 0, 2)), by_yz[1]])
-    arrived = jnp.where(core == 0, of_core, of_core[::-1]).reshape(64)
-    ring = grid[y, zl, core, zh]
-    queries = jnp.concatenate([ring[(x - r) % 4] for r in STEPS])
+    i = jnp.arange(48, dtype=i32)
+    is_key = i < 32
+    low, high = (i // 2) % 4, (i // 8) % 4
+    low, high = low ^ (low >> 1), high ^ (high >> 1)
+    at_y = jnp.where(is_key, (y - jnp.where(core == 0, low, high)) % 4, y)
+    at_z = jnp.where(is_key, (z - jnp.where(core == 0, high, low)) % 4, z)
+    at_x = jnp.where(is_key, x, (x - low) % 4)
+    at_core = jnp.where(is_key | (i < 40), core, 1 - core)
+    slot = ((((at_y * 2 + at_z % 2) * 2 + at_core) * 2 + at_z // 2) * 4 + at_x) * 2 + i % 2
+    spans = jnp.sum(jnp.where(slot[:, None] == jnp.arange(256)[None, :], span_slot[None, :], 0), axis=1)
+    arrived, queries = spans[:32], spans[32:]
 
     def rank(a, among):
         return jnp.sum((among[None, :] < a[:, None]).astype(i32), axis=1)
 
     place = rank(queries, queries)
-    eight = jnp.arange(8, dtype=i32)
-    hit = (place[None, :] == eight[:, None]).astype(i32)
+    every = jnp.arange(UNITS, dtype=i32)
+    hit = (place[None, :] == every[:, None]).astype(i32)
     spans = jnp.sum(hit * queries[None, :], axis=1)
     below = rank(spans, arrived)
     own = jnp.any(arrived[None, :] == spans[:, None], axis=1).astype(i32)
-    far = jnp.sum(hit[:, 6:], axis=1)
-    before = jnp.sum(jnp.tril(jnp.ones((8, 8), i32), -1) * far[None, :], axis=1)
-    order = jnp.stack([eight, jnp.where(far == 0, eight - before, 9), jnp.where(far == 1, before, 9)])
-    taken = (order[:, None, :] == eight[None, :, None]).astype(i32)
-    canon = jnp.sum(taken * eight, axis=2)
+    group = jnp.where((every // 2) % 4 == 3, FAR, jnp.where(every < 8, NEAR, OTHER))
+    group = jnp.sum(hit * group, axis=1)
+    members = (group[None, :] == jnp.arange(4)[:, None]) | (jnp.arange(4)[:, None] == ALL)
+    lower = jnp.tril(jnp.ones((UNITS, UNITS), i32), -1)
+    before = jnp.sum(lower[None] * members.astype(i32)[:, None, :], axis=2)
+    order = jnp.where(members, before, 99)
+    taken = (order[:, None, :] == every[None, :, None]).astype(i32)
+    canon = jnp.sum(taken * every, axis=2)
     units = jnp.sum(order[:, None, :] * hit.T[None], axis=2)
     token = jnp.tile(jnp.arange(SPAN, dtype=i32), 2)
-    seen = below[:, None] * SPAN + own[:, None] * (token[None, :] + 1)
-    seen = jnp.sum(taken[:, :, :, None] * seen[None, None], axis=2)
+    count, diagonal = jnp.sum(taken * below, axis=2), jnp.sum(taken * own, axis=2)
+    seen = count[:, :, None] * SPAN + diagonal[:, :, None] * (token + 1)
     a, b = seen[:, 0::2], seen[:, 1::2]
-    lim = jnp.stack([a, a, a, b, b, b], axis=2).reshape(3, GROUPS, R)
-    lim = jnp.concatenate([lim, jnp.zeros((3, 4, R), i32)], axis=1)
-    tiles = ((below + own) * SPAN + KB - 1) // KB
-    tiles = jnp.sum(taken * tiles, axis=2)
-    each = jnp.stack([tiles[:, 0::2], tiles[:, 1::2], tiles[:, 1::2]], axis=2).reshape(3, GROUPS)
+    lim = jnp.stack([a, a, a, b, b, b], axis=2).reshape(4, GROUPS, R)
+    lim = jnp.concatenate([lim, jnp.zeros((4, 8, R), i32)], axis=1)
+    tiles = ((count + diagonal) * SPAN + KB - 1) // KB
+    each = jnp.stack([tiles[:, 0::2], tiles[:, 1::2], tiles[:, 1::2]], axis=2).reshape(4, GROUPS)
     end = jnp.sum(jnp.tril(jnp.ones((GROUPS, GROUPS), i32)) * each[:, None, :], axis=2)
     t = jnp.arange(LIST, dtype=i32)
     past = (t[None, :, None] >= end[:, None, :]).astype(i32)
-    group = jnp.minimum(jnp.sum(past, axis=2), jnp.array([[12], [9], [3]], i32))
+    last = jnp.array([[3 * len(ids)] for ids in IDS], i32)
+    group = jnp.minimum(jnp.sum(past, axis=2), last)
     block = jnp.where(t[None] < end[:, -1:], t[None] - jnp.sum(past * each[:, None, :], axis=2), 0)
     lists = jnp.concatenate([units, canon, end[:, -1:], group, block], axis=1)
     return jnp.concatenate([rank(arrived, arrived), lists.reshape(-1)]).astype(i32), lim
@@ -357,18 +367,22 @@
     near = [qd, x_shift(qd, 1), x_shift(qd, 3)]
     near[1], near[2], later = lax.optimization_barrier((near[1], near[2], qd))
     far = x_shift(later, 2)
-    kvs[0], kvs[1], span_slot = lax.optimization_barrier((kvs[0], kvs[1], span_slot))
+    other = [core_swap(a) for a in near]
+    kvs[1], span_slot = lax.optimization_barrier((kvs[1], span_slot))
     meta, lim = plan(span_slot)
-    kvs = kvs + [core_swap(a) for a in kvs]
-    arrays = near + [far] + kvs
 
     part = stats(NEAR, meta, lim, near, kvs)
-    part = stats(FAR, meta, lim, [far], kvs, part)
+    part, far = lax.optimization_barrier((part, far))
+    far_other = core_swap(far)
+    part = stats(OTHER, meta, lim, other, kvs, part)
+    part = stats(FAR, meta, lim, [far, far_other], kvs, part)
+    got = core_swap(part)
+    part = jnp.stack(merged(part[0], part[1], got[0], got[1]))
     got = permute(part, lambda y, z, core, x: (y, z, core, x ^ 1))
     part = jnp.stack(merged(part[0], part[1], got[0], got[1]))
     got = permute(part, lambda y, z, core, x: (y, z, core, x ^ 2))
-    results = grads(meta, lim, (part, got), arrays)
-    dqs, dkv, dkv_other = results[:4], results[4:8], results[8]
+    results = grads(meta, lim, (part, got), near + [far] + other + [far_other], kvs)
+    dqs, dq_other, dkv = results[:4], results[4], results[5:]
 
     def total(*parts):
         out = parts[0].astype(jnp.float32)
@@ -376,12 +390,16 @@
             out = out + part.astype(jnp.float32)
         return out
 
-    dq = total(dqs[0], *[x_shift(a, -r) for r, a in zip(STEPS[1:], dqs[1:])])
-    other = core_swap(dkv_other)
-    pairs = [total(a, other[i]).astype(jnp.bfloat16) for i, a in enumerate(dkv)]
-    some = total(pairs[0], *[second_shift(a, -r) for r, a in zip(STEPS[1:], pairs[1:])])
+    swapped = core_swap(dq_other)
+    first = [second_shift(a, -r) for r, a in zip(STEPS[1:3], dkv[1:3])]
+    last, swapped = lax.optimization_barrier((dkv[3], swapped))
+    some = total(dkv[0], *first, second_shift(last, -2))
+    pairs = [total(a, swapped[i]) for i, a in enumerate(dqs)]
+    back = [x_shift(a.astype(jnp.bfloat16), -r) for r, a in zip(STEPS[1:], pairs[1:])]
+    some, back[0], back[1] = lax.optimization_barrier((some, back[0], back[1]))
     sent = [first_shift(some[i].astype(jnp.bfloat16), -r) for i, r in ((1, 1), (2, 3), (3, 2))]
     summed = total(some[0], *sent)
+    dq = total(pairs[0], *back)
     return (
         dq.astype(jnp.bfloat16),
         summed[:, :HD].astype(jnp.bfloat16),

time: 103 us -> 111 us (1.078)
  starting transfers between devices: 29.6 us -> 38.2 us
  waiting for transfers between devices: 24 us -> 21.1 us
  Pallas kernels: 40.8 us -> 42.4 us
    ppermute x25 -> x26, starting transfers between devices: 29.6 us -> 38.2 us  [permute(): return lax.ppermute(a, AXES, pairs)]
    ppermute x25 -> x26, waiting for transfers between devices: 24 us -> 21.1 us  [permute(): return lax.ppermute(a, AXES, pairs)]
    pallas_call x2 -> x3, Pallas kernels: 16.4 us -> 17 us  [stats(): pl.pallas_call(functools.partial(stats_kernel, which), out_shape=jax.Shap...]
  transfers between devices with their start and end apart: 25 -> 26, of which waited for: 13 -> 11; matrix products, arithmetic and copies ran while one was open for 6% -> 5% of each run, Pallas kernels for 11% -> 11%
where the time goes in v6:
time: 111 us; the launch traced here: 110 us
  Pallas kernels  42.4 us (38%)
  starting transfers between devices  38.2 us (34%)
  waiting for transfers between devices  21.1 us (19%)
  other arithmetic  4.41 us (4%)
  local copies, waits for them, and re-layouts  3.37 us (3%)
    ppermute x26, starting transfers between devices, permute(): return lax.ppermute(a, AXES, pairs)  38.2 us
    pallas_call x1, Pallas kernels, grads(): pl.pallas_call(grads_kernel, out_shape=dq + dkv, in_specs=[SM] + [VM] * 1...  25.4 us
    ppermute x26, waiting for transfers between devices, permute(): return lax.ppermute(a, AXES, pairs)  21.1 us
    pallas_call x3, Pallas kernels, stats(): pl.pallas_call(functools.partial(stats_kernel, which), out_shape=jax.Shap...  17 us
  transfers between devices with their start and end apart: 26, of which 11 were waited for; matrix products, arithmetic and copies ran while one was open for 5% of the time, Pallas kernels for 11%

profile of v6, /device:TPU:0, one launch (start us, length us, event | category | flops | bytes accessed | tf_op | source)
XLA Modules:
  0.0 110.5 jit_solution(18157025248008768005)
XLA Ops:
  1.4 3.4 %collective-permute-start.2 = (bf16[1,128,256]{2,1,0:T(8,128)(2,1)S(1)}, bf16[1,128,256]{2,1,0:T(8,128)(2,1)S(1)}, u32[]{:S(2)}, u32[]{:S(2)}) collective-permute-start(bf16[1,128,256]{2,1,0:T(8,128)(2,1)S(1)} %maximum_bitcast_fusion), channel_id=1, source_target_pairs={{0,64},{1,65},{2,66},{3,67},{4,68},{5,69},{6,70},{7,71},{8,12},{9,... | collective-permute-start | bytes 196616 | tf_op jit(solution)/shard_map/ppermute | solution.py:291
  4.8 1.1 collective-permute-start.1
  7.9 2.8 %collective-permute-start.5 = (bf16[128,1536]{1,0:T(8,128)(2,1)S(1)}, bf16[128,1536]{1,0:T(8,128)(2,1)S(1)}, u32[]{:S(2)}, u32[]{:S(2)}) collective-permute-start(bf16[128,1536]{1,0:T(8,128)(2,1)S(1)} %constant_dynamic-update-slice_fusion.refs_0_), channel_id=1, source_target_pairs={{0,3},{1,0},{2,1},{3,2},{4,7},{5,4},{6,5},{7,6},{8,11},{9,8},{10,9... | collective-permute-start | bytes 1179656 | tf_op jit(solution)/shard_map/ppermute | solution.py:291
  11.3 2.0 %collective-permute-start.3 = (bf16[4,128,256]{2,1,0:T(8,128)(2,1)S(1)}, bf16[4,128,256]{2,1,0:T(8,128)(2,1)S(1)}, u32[]{:S(2)}, u32[]{:S(2)}) collective-permute-start(bf16[4,128,256]{2,1,0:T(8,128)(2,1)S(1)} %pad_maximum_fusion.refs_3_.refs_2_.refs_8_), channel_id=1, source_target_pairs={{0,16},{1,17},{2,18},{3,19},{4,20},{5,21},{6,22},{7,23},{8,40},{9,... | collective-permute-start | bytes 786440 | tf_op jit(solution)/shard_map/ppermute | solution.py:291
  13.5 3.6 %collective-permute-start.7 = (bf16[4,128,256]{2,1,0:T(8,128)(2,1)S(1)}, bf16[4,128,256]{2,1,0:T(8,128)(2,1)S(1)}, u32[]{:S(2)}, u32[]{:S(2)}) collective-permute-start(bf16[4,128,256]{2,1,0:T(8,128)(2,1)S(1)} %pad_maximum_fusion.refs_3_.refs_2_.refs_8_), channel_id=1, source_target_pairs={{0,4},{1,5},{2,6},{3,7},{4,0},{5,1},{6,2},{7,3},{8,72},{9,73},{10,... | collective-permute-start | bytes 786440 | tf_op jit(solution)/shard_map/ppermute | solution.py:291
  17.1 2.7 %collective-permute-done.3.refs_4_.refs_3_.refs_9_ = bf16[4,128,256]{2,1,0:T(8,128)(2,1)S(1)} collective-permute-done((bf16[4,128,256]{2,1,0:T(8,128)(2,1)S(1)}, bf16[4,128,256]{2,1,0:T(8,128)(2,1)S(1)}, u32[]{:S(2)}, u32[]{:S(2)}) %collective-permute-start.3) | collective-permute-done | bytes 262176 | tf_op jit(solution)/shard_map/ppermute | solution.py:291
  19.8 2.0 %collective-permute-start.6 = (bf16[4,128,256]{2,1,0:T(8,128)(2,1)S(1)}, bf16[4,128,256]{2,1,0:T(8,128)(2,1)S(1)}, u32[]{:S(2)}, u32[]{:S(2)}) collective-permute-start(bf16[4,128,256]{2,1,0:T(8,128)(2,1)S(1)} %pad_maximum_fusion.refs_3_.refs_2_.refs_8_), channel_id=1, source_target_pairs={{0,20},{1,21},{2,22},{3,23},{4,16},{5,17},{6,18},{7,19},{8,104},{9... | collective-permute-start | bytes 786440 | tf_op jit(solution)/shard_map/ppermute | solution.py:291
  25.2 3.1 %collective-permute-start.8 = (bf16[128,1536]{1,0:T(8,128)(2,1)S(1)}, bf16[128,1536]{1,0:T(8,128)(2,1)S(1)}, u32[]{:S(2)}, u32[]{:S(2)}) collective-permute-start(bf16[128,1536]{1,0:T(8,128)(2,1)S(1)} %constant_dynamic-update-slice_fusion.refs_0_), channel_id=1, source_target_pairs={{0,2},{1,3},{2,0},{3,1},{4,6},{5,7},{6,4},{7,5},{8,10},{9,11},{10,... | collective-permute-start | bytes 1179656 | tf_op jit(solution)/shard_map/ppermute | solution.py:291
  29.5 6.3 %stats_near.1.refs_7_ = f32[2,48,128]{2,1,0:T(8,128)S(1)} custom-call(s32[1252]{0:T(1024)S(1)} %pad_add_fusion.meta, s32[4,32,256]{2,1,0:T(8,128)S(1)} %concatenate.22.lim, bf16[128,1536]{1,0:T(8,128)(2,1)S(1)} %constant_dynamic-update-slice_fusion.refs_0_, bf16[128,1536]{1,0:T(8,128)(2,1)S(1)} %collective-permute-done.4.refs_1_, ...), custom_call_target="tpu_custom_call" | custom-call | flops 2400000000 | bytes 4000000 | tf_op jit(solution)/shard_map/stats_near/pallas_call | solution.py:252
  36.0 6.0 %stats_other.1.refs_6_ = f32[2,48,128]{2,1,0:T(8,128)S(1)} custom-call(s32[1252]{0:T(1024)S(1)} %pad_add_fusion.meta, s32[4,32,256]{2,1,0:T(8,128)S(1)} %concatenate.22.lim, bf16[128,1536]{1,0:T(8,128)(2,1)S(1)} %collective-permute-done.10.refs_0_.refs_4_, bf16[128,1536]{1,0:T(8,128)(2,1)S(1)} %collective-permute-done.11.refs_1_.refs_5_, ...), custom_call_target="tpu_custom_call" | custom-call | flops 2400000000 | bytes 4000000 | tf_op jit(solution)/shard_map/stats_other/pallas_call | solution.py:252
  42.1 4.6 %stats_far.1 = f32[2,48,128]{2,1,0:T(8,128)S(1)} custom-call(s32[1252]{0:T(1024)S(1)} %pad_add_fusion.meta, s32[4,32,256]{2,1,0:T(8,128)S(1)} %concatenate.22.lim, bf16[128,1536]{1,0:T(8,128)(2,1)S(1)} %collective-permute-done.8.refs_0_.refs_3_, bf16[128,1536]{1,0:T(8,128)(2,1)S(1)} %collective-permute-done.9.refs_1_.refs_7_, ...), custom_call_target="tpu_custom_call" | custom-call | flops 1600000000 | bytes 4000000 | tf_op jit(solution)/shard_map/stats_far/pallas_call | solution.py:252
  49.0 3.3 %collective-permute-done.14 = f32[2,48,128]{2,1,0:T(8,128)S(1)} collective-permute-done((f32[2,48,128]{2,1,0:T(8,128)S(1)}, f32[2,48,128]{2,1,0:T(8,128)S(1)}, u32[]{:S(2)}, u32[]{:S(2)}) %collective-permute-start.14) | collective-permute-done | bytes 49184 | tf_op jit(solution)/shard_map/ppermute | solution.py:291
  52.4 1.8 %collective-permute-start.15 = (f32[2,48,128]{2,1,0:T(8,128)S(1)}, f32[2,48,128]{2,1,0:T(8,128)S(1)}, u32[]{:S(2)}, u32[]{:S(2)}) collective-permute-start(f32[2,48,128]{2,1,0:T(8,128)S(1)} %pad_maximum_fusion.2.st0), channel_id=1, source_target_pairs={{0,2},{1,3},{2,0},{3,1},{4,6},{5,7},{6,4},{7,5},{8,10},{9,11},{10,... | collective-permute-start | bytes 147464 | tf_op jit(solution)/shard_map/ppermute | solution.py:291
  54.2 4.1 %collective-permute-done.15.st1 = f32[2,48,128]{2,1,0:T(8,128)S(1)} collective-permute-done((f32[2,48,128]{2,1,0:T(8,128)S(1)}, f32[2,48,128]{2,1,0:T(8,128)S(1)}, u32[]{:S(2)}, u32[]{:S(2)}) %collective-permute-start.15) | collective-permute-done | bytes 49184 | tf_op jit(solution)/shard_map/ppermute | solution.py:291
  58.3 25.4 %grads.1 = (f32[128,768]{1,0:T(8,128)S(1)}, f32[128,768]{1,0:T(8,128)S(1)}, f32[128,768]{1,0:T(8,128)S(1)}, f32[128,768]{1,0:T(8,128)S(1)}, bf16[4,128,768]{2,1,...) custom-call(s32[1252]{0:T(1024)S(1)} %pad_add_fusion.meta, ...), custom_call_target="tpu_custom_call" | custom-call | tf_op jit(solution)/shard_map/grads/pallas_call | solution.py:268
  83.7 2.9 %collective-permute-start.17 = (bf16[4,128,256]{2,1,0:T(8,128)(2,1)S(1)}, bf16[4,128,256]{2,1,0:T(8,128)(2,1)S(1)}, u32[]{:S(2)}, u32[]{:S(2)}) collective-permute-start(bf16[4,128,256]{2,1,0:T(8,128)(2,1)S(1)} %get-tuple-element.36), channel_id=1, source_target_pairs={{0,20},{1,21},{2,22},{3,23},{4,16},{5,17},{6,18},{7,19},{8,104},{9... | collective-permute-start | bytes 786440 | tf_op jit(solution)/shard_map/ppermute | solution.py:291
  86.6 2.9 %collective-permute-start.19 = (bf16[4,128,256]{2,1,0:T(8,128)(2,1)S(1)}, bf16[4,128,256]{2,1,0:T(8,128)(2,1)S(1)}, u32[]{:S(2)}, u32[]{:S(2)}) collective-permute-start(bf16[4,128,256]{2,1,0:T(8,128)(2,1)S(1)} %get-tuple-element.38), channel_id=1, source_target_pairs={{0,4},{1,5},{2,6},{3,7},{4,0},{5,1},{6,2},{7,3},{8,72},{9,73},{10,... | collective-permute-start | bytes 786440 | tf_op jit(solution)/shard_map/ppermute | solution.py:291
  90.4 4.0 %collective-permute-start.22 = (bf16[128,768]{1,0:T(8,128)(2,1)S(1)}, bf16[128,768]{1,0:T(8,128)(2,1)S(1)}, u32[]{:S(2)}, u32[]{:S(2)}) collective-permute-start(bf16[128,768]{1,0:T(8,128)(2,1)S(1)} %get-tuple-element.54), channel_id=1, source_target_pairs={{0,2},{1,3},{2,0},{3,1},{4,6},{5,7},{6,4},{7,5},{8,10},{9,11},{10,... | collective-permute-start | bytes 589832 | tf_op jit(solution)/shard_map/ppermute | solution.py:291
  95.0 2.0 %collective-permute-done.18 = bf16[4,128,256]{2,1,0:T(8,128)(2,1)S(1)} collective-permute-done((bf16[4,128,256]{2,1,0:T(8,128)(2,1)S(1)}, bf16[4,128,256]{2,1,0:T(8,128)(2,1)S(1)}, u32[]{:S(2)}, u32[]{:S(2)}) %collective-permute-start.18) | collective-permute-done | bytes 262176 | tf_op jit(solution)/shard_map/ppermute | solution.py:291
  97.1 1.3 %collective-permute-done.21 = bf16[128,768]{1,0:T(8,128)(2,1)S(1)} collective-permute-done((bf16[128,768]{1,0:T(8,128)(2,1)S(1)}, bf16[128,768]{1,0:T(8,128)(2,1)S(1)}, u32[]{:S(2)}, u32[]{:S(2)}) %collective-permute-start.21) | collective-permute-done | bytes 196640 | tf_op jit(solution)/shard_map/ppermute | solution.py:291
  98.4 1.6 %collective-permute-done.20 = bf16[128,768]{1,0:T(8,128)(2,1)S(1)} collective-permute-done((bf16[128,768]{1,0:T(8,128)(2,1)S(1)}, bf16[128,768]{1,0:T(8,128)(2,1)S(1)}, u32[]{:S(2)}, u32[]{:S(2)}) %collective-permute-start.20) | collective-permute-done | bytes 196640 | tf_op jit(solution)/shard_map/ppermute | solution.py:291
  100.1 3.1 %collective-permute-start.23 = (bf16[128,256]{1,0:T(8,128)(2,1)S(1)}, bf16[128,256]{1,0:T(8,128)(2,1)S(1)}, u32[]{:S(2)}, u32[]{:S(2)}) collective-permute-start(bf16[128,256]{1,0:T(8,128)(2,1)S(1)} %get-tuple-element.56), channel_id=1, source_target_pairs={{0,96},{1,97},{2,98},{3,99},{4,100},{5,101},{6,102},{7,103},{8,28}... | collective-permute-start | bytes 196616 | tf_op jit(solution)/shard_map/ppermute | solution.py:291
  103.2 1.2 %collective-permute-start.25 = (bf16[128,256]{1,0:T(8,128)(2,1)S(1)}, bf16[128,256]{1,0:T(8,128)(2,1)S(1)}, u32[]{:S(2)}, u32[]{:S(2)}) collective-permute-start(bf16[128,256]{1,0:T(8,128)(2,1)S(1)} %get-tuple-element.57), channel_id=1, source_target_pairs={{0,64},{1,65},{2,66},{3,67},{4,68},{5,69},{6,70},{7,71},{8,12},{9,... | collective-permute-start | bytes 196616 | tf_op jit(solution)/shard_map/ppermute | solution.py:291
  105.7 3.3 %collective-permute-done.25 = bf16[128,256]{1,0:T(8,128)(2,1)S(1)} collective-permute-done((bf16[128,256]{1,0:T(8,128)(2,1)S(1)}, bf16[128,256]{1,0:T(8,128)(2,1)S(1)}, u32[]{:S(2)}, u32[]{:S(2)}) %collective-permute-start.25) | collective-permute-done | bytes 65568 | tf_op jit(solution)/shard_map/ppermute | solution.py:291
  (99 shorter events, 15.1 us)
Async XLA Ops:
  1.4 9.3 %collective-permute-start.2 = (bf16[1,128,256]{2,1,0:T(8,128)(2,1)S(1)}, bf16[1,128,256]{2,1,0:T(8,128)(2,1)S(1)}, u32[]{:S(2)}, u32[]{:S(2)}) collective-permute-start(bf16[1,128,256]{2,1,0:T(8,128)(2,1)S(1)} %maximum_bitcast_fusion), channel_id=1, source_target_pairs={{0,64},{1,65},{2,66},{3,67},{4,68},{5,69},{6,70},{7,71},{8,12},{9,... | collective-permute-start | bytes 196616 | tf_op jit(solution)/shard_map/ppermute | solution.py:291
  4.8 6.1 %collective-permute-start.1 = (bf16[1,128,256]{2,1,0:T(8,128)(2,1)S(1)}, bf16[1,128,256]{2,1,0:T(8,128)(2,1)S(1)}, u32[]{:S(2)}, u32[]{:S(2)}) collective-permute-start(bf16[1,128,256]{2,1,0:T(8,128)(2,1)S(1)} %maximum_bitcast_fusion), channel_id=1, source_target_pairs={{0,96},{1,97},{2,98},{3,99},{4,100},{5,101},{6,102},{7,103},{8,28}... | collective-permute-start | bytes 196616 | tf_op jit(solution)/shard_map/ppermute | solution.py:291
  5.8 5.5 %collective-permute-start = (bf16[1,128,256]{2,1,0:T(8,128)(2,1)S(1)}, bf16[1,128,256]{2,1,0:T(8,128)(2,1)S(1)}, u32[]{:S(2)}, u32[]{:S(2)}) collective-permute-start(bf16[1,128,256]{2,1,0:T(8,128)(2,1)S(1)} %maximum_bitcast_fusion), channel_id=1, source_target_pairs={{0,32},{1,33},{2,34},{3,35},{4,36},{5,37},{6,38},{7,39},{8,24},{9,... | collective-permute-start | bytes 196616 | tf_op jit(solution)/shard_map/ppermute | solution.py:291
  7.8 28.2 %collective-permute-start.10 = (bf16[128,1536]{1,0:T(8,128)(2,1)S(1)}, bf16[128,1536]{1,0:T(8,128)(2,1)S(1)}, u32[]{:S(2)}, u32[]{:S(2)}) collective-permute-start(bf16[128,1536]{1,0:T(8,128)(2,1)S(1)} %constant_dynamic-update-slice_fusion.refs_0_), channel_id=1, source_target_pairs={{0,8},{1,9},{2,10},{3,11},{4,12},{5,13},{6,14},{7,15},{8,0},{9,1},... | collective-permute-start | bytes 1179656 | tf_op jit(solution)/shard_map/ppermute | solution.py:291
  7.9 17.3 %collective-permute-start.5 = (bf16[128,1536]{1,0:T(8,128)(2,1)S(1)}, bf16[128,1536]{1,0:T(8,128)(2,1)S(1)}, u32[]{:S(2)}, u32[]{:S(2)}) collective-permute-start(bf16[128,1536]{1,0:T(8,128)(2,1)S(1)} %constant_dynamic-update-slice_fusion.refs_0_), channel_id=1, source_target_pairs={{0,3},{1,0},{2,1},{3,2},{4,7},{5,4},{6,5},{7,6},{8,11},{9,8},{10,9... | collective-permute-start | bytes 1179656 | tf_op jit(solution)/shard_map/ppermute | solution.py:291
  10.8 14.4 %collective-permute-start.4 = (bf16[128,1536]{1,0:T(8,128)(2,1)S(1)}, bf16[128,1536]{1,0:T(8,128)(2,1)S(1)}, u32[]{:S(2)}, u32[]{:S(2)}) collective-permute-start(bf16[128,1536]{1,0:T(8,128)(2,1)S(1)} %constant_dynamic-update-slice_fusion.refs_0_), channel_id=1, source_target_pairs={{0,1},{1,2},{2,3},{3,0},{4,5},{5,6},{6,7},{7,4},{8,9},{9,10},{10,1... | collective-permute-start | bytes 1179656 | tf_op jit(solution)/shard_map/ppermute | solution.py:291
  11.3 8.5 %collective-permute-start.3 = (bf16[4,128,256]{2,1,0:T(8,128)(2,1)S(1)}, bf16[4,128,256]{2,1,0:T(8,128)(2,1)S(1)}, u32[]{:S(2)}, u32[]{:S(2)}) collective-permute-start(bf16[4,128,256]{2,1,0:T(8,128)(2,1)S(1)} %pad_maximum_fusion.refs_3_.refs_2_.refs_8_), channel_id=1, source_target_pairs={{0,16},{1,17},{2,18},{3,19},{4,20},{5,21},{6,22},{7,23},{8,40},{9,... | collective-permute-start | bytes 786440 | tf_op jit(solution)/shard_map/ppermute | solution.py:291
  13.5 15.5 %collective-permute-start.7 = (bf16[4,128,256]{2,1,0:T(8,128)(2,1)S(1)}, bf16[4,128,256]{2,1,0:T(8,128)(2,1)S(1)}, u32[]{:S(2)}, u32[]{:S(2)}) collective-permute-start(bf16[4,128,256]{2,1,0:T(8,128)(2,1)S(1)} %pad_maximum_fusion.refs_3_.refs_2_.refs_8_), channel_id=1, source_target_pairs={{0,4},{1,5},{2,6},{3,7},{4,0},{5,1},{6,2},{7,3},{8,72},{9,73},{10,... | collective-permute-start | bytes 786440 | tf_op jit(solution)/shard_map/ppermute | solution.py:291
  19.8 9.7 %collective-permute-start.6 = (bf16[4,128,256]{2,1,0:T(8,128)(2,1)S(1)}, bf16[4,128,256]{2,1,0:T(8,128)(2,1)S(1)}, u32[]{:S(2)}, u32[]{:S(2)}) collective-permute-start(bf16[4,128,256]{2,1,0:T(8,128)(2,1)S(1)} %pad_maximum_fusion.refs_3_.refs_2_.refs_8_), channel_id=1, source_target_pairs={{0,20},{1,21},{2,22},{3,23},{4,16},{5,17},{6,18},{7,19},{8,104},{9... | collective-permute-start | bytes 786440 | tf_op jit(solution)/shard_map/ppermute | solution.py:291
  25.2 10.7 %collective-permute-start.8 = (bf16[128,1536]{1,0:T(8,128)(2,1)S(1)}, bf16[128,1536]{1,0:T(8,128)(2,1)S(1)}, u32[]{:S(2)}, u32[]{:S(2)}) collective-permute-start(bf16[128,1536]{1,0:T(8,128)(2,1)S(1)} %constant_dynamic-update-slice_fusion.refs_0_), channel_id=1, source_target_pairs={{0,2},{1,3},{2,0},{3,1},{4,6},{5,7},{6,4},{7,5},{8,10},{9,11},{10,... | collective-permute-start | bytes 1179656 | tf_op jit(solution)/shard_map/ppermute | solution.py:291
  29.0 7.0 %collective-permute-start.11 = (bf16[128,1536]{1,0:T(8,128)(2,1)S(1)}, bf16[128,1536]{1,0:T(8,128)(2,1)S(1)}, u32[]{:S(2)}, u32[]{:S(2)}) collective-permute-start(bf16[128,1536]{1,0:T(8,128)(2,1)S(1)} %collective-permute-done.4.refs_1_), channel_id=1, source_target_pairs={{0,8},{1,9},{2,10},{3,11},{4,12},{5,13},{6,14},{7,15},{8,0},{9,1},... | collective-permute-start | bytes 1179656 | tf_op jit(solution)/shard_map/ppermute | solution.py:291
  29.0 7.0 %collective-permute-start.12 = (bf16[128,1536]{1,0:T(8,128)(2,1)S(1)}, bf16[128,1536]{1,0:T(8,128)(2,1)S(1)}, u32[]{:S(2)}, u32[]{:S(2)}) collective-permute-start(bf16[128,1536]{1,0:T(8,128)(2,1)S(1)} %collective-permute-done.5.refs_2_), channel_id=1, source_target_pairs={{0,8},{1,9},{2,10},{3,11},{4,12},{5,13},{6,14},{7,15},{8,0},{9,1},... | collective-permute-start | bytes 1179656 | tf_op jit(solution)/shard_map/ppermute | solution.py:291
  35.9 6.2 %collective-permute-start.9 = (bf16[128,1536]{1,0:T(8,128)(2,1)S(1)}, bf16[128,1536]{1,0:T(8,128)(2,1)S(1)}, u32[]{:S(2)}, u32[]{:S(2)}) collective-permute-start(bf16[128,1536]{1,0:T(8,128)(2,1)S(1)} %collective-permute-done.8.refs_0_.refs_3_), channel_id=1, source_target_pairs={{0,8},{1,9},{2,10},{3,11},{4,12},{5,13},{6,14},{7,15},{8,0},{9,1},... | collective-permute-start | bytes 1179656 | tf_op jit(solution)/shard_map/ppermute | solution.py:291
  48.2 4.2 %collective-permute-start.14 = (f32[2,48,128]{2,1,0:T(8,128)S(1)}, f32[2,48,128]{2,1,0:T(8,128)S(1)}, u32[]{:S(2)}, u32[]{:S(2)}) collective-permute-start(f32[2,48,128]{2,1,0:T(8,128)S(1)} %pad_maximum_fusion.1), channel_id=1, source_target_pairs={{0,1},{1,0},{2,3},{3,2},{4,5},{5,4},{6,7},{7,6},{8,9},{9,8},{10,11... | collective-permute-start | bytes 147464 | tf_op jit(solution)/shard_map/ppermute | solution.py:291
  52.4 5.9 %collective-permute-start.15 = (f32[2,48,128]{2,1,0:T(8,128)S(1)}, f32[2,48,128]{2,1,0:T(8,128)S(1)}, u32[]{:S(2)}, u32[]{:S(2)}) collective-permute-start(f32[2,48,128]{2,1,0:T(8,128)S(1)} %pad_maximum_fusion.2.st0), channel_id=1, source_target_pairs={{0,2},{1,3},{2,0},{3,1},{4,6},{5,7},{6,4},{7,5},{8,10},{9,11},{10,... | collective-permute-start | bytes 147464 | tf_op jit(solution)/shard_map/ppermute | solution.py:291
  83.7 10.7 %collective-permute-start.17 = (bf16[4,128,256]{2,1,0:T(8,128)(2,1)S(1)}, bf16[4,128,256]{2,1,0:T(8,128)(2,1)S(1)}, u32[]{:S(2)}, u32[]{:S(2)}) collective-permute-start(bf16[4,128,256]{2,1,0:T(8,128)(2,1)S(1)} %get-tuple-element.36), channel_id=1, source_target_pairs={{0,20},{1,21},{2,22},{3,23},{4,16},{5,17},{6,18},{7,19},{8,104},{9... | collective-permute-start | bytes 786440 | tf_op jit(solution)/shard_map/ppermute | solution.py:291
  86.6 10.4 %collective-permute-start.18 = (bf16[4,128,256]{2,1,0:T(8,128)(2,1)S(1)}, bf16[4,128,256]{2,1,0:T(8,128)(2,1)S(1)}, u32[]{:S(2)}, u32[]{:S(2)}) collective-permute-start(bf16[4,128,256]{2,1,0:T(8,128)(2,1)S(1)} %get-tuple-element.37), channel_id=1, source_target_pairs={{0,16},{1,17},{2,18},{3,19},{4,20},{5,21},{6,22},{7,23},{8,40},{9,... | collective-permute-start | bytes 786440 | tf_op jit(solution)/shard_map/ppermute | solution.py:291
  86.6 10.4 %collective-permute-start.19 = (bf16[4,128,256]{2,1,0:T(8,128)(2,1)S(1)}, bf16[4,128,256]{2,1,0:T(8,128)(2,1)S(1)}, u32[]{:S(2)}, u32[]{:S(2)}) collective-permute-start(bf16[4,128,256]{2,1,0:T(8,128)(2,1)S(1)} %get-tuple-element.38), channel_id=1, source_target_pairs={{0,4},{1,5},{2,6},{3,7},{4,0},{5,1},{6,2},{7,3},{8,72},{9,73},{10,... | collective-permute-start | bytes 786440 | tf_op jit(solution)/shard_map/ppermute | solution.py:291
  89.6 8.9 %collective-permute-start.21 = (bf16[128,768]{1,0:T(8,128)(2,1)S(1)}, bf16[128,768]{1,0:T(8,128)(2,1)S(1)}, u32[]{:S(2)}, u32[]{:S(2)}) collective-permute-start(bf16[128,768]{1,0:T(8,128)(2,1)S(1)} %get-tuple-element.53), channel_id=1, source_target_pairs={{0,1},{1,2},{2,3},{3,0},{4,5},{5,6},{6,7},{7,4},{8,9},{9,10},{10,1... | collective-permute-start | bytes 589832 | tf_op jit(solution)/shard_map/ppermute | solution.py:291
  90.4 14.0 %collective-permute-start.22 = (bf16[128,768]{1,0:T(8,128)(2,1)S(1)}, bf16[128,768]{1,0:T(8,128)(2,1)S(1)}, u32[]{:S(2)}, u32[]{:S(2)}) collective-permute-start(bf16[128,768]{1,0:T(8,128)(2,1)S(1)} %get-tuple-element.54), channel_id=1, source_target_pairs={{0,2},{1,3},{2,0},{3,1},{4,6},{5,7},{6,4},{7,5},{8,10},{9,11},{10,... | collective-permute-start | bytes 589832 | tf_op jit(solution)/shard_map/ppermute | solution.py:291
  94.4 5.7 %collective-permute-start.20 = (bf16[128,768]{1,0:T(8,128)(2,1)S(1)}, bf16[128,768]{1,0:T(8,128)(2,1)S(1)}, u32[]{:S(2)}, u32[]{:S(2)}) collective-permute-start(bf16[128,768]{1,0:T(8,128)(2,1)S(1)} %get-tuple-element.55), channel_id=1, source_target_pairs={{0,3},{1,0},{2,1},{3,2},{4,7},{5,4},{6,5},{7,6},{8,11},{9,8},{10,9... | collective-permute-start | bytes 589832 | tf_op jit(solution)/shard_map/ppermute | solution.py:291
  100.1 5.6 %collective-permute-start.23 = (bf16[128,256]{1,0:T(8,128)(2,1)S(1)}, bf16[128,256]{1,0:T(8,128)(2,1)S(1)}, u32[]{:S(2)}, u32[]{:S(2)}) collective-permute-start(bf16[128,256]{1,0:T(8,128)(2,1)S(1)} %get-tuple-element.56), channel_id=1, source_target_pairs={{0,96},{1,97},{2,98},{3,99},{4,100},{5,101},{6,102},{7,103},{8,28}... | collective-permute-start | bytes 196616 | tf_op jit(solution)/shard_map/ppermute | solution.py:291
  103.2 5.8 %collective-permute-start.25 = (bf16[128,256]{1,0:T(8,128)(2,1)S(1)}, bf16[128,256]{1,0:T(8,128)(2,1)S(1)}, u32[]{:S(2)}, u32[]{:S(2)}) collective-permute-start(bf16[128,256]{1,0:T(8,128)(2,1)S(1)} %get-tuple-element.57), channel_id=1, source_target_pairs={{0,64},{1,65},{2,66},{3,67},{4,68},{5,69},{6,70},{7,71},{8,12},{9,... | collective-permute-start | bytes 196616 | tf_op jit(solution)/shard_map/ppermute | solution.py:291
  104.3 5.5 %collective-permute-start.24 = (bf16[128,256]{1,0:T(8,128)(2,1)S(1)}, bf16[128,256]{1,0:T(8,128)(2,1)S(1)}, u32[]{:S(2)}, u32[]{:S(2)}) collective-permute-start(bf16[128,256]{1,0:T(8,128)(2,1)S(1)} %get-tuple-element.58), channel_id=1, source_target_pairs={{0,32},{1,33},{2,34},{3,35},{4,36},{5,37},{6,38},{7,39},{8,24},{9,... | collective-permute-start | bytes 196616 | tf_op jit(solution)/shard_map/ppermute | solution.py:291
  (8 other events, 36.5 us)

commit v7 on v5

--- a/solution.py
+++ b/solution.py
@@ -23,11 +23,11 @@
 KB = 256
 R = 256
 GROUPS = 12
-UNROLL = 8
-LIST = 136
+MANY, FEW = 16, 8
+LIST = 144
 IN = 0
 ALL, NEAR, FAR = range(3)
-UNIT, CANON, COUNT, GROUP = 0, 8, 16, 17
+UNIT, CANON, FULL, COUNT, GROUP = 0, 8, 16, 17, 18
 BLOCK = GROUP + LIST
 SIZE = BLOCK + LIST
 
@@ -63,20 +63,18 @@
     return top + jnp.log2(total), (w * delta + w_b * delta_b) / total
 
 
-def tiles_loop(count, step):
-    def many(i, carry):
-        for v in range(UNROLL):
-            step(i * UNROLL + v, v)
-        return carry
-
-    def few(i, carry):
-        for v in range(2):
-            step(i * 2 + v, v)
-        return carry
-
-    bodies = count // UNROLL
-    lax.fori_loop(0, bodies, many, 0)
-    lax.fori_loop(bodies * (UNROLL // 2), (count + 1) // 2, few, 0)
+def tiles_loop(full, count, step):
+    def body(size, masked):
+        def run(i, carry):
+            for v in range(size):
+                step(i * size + v, v, masked)
+            return carry
+
+        return run
+
+    bodies = full // MANY
+    lax.fori_loop(0, bodies, body(MANY, False), 0)
+    lax.fori_loop(bodies * (MANY // FEW), (count + FEW - 1) // FEW, body(FEW, True), 0)
 
 
 def load_sorted(meta, kvs, kv_s):
@@ -129,11 +127,13 @@
     d_s[...] = jnp.zeros_like(d_s)
     iota = lax.broadcasted_iota(jnp.int32, (KB, R), 0)
 
-    def online(t, s_b, dp_b):
+    def online(t, s_b, dp_b, masked):
         g = meta[base + GROUP + t]
-        limit = lim[which, pl.ds(g, 1), :] - meta[base + BLOCK + t] * KB
         rows = [slice(8 * i, 8 * i + 8) for i in range(KB // 8)]
-        s = [jnp.where(iota[r] < limit, s_b[r, :] * C2, NEG) for r in rows]
+        s = [s_b[r, :] * C2 for r in rows]
+        if masked:
+            limit = lim[which, pl.ds(g, 1), :] - meta[base + BLOCK + t] * KB
+            s = [jnp.where(iota[r] < limit, x, NEG) for r, x in zip(rows, s)]
         m = m_s[g]
         top = jnp.maximum(m, tree(jnp.maximum, s))
         a = jnp.exp2(m - top)
@@ -145,11 +145,11 @@
     ss, dps = (s0, s1), (dp0, dp1)
     products(meta, base, 0, q_s, do_s, kv_s, s0, dp0)
 
-    def step(t, v):
+    def step(t, v, masked):
         products(meta, base, t + 1, q_s, do_s, kv_s, ss[(v + 1) % 2], dps[(v + 1) % 2])
-        online(t, ss[v % 2], dps[v % 2])
-
-    tiles_loop(meta[base + COUNT], step)
+        online(t, ss[v % 2], dps[v % 2], masked)
+
+    tiles_loop(meta[base + FULL], meta[base + COUNT], step)
     out[...] = before[...] if which == FAR else jnp.zeros_like(out)
     for g in range(groups):
         m = m_s[g]
@@ -188,10 +188,12 @@
             delta[g : g + 1, at] = all_delta[row : row + 1]
     iota = lax.broadcasted_iota(jnp.int32, (KB, R), 0)
 
-    def weights(t, s_b, dp_b, p_b, ds_b):
+    def weights(t, s_b, dp_b, p_b, ds_b, masked):
         g = meta[base + GROUP + t]
-        limit = lim[ALL, pl.ds(g, 1), :] - meta[base + BLOCK + t] * KB
-        p = jnp.where(iota < limit, jnp.exp2(s_b[...] * C2 - lse[pl.ds(g, 1), :]), 0.0)
+        p = jnp.exp2(s_b[...] * C2 - lse[pl.ds(g, 1), :])
+        if masked:
+            limit = lim[ALL, pl.ds(g, 1), :] - meta[base + BLOCK + t] * KB
+            p = jnp.where(iota < limit, p, 0.0)
         p_b[...] = p.astype(jnp.bfloat16)
         ds_b[...] = (p * (dp_b[...] - delta[pl.ds(g, 1), :])).astype(jnp.bfloat16)
 
@@ -207,15 +209,15 @@
     ss, dps, ps, dss = (s0, s1), (dp0, dp1), (p0, p1), (ds0, ds1)
     products(meta, base, 0, q_s, do_s, kv_s, s0, dp0)
     products(meta, base, 1, q_s, do_s, kv_s, s1, dp1)
-    weights(0, s0, dp0, p0, ds0)
-
-    def step(t, v):
+    weights(0, s0, dp0, p0, ds0, True)
+
+    def step(t, v, masked):
         a, b = v % 2, 1 - v % 2
         products(meta, base, t + 2, q_s, do_s, kv_s, ss[a], dps[a])
-        weights(t + 1, ss[b], dps[b], ps[b], dss[b])
+        weights(t + 1, ss[b], dps[b], ps[b], dss[b], masked or v == MANY - 1)
         sums(t, ps[a], dss[a])
 
-    tiles_loop(meta[base + COUNT], step)
+    tiles_loop(meta[base + FULL], meta[base + COUNT], step)
     for d in range(4):
         for half in range(2):
             place = meta[base + UNIT + 2 * d + half]
@@ -337,15 +339,21 @@
     a, b = seen[:, 0::2], seen[:, 1::2]
     lim = jnp.stack([a, a, a, b, b, b], axis=2).reshape(3, GROUPS, R)
     lim = jnp.concatenate([lim, jnp.zeros((3, 4, R), i32)], axis=1)
-    tiles = ((below + own) * SPAN + KB - 1) // KB
-    tiles = jnp.sum(taken * tiles, axis=2)
-    each = jnp.stack([tiles[:, 0::2], tiles[:, 1::2], tiles[:, 1::2]], axis=2).reshape(3, GROUPS)
-    end = jnp.sum(jnp.tril(jnp.ones((GROUPS, GROUPS), i32)) * each[:, None, :], axis=2)
+    most = (jnp.sum(taken * (below + own), axis=2) * SPAN + KB - 1) // KB
+    least = jnp.sum(taken * below, axis=2) * SPAN // KB
+    most = jnp.stack([most[:, 0::2], most[:, 1::2], most[:, 1::2]], axis=2).reshape(3, GROUPS)
+    least = jnp.stack([least[:, 0::2], least[:, 0::2], least[:, 1::2]], axis=2).reshape(3, GROUPS)
+    each = jnp.concatenate([least, most - least], axis=1)
+    first = jnp.concatenate([jnp.zeros_like(least), least], axis=1)
+    end = jnp.sum(jnp.tril(jnp.ones((2 * GROUPS, 2 * GROUPS), i32)) * each[:, None, :], axis=2)
     t = jnp.arange(LIST, dtype=i32)
-    past = (t[None, :, None] >= end[:, None, :]).astype(i32)
-    group = jnp.minimum(jnp.sum(past, axis=2), jnp.array([[12], [9], [3]], i32))
-    block = jnp.where(t[None] < end[:, -1:], t[None] - jnp.sum(past * each[:, None, :], axis=2), 0)
-    lists = jnp.concatenate([units, canon, end[:, -1:], group, block], axis=1)
+    begin = end - each
+    inside = ((t[None, :, None] >= begin[:, None, :]) & (t[None, :, None] < end[:, None, :])).astype(i32)
+    number = jnp.tile(jnp.arange(GROUPS, dtype=i32), 2)
+    group = jnp.sum(inside * number, axis=2)
+    block = jnp.sum(inside * (t[None, :, None] - (begin - first)[:, None, :]), axis=2)
+    group = jnp.where(t[None] < end[:, -1:], group, jnp.array([[12], [9], [3]], i32))
+    lists = jnp.concatenate([units, canon, end[:, GROUPS - 1 : GROUPS], end[:, -1:], group, block], axis=1)
     return jnp.concatenate([rank(arrived, arrived), lists.reshape(-1)]).astype(i32), lim
 
 
@@ -357,7 +365,7 @@
     near = [qd, x_shift(qd, 1), x_shift(qd, 3)]
     near[1], near[2], later = lax.optimization_barrier((near[1], near[2], qd))
     far = x_shift(later, 2)
-    kvs[0], kvs[1], span_slot = lax.optimization_barrier((kvs[0], kvs[1], span_slot))
+    kvs[1], span_slot = lax.optimization_barrier((kvs[1], span_slot))
     meta, lim = plan(span_slot)
     kvs = kvs + [core_swap(a) for a in kvs]
     arrays = near + [far] + kvs

time: 103 us -> 105 us (1.019)
  starting transfers between devices: 29.6 us -> 36.2 us
  Pallas kernels: 40.8 us -> 37.6 us
  waiting for transfers between devices: 24 us -> 20.9 us
  local copies, waits for them, and re-layouts: 3.36 us -> 4.48 us
    ppermute x25, starting transfers between devices: 29.6 us -> 36.2 us  [permute(): return lax.ppermute(a, AXES, pairs)]
    ppermute x25, waiting for transfers between devices: 24 us -> 20.9 us  [permute(): return lax.ppermute(a, AXES, pairs)]
    pallas_call x2, Pallas kernels: 16.4 us -> 13.3 us  [stats(): pl.pallas_call(functools.partial(stats_kernel, which, n), out_shape=jax.S...]
  transfers between devices with their start and end apart: 25 -> 25, of which waited for: 13 -> 13; matrix products, arithmetic and copies ran while one was open for 6% -> 6% of each run, Pallas kernels for 11% -> 9%
where the time goes in v7:
time: 105 us
  Pallas kernels  37.6 us (36%)
  starting transfers between devices  36.2 us (34%)
  waiting for transfers between devices  20.9 us (20%)
  other arithmetic  4.5 us (4%)
  local copies, waits for them, and re-layouts  4.48 us (4%)
    ppermute x25, starting transfers between devices, permute(): return lax.ppermute(a, AXES, pairs)  36.2 us
    pallas_call x1, Pallas kernels, grads(): pl.pallas_call(grads_kernel, out_shape=dq + dkv, in_specs=[SM] + [VM] * 1...  24.2 us
    ppermute x25, waiting for transfers between devices, permute(): return lax.ppermute(a, AXES, pairs)  20.9 us
    pallas_call x2, Pallas kernels, stats(): pl.pallas_call(functools.partial(stats_kernel, which, n), out_shape=jax.S...  13.3 us
  transfers between devices with their start and end apart: 25, of which 13 were waited for; matrix products, arithmetic and copies ran while one was open for 6% of the time, Pallas kernels for 9%

profile of v7, /device:TPU:0, one launch (start us, length us, event | category | flops | bytes accessed | tf_op | source)
XLA Modules:
  0.0 104.7 jit_solution(13400736213677320551)
XLA Ops:
  1.4 3.4 %collective-permute-start.2 = (bf16[1,128,256]{2,1,0:T(8,128)(2,1)S(1)}, bf16[1,128,256]{2,1,0:T(8,128)(2,1)S(1)}, u32[]{:S(2)}, u32[]{:S(2)}) collective-permute-start(bf16[1,128,256]{2,1,0:T(8,128)(2,1)S(1)} %maximum_bitcast_fusion), channel_id=1, source_target_pairs={{0,64},{1,65},{2,66},{3,67},{4,68},{5,69},{6,70},{7,71},{8,12},{9,... | collective-permute-start | bytes 196616 | tf_op jit(solution)/shard_map/ppermute | solution.py:288
  7.8 2.8 %collective-permute-start.5 = (bf16[128,1536]{1,0:T(8,128)(2,1)S(1)}, bf16[128,1536]{1,0:T(8,128)(2,1)S(1)}, u32[]{:S(2)}, u32[]{:S(2)}) collective-permute-start(bf16[128,1536]{1,0:T(8,128)(2,1)S(1)} %constant_dynamic-update-slice_fusion.6.refs_0_), channel_id=1, source_target_pairs={{0,3},{1,0},{2,1},{3,2},{4,7},{5,4},{6,5},{7,6},{8,11},{9,8},{10,9... | collective-permute-start | bytes 1179656 | tf_op jit(solution)/shard_map/ppermute | solution.py:288
  11.3 2.0 %collective-permute-start.3 = (bf16[4,128,256]{2,1,0:T(8,128)(2,1)S(1)}, bf16[4,128,256]{2,1,0:T(8,128)(2,1)S(1)}, u32[]{:S(2)}, u32[]{:S(2)}) collective-permute-start(bf16[4,128,256]{2,1,0:T(8,128)(2,1)S(1)} %pad_maximum_fusion.refs_3_.refs_1_.refs_4_), channel_id=1, source_target_pairs={{0,16},{1,17},{2,18},{3,19},{4,20},{5,21},{6,22},{7,23},{8,40},{9,... | collective-permute-start | bytes 786440 | tf_op jit(solution)/shard_map/ppermute | solution.py:288
  13.6 3.7 %collective-permute-start.8 = (bf16[4,128,256]{2,1,0:T(8,128)(2,1)S(1)}, bf16[4,128,256]{2,1,0:T(8,128)(2,1)S(1)}, u32[]{:S(2)}, u32[]{:S(2)}) collective-permute-start(bf16[4,128,256]{2,1,0:T(8,128)(2,1)S(1)} %pad_maximum_fusion.refs_3_.refs_1_.refs_4_), channel_id=1, source_target_pairs={{0,4},{1,5},{2,6},{3,7},{4,0},{5,1},{6,2},{7,3},{8,72},{9,73},{10,... | collective-permute-start | bytes 786440 | tf_op jit(solution)/shard_map/ppermute | solution.py:288
  17.3 2.5 %collective-permute-done.3.refs_4_.refs_2_.refs_5_ = bf16[4,128,256]{2,1,0:T(8,128)(2,1)S(1)} collective-permute-done((bf16[4,128,256]{2,1,0:T(8,128)(2,1)S(1)}, bf16[4,128,256]{2,1,0:T(8,128)(2,1)S(1)}, u32[]{:S(2)}, u32[]{:S(2)}) %collective-permute-start.3) | collective-permute-done | bytes 262176 | tf_op jit(solution)/shard_map/ppermute | solution.py:288
  19.8 2.0 %collective-permute-start.7 = (bf16[4,128,256]{2,1,0:T(8,128)(2,1)S(1)}, bf16[4,128,256]{2,1,0:T(8,128)(2,1)S(1)}, u32[]{:S(2)}, u32[]{:S(2)}) collective-permute-start(bf16[4,128,256]{2,1,0:T(8,128)(2,1)S(1)} %pad_maximum_fusion.refs_3_.refs_1_.refs_4_), channel_id=1, source_target_pairs={{0,20},{1,21},{2,22},{3,23},{4,16},{5,17},{6,18},{7,19},{8,104},{9... | collective-permute-start | bytes 786440 | tf_op jit(solution)/shard_map/ppermute | solution.py:288
  27.9 3.5 %collective-permute-start.6 = (bf16[128,1536]{1,0:T(8,128)(2,1)S(1)}, bf16[128,1536]{1,0:T(8,128)(2,1)S(1)}, u32[]{:S(2)}, u32[]{:S(2)}) collective-permute-start(bf16[128,1536]{1,0:T(8,128)(2,1)S(1)} %constant_dynamic-update-slice_fusion.6.refs_0_), channel_id=1, source_target_pairs={{0,2},{1,3},{2,0},{3,1},{4,6},{5,7},{6,4},{7,5},{8,10},{9,11},{10,... | collective-permute-start | bytes 1179656 | tf_op jit(solution)/shard_map/ppermute | solution.py:288
  31.4 8.9 %stats_near.1.refs_9_ = f32[2,24,128]{2,1,0:T(8,128)S(1)} custom-call(s32[982]{0:T(1024)S(1)} %pad_add_fusion.5.meta, s32[3,16,256]{2,1,0:T(8,128)S(1)} %concatenate.38.lim, bf16[128,1536]{1,0:T(8,128)(2,1)S(1)} %constant_dynamic-update-slice_fusion.6.refs_0_, bf16[128,1536]{1,0:T(8,128)(2,1)S(1)} %collective-permute-done.4.refs_1_, ...), custom_call_target="tpu_custom_call" | custom-call | flops 4800000000 | bytes 4000000 | tf_op jit(solution)/shard_map/stats_near/pallas_call | solution.py:249
  41.0 4.4 %stats_far.1 = f32[2,24,128]{2,1,0:T(8,128)S(1)} custom-call(s32[982]{0:T(1024)S(1)} %pad_add_fusion.5.meta, s32[3,16,256]{2,1,0:T(8,128)S(1)} %concatenate.38.lim, bf16[128,1536]{1,0:T(8,128)(2,1)S(1)} %collective-permute-done.6.refs_0_.refs_3_, bf16[4,128,256]{2,1,0:T(8,128)(2,1)S(1)} %pad_maximum_fusion.refs_3_.refs_1_.refs_4_, ...), custom_call_target="tpu_custom_call" | custom-call | flops 1600000000 | bytes 4000000 | tf_op jit(solution)/shard_map/stats_far/pallas_call | solution.py:249
  45.5 2.0 %collective-permute-start.13 = (f32[2,24,128]{2,1,0:T(8,128)S(1)}, f32[2,24,128]{2,1,0:T(8,128)S(1)}, u32[]{:S(2)}, u32[]{:S(2)}) collective-permute-start(f32[2,24,128]{2,1,0:T(8,128)S(1)} %stats_far.1), channel_id=1, source_target_pairs={{0,1},{1,0},{2,3},{3,2},{4,5},{5,4},{6,7},{7,6},{8,9},{9,8},{10,11... | collective-permute-start | bytes 73736 | tf_op jit(solution)/shard_map/ppermute | solution.py:288
  47.4 2.3 %collective-permute-done.13 = f32[2,24,128]{2,1,0:T(8,128)S(1)} collective-permute-done((f32[2,24,128]{2,1,0:T(8,128)S(1)}, f32[2,24,128]{2,1,0:T(8,128)S(1)}, u32[]{:S(2)}, u32[]{:S(2)}) %collective-permute-start.13) | collective-permute-done | bytes 24608 | tf_op jit(solution)/shard_map/ppermute | solution.py:288
  49.7 3.2 %collective-permute-start.14 = (f32[2,24,128]{2,1,0:T(8,128)S(1)}, f32[2,24,128]{2,1,0:T(8,128)S(1)}, u32[]{:S(2)}, u32[]{:S(2)}) collective-permute-start(f32[2,24,128]{2,1,0:T(8,128)S(1)} %pad_maximum_fusion.1.st0), channel_id=1, source_target_pairs={{0,2},{1,3},{2,0},{3,1},{4,6},{5,7},{6,4},{7,5},{8,10},{9,11},{10,... | collective-permute-start | bytes 73736 | tf_op jit(solution)/shard_map/ppermute | solution.py:288
  52.9 2.2 %collective-permute-done.14.st1 = f32[2,24,128]{2,1,0:T(8,128)S(1)} collective-permute-done((f32[2,24,128]{2,1,0:T(8,128)S(1)}, f32[2,24,128]{2,1,0:T(8,128)S(1)}, u32[]{:S(2)}, u32[]{:S(2)}) %collective-permute-start.14) | collective-permute-done | bytes 24608 | tf_op jit(solution)/shard_map/ppermute | solution.py:288
  55.1 24.2 %grads.1 = (f32[128,768]{1,0:T(8,128)S(1)}, bf16[128,768]{1,0:T(8,128)(2,1)S(1)}, bf16[128,768]{1,0:T(8,128)(2,1)S(1)}, bf16[128,768]{1,0:T(8,128)(2,1)S(1)}, bf...) custom-call(s32[982]{0:T(1024)S(1)} %pad_add_fusion.5.meta, ...), custom_call_target="tpu_custom_call" | custom-call | tf_op jit(solution)/shard_map/grads/pallas_call | solution.py:265
  79.4 2.9 %collective-permute-done.18 = bf16[4,4,128,256]{3,2,1,0:T(8,128)(2,1)S(1)} collective-permute-done((bf16[4,4,128,256]{3,2,1,0:T(8,128)(2,1)}, bf16[4,4,128,256]{3,2,1,0:T(8,128)(2,1)S(1)}, u32[]{:S(2)}, u32[]{:S(2)}) %collective-permute-start.18) | collective-permute-done | bytes 1048608 | tf_op jit(solution)/shard_map/ppermute | solution.py:288
  82.5 3.9 %collective-permute-start.19 = (bf16[4,128,256]{2,1,0:T(8,128)(2,1)S(1)}, bf16[4,128,256]{2,1,0:T(8,128)(2,1)S(1)}, u32[]{:S(2)}, u32[]{:S(2)}) collective-permute-start(bf16[4,128,256]{2,1,0:T(8,128)(2,1)S(1)} %get-tuple-element.41), channel_id=1, source_target_pairs={{0,20},{1,21},{2,22},{3,23},{4,16},{5,17},{6,18},{7,19},{8,104},{9... | collective-permute-start | bytes 786440 | tf_op jit(solution)/shard_map/ppermute | solution.py:288
  87.4 1.4 %collective-permute-start.15 = (bf16[128,768]{1,0:T(8,128)(2,1)S(1)}, bf16[128,768]{1,0:T(8,128)(2,1)S(1)}, u32[]{:S(2)}, u32[]{:S(2)}) collective-permute-start(bf16[128,768]{1,0:T(8,128)(2,1)S(1)} %get-tuple-element.23), channel_id=1, source_target_pairs={{0,3},{1,0},{2,1},{3,2},{4,7},{5,4},{6,5},{7,6},{8,11},{9,8},{10,9... | collective-permute-start | bytes 589832 | tf_op jit(solution)/shard_map/ppermute | solution.py:288
  89.4 3.7 %collective-permute-done.19 = bf16[4,128,256]{2,1,0:T(8,128)(2,1)S(1)} collective-permute-done((bf16[4,128,256]{2,1,0:T(8,128)(2,1)S(1)}, bf16[4,128,256]{2,1,0:T(8,128)(2,1)S(1)}, u32[]{:S(2)}, u32[]{:S(2)}) %collective-permute-start.19) | collective-permute-done | bytes 262176 | tf_op jit(solution)/shard_map/ppermute | solution.py:288
  93.1 2.1 %collective-permute-start.17 = (bf16[128,768]{1,0:T(8,128)(2,1)S(1)}, bf16[128,768]{1,0:T(8,128)(2,1)S(1)}, u32[]{:S(2)}, u32[]{:S(2)}) collective-permute-start(bf16[128,768]{1,0:T(8,128)(2,1)S(1)} %get-tuple-element.25), channel_id=1, source_target_pairs={{0,2},{1,3},{2,0},{3,1},{4,6},{5,7},{6,4},{7,5},{8,10},{9,11},{10,... | collective-permute-start | bytes 589832 | tf_op jit(solution)/shard_map/ppermute | solution.py:288
  95.2 1.6 %collective-permute-done.20 = bf16[4,128,256]{2,1,0:T(8,128)(2,1)S(1)} collective-permute-done((bf16[4,128,256]{2,1,0:T(8,128)(2,1)S(1)}, bf16[4,128,256]{2,1,0:T(8,128)(2,1)S(1)}, u32[]{:S(2)}, u32[]{:S(2)}) %collective-permute-start.20) | collective-permute-done | bytes 262176 | tf_op jit(solution)/shard_map/ppermute | solution.py:288
  97.2 1.9 %collective-permute-start.23 = (bf16[128,256]{1,0:T(8,128)(2,1)S(1)}, bf16[128,256]{1,0:T(8,128)(2,1)S(1)}, u32[]{:S(2)}, u32[]{:S(2)}) collective-permute-start(bf16[128,256]{1,0:T(8,128)(2,1)S(1)} %get-tuple-element.46), channel_id=1, source_target_pairs={{0,32},{1,33},{2,34},{3,35},{4,36},{5,37},{6,38},{7,39},{8,24},{9,... | collective-permute-start | bytes 196616 | tf_op jit(solution)/shard_map/ppermute | solution.py:288
  99.1 1.2 %collective-permute-done.17 = bf16[128,768]{1,0:T(8,128)(2,1)S(1)} collective-permute-done((bf16[128,768]{1,0:T(8,128)(2,1)S(1)}, bf16[128,768]{1,0:T(8,128)(2,1)S(1)}, u32[]{:S(2)}, u32[]{:S(2)}) %collective-permute-start.17) | collective-permute-done | bytes 196640 | tf_op jit(solution)/shard_map/ppermute | solution.py:288
  101.3 1.6 %collective-permute-done.24 = bf16[128,256]{1,0:T(8,128)(2,1)S(1)} collective-permute-done((bf16[128,256]{1,0:T(8,128)(2,1)S(1)}, bf16[128,256]{1,0:T(8,128)(2,1)S(1)}, u32[]{:S(2)}, u32[]{:S(2)}) %collective-permute-start.24) | collective-permute-done | bytes 65568 | tf_op jit(solution)/shard_map/ppermute | solution.py:288
  102.9 1.1 %collective-permute-done.23 = bf16[128,256]{1,0:T(8,128)(2,1)S(1)} collective-permute-done((bf16[128,256]{1,0:T(8,128)(2,1)S(1)}, bf16[128,256]{1,0:T(8,128)(2,1)S(1)}, u32[]{:S(2)}, u32[]{:S(2)}) %collective-permute-start.23) | collective-permute-done | bytes 65568 | tf_op jit(solution)/shard_map/ppermute | solution.py:288
  (118 shorter events, 15.2 us)
Async XLA Ops:
  1.4 9.2 %collective-permute-start.2 = (bf16[1,128,256]{2,1,0:T(8,128)(2,1)S(1)}, bf16[1,128,256]{2,1,0:T(8,128)(2,1)S(1)}, u32[]{:S(2)}, u32[]{:S(2)}) collective-permute-start(bf16[1,128,256]{2,1,0:T(8,128)(2,1)S(1)} %maximum_bitcast_fusion), channel_id=1, source_target_pairs={{0,64},{1,65},{2,66},{3,67},{4,68},{5,69},{6,70},{7,71},{8,12},{9,... | collective-permute-start | bytes 196616 | tf_op jit(solution)/shard_map/ppermute | solution.py:288
  4.8 5.8 %collective-permute-start.1 = (bf16[1,128,256]{2,1,0:T(8,128)(2,1)S(1)}, bf16[1,128,256]{2,1,0:T(8,128)(2,1)S(1)}, u32[]{:S(2)}, u32[]{:S(2)}) collective-permute-start(bf16[1,128,256]{2,1,0:T(8,128)(2,1)S(1)} %maximum_bitcast_fusion), channel_id=1, source_target_pairs={{0,96},{1,97},{2,98},{3,99},{4,100},{5,101},{6,102},{7,103},{8,28}... | collective-permute-start | bytes 196616 | tf_op jit(solution)/shard_map/ppermute | solution.py:288
  5.8 5.5 %collective-permute-start = (bf16[1,128,256]{2,1,0:T(8,128)(2,1)S(1)}, bf16[1,128,256]{2,1,0:T(8,128)(2,1)S(1)}, u32[]{:S(2)}, u32[]{:S(2)}) collective-permute-start(bf16[1,128,256]{2,1,0:T(8,128)(2,1)S(1)} %maximum_bitcast_fusion), channel_id=1, source_target_pairs={{0,32},{1,33},{2,34},{3,35},{4,36},{5,37},{6,38},{7,39},{8,24},{9,... | collective-permute-start | bytes 196616 | tf_op jit(solution)/shard_map/ppermute | solution.py:288
  7.8 18.8 %collective-permute-start.5 = (bf16[128,1536]{1,0:T(8,128)(2,1)S(1)}, bf16[128,1536]{1,0:T(8,128)(2,1)S(1)}, u32[]{:S(2)}, u32[]{:S(2)}) collective-permute-start(bf16[128,1536]{1,0:T(8,128)(2,1)S(1)} %constant_dynamic-update-slice_fusion.6.refs_0_), channel_id=1, source_target_pairs={{0,3},{1,0},{2,1},{3,2},{4,7},{5,4},{6,5},{7,6},{8,11},{9,8},{10,9... | collective-permute-start | bytes 1179656 | tf_op jit(solution)/shard_map/ppermute | solution.py:288
  10.6 17.3 %collective-permute-start.4 = (bf16[128,1536]{1,0:T(8,128)(2,1)S(1)}, bf16[128,1536]{1,0:T(8,128)(2,1)S(1)}, u32[]{:S(2)}, u32[]{:S(2)}) collective-permute-start(bf16[128,1536]{1,0:T(8,128)(2,1)S(1)} %constant_dynamic-update-slice_fusion.6.refs_0_), channel_id=1, source_target_pairs={{0,1},{1,2},{2,3},{3,0},{4,5},{5,6},{6,7},{7,4},{8,9},{9,10},{10,1... | collective-permute-start | bytes 1179656 | tf_op jit(solution)/shard_map/ppermute | solution.py:288
  11.3 8.5 %collective-permute-start.3 = (bf16[4,128,256]{2,1,0:T(8,128)(2,1)S(1)}, bf16[4,128,256]{2,1,0:T(8,128)(2,1)S(1)}, u32[]{:S(2)}, u32[]{:S(2)}) collective-permute-start(bf16[4,128,256]{2,1,0:T(8,128)(2,1)S(1)} %pad_maximum_fusion.refs_3_.refs_1_.refs_4_), channel_id=1, source_target_pairs={{0,16},{1,17},{2,18},{3,19},{4,20},{5,21},{6,22},{7,23},{8,40},{9,... | collective-permute-start | bytes 786440 | tf_op jit(solution)/shard_map/ppermute | solution.py:288
  13.5 17.9 %collective-permute-start.9 = (bf16[4,128,256]{2,1,0:T(8,128)(2,1)S(1)}, bf16[4,128,256]{2,1,0:T(8,128)(2,1)S(1)}, u32[]{:S(2)}, u32[]{:S(2)}) collective-permute-start(bf16[4,128,256]{2,1,0:T(8,128)(2,1)S(1)} %pad_maximum_fusion.refs_3_.refs_1_.refs_4_), channel_id=1, source_target_pairs={{0,8},{1,9},{2,10},{3,11},{4,12},{5,13},{6,14},{7,15},{8,0},{9,1},... | collective-permute-start | bytes 786440 | tf_op jit(solution)/shard_map/ppermute | solution.py:288
  13.6 12.4 %collective-permute-start.8 = (bf16[4,128,256]{2,1,0:T(8,128)(2,1)S(1)}, bf16[4,128,256]{2,1,0:T(8,128)(2,1)S(1)}, u32[]{:S(2)}, u32[]{:S(2)}) collective-permute-start(bf16[4,128,256]{2,1,0:T(8,128)(2,1)S(1)} %pad_maximum_fusion.refs_3_.refs_1_.refs_4_), channel_id=1, source_target_pairs={{0,4},{1,5},{2,6},{3,7},{4,0},{5,1},{6,2},{7,3},{8,72},{9,73},{10,... | collective-permute-start | bytes 786440 | tf_op jit(solution)/shard_map/ppermute | solution.py:288
  19.8 6.4 %collective-permute-start.7 = (bf16[4,128,256]{2,1,0:T(8,128)(2,1)S(1)}, bf16[4,128,256]{2,1,0:T(8,128)(2,1)S(1)}, u32[]{:S(2)}, u32[]{:S(2)}) collective-permute-start(bf16[4,128,256]{2,1,0:T(8,128)(2,1)S(1)} %pad_maximum_fusion.refs_3_.refs_1_.refs_4_), channel_id=1, source_target_pairs={{0,20},{1,21},{2,22},{3,23},{4,16},{5,17},{6,18},{7,19},{8,104},{9... | collective-permute-start | bytes 786440 | tf_op jit(solution)/shard_map/ppermute | solution.py:288
  26.0 5.4 %collective-permute-start.10 = (bf16[4,128,256]{2,1,0:T(8,128)(2,1)S(1)}, bf16[4,128,256]{2,1,0:T(8,128)(2,1)S(1)}, u32[]{:S(2)}, u32[]{:S(2)}) collective-permute-start(bf16[4,128,256]{2,1,0:T(8,128)(2,1)S(1)} %collective-permute-done.3.refs_4_.refs_2_.refs_5_), channel_id=1, source_target_pairs={{0,8},{1,9},{2,10},{3,11},{4,12},{5,13},{6,14},{7,15},{8,0},{9,1},... | collective-permute-start | bytes 786440 | tf_op jit(solution)/shard_map/ppermute | solution.py:288
  26.2 5.2 %collective-permute-start.12 = (bf16[4,128,256]{2,1,0:T(8,128)(2,1)S(1)}, bf16[4,128,256]{2,1,0:T(8,128)(2,1)S(1)}, u32[]{:S(2)}, u32[]{:S(2)}) collective-permute-start(bf16[4,128,256]{2,1,0:T(8,128)(2,1)S(1)} %collective-permute-done.8.refs_6_.refs_4_.refs_7_), channel_id=1, source_target_pairs={{0,8},{1,9},{2,10},{3,11},{4,12},{5,13},{6,14},{7,15},{8,0},{9,1},... | collective-permute-start | bytes 786440 | tf_op jit(solution)/shard_map/ppermute | solution.py:288
  26.6 4.8 %collective-permute-start.11 = (bf16[4,128,256]{2,1,0:T(8,128)(2,1)S(1)}, bf16[4,128,256]{2,1,0:T(8,128)(2,1)S(1)}, u32[]{:S(2)}, u32[]{:S(2)}) collective-permute-start(bf16[4,128,256]{2,1,0:T(8,128)(2,1)S(1)} %collective-permute-done.7.refs_5_.refs_3_.refs_6_), channel_id=1, source_target_pairs={{0,8},{1,9},{2,10},{3,11},{4,12},{5,13},{6,14},{7,15},{8,0},{9,1},... | collective-permute-start | bytes 786440 | tf_op jit(solution)/shard_map/ppermute | solution.py:288
  27.9 13.1 %collective-permute-start.6 = (bf16[128,1536]{1,0:T(8,128)(2,1)S(1)}, bf16[128,1536]{1,0:T(8,128)(2,1)S(1)}, u32[]{:S(2)}, u32[]{:S(2)}) collective-permute-start(bf16[128,1536]{1,0:T(8,128)(2,1)S(1)} %constant_dynamic-update-slice_fusion.6.refs_0_), channel_id=1, source_target_pairs={{0,2},{1,3},{2,0},{3,1},{4,6},{5,7},{6,4},{7,5},{8,10},{9,11},{10,... | collective-permute-start | bytes 1179656 | tf_op jit(solution)/shard_map/ppermute | solution.py:288
  45.5 4.2 %collective-permute-start.13 = (f32[2,24,128]{2,1,0:T(8,128)S(1)}, f32[2,24,128]{2,1,0:T(8,128)S(1)}, u32[]{:S(2)}, u32[]{:S(2)}) collective-permute-start(f32[2,24,128]{2,1,0:T(8,128)S(1)} %stats_far.1), channel_id=1, source_target_pairs={{0,1},{1,0},{2,3},{3,2},{4,5},{5,4},{6,7},{7,6},{8,9},{9,8},{10,11... | collective-permute-start | bytes 73736 | tf_op jit(solution)/shard_map/ppermute | solution.py:288
  49.7 5.4 %collective-permute-start.14 = (f32[2,24,128]{2,1,0:T(8,128)S(1)}, f32[2,24,128]{2,1,0:T(8,128)S(1)}, u32[]{:S(2)}, u32[]{:S(2)}) collective-permute-start(f32[2,24,128]{2,1,0:T(8,128)S(1)} %pad_maximum_fusion.1.st0), channel_id=1, source_target_pairs={{0,2},{1,3},{2,0},{3,1},{4,6},{5,7},{6,4},{7,5},{8,10},{9,11},{10,... | collective-permute-start | bytes 73736 | tf_op jit(solution)/shard_map/ppermute | solution.py:288
  82.5 10.6 %collective-permute-start.19 = (bf16[4,128,256]{2,1,0:T(8,128)(2,1)S(1)}, bf16[4,128,256]{2,1,0:T(8,128)(2,1)S(1)}, u32[]{:S(2)}, u32[]{:S(2)}) collective-permute-start(bf16[4,128,256]{2,1,0:T(8,128)(2,1)S(1)} %get-tuple-element.41), channel_id=1, source_target_pairs={{0,20},{1,21},{2,22},{3,23},{4,16},{5,17},{6,18},{7,19},{8,104},{9... | collective-permute-start | bytes 786440 | tf_op jit(solution)/shard_map/ppermute | solution.py:288
  86.4 8.8 %collective-permute-start.21 = (bf16[4,128,256]{2,1,0:T(8,128)(2,1)S(1)}, bf16[4,128,256]{2,1,0:T(8,128)(2,1)S(1)}, u32[]{:S(2)}, u32[]{:S(2)}) collective-permute-start(bf16[4,128,256]{2,1,0:T(8,128)(2,1)S(1)} %get-tuple-element.42), channel_id=1, source_target_pairs={{0,4},{1,5},{2,6},{3,7},{4,0},{5,1},{6,2},{7,3},{8,72},{9,73},{10,... | collective-permute-start | bytes 786440 | tf_op jit(solution)/shard_map/ppermute | solution.py:288
  86.4 10.4 %collective-permute-start.20 = (bf16[4,128,256]{2,1,0:T(8,128)(2,1)S(1)}, bf16[4,128,256]{2,1,0:T(8,128)(2,1)S(1)}, u32[]{:S(2)}, u32[]{:S(2)}) collective-permute-start(bf16[4,128,256]{2,1,0:T(8,128)(2,1)S(1)} %get-tuple-element.43), channel_id=1, source_target_pairs={{0,16},{1,17},{2,18},{3,19},{4,20},{5,21},{6,22},{7,23},{8,40},{9,... | collective-permute-start | bytes 786440 | tf_op jit(solution)/shard_map/ppermute | solution.py:288
  87.4 9.8 %collective-permute-start.15 = (bf16[128,768]{1,0:T(8,128)(2,1)S(1)}, bf16[128,768]{1,0:T(8,128)(2,1)S(1)}, u32[]{:S(2)}, u32[]{:S(2)}) collective-permute-start(bf16[128,768]{1,0:T(8,128)(2,1)S(1)} %get-tuple-element.23), channel_id=1, source_target_pairs={{0,3},{1,0},{2,1},{3,2},{4,7},{5,4},{6,5},{7,6},{8,11},{9,8},{10,9... | collective-permute-start | bytes 589832 | tf_op jit(solution)/shard_map/ppermute | solution.py:288
  88.8 10.3 %collective-permute-start.16 = (bf16[128,768]{1,0:T(8,128)(2,1)S(1)}, bf16[128,768]{1,0:T(8,128)(2,1)S(1)}, u32[]{:S(2)}, u32[]{:S(2)}) collective-permute-start(bf16[128,768]{1,0:T(8,128)(2,1)S(1)} %get-tuple-element.24), channel_id=1, source_target_pairs={{0,1},{1,2},{2,3},{3,0},{4,5},{5,6},{6,7},{7,4},{8,9},{9,10},{10,1... | collective-permute-start | bytes 589832 | tf_op jit(solution)/shard_map/ppermute | solution.py:288
  93.1 7.2 %collective-permute-start.17 = (bf16[128,768]{1,0:T(8,128)(2,1)S(1)}, bf16[128,768]{1,0:T(8,128)(2,1)S(1)}, u32[]{:S(2)}, u32[]{:S(2)}) collective-permute-start(bf16[128,768]{1,0:T(8,128)(2,1)S(1)} %get-tuple-element.25), channel_id=1, source_target_pairs={{0,2},{1,3},{2,0},{3,1},{4,6},{5,7},{6,4},{7,5},{8,10},{9,11},{10,... | collective-permute-start | bytes 589832 | tf_op jit(solution)/shard_map/ppermute | solution.py:288
  97.0 4.3 %collective-permute-start.22 = (bf16[128,256]{1,0:T(8,128)(2,1)S(1)}, bf16[128,256]{1,0:T(8,128)(2,1)S(1)}, u32[]{:S(2)}, u32[]{:S(2)}) collective-permute-start(bf16[128,256]{1,0:T(8,128)(2,1)S(1)} %get-tuple-element.44), channel_id=1, source_target_pairs={{0,96},{1,97},{2,98},{3,99},{4,100},{5,101},{6,102},{7,103},{8,28}... | collective-permute-start | bytes 196616 | tf_op jit(solution)/shard_map/ppermute | solution.py:288
  97.1 5.8 %collective-permute-start.24 = (bf16[128,256]{1,0:T(8,128)(2,1)S(1)}, bf16[128,256]{1,0:T(8,128)(2,1)S(1)}, u32[]{:S(2)}, u32[]{:S(2)}) collective-permute-start(bf16[128,256]{1,0:T(8,128)(2,1)S(1)} %get-tuple-element.45), channel_id=1, source_target_pairs={{0,64},{1,65},{2,66},{3,67},{4,68},{5,69},{6,70},{7,71},{8,12},{9,... | collective-permute-start | bytes 196616 | tf_op jit(solution)/shard_map/ppermute | solution.py:288
  97.2 6.8 %collective-permute-start.23 = (bf16[128,256]{1,0:T(8,128)(2,1)S(1)}, bf16[128,256]{1,0:T(8,128)(2,1)S(1)}, u32[]{:S(2)}, u32[]{:S(2)}) collective-permute-start(bf16[128,256]{1,0:T(8,128)(2,1)S(1)} %get-tuple-element.46), channel_id=1, source_target_pairs={{0,32},{1,33},{2,34},{3,35},{4,36},{5,37},{6,38},{7,39},{8,24},{9,... | collective-permute-start | bytes 196616 | tf_op jit(solution)/shard_map/ppermute | solution.py:288
  (4 other events, 18.2 us)

commit v8 on v7

--- a/solution.py
+++ b/solution.py
@@ -253,7 +253,7 @@
         out_specs=VM,
         scratch_shapes=COPIES + [pltpu.VMEM((3 * n + 1, 8, R), jnp.float32)] * 3,
         compiler_params=PARAMS,
-        cost_estimate=pl.CostEstimate(flops=n * 1_600_000_000, bytes_accessed=4_000_000, transcendentals=0),
+        cost_estimate=pl.CostEstimate(flops=n * 1_000_000, bytes_accessed=100_000, transcendentals=0),
         name="stats_near" if which == NEAR else "stats_far",
     )(meta, lim, *qds, *kvs, *before)
 
@@ -308,15 +308,17 @@
     i32 = jnp.int32
     y, zl, core, zh, x = (lax.axis_index(a) for a in AXES)
     z = 2 * zh + zl
-    grid = span_slot.reshape(*SIZES, 2)
-    own_x = jnp.transpose(lax.dynamic_index_in_dim(grid, x, 4, keepdims=False), (2, 0, 3, 1, 4))
-    own_x = own_x.reshape(2, 4, 4, 2)
-    by_y = jnp.stack([lax.dynamic_index_in_dim(own_x, (y - r) % 4, 1, keepdims=False) for r in STEPS], 1)
-    by_yz = jnp.stack([lax.dynamic_index_in_dim(by_y, (z - r) % 4, 2, keepdims=False) for r in STEPS], 2)
-    of_core = jnp.stack([jnp.transpose(by_yz[0], (1, 0, 2)), by_yz[1]])
-    arrived = jnp.where(core == 0, of_core, of_core[::-1]).reshape(64)
-    ring = grid[y, zl, core, zh]
-    queries = jnp.concatenate([ring[(x - r) % 4] for r in STEPS])
+    i = jnp.arange(72, dtype=i32)
+    is_key = i < 64
+    low, high = (i // 2) % 4, (i // 8) % 4
+    low, high = low ^ (low >> 1), high ^ (high >> 1)
+    at_core = jnp.where(is_key & (i >= 32), 1 - core, core)
+    at_y = jnp.where(is_key, (y - jnp.where(at_core == 0, low, high)) % 4, y)
+    at_z = jnp.where(is_key, (z - jnp.where(at_core == 0, high, low)) % 4, z)
+    at_x = jnp.where(is_key, x, (x - low) % 4)
+    slot = ((((at_y * 2 + at_z % 2) * 2 + at_core) * 2 + at_z // 2) * 4 + at_x) * 2 + i % 2
+    spans = jnp.sum(jnp.where(slot[:, None] == jnp.arange(256)[None, :], span_slot[None, :], 0), axis=1)
+    arrived, queries = spans[:64], spans[64:]
 
     def rank(a, among):
         return jnp.sum((among[None, :] < a[:, None]).astype(i32), axis=1)
@@ -365,7 +367,7 @@
     near = [qd, x_shift(qd, 1), x_shift(qd, 3)]
     near[1], near[2], later = lax.optimization_barrier((near[1], near[2], qd))
     far = x_shift(later, 2)
-    kvs[1], span_slot = lax.optimization_barrier((kvs[1], span_slot))
+    kvs[0], kvs[1], span_slot = lax.optimization_barrier((kvs[0], kvs[1], span_slot))
     meta, lim = plan(span_slot)
     kvs = kvs + [core_swap(a) for a in kvs]
     arrays = near + [far] + kvs
@@ -384,11 +386,13 @@
             out = out + part.astype(jnp.float32)
         return out
 
-    dq = total(dqs[0], *[x_shift(a, -r) for r, a in zip(STEPS[1:], dqs[1:])])
     other = core_swap(dkv_other)
     pairs = [total(a, other[i]).astype(jnp.bfloat16) for i, a in enumerate(dkv)]
     some = total(pairs[0], *[second_shift(a, -r) for r, a in zip(STEPS[1:], pairs[1:])])
+    back = [x_shift(dqs[1], -1), x_shift(dqs[2], -3)]
+    some, back[0], back[1], last = lax.optimization_barrier((some, back[0], back[1], dqs[3]))
     sent = [first_shift(some[i].astype(jnp.bfloat16), -r) for i, r in ((1, 1), (2, 3), (3, 2))]
+    dq = total(dqs[0], *back, x_shift(last, -2))
     summed = total(some[0], *sent)
     return (
         dq.astype(jnp.bfloat16),

time: 105 us -> 106 us (level)
  waiting for transfers between devices: 20.9 us -> 24.1 us
  starting transfers between devices: 36.2 us -> 34.7 us
    ppermute x25, waiting for transfers between devices: 20.9 us -> 24.1 us  [permute(): return lax.ppermute(a, AXES, pairs)]
    ppermute x25, starting transfers between devices: 36.2 us -> 34.7 us  [permute(): return lax.ppermute(a, AXES, pairs)]
  transfers between devices with their start and end apart: 25 -> 25, of which waited for: 13 -> 14; matrix products, arithmetic and copies ran while one was open for 6% -> 6% of each run, Pallas kernels for 9% -> 8%
where the time goes in v8:
time: 106 us; the launch traced here: 107 us
  Pallas kernels  38.4 us (36%)
  starting transfers between devices  34.7 us (33%)
  waiting for transfers between devices  24.1 us (23%)
  other arithmetic  4.66 us (4%)
  local copies, waits for them, and re-layouts  3.75 us (4%)
    ppermute x25, starting transfers between devices, permute(): return lax.ppermute(a, AXES, pairs)  34.7 us
    pallas_call x1, Pallas kernels, grads(): pl.pallas_call(grads_kernel, out_shape=dq + dkv, in_specs=[SM] + [VM] * 1...  24.6 us
    ppermute x25, waiting for transfers between devices, permute(): return lax.ppermute(a, AXES, pairs)  24.1 us
    pallas_call x2, Pallas kernels, stats(): pl.pallas_call(functools.partial(stats_kernel, which, n), out_shape=jax.S...  13.8 us
  transfers between devices with their start and end apart: 25, of which 14 were waited for; matrix products, arithmetic and copies ran while one was open for 6% of the time, Pallas kernels for 8%

profile of v8, /device:TPU:0, one launch (start us, length us, event | category | flops | bytes accessed | tf_op | source)
XLA Modules:
  0.0 106.5 jit_solution(14425310364045468171)
XLA Ops:
  1.4 3.4 %collective-permute-start.2 = (bf16[1,128,256]{2,1,0:T(8,128)(2,1)S(1)}, bf16[1,128,256]{2,1,0:T(8,128)(2,1)S(1)}, u32[]{:S(2)}, u32[]{:S(2)}) collective-permute-start(bf16[1,128,256]{2,1,0:T(8,128)(2,1)S(1)} %maximum_bitcast_fusion), channel_id=1, source_target_pairs={{0,64},{1,65},{2,66},{3,67},{4,68},{5,69},{6,70},{7,71},{8,12},{9,... | collective-permute-start | bytes 196616 | tf_op jit(solution)/shard_map/ppermute | solution.py:288
  7.8 2.8 %collective-permute-start.5 = (bf16[128,1536]{1,0:T(8,128)(2,1)S(1)}, bf16[128,1536]{1,0:T(8,128)(2,1)S(1)}, u32[]{:S(2)}, u32[]{:S(2)}) collective-permute-start(bf16[128,1536]{1,0:T(8,128)(2,1)S(1)} %constant_dynamic-update-slice_fusion.6.refs_0_), channel_id=1, source_target_pairs={{0,3},{1,0},{2,1},{3,2},{4,7},{5,4},{6,5},{7,6},{8,11},{9,8},{10,9... | collective-permute-start | bytes 1179656 | tf_op jit(solution)/shard_map/ppermute | solution.py:288
  11.3 2.0 %collective-permute-start.3 = (bf16[4,128,256]{2,1,0:T(8,128)(2,1)S(1)}, bf16[4,128,256]{2,1,0:T(8,128)(2,1)S(1)}, u32[]{:S(2)}, u32[]{:S(2)}) collective-permute-start(bf16[4,128,256]{2,1,0:T(8,128)(2,1)S(1)} %pad_maximum_fusion.refs_3_.refs_1_.refs_4_), channel_id=1, source_target_pairs={{0,16},{1,17},{2,18},{3,19},{4,20},{5,21},{6,22},{7,23},{8,40},{9,... | collective-permute-start | bytes 786440 | tf_op jit(solution)/shard_map/ppermute | solution.py:288
  13.6 3.7 %collective-permute-start.8 = (bf16[4,128,256]{2,1,0:T(8,128)(2,1)S(1)}, bf16[4,128,256]{2,1,0:T(8,128)(2,1)S(1)}, u32[]{:S(2)}, u32[]{:S(2)}) collective-permute-start(bf16[4,128,256]{2,1,0:T(8,128)(2,1)S(1)} %pad_maximum_fusion.refs_3_.refs_1_.refs_4_), channel_id=1, source_target_pairs={{0,4},{1,5},{2,6},{3,7},{4,0},{5,1},{6,2},{7,3},{8,72},{9,73},{10,... | collective-permute-start | bytes 786440 | tf_op jit(solution)/shard_map/ppermute | solution.py:288
  18.2 1.6 %collective-permute-done.3.refs_4_.refs_2_.refs_5_ = bf16[4,128,256]{2,1,0:T(8,128)(2,1)S(1)} collective-permute-done((bf16[4,128,256]{2,1,0:T(8,128)(2,1)S(1)}, bf16[4,128,256]{2,1,0:T(8,128)(2,1)S(1)}, u32[]{:S(2)}, u32[]{:S(2)}) %collective-permute-start.3) | collective-permute-done | bytes 262176 | tf_op jit(solution)/shard_map/ppermute | solution.py:288
  24.7 3.4 %collective-permute-start.6 = (bf16[128,1536]{1,0:T(8,128)(2,1)S(1)}, bf16[128,1536]{1,0:T(8,128)(2,1)}, u32[]{:S(2)}, u32[]{:S(2)}) collective-permute-start(bf16[128,1536]{1,0:T(8,128)(2,1)S(1)} %constant_dynamic-update-slice_fusion.6.refs_0_), channel_id=1, source_target_pairs={{0,2},{1,3},{2,0},{3,1},{4,6},{5,7},{6,4},{7,5},{8,10},{9,11},{10,... | collective-permute-start | bytes 1179656 | tf_op jit(solution)/shard_map/ppermute | solution.py:288
  29.4 8.9 %stats_near.1.refs_9_ = f32[2,24,128]{2,1,0:T(8,128)S(1)} custom-call(s32[982]{0:T(1024)S(1)} %pad_add_fusion.2.meta, s32[3,16,256]{2,1,0:T(8,128)S(1)} %concatenate.34.lim, bf16[128,1536]{1,0:T(8,128)(2,1)S(1)} %constant_dynamic-update-slice_fusion.6.refs_0_, bf16[128,1536]{1,0:T(8,128)(2,1)S(1)} %collective-permute-done.4.refs_1_, ...), custom_call_target="tpu_custom_call" | custom-call | flops 3000000 | bytes 100000 | tf_op jit(solution)/shard_map/stats_near/pallas_call | solution.py:249
  38.3 4.8 %stats_far.1 = f32[2,24,128]{2,1,0:T(8,128)S(1)} custom-call(s32[982]{0:T(1024)S(1)} %pad_add_fusion.2.meta, s32[3,16,256]{2,1,0:T(8,128)S(1)} %concatenate.34.lim, bf16[128,1536]{1,0:T(8,128)(2,1)} %collective-permute-done.6.refs_0_.refs_3_, bf16[4,128,256]{2,1,0:T(8,128)(2,1)S(1)} %pad_maximum_fusion.refs_3_.refs_1_.refs_4_, ...), custom_call_target="tpu_custom_call" | custom-call | flops 1000000 | bytes 100000 | tf_op jit(solution)/shard_map/stats_far/pallas_call | solution.py:249
  43.1 1.4 %collective-permute-start.13 = (f32[2,24,128]{2,1,0:T(8,128)S(1)}, f32[2,24,128]{2,1,0:T(8,128)S(1)}, u32[]{:S(2)}, u32[]{:S(2)}) collective-permute-start(f32[2,24,128]{2,1,0:T(8,128)S(1)} %stats_far.1), channel_id=1, source_target_pairs={{0,1},{1,0},{2,3},{3,2},{4,5},{5,4},{6,7},{7,6},{8,9},{9,8},{10,11... | collective-permute-start | bytes 73736 | tf_op jit(solution)/shard_map/ppermute | solution.py:288
  44.5 2.5 %collective-permute-done.13 = f32[2,24,128]{2,1,0:T(8,128)S(1)} collective-permute-done((f32[2,24,128]{2,1,0:T(8,128)S(1)}, f32[2,24,128]{2,1,0:T(8,128)S(1)}, u32[]{:S(2)}, u32[]{:S(2)}) %collective-permute-start.13) | collective-permute-done | bytes 24608 | tf_op jit(solution)/shard_map/ppermute | solution.py:288
  47.1 3.1 %collective-permute-start.14 = (f32[2,24,128]{2,1,0:T(8,128)S(1)}, f32[2,24,128]{2,1,0:T(8,128)S(1)}, u32[]{:S(2)}, u32[]{:S(2)}) collective-permute-start(f32[2,24,128]{2,1,0:T(8,128)S(1)} %pad_maximum_fusion.1.st0), channel_id=1, source_target_pairs={{0,2},{1,3},{2,0},{3,1},{4,6},{5,7},{6,4},{7,5},{8,10},{9,11},{10,... | collective-permute-start | bytes 73736 | tf_op jit(solution)/shard_map/ppermute | solution.py:288
  50.2 2.5 %collective-permute-done.14.st1 = f32[2,24,128]{2,1,0:T(8,128)S(1)} collective-permute-done((f32[2,24,128]{2,1,0:T(8,128)S(1)}, f32[2,24,128]{2,1,0:T(8,128)S(1)}, u32[]{:S(2)}, u32[]{:S(2)}) %collective-permute-start.14) | collective-permute-done | bytes 24608 | tf_op jit(solution)/shard_map/ppermute | solution.py:288
  52.7 24.6 %grads.1 = (f32[128,768]{1,0:T(8,128)S(1)}, bf16[128,768]{1,0:T(8,128)(2,1)S(1)}, bf16[128,768]{1,0:T(8,128)(2,1)S(1)}, bf16[128,768]{1,0:T(8,128)(2,1)S(1)}, bf...) custom-call(s32[982]{0:T(1024)S(1)} %pad_add_fusion.2.meta, ...), custom_call_target="tpu_custom_call" | custom-call | tf_op jit(solution)/shard_map/grads/pallas_call | solution.py:265
  77.3 2.9 %collective-permute-done.15 = bf16[4,4,128,256]{3,2,1,0:T(8,128)(2,1)S(1)} collective-permute-done((bf16[4,4,128,256]{3,2,1,0:T(8,128)(2,1)}, bf16[4,4,128,256]{3,2,1,0:T(8,128)(2,1)S(1)}, u32[]{:S(2)}, u32[]{:S(2)}) %collective-permute-start.15) | collective-permute-done | bytes 1048608 | tf_op jit(solution)/shard_map/ppermute | solution.py:288
  80.4 2.2 %collective-permute-start.16 = (bf16[4,128,256]{2,1,0:T(8,128)(2,1)S(1)}, bf16[4,128,256]{2,1,0:T(8,128)(2,1)S(1)}, u32[]{:S(2)}, u32[]{:S(2)}) collective-permute-start(bf16[4,128,256]{2,1,0:T(8,128)(2,1)S(1)} %get-tuple-element.49), channel_id=1, source_target_pairs={{0,20},{1,21},{2,22},{3,23},{4,16},{5,17},{6,18},{7,19},{8,104},{9... | collective-permute-start | bytes 786440 | tf_op jit(solution)/shard_map/ppermute | solution.py:288
  84.2 3.6 %collective-permute-start.19 = (bf16[128,768]{1,0:T(8,128)(2,1)S(1)}, bf16[128,768]{1,0:T(8,128)(2,1)S(1)}, u32[]{:S(2)}, u32[]{:S(2)}) collective-permute-start(bf16[128,768]{1,0:T(8,128)(2,1)S(1)} %get-tuple-element.34), channel_id=1, source_target_pairs={{0,3},{1,0},{2,1},{3,2},{4,7},{5,4},{6,5},{7,6},{8,11},{9,8},{10,9... | collective-permute-start | bytes 589832 | tf_op jit(solution)/shard_map/ppermute | solution.py:288
  87.9 1.5 %collective-permute-done.16 = bf16[4,128,256]{2,1,0:T(8,128)(2,1)S(1)} collective-permute-done((bf16[4,128,256]{2,1,0:T(8,128)(2,1)S(1)}, bf16[4,128,256]{2,1,0:T(8,128)(2,1)S(1)}, u32[]{:S(2)}, u32[]{:S(2)}) %collective-permute-start.16) | collective-permute-done | bytes 262176 | tf_op jit(solution)/shard_map/ppermute | solution.py:288
  89.4 1.2 %collective-permute-done.18 = bf16[4,128,256]{2,1,0:T(8,128)(2,1)S(1)} collective-permute-done((bf16[4,128,256]{2,1,0:T(8,128)(2,1)S(1)}, bf16[4,128,256]{2,1,0:T(8,128)(2,1)S(1)}, u32[]{:S(2)}, u32[]{:S(2)}) %collective-permute-start.18) | collective-permute-done | bytes 262176 | tf_op jit(solution)/shard_map/ppermute | solution.py:288
  90.6 2.7 %collective-permute-done.17 = bf16[4,128,256]{2,1,0:T(8,128)(2,1)S(1)} collective-permute-done((bf16[4,128,256]{2,1,0:T(8,128)(2,1)S(1)}, bf16[4,128,256]{2,1,0:T(8,128)(2,1)S(1)}, u32[]{:S(2)}, u32[]{:S(2)}) %collective-permute-start.17) | collective-permute-done | bytes 262176 | tf_op jit(solution)/shard_map/ppermute | solution.py:288
  93.5 1.2 %collective-permute-done.20 = bf16[128,768]{1,0:T(8,128)(2,1)S(1)} collective-permute-done((bf16[128,768]{1,0:T(8,128)(2,1)S(1)}, bf16[128,768]{1,0:T(8,128)(2,1)S(1)}, u32[]{:S(2)}, u32[]{:S(2)}) %collective-permute-start.20) | collective-permute-done | bytes 196640 | tf_op jit(solution)/shard_map/ppermute | solution.py:288
  94.8 2.1 %collective-permute-start.22 = (bf16[128,256]{1,0:T(8,128)(2,1)S(1)}, bf16[128,256]{1,0:T(8,128)(2,1)S(1)}, u32[]{:S(2)}, u32[]{:S(2)}) collective-permute-start(bf16[128,256]{1,0:T(8,128)(2,1)S(1)} %get-tuple-element.52), channel_id=1, source_target_pairs={{0,96},{1,97},{2,98},{3,99},{4,100},{5,101},{6,102},{7,103},{8,28}... | collective-permute-start | bytes 196616 | tf_op jit(solution)/shard_map/ppermute | solution.py:288
  97.2 1.3 %collective-permute-start.23 = (bf16[128,256]{1,0:T(8,128)(2,1)S(1)}, bf16[128,256]{1,0:T(8,128)(2,1)S(1)}, u32[]{:S(2)}, u32[]{:S(2)}) collective-permute-start(bf16[128,256]{1,0:T(8,128)(2,1)S(1)} %get-tuple-element.54), channel_id=1, source_target_pairs={{0,32},{1,33},{2,34},{3,35},{4,36},{5,37},{6,38},{7,39},{8,24},{9,... | collective-permute-start | bytes 196616 | tf_op jit(solution)/shard_map/ppermute | solution.py:288
  99.1 3.6 %collective-permute-done.24 = bf16[128,256]{1,0:T(8,128)(2,1)S(1)} collective-permute-done((bf16[128,256]{1,0:T(8,128)(2,1)S(1)}, bf16[128,256]{1,0:T(8,128)(2,1)S(1)}, u32[]{:S(2)}, u32[]{:S(2)}) %collective-permute-start.24) | collective-permute-done | bytes 65568 | tf_op jit(solution)/shard_map/ppermute | solution.py:288
  104.0 1.7 %collective-permute-done.21 = bf16[128,768]{1,0:T(8,128)(2,1)S(1)} collective-permute-done((bf16[128,768]{1,0:T(8,128)(2,1)S(1)}, bf16[128,768]{1,0:T(8,128)(2,1)S(1)}, u32[]{:S(2)}, u32[]{:S(2)}) %collective-permute-start.21) | collective-permute-done | bytes 196640 | tf_op jit(solution)/shard_map/ppermute | solution.py:288
  (106 shorter events, 16.8 us)
Async XLA Ops:
  1.4 9.2 %collective-permute-start.2 = (bf16[1,128,256]{2,1,0:T(8,128)(2,1)S(1)}, bf16[1,128,256]{2,1,0:T(8,128)(2,1)S(1)}, u32[]{:S(2)}, u32[]{:S(2)}) collective-permute-start(bf16[1,128,256]{2,1,0:T(8,128)(2,1)S(1)} %maximum_bitcast_fusion), channel_id=1, source_target_pairs={{0,64},{1,65},{2,66},{3,67},{4,68},{5,69},{6,70},{7,71},{8,12},{9,... | collective-permute-start | bytes 196616 | tf_op jit(solution)/shard_map/ppermute | solution.py:288
  4.8 5.8 %collective-permute-start.1 = (bf16[1,128,256]{2,1,0:T(8,128)(2,1)S(1)}, bf16[1,128,256]{2,1,0:T(8,128)(2,1)S(1)}, u32[]{:S(2)}, u32[]{:S(2)}) collective-permute-start(bf16[1,128,256]{2,1,0:T(8,128)(2,1)S(1)} %maximum_bitcast_fusion), channel_id=1, source_target_pairs={{0,96},{1,97},{2,98},{3,99},{4,100},{5,101},{6,102},{7,103},{8,28}... | collective-permute-start | bytes 196616 | tf_op jit(solution)/shard_map/ppermute | solution.py:288
  5.8 5.5 %collective-permute-start = (bf16[1,128,256]{2,1,0:T(8,128)(2,1)S(1)}, bf16[1,128,256]{2,1,0:T(8,128)(2,1)S(1)}, u32[]{:S(2)}, u32[]{:S(2)}) collective-permute-start(bf16[1,128,256]{2,1,0:T(8,128)(2,1)S(1)} %maximum_bitcast_fusion), channel_id=1, source_target_pairs={{0,32},{1,33},{2,34},{3,35},{4,36},{5,37},{6,38},{7,39},{8,24},{9,... | collective-permute-start | bytes 196616 | tf_op jit(solution)/shard_map/ppermute | solution.py:288
  7.8 16.8 %collective-permute-start.5 = (bf16[128,1536]{1,0:T(8,128)(2,1)S(1)}, bf16[128,1536]{1,0:T(8,128)(2,1)S(1)}, u32[]{:S(2)}, u32[]{:S(2)}) collective-permute-start(bf16[128,1536]{1,0:T(8,128)(2,1)S(1)} %constant_dynamic-update-slice_fusion.6.refs_0_), channel_id=1, source_target_pairs={{0,3},{1,0},{2,1},{3,2},{4,7},{5,4},{6,5},{7,6},{8,11},{9,8},{10,9... | collective-permute-start | bytes 1179656 | tf_op jit(solution)/shard_map/ppermute | solution.py:288
  10.6 14.1 %collective-permute-start.4 = (bf16[128,1536]{1,0:T(8,128)(2,1)S(1)}, bf16[128,1536]{1,0:T(8,128)(2,1)S(1)}, u32[]{:S(2)}, u32[]{:S(2)}) collective-permute-start(bf16[128,1536]{1,0:T(8,128)(2,1)S(1)} %constant_dynamic-update-slice_fusion.6.refs_0_), channel_id=1, source_target_pairs={{0,1},{1,2},{2,3},{3,0},{4,5},{5,6},{6,7},{7,4},{8,9},{9,10},{10,1... | collective-permute-start | bytes 1179656 | tf_op jit(solution)/shard_map/ppermute | solution.py:288
  11.3 8.5 %collective-permute-start.3 = (bf16[4,128,256]{2,1,0:T(8,128)(2,1)S(1)}, bf16[4,128,256]{2,1,0:T(8,128)(2,1)S(1)}, u32[]{:S(2)}, u32[]{:S(2)}) collective-permute-start(bf16[4,128,256]{2,1,0:T(8,128)(2,1)S(1)} %pad_maximum_fusion.refs_3_.refs_1_.refs_4_), channel_id=1, source_target_pairs={{0,16},{1,17},{2,18},{3,19},{4,20},{5,21},{6,22},{7,23},{8,40},{9,... | collective-permute-start | bytes 786440 | tf_op jit(solution)/shard_map/ppermute | solution.py:288
  13.6 10.5 %collective-permute-start.8 = (bf16[4,128,256]{2,1,0:T(8,128)(2,1)S(1)}, bf16[4,128,256]{2,1,0:T(8,128)(2,1)S(1)}, u32[]{:S(2)}, u32[]{:S(2)}) collective-permute-start(bf16[4,128,256]{2,1,0:T(8,128)(2,1)S(1)} %pad_maximum_fusion.refs_3_.refs_1_.refs_4_), channel_id=1, source_target_pairs={{0,4},{1,5},{2,6},{3,7},{4,0},{5,1},{6,2},{7,3},{8,72},{9,73},{10,... | collective-permute-start | bytes 786440 | tf_op jit(solution)/shard_map/ppermute | solution.py:288
  17.2 6.9 %collective-permute-start.7 = (bf16[4,128,256]{2,1,0:T(8,128)(2,1)S(1)}, bf16[4,128,256]{2,1,0:T(8,128)(2,1)S(1)}, u32[]{:S(2)}, u32[]{:S(2)}) collective-permute-start(bf16[4,128,256]{2,1,0:T(8,128)(2,1)S(1)} %pad_maximum_fusion.refs_3_.refs_1_.refs_4_), channel_id=1, source_target_pairs={{0,20},{1,21},{2,22},{3,23},{4,16},{5,17},{6,18},{7,19},{8,104},{9... | collective-permute-start | bytes 786440 | tf_op jit(solution)/shard_map/ppermute | solution.py:288
  23.1 6.2 %collective-permute-start.9 = (bf16[4,128,256]{2,1,0:T(8,128)(2,1)S(1)}, bf16[4,128,256]{2,1,0:T(8,128)(2,1)S(1)}, u32[]{:S(2)}, u32[]{:S(2)}) collective-permute-start(bf16[4,128,256]{2,1,0:T(8,128)(2,1)S(1)} %pad_maximum_fusion.refs_3_.refs_1_.refs_4_), channel_id=1, source_target_pairs={{0,8},{1,9},{2,10},{3,11},{4,12},{5,13},{6,14},{7,15},{8,0},{9,1},... | collective-permute-start | bytes 786440 | tf_op jit(solution)/shard_map/ppermute | solution.py:288
  24.1 5.3 %collective-permute-start.10 = (bf16[4,128,256]{2,1,0:T(8,128)(2,1)S(1)}, bf16[4,128,256]{2,1,0:T(8,128)(2,1)S(1)}, u32[]{:S(2)}, u32[]{:S(2)}) collective-permute-start(bf16[4,128,256]{2,1,0:T(8,128)(2,1)S(1)} %collective-permute-done.3.refs_4_.refs_2_.refs_5_), channel_id=1, source_target_pairs={{0,8},{1,9},{2,10},{3,11},{4,12},{5,13},{6,14},{7,15},{8,0},{9,1},... | collective-permute-start | bytes 786440 | tf_op jit(solution)/shard_map/ppermute | solution.py:288
  24.1 5.2 %collective-permute-start.12 = (bf16[4,128,256]{2,1,0:T(8,128)(2,1)S(1)}, bf16[4,128,256]{2,1,0:T(8,128)(2,1)S(1)}, u32[]{:S(2)}, u32[]{:S(2)}) collective-permute-start(bf16[4,128,256]{2,1,0:T(8,128)(2,1)S(1)} %collective-permute-done.8.refs_6_.refs_4_.refs_7_), channel_id=1, source_target_pairs={{0,8},{1,9},{2,10},{3,11},{4,12},{5,13},{6,14},{7,15},{8,0},{9,1},... | collective-permute-start | bytes 786440 | tf_op jit(solution)/shard_map/ppermute | solution.py:288
  24.6 4.7 %collective-permute-start.11 = (bf16[4,128,256]{2,1,0:T(8,128)(2,1)S(1)}, bf16[4,128,256]{2,1,0:T(8,128)(2,1)S(1)}, u32[]{:S(2)}, u32[]{:S(2)}) collective-permute-start(bf16[4,128,256]{2,1,0:T(8,128)(2,1)S(1)} %collective-permute-done.7.refs_5_.refs_3_.refs_6_), channel_id=1, source_target_pairs={{0,8},{1,9},{2,10},{3,11},{4,12},{5,13},{6,14},{7,15},{8,0},{9,1},... | collective-permute-start | bytes 786440 | tf_op jit(solution)/shard_map/ppermute | solution.py:288
  24.7 13.6 %collective-permute-start.6 = (bf16[128,1536]{1,0:T(8,128)(2,1)S(1)}, bf16[128,1536]{1,0:T(8,128)(2,1)}, u32[]{:S(2)}, u32[]{:S(2)}) collective-permute-start(bf16[128,1536]{1,0:T(8,128)(2,1)S(1)} %constant_dynamic-update-slice_fusion.6.refs_0_), channel_id=1, source_target_pairs={{0,2},{1,3},{2,0},{3,1},{4,6},{5,7},{6,4},{7,5},{8,10},{9,11},{10,... | collective-permute-start | bytes 1179656 | tf_op jit(solution)/shard_map/ppermute | solution.py:288
  43.1 3.9 %collective-permute-start.13 = (f32[2,24,128]{2,1,0:T(8,128)S(1)}, f32[2,24,128]{2,1,0:T(8,128)S(1)}, u32[]{:S(2)}, u32[]{:S(2)}) collective-permute-start(f32[2,24,128]{2,1,0:T(8,128)S(1)} %stats_far.1), channel_id=1, source_target_pairs={{0,1},{1,0},{2,3},{3,2},{4,5},{5,4},{6,7},{7,6},{8,9},{9,8},{10,11... | collective-permute-start | bytes 73736 | tf_op jit(solution)/shard_map/ppermute | solution.py:288
  47.1 5.6 %collective-permute-start.14 = (f32[2,24,128]{2,1,0:T(8,128)S(1)}, f32[2,24,128]{2,1,0:T(8,128)S(1)}, u32[]{:S(2)}, u32[]{:S(2)}) collective-permute-start(f32[2,24,128]{2,1,0:T(8,128)S(1)} %pad_maximum_fusion.1.st0), channel_id=1, source_target_pairs={{0,2},{1,3},{2,0},{3,1},{4,6},{5,7},{6,4},{7,5},{8,10},{9,11},{10,... | collective-permute-start | bytes 73736 | tf_op jit(solution)/shard_map/ppermute | solution.py:288
  80.4 9.0 %collective-permute-start.16 = (bf16[4,128,256]{2,1,0:T(8,128)(2,1)S(1)}, bf16[4,128,256]{2,1,0:T(8,128)(2,1)S(1)}, u32[]{:S(2)}, u32[]{:S(2)}) collective-permute-start(bf16[4,128,256]{2,1,0:T(8,128)(2,1)S(1)} %get-tuple-element.49), channel_id=1, source_target_pairs={{0,20},{1,21},{2,22},{3,23},{4,16},{5,17},{6,18},{7,19},{8,104},{9... | collective-permute-start | bytes 786440 | tf_op jit(solution)/shard_map/ppermute | solution.py:288
  82.6 8.0 %collective-permute-start.18 = (bf16[4,128,256]{2,1,0:T(8,128)(2,1)S(1)}, bf16[4,128,256]{2,1,0:T(8,128)(2,1)S(1)}, u32[]{:S(2)}, u32[]{:S(2)}) collective-permute-start(bf16[4,128,256]{2,1,0:T(8,128)(2,1)S(1)} %get-tuple-element.50), channel_id=1, source_target_pairs={{0,4},{1,5},{2,6},{3,7},{4,0},{5,1},{6,2},{7,3},{8,72},{9,73},{10,... | collective-permute-start | bytes 786440 | tf_op jit(solution)/shard_map/ppermute | solution.py:288
  83.0 10.3 %collective-permute-start.17 = (bf16[4,128,256]{2,1,0:T(8,128)(2,1)S(1)}, bf16[4,128,256]{2,1,0:T(8,128)(2,1)S(1)}, u32[]{:S(2)}, u32[]{:S(2)}) collective-permute-start(bf16[4,128,256]{2,1,0:T(8,128)(2,1)S(1)} %get-tuple-element.51), channel_id=1, source_target_pairs={{0,16},{1,17},{2,18},{3,19},{4,20},{5,21},{6,22},{7,23},{8,40},{9,... | collective-permute-start | bytes 786440 | tf_op jit(solution)/shard_map/ppermute | solution.py:288
  84.2 9.3 %collective-permute-start.19 = (bf16[128,768]{1,0:T(8,128)(2,1)S(1)}, bf16[128,768]{1,0:T(8,128)(2,1)S(1)}, u32[]{:S(2)}, u32[]{:S(2)}) collective-permute-start(bf16[128,768]{1,0:T(8,128)(2,1)S(1)} %get-tuple-element.34), channel_id=1, source_target_pairs={{0,3},{1,0},{2,1},{3,2},{4,7},{5,4},{6,5},{7,6},{8,11},{9,8},{10,9... | collective-permute-start | bytes 589832 | tf_op jit(solution)/shard_map/ppermute | solution.py:288
  87.9 6.9 %collective-permute-start.20 = (bf16[128,768]{1,0:T(8,128)(2,1)S(1)}, bf16[128,768]{1,0:T(8,128)(2,1)S(1)}, u32[]{:S(2)}, u32[]{:S(2)}) collective-permute-start(bf16[128,768]{1,0:T(8,128)(2,1)S(1)} %get-tuple-element.35), channel_id=1, source_target_pairs={{0,1},{1,2},{2,3},{3,0},{4,5},{5,6},{6,7},{7,4},{8,9},{9,10},{10,1... | collective-permute-start | bytes 589832 | tf_op jit(solution)/shard_map/ppermute | solution.py:288
  94.8 4.3 %collective-permute-start.22 = (bf16[128,256]{1,0:T(8,128)(2,1)S(1)}, bf16[128,256]{1,0:T(8,128)(2,1)S(1)}, u32[]{:S(2)}, u32[]{:S(2)}) collective-permute-start(bf16[128,256]{1,0:T(8,128)(2,1)S(1)} %get-tuple-element.52), channel_id=1, source_target_pairs={{0,96},{1,97},{2,98},{3,99},{4,100},{5,101},{6,102},{7,103},{8,28}... | collective-permute-start | bytes 196616 | tf_op jit(solution)/shard_map/ppermute | solution.py:288
  96.9 5.8 %collective-permute-start.24 = (bf16[128,256]{1,0:T(8,128)(2,1)S(1)}, bf16[128,256]{1,0:T(8,128)(2,1)S(1)}, u32[]{:S(2)}, u32[]{:S(2)}) collective-permute-start(bf16[128,256]{1,0:T(8,128)(2,1)S(1)} %get-tuple-element.53), channel_id=1, source_target_pairs={{0,64},{1,65},{2,66},{3,67},{4,68},{5,69},{6,70},{7,71},{8,12},{9,... | collective-permute-start | bytes 196616 | tf_op jit(solution)/shard_map/ppermute | solution.py:288
  97.2 6.1 %collective-permute-start.23 = (bf16[128,256]{1,0:T(8,128)(2,1)S(1)}, bf16[128,256]{1,0:T(8,128)(2,1)S(1)}, u32[]{:S(2)}, u32[]{:S(2)}) collective-permute-start(bf16[128,256]{1,0:T(8,128)(2,1)S(1)} %get-tuple-element.54), channel_id=1, source_target_pairs={{0,32},{1,33},{2,34},{3,35},{4,36},{5,37},{6,38},{7,39},{8,24},{9,... | collective-permute-start | bytes 196616 | tf_op jit(solution)/shard_map/ppermute | solution.py:288
  98.6 7.2 %collective-permute-start.21 = (bf16[128,768]{1,0:T(8,128)(2,1)S(1)}, bf16[128,768]{1,0:T(8,128)(2,1)S(1)}, u32[]{:S(2)}, u32[]{:S(2)}) collective-permute-start(bf16[128,768]{1,0:T(8,128)(2,1)S(1)} %get-tuple-element.39), channel_id=1, source_target_pairs={{0,2},{1,3},{2,0},{3,1},{4,6},{5,7},{6,4},{7,5},{8,10},{9,11},{10,... | collective-permute-start | bytes 589832 | tf_op jit(solution)/shard_map/ppermute | solution.py:288
  (4 other events, 16.1 us)

commit v9 on v8

--- a/solution.py
+++ b/solution.py
@@ -32,8 +32,11 @@
 SIZE = BLOCK + LIST
 
 
+OWNER = 64
+
+
 def of(which):
-    return 64 + which * SIZE
+    return 68 + which * SIZE
 
 
 NT = (((1,), (1,)), ((), ()))
@@ -170,8 +173,8 @@
 
 def grads_kernel(meta, lim, st0, st1, *refs):
     qds, kvs = refs[:4], refs[4:12]
-    dqs, dkvs, dkv_other = refs[12:16], refs[16:20], refs[20]
-    q_s, do_s, kv_s, s0, s1, dp0, dp1, acc, dq_s, p0, p1, ds0, ds1, lse, delta = refs[21:]
+    dqs, dkvs, dkv_other = refs[12], refs[13:17], refs[17]
+    q_s, do_s, kv_s, s0, s1, dp0, dp1, acc, dq_s, p0, p1, ds0, ds1, lse, delta = refs[18:]
     load_sorted(meta, kvs, kv_s)
     base = of(ALL)
     load_rows(meta, base, qds, q_s, do_s)
@@ -224,7 +227,7 @@
             t = slice(half * SPAN, (half + 1) * SPAN)
             for h in range(HEADS):
                 got = dq_s[pl.ds(row_of(place, h), SPAN), :] * SCALE
-                dqs[d][t, h * HD : (h + 1) * HD] = got.astype(dqs[d].dtype)
+                dqs[meta[OWNER + d], t, h * HD : (h + 1) * HD] = got
     for s in range(64):
         r = aligned(meta[IN + s], SPAN)
         t = slice((s % 2) * SPAN, (s % 2 + 1) * SPAN)
@@ -259,14 +262,14 @@
 
 
 def grads(meta, lim, sts, arrays):
-    dq = [jax.ShapeDtypeStruct((2 * SPAN, WIDE), t) for t in (jnp.float32,) + (jnp.bfloat16,) * 3]
+    dq = [jax.ShapeDtypeStruct((4, 2 * SPAN, WIDE), jnp.float32)]
     dkv = [jax.ShapeDtypeStruct((4, 2 * SPAN, 2 * HD), jnp.bfloat16)] * 4
     dkv += [jax.ShapeDtypeStruct((4, 4, 2 * SPAN, 2 * HD), jnp.bfloat16)]
     return pl.pallas_call(
         grads_kernel,
         out_shape=dq + dkv,
         in_specs=[SM] + [VM] * 15,
-        out_specs=[VM] * 9,
+        out_specs=[VM] * 6,
         scratch_shapes=COPIES
         + [
             pltpu.VMEM((KEYS, 2 * HD), jnp.float32),
@@ -356,7 +359,8 @@
     block = jnp.sum(inside * (t[None, :, None] - (begin - first)[:, None, :]), axis=2)
     group = jnp.where(t[None] < end[:, -1:], group, jnp.array([[12], [9], [3]], i32))
     lists = jnp.concatenate([units, canon, end[:, GROUPS - 1 : GROUPS], end[:, -1:], group, block], axis=1)
-    return jnp.concatenate([rank(arrived, arrived), lists.reshape(-1)]).astype(i32), lim
+    owners = (x - jnp.array(STEPS, i32)) % 4
+    return jnp.concatenate([rank(arrived, arrived), owners, lists.reshape(-1)]).astype(i32), lim
 
 
 def local(queries, keys, values, grad_out, span_slot):
@@ -378,7 +382,7 @@
     part = jnp.stack(merged(part[0], part[1], got[0], got[1]))
     got = permute(part, lambda y, z, core, x: (y, z, core, x ^ 2))
     results = grads(meta, lim, (part, got), arrays)
-    dqs, dkv, dkv_other = results[:4], results[4:8], results[8]
+    dqs, dkv, dkv_other = results[0], results[1:5], results[5]
 
     def total(*parts):
         out = parts[0].astype(jnp.float32)
@@ -386,13 +390,11 @@
             out = out + part.astype(jnp.float32)
         return out
 
+    dq = lax.psum_scatter(dqs, "x", scatter_dimension=0, tiled=False)
     other = core_swap(dkv_other)
     pairs = [total(a, other[i]).astype(jnp.bfloat16) for i, a in enumerate(dkv)]
     some = total(pairs[0], *[second_shift(a, -r) for r, a in zip(STEPS[1:], pairs[1:])])
-    back = [x_shift(dqs[1], -1), x_shift(dqs[2], -3)]
-    some, back[0], back[1], last = lax.optimization_barrier((some, back[0], back[1], dqs[3]))
     sent = [first_shift(some[i].astype(jnp.bfloat16), -r) for i, r in ((1, 1), (2, 3), (3, 2))]
-    dq = total(dqs[0], *back, x_shift(last, -2))
     summed = total(some[0], *sent)
     return (
         dq.astype(jnp.bfloat16),

time: 106 us -> 123 us (1.16); the launches traced: 107 us -> 122 us
  between operations: 0.91 us -> 14.3 us
  local copies, waits for them, and re-layouts: 3.75 us -> 8.27 us
  starting transfers between devices: 34.7 us -> 31.9 us
  other arithmetic: 4.66 us -> 6.88 us
  Pallas kernels: 38.4 us -> 37 us
    unnamed x12 -> x24, local copies, waits for them, and re-layouts: 1.64 us -> 5.24 us
    ppermute x25 -> x22, starting transfers between devices: 34.7 us -> 31.8 us  [permute(): return lax.ppermute(a, AXES, pairs)]
    pallas_call x1, Pallas kernels: 24.6 us -> 23.2 us  [grads(): pl.pallas_call(grads_kernel, out_shape=dq + dkv, in_specs=[SM] + [VM] * 1...]
    ppermute x25 -> x22, waiting for transfers between devices: 24.1 us -> 23.2 us  [permute(): return lax.ppermute(a, AXES, pairs)]
  transfers between devices with their start and end apart: 25 -> 23, of which waited for: 14 -> 13; matrix products, arithmetic and copies ran while one was open for 6% -> 7% of each run, Pallas kernels for 8% -> 7%
where the time goes in v9:
time: 123 us; the launch traced here: 122 us
  Pallas kernels  37 us (30%)
  starting transfers between devices  31.9 us (26%)
  waiting for transfers between devices  23.5 us (19%)
  between operations  14.3 us (12%)
  local copies, waits for them, and re-layouts  8.27 us (7%)
  other arithmetic  6.88 us (6%)
    ppermute x22, starting transfers between devices, permute(): return lax.ppermute(a, AXES, pairs)  31.8 us
    ppermute x22, waiting for transfers between devices, permute(): return lax.ppermute(a, AXES, pairs)  23.2 us
    pallas_call x1, Pallas kernels, grads(): pl.pallas_call(grads_kernel, out_shape=dq + dkv, in_specs=[SM] + [VM] * 1...  23.2 us
    pallas_call x2, Pallas kernels, stats(): pl.pallas_call(functools.partial(stats_kernel, which, n), out_shape=jax.S...  13.8 us
    unnamed x24, local copies, waits for them, and re-layouts  5.24 us
  transfers between devices with their start and end apart: 23, of which 13 were waited for; matrix products, arithmetic and copies ran while one was open for 7% of the time, Pallas kernels for 7%

profile of v9, /device:TPU:0, one launch (start us, length us, event | category | flops | bytes accessed | tf_op | source)
XLA Modules:
  0.0 121.8 jit_solution(4473562531548881979)
XLA Ops:
  8.0 3.4 %collective-permute-start.2 = (bf16[1,128,256]{2,1,0:T(8,128)(2,1)S(1)}, bf16[1,128,256]{2,1,0:T(8,128)(2,1)S(1)}, u32[]{:S(2)}, u32[]{:S(2)}) collective-permute-start(bf16[1,128,256]{2,1,0:T(8,128)(2,1)S(1)} %maximum_bitcast_fusion), channel_id=1, source_target_pairs={{0,64},{1,65},{2,66},{3,67},{4,68},{5,69},{6,70},{7,71},{8,12},{9,... | collective-permute-start | bytes 196616 | tf_op jit(solution)/shard_map/ppermute | solution.py:291
  11.4 1.1 collective-permute-start.1
  15.3 2.8 %collective-permute-start.5 = (bf16[128,1536]{1,0:T(8,128)(2,1)S(1)}, bf16[128,1536]{1,0:T(8,128)(2,1)S(1)}, u32[]{:S(2)}, u32[]{:S(2)}) collective-permute-start(bf16[128,1536]{1,0:T(8,128)(2,1)S(1)} %constant_dynamic-update-slice_fusion.6.refs_0_), channel_id=1, source_target_pairs={{0,3},{1,0},{2,1},{3,2},{4,7},{5,4},{6,5},{7,6},{8,11},{9,8},{10,9... | collective-permute-start | bytes 1179656 | tf_op jit(solution)/shard_map/ppermute | solution.py:291
  18.2 2.0 %collective-permute-start.3 = (bf16[4,128,256]{2,1,0:T(8,128)(2,1)S(1)}, bf16[4,128,256]{2,1,0:T(8,128)(2,1)S(1)}, u32[]{:S(2)}, u32[]{:S(2)}) collective-permute-start(bf16[4,128,256]{2,1,0:T(8,128)(2,1)S(1)} %pad_maximum_fusion.refs_3_.refs_1_.refs_4_), channel_id=1, source_target_pairs={{0,16},{1,17},{2,18},{3,19},{4,20},{5,21},{6,22},{7,23},{8,40},{9,... | collective-permute-start | bytes 786440 | tf_op jit(solution)/shard_map/ppermute | solution.py:291
  21.1 3.6 %collective-permute-start.8 = (bf16[4,128,256]{2,1,0:T(8,128)(2,1)S(1)}, bf16[4,128,256]{2,1,0:T(8,128)(2,1)S(1)}, u32[]{:S(2)}, u32[]{:S(2)}) collective-permute-start(bf16[4,128,256]{2,1,0:T(8,128)(2,1)S(1)} %pad_maximum_fusion.refs_3_.refs_1_.refs_4_), channel_id=1, source_target_pairs={{0,4},{1,5},{2,6},{3,7},{4,0},{5,1},{6,2},{7,3},{8,72},{9,73},{10,... | collective-permute-start | bytes 786440 | tf_op jit(solution)/shard_map/ppermute | solution.py:291
  32.0 2.7 %collective-permute-start.6 = (bf16[128,1536]{1,0:T(8,128)(2,1)S(1)}, bf16[128,1536]{1,0:T(8,128)(2,1)}, u32[]{:S(2)}, u32[]{:S(2)}) collective-permute-start(bf16[128,1536]{1,0:T(8,128)(2,1)S(1)} %constant_dynamic-update-slice_fusion.6.refs_0_), channel_id=1, source_target_pairs={{0,2},{1,3},{2,0},{3,1},{4,6},{5,7},{6,4},{7,5},{8,10},{9,11},{10,... | collective-permute-start | bytes 1179656 | tf_op jit(solution)/shard_map/ppermute | solution.py:291
  35.3 8.9 %stats_near.1.refs_9_ = f32[2,24,128]{2,1,0:T(8,128)S(1)} custom-call(s32[986]{0:T(1024)S(1)} %pad_add_fusion.2.meta, s32[3,16,256]{2,1,0:T(8,128)S(1)} %concatenate.34.lim, bf16[128,1536]{1,0:T(8,128)(2,1)S(1)} %constant_dynamic-update-slice_fusion.6.refs_0_, bf16[128,1536]{1,0:T(8,128)(2,1)S(1)} %collective-permute-done.4.refs_1_, ...), custom_call_target="tpu_custom_call" | custom-call | flops 3000000 | bytes 100000 | tf_op jit(solution)/shard_map/stats_near/pallas_call | solution.py:252
  44.7 4.8 %stats_far.1 = f32[2,24,128]{2,1,0:T(8,128)S(1)} custom-call(s32[986]{0:T(1024)S(1)} %pad_add_fusion.2.meta, s32[3,16,256]{2,1,0:T(8,128)S(1)} %concatenate.34.lim, bf16[128,1536]{1,0:T(8,128)(2,1)} %collective-permute-done.6.refs_0_.refs_3_, bf16[4,128,256]{2,1,0:T(8,128)(2,1)S(1)} %pad_maximum_fusion.refs_3_.refs_1_.refs_4_, ...), custom_call_target="tpu_custom_call" | custom-call | flops 1000000 | bytes 100000 | tf_op jit(solution)/shard_map/stats_far/pallas_call | solution.py:252
  49.5 1.3 %collective-permute-start.13 = (f32[2,24,128]{2,1,0:T(8,128)S(1)}, f32[2,24,128]{2,1,0:T(8,128)S(1)}, u32[]{:S(2)}, u32[]{:S(2)}) collective-permute-start(f32[2,24,128]{2,1,0:T(8,128)S(1)} %stats_far.1), channel_id=1, source_target_pairs={{0,1},{1,0},{2,3},{3,2},{4,5},{5,4},{6,7},{7,6},{8,9},{9,8},{10,11... | collective-permute-start | bytes 73736 | tf_op jit(solution)/shard_map/ppermute | solution.py:291
  50.8 2.6 %collective-permute-done.13 = f32[2,24,128]{2,1,0:T(8,128)S(1)} collective-permute-done((f32[2,24,128]{2,1,0:T(8,128)S(1)}, f32[2,24,128]{2,1,0:T(8,128)S(1)}, u32[]{:S(2)}, u32[]{:S(2)}) %collective-permute-start.13) | collective-permute-done | bytes 24608 | tf_op jit(solution)/shard_map/ppermute | solution.py:291
  53.5 2.9 %collective-permute-start.14 = (f32[2,24,128]{2,1,0:T(8,128)S(1)}, f32[2,24,128]{2,1,0:T(8,128)S(1)}, u32[]{:S(2)}, u32[]{:S(2)}) collective-permute-start(f32[2,24,128]{2,1,0:T(8,128)S(1)} %pad_maximum_fusion.1.st0), channel_id=1, source_target_pairs={{0,2},{1,3},{2,0},{3,1},{4,6},{5,7},{6,4},{7,5},{8,10},{9,11},{10,... | collective-permute-start | bytes 73736 | tf_op jit(solution)/shard_map/ppermute | solution.py:291
  56.4 2.7 %collective-permute-done.14.st1 = f32[2,24,128]{2,1,0:T(8,128)S(1)} collective-permute-done((f32[2,24,128]{2,1,0:T(8,128)S(1)}, f32[2,24,128]{2,1,0:T(8,128)S(1)}, u32[]{:S(2)}, u32[]{:S(2)}) %collective-permute-start.14) | collective-permute-done | bytes 24608 | tf_op jit(solution)/shard_map/ppermute | solution.py:291
  59.1 23.2 %grads.1 = (f32[4,128,768]{2,1,0:T(8,128)}, bf16[4,128,256]{2,1,0:T(8,128)(2,1)S(1)}, bf16[4,128,256]{2,1,0:T(8,128)(2,1)S(1)}, bf16[4,128,256]{2,1,0:T(8,128)(2...) custom-call(s32[986]{0:T(1024)S(1)} %pad_add_fusion.2.meta, ...), custom_call_target="tpu_custom_call" | custom-call | tf_op jit(solution)/shard_map/grads/pallas_call | solution.py:268
  85.4 1.2 copy-done.7
  86.5 2.7 %collective-permute-done.15 = bf16[4,4,128,256]{3,2,1,0:T(8,128)(2,1)S(1)} collective-permute-done((bf16[4,4,128,256]{3,2,1,0:T(8,128)(2,1)S(1)}, bf16[4,4,128,256]{3,2,1,0:T(8,128)(2,1)S(1)}, u32[]{:S(2)}, u32[]{:S(2)}) %collective-permute-start.15) | collective-permute-done | bytes 1048608 | tf_op jit(solution)/shard_map/ppermute | solution.py:291
  89.4 4.1 %collective-permute-start.16 = (bf16[4,128,256]{2,1,0:T(8,128)(2,1)S(1)}, bf16[4,128,256]{2,1,0:T(8,128)(2,1)S(1)}, u32[]{:S(2)}, u32[]{:S(2)}) collective-permute-start(bf16[4,128,256]{2,1,0:T(8,128)(2,1)S(1)} %get-tuple-element.37), channel_id=1, source_target_pairs={{0,20},{1,21},{2,22},{3,23},{4,16},{5,17},{6,18},{7,19},{8,104},{9... | collective-permute-start | bytes 786440 | tf_op jit(solution)/shard_map/ppermute | solution.py:291
  93.5 2.5 %collective-permute-start.18 = (bf16[4,128,256]{2,1,0:T(8,128)(2,1)S(1)}, bf16[4,128,256]{2,1,0:T(8,128)(2,1)S(1)}, u32[]{:S(2)}, u32[]{:S(2)}) collective-permute-start(bf16[4,128,256]{2,1,0:T(8,128)(2,1)S(1)} %get-tuple-element.38), channel_id=1, source_target_pairs={{0,4},{1,5},{2,6},{3,7},{4,0},{5,1},{6,2},{7,3},{8,72},{9,73},{10,... | collective-permute-start | bytes 786440 | tf_op jit(solution)/shard_map/ppermute | solution.py:291
  96.0 2.3 %collective-permute-done.16 = bf16[4,128,256]{2,1,0:T(8,128)(2,1)S(1)} collective-permute-done((bf16[4,128,256]{2,1,0:T(8,128)(2,1)S(1)}, bf16[4,128,256]{2,1,0:T(8,128)(2,1)S(1)}, u32[]{:S(2)}, u32[]{:S(2)}) %collective-permute-start.16) | collective-permute-done | bytes 262176 | tf_op jit(solution)/shard_map/ppermute | solution.py:291
  98.3 3.2 %collective-permute-done.18 = bf16[4,128,256]{2,1,0:T(8,128)(2,1)S(1)} collective-permute-done((bf16[4,128,256]{2,1,0:T(8,128)(2,1)S(1)}, bf16[4,128,256]{2,1,0:T(8,128)(2,1)S(1)}, u32[]{:S(2)}, u32[]{:S(2)}) %collective-permute-start.18) | collective-permute-done | bytes 262176 | tf_op jit(solution)/shard_map/ppermute | solution.py:291
  101.5 2.7 %collective-permute-done.17 = bf16[4,128,256]{2,1,0:T(8,128)(2,1)S(1)} collective-permute-done((bf16[4,128,256]{2,1,0:T(8,128)(2,1)S(1)}, bf16[4,128,256]{2,1,0:T(8,128)(2,1)S(1)}, u32[]{:S(2)}, u32[]{:S(2)}) %collective-permute-start.17) | collective-permute-done | bytes 262176 | tf_op jit(solution)/shard_map/ppermute | solution.py:291
  104.4 1.5 %collective-permute-start.19 = (bf16[128,256]{1,0:T(8,128)(2,1)S(1)}, bf16[128,256]{1,0:T(8,128)(2,1)S(1)}, u32[]{:S(2)}, u32[]{:S(2)}) collective-permute-start(bf16[128,256]{1,0:T(8,128)(2,1)S(1)} %get-tuple-element.40), channel_id=1, source_target_pairs={{0,96},{1,97},{2,98},{3,99},{4,100},{5,101},{6,102},{7,103},{8,28}... | collective-permute-start | bytes 196616 | tf_op jit(solution)/shard_map/ppermute | solution.py:291
  106.8 1.9 %collective-permute-done.19 = bf16[128,256]{1,0:T(8,128)(2,1)S(1)} collective-permute-done((bf16[128,256]{1,0:T(8,128)(2,1)S(1)}, bf16[128,256]{1,0:T(8,128)(2,1)S(1)}, u32[]{:S(2)}, u32[]{:S(2)}) %collective-permute-start.19) | collective-permute-done | bytes 65568 | tf_op jit(solution)/shard_map/ppermute | solution.py:291
  108.7 3.0 %collective-permute-done.21 = bf16[128,256]{1,0:T(8,128)(2,1)S(1)} collective-permute-done((bf16[128,256]{1,0:T(8,128)(2,1)S(1)}, bf16[128,256]{1,0:T(8,128)(2,1)S(1)}, u32[]{:S(2)}, u32[]{:S(2)}) %collective-permute-start.21) | collective-permute-done | bytes 65568 | tf_op jit(solution)/shard_map/ppermute | solution.py:291
  113.2 1.7 %convert_bitcast_fusion = bf16[128,768]{1,0:T(8,128)(2,1)} fusion(f32[1,128,768]{2,1,0:T(8,128)} %reduce-scatter.2.cloned.1.call-done), kind=kLoop, calls=%fused_computation.14 | loop fusion | flops 98304 | bytes 589824 | tf_op jit(solution)/shard_map/convert_element_type | solution.py:400
  (115 shorter events, 18.8 us)
Async XLA Ops:
  7.2 27.5 %copy-start.8 = (s32[3]{0:T(128)S(1)}, s32[3]{0:T(128)}, u32[]{:S(2)}) copy-start(s32[3]{0:T(128)} %constant.186) | copy-start | bytes 40
  7.2 106.0 %reduce-scatter.2.cloned.1.call-start = ((), (), s32[]{:S(2)}) async-start(), calls=%async_computation.1 | async-start | bytes 1966080 | tf_op jit(solution)/shard_map/reduce_scatter | solution.py:393
  8.0 10.1 %collective-permute-start.2 = (bf16[1,128,256]{2,1,0:T(8,128)(2,1)S(1)}, bf16[1,128,256]{2,1,0:T(8,128)(2,1)S(1)}, u32[]{:S(2)}, u32[]{:S(2)}) collective-permute-start(bf16[1,128,256]{2,1,0:T(8,128)(2,1)S(1)} %maximum_bitcast_fusion), channel_id=1, source_target_pairs={{0,64},{1,65},{2,66},{3,67},{4,68},{5,69},{6,70},{7,71},{8,12},{9,... | collective-permute-start | bytes 196616 | tf_op jit(solution)/shard_map/ppermute | solution.py:291
  11.4 6.8 %collective-permute-start.1 = (bf16[1,128,256]{2,1,0:T(8,128)(2,1)S(1)}, bf16[1,128,256]{2,1,0:T(8,128)(2,1)S(1)}, u32[]{:S(2)}, u32[]{:S(2)}) collective-permute-start(bf16[1,128,256]{2,1,0:T(8,128)(2,1)S(1)} %maximum_bitcast_fusion), channel_id=1, source_target_pairs={{0,96},{1,97},{2,98},{3,99},{4,100},{5,101},{6,102},{7,103},{8,28}... | collective-permute-start | bytes 196616 | tf_op jit(solution)/shard_map/ppermute | solution.py:291
  12.4 5.7 %collective-permute-start = (bf16[1,128,256]{2,1,0:T(8,128)(2,1)S(1)}, bf16[1,128,256]{2,1,0:T(8,128)(2,1)S(1)}, u32[]{:S(2)}, u32[]{:S(2)}) collective-permute-start(bf16[1,128,256]{2,1,0:T(8,128)(2,1)S(1)} %maximum_bitcast_fusion), channel_id=1, source_target_pairs={{0,32},{1,33},{2,34},{3,35},{4,36},{5,37},{6,38},{7,39},{8,24},{9,... | collective-permute-start | bytes 196616 | tf_op jit(solution)/shard_map/ppermute | solution.py:291
  15.3 16.3 %collective-permute-start.5 = (bf16[128,1536]{1,0:T(8,128)(2,1)S(1)}, bf16[128,1536]{1,0:T(8,128)(2,1)S(1)}, u32[]{:S(2)}, u32[]{:S(2)}) collective-permute-start(bf16[128,1536]{1,0:T(8,128)(2,1)S(1)} %constant_dynamic-update-slice_fusion.6.refs_0_), channel_id=1, source_target_pairs={{0,3},{1,0},{2,1},{3,2},{4,7},{5,4},{6,5},{7,6},{8,11},{9,8},{10,9... | collective-permute-start | bytes 1179656 | tf_op jit(solution)/shard_map/ppermute | solution.py:291
  18.1 13.9 %collective-permute-start.4 = (bf16[128,1536]{1,0:T(8,128)(2,1)S(1)}, bf16[128,1536]{1,0:T(8,128)(2,1)S(1)}, u32[]{:S(2)}, u32[]{:S(2)}) collective-permute-start(bf16[128,1536]{1,0:T(8,128)(2,1)S(1)} %constant_dynamic-update-slice_fusion.6.refs_0_), channel_id=1, source_target_pairs={{0,1},{1,2},{2,3},{3,0},{4,5},{5,6},{6,7},{7,4},{8,9},{9,10},{10,1... | collective-permute-start | bytes 1179656 | tf_op jit(solution)/shard_map/ppermute | solution.py:291
  18.2 8.5 %collective-permute-start.3 = (bf16[4,128,256]{2,1,0:T(8,128)(2,1)S(1)}, bf16[4,128,256]{2,1,0:T(8,128)(2,1)S(1)}, u32[]{:S(2)}, u32[]{:S(2)}) collective-permute-start(bf16[4,128,256]{2,1,0:T(8,128)(2,1)S(1)} %pad_maximum_fusion.refs_3_.refs_1_.refs_4_), channel_id=1, source_target_pairs={{0,16},{1,17},{2,18},{3,19},{4,20},{5,21},{6,22},{7,23},{8,40},{9,... | collective-permute-start | bytes 786440 | tf_op jit(solution)/shard_map/ppermute | solution.py:291
  21.1 9.9 %collective-permute-start.8 = (bf16[4,128,256]{2,1,0:T(8,128)(2,1)S(1)}, bf16[4,128,256]{2,1,0:T(8,128)(2,1)S(1)}, u32[]{:S(2)}, u32[]{:S(2)}) collective-permute-start(bf16[4,128,256]{2,1,0:T(8,128)(2,1)S(1)} %pad_maximum_fusion.refs_3_.refs_1_.refs_4_), channel_id=1, source_target_pairs={{0,4},{1,5},{2,6},{3,7},{4,0},{5,1},{6,2},{7,3},{8,72},{9,73},{10,... | collective-permute-start | bytes 786440 | tf_op jit(solution)/shard_map/ppermute | solution.py:291
  24.7 6.8 %collective-permute-start.7 = (bf16[4,128,256]{2,1,0:T(8,128)(2,1)S(1)}, bf16[4,128,256]{2,1,0:T(8,128)(2,1)S(1)}, u32[]{:S(2)}, u32[]{:S(2)}) collective-permute-start(bf16[4,128,256]{2,1,0:T(8,128)(2,1)S(1)} %pad_maximum_fusion.refs_3_.refs_1_.refs_4_), channel_id=1, source_target_pairs={{0,20},{1,21},{2,22},{3,23},{4,16},{5,17},{6,18},{7,19},{8,104},{9... | collective-permute-start | bytes 786440 | tf_op jit(solution)/shard_map/ppermute | solution.py:291
  30.6 4.6 %collective-permute-start.9 = (bf16[4,128,256]{2,1,0:T(8,128)(2,1)S(1)}, bf16[4,128,256]{2,1,0:T(8,128)(2,1)S(1)}, u32[]{:S(2)}, u32[]{:S(2)}) collective-permute-start(bf16[4,128,256]{2,1,0:T(8,128)(2,1)S(1)} %pad_maximum_fusion.refs_3_.refs_1_.refs_4_), channel_id=1, source_target_pairs={{0,8},{1,9},{2,10},{3,11},{4,12},{5,13},{6,14},{7,15},{8,0},{9,1},... | collective-permute-start | bytes 786440 | tf_op jit(solution)/shard_map/ppermute | solution.py:291
  30.9 4.4 %collective-permute-start.10 = (bf16[4,128,256]{2,1,0:T(8,128)(2,1)S(1)}, bf16[4,128,256]{2,1,0:T(8,128)(2,1)S(1)}, u32[]{:S(2)}, u32[]{:S(2)}) collective-permute-start(bf16[4,128,256]{2,1,0:T(8,128)(2,1)S(1)} %collective-permute-done.3.refs_4_.refs_2_.refs_5_), channel_id=1, source_target_pairs={{0,8},{1,9},{2,10},{3,11},{4,12},{5,13},{6,14},{7,15},{8,0},{9,1},... | collective-permute-start | bytes 786440 | tf_op jit(solution)/shard_map/ppermute | solution.py:291
  31.4 3.8 %collective-permute-start.12 = (bf16[4,128,256]{2,1,0:T(8,128)(2,1)S(1)}, bf16[4,128,256]{2,1,0:T(8,128)(2,1)S(1)}, u32[]{:S(2)}, u32[]{:S(2)}) collective-permute-start(bf16[4,128,256]{2,1,0:T(8,128)(2,1)S(1)} %collective-permute-done.8.refs_6_.refs_4_.refs_7_), channel_id=1, source_target_pairs={{0,8},{1,9},{2,10},{3,11},{4,12},{5,13},{6,14},{7,15},{8,0},{9,1},... | collective-permute-start | bytes 786440 | tf_op jit(solution)/shard_map/ppermute | solution.py:291
  31.6 3.7 %collective-permute-start.11 = (bf16[4,128,256]{2,1,0:T(8,128)(2,1)S(1)}, bf16[4,128,256]{2,1,0:T(8,128)(2,1)S(1)}, u32[]{:S(2)}, u32[]{:S(2)}) collective-permute-start(bf16[4,128,256]{2,1,0:T(8,128)(2,1)S(1)} %collective-permute-done.7.refs_5_.refs_3_.refs_6_), channel_id=1, source_target_pairs={{0,8},{1,9},{2,10},{3,11},{4,12},{5,13},{6,14},{7,15},{8,0},{9,1},... | collective-permute-start | bytes 786440 | tf_op jit(solution)/shard_map/ppermute | solution.py:291
  32.0 12.7 %collective-permute-start.6 = (bf16[128,1536]{1,0:T(8,128)(2,1)S(1)}, bf16[128,1536]{1,0:T(8,128)(2,1)}, u32[]{:S(2)}, u32[]{:S(2)}) collective-permute-start(bf16[128,1536]{1,0:T(8,128)(2,1)S(1)} %constant_dynamic-update-slice_fusion.6.refs_0_), channel_id=1, source_target_pairs={{0,2},{1,3},{2,0},{3,1},{4,6},{5,7},{6,4},{7,5},{8,10},{9,11},{10,... | collective-permute-start | bytes 1179656 | tf_op jit(solution)/shard_map/ppermute | solution.py:291
  49.5 3.9 %collective-permute-start.13 = (f32[2,24,128]{2,1,0:T(8,128)S(1)}, f32[2,24,128]{2,1,0:T(8,128)S(1)}, u32[]{:S(2)}, u32[]{:S(2)}) collective-permute-start(f32[2,24,128]{2,1,0:T(8,128)S(1)} %stats_far.1), channel_id=1, source_target_pairs={{0,1},{1,0},{2,3},{3,2},{4,5},{5,4},{6,7},{7,6},{8,9},{9,8},{10,11... | collective-permute-start | bytes 73736 | tf_op jit(solution)/shard_map/ppermute | solution.py:291
  53.5 5.6 %collective-permute-start.14 = (f32[2,24,128]{2,1,0:T(8,128)S(1)}, f32[2,24,128]{2,1,0:T(8,128)S(1)}, u32[]{:S(2)}, u32[]{:S(2)}) collective-permute-start(f32[2,24,128]{2,1,0:T(8,128)S(1)} %pad_maximum_fusion.1.st0), channel_id=1, source_target_pairs={{0,2},{1,3},{2,0},{3,1},{4,6},{5,7},{6,4},{7,5},{8,10},{9,11},{10,... | collective-permute-start | bytes 73736 | tf_op jit(solution)/shard_map/ppermute | solution.py:291
  86.5 2.7 %collective-permute-start.15 = (bf16[4,4,128,256]{3,2,1,0:T(8,128)(2,1)S(1)}, bf16[4,4,128,256]{3,2,1,0:T(8,128)(2,1)S(1)}, u32[]{:S(2)}, u32[]{:S(2)}) collective-permute-start(bf16[4,4,128,256]{3,2,1,0:T(8,128)(2,1)S(1)} %copy-done.7), channel_id=1, source_target_pairs={{0,8},{1,9},{2,10},{3,11},{4,12},{5,13},{6,14},{7,15},{8,0},{9,1},... | collective-permute-start | bytes 3145736 | tf_op jit(solution)/shard_map/ppermute | solution.py:291
  89.4 8.8 %collective-permute-start.16 = (bf16[4,128,256]{2,1,0:T(8,128)(2,1)S(1)}, bf16[4,128,256]{2,1,0:T(8,128)(2,1)S(1)}, u32[]{:S(2)}, u32[]{:S(2)}) collective-permute-start(bf16[4,128,256]{2,1,0:T(8,128)(2,1)S(1)} %get-tuple-element.37), channel_id=1, source_target_pairs={{0,20},{1,21},{2,22},{3,23},{4,16},{5,17},{6,18},{7,19},{8,104},{9... | collective-permute-start | bytes 786440 | tf_op jit(solution)/shard_map/ppermute | solution.py:291
  93.5 7.9 %collective-permute-start.18 = (bf16[4,128,256]{2,1,0:T(8,128)(2,1)S(1)}, bf16[4,128,256]{2,1,0:T(8,128)(2,1)S(1)}, u32[]{:S(2)}, u32[]{:S(2)}) collective-permute-start(bf16[4,128,256]{2,1,0:T(8,128)(2,1)S(1)} %get-tuple-element.38), channel_id=1, source_target_pairs={{0,4},{1,5},{2,6},{3,7},{4,0},{5,1},{6,2},{7,3},{8,72},{9,73},{10,... | collective-permute-start | bytes 786440 | tf_op jit(solution)/shard_map/ppermute | solution.py:291
  96.0 8.2 %collective-permute-start.17 = (bf16[4,128,256]{2,1,0:T(8,128)(2,1)S(1)}, bf16[4,128,256]{2,1,0:T(8,128)(2,1)S(1)}, u32[]{:S(2)}, u32[]{:S(2)}) collective-permute-start(bf16[4,128,256]{2,1,0:T(8,128)(2,1)S(1)} %get-tuple-element.39), channel_id=1, source_target_pairs={{0,16},{1,17},{2,18},{3,19},{4,20},{5,21},{6,22},{7,23},{8,40},{9,... | collective-permute-start | bytes 786440 | tf_op jit(solution)/shard_map/ppermute | solution.py:291
  104.4 4.3 %collective-permute-start.19 = (bf16[128,256]{1,0:T(8,128)(2,1)S(1)}, bf16[128,256]{1,0:T(8,128)(2,1)S(1)}, u32[]{:S(2)}, u32[]{:S(2)}) collective-permute-start(bf16[128,256]{1,0:T(8,128)(2,1)S(1)} %get-tuple-element.40), channel_id=1, source_target_pairs={{0,96},{1,97},{2,98},{3,99},{4,100},{5,101},{6,102},{7,103},{8,28}... | collective-permute-start | bytes 196616 | tf_op jit(solution)/shard_map/ppermute | solution.py:291
  105.9 5.8 %collective-permute-start.21 = (bf16[128,256]{1,0:T(8,128)(2,1)S(1)}, bf16[128,256]{1,0:T(8,128)(2,1)S(1)}, u32[]{:S(2)}, u32[]{:S(2)}) collective-permute-start(bf16[128,256]{1,0:T(8,128)(2,1)S(1)} %get-tuple-element.41), channel_id=1, source_target_pairs={{0,64},{1,65},{2,66},{3,67},{4,68},{5,69},{6,70},{7,71},{8,12},{9,... | collective-permute-start | bytes 196616 | tf_op jit(solution)/shard_map/ppermute | solution.py:291
  106.2 6.2 %collective-permute-start.20 = (bf16[128,256]{1,0:T(8,128)(2,1)S(1)}, bf16[128,256]{1,0:T(8,128)(2,1)S(1)}, u32[]{:S(2)}, u32[]{:S(2)}) collective-permute-start(bf16[128,256]{1,0:T(8,128)(2,1)S(1)} %get-tuple-element.42), channel_id=1, source_target_pairs={{0,32},{1,33},{2,34},{3,35},{4,36},{5,37},{6,38},{7,39},{8,24},{9,... | collective-permute-start | bytes 196616 | tf_op jit(solution)/shard_map/ppermute | solution.py:291
  (8 other events, 30.9 us)
Sparse Core Ops, SparseCore 0:
  85.5 27.7 reduce-scatter.1

commit v10 on v8

--- a/solution.py
+++ b/solution.py
@@ -23,7 +23,7 @@
 KB = 256
 R = 256
 GROUPS = 12
-MANY, FEW = 16, 8
+MANY, SOME, FEW = 16, 8, 2
 LIST = 144
 IN = 0
 ALL, NEAR, FAR = range(3)
@@ -74,7 +74,8 @@
 
     bodies = full // MANY
     lax.fori_loop(0, bodies, body(MANY, False), 0)
-    lax.fori_loop(bodies * (MANY // FEW), (count + FEW - 1) // FEW, body(FEW, True), 0)
+    lax.fori_loop(bodies * (MANY // SOME), count // SOME, body(SOME, True), 0)
+    lax.fori_loop(count // SOME * (SOME // FEW), (count + FEW - 1) // FEW, body(FEW, True), 0)
 
 
 def load_sorted(meta, kvs, kv_s):
@@ -389,10 +390,8 @@
     other = core_swap(dkv_other)
     pairs = [total(a, other[i]).astype(jnp.bfloat16) for i, a in enumerate(dkv)]
     some = total(pairs[0], *[second_shift(a, -r) for r, a in zip(STEPS[1:], pairs[1:])])
-    back = [x_shift(dqs[1], -1), x_shift(dqs[2], -3)]
-    some, back[0], back[1], last = lax.optimization_barrier((some, back[0], back[1], dqs[3]))
+    dq = total(dqs[0], *[x_shift(a, -r) for r, a in zip(STEPS[1:], dqs[1:])])
     sent = [first_shift(some[i].astype(jnp.bfloat16), -r) for i, r in ((1, 1), (2, 3), (3, 2))]
-    dq = total(dqs[0], *back, x_shift(last, -2))
     summed = total(some[0], *sent)
     return (
         dq.astype(jnp.bfloat16),

time: 106 us -> 102 us (0.962); the launches traced: 107 us -> 101 us
  starting transfers between devices: 34.7 us -> 31.7 us
  Pallas kernels: 38.4 us -> 37.3 us
  waiting for transfers between devices: 24.1 us -> 23 us
    ppermute x25, starting transfers between devices: 34.7 us -> 31.7 us  [permute(): return lax.ppermute(a, AXES, pairs)]
    pallas_call x1, Pallas kernels: 24.6 us -> 23.1 us  [grads(): pl.pallas_call(grads_kernel, out_shape=dq + dkv, in_specs=[SM] + [VM] * 1...]
    ppermute x25, waiting for transfers between devices: 24.1 us -> 23 us  [permute(): return lax.ppermute(a, AXES, pairs)]
  transfers between devices with their start and end apart: 25 -> 25, of which waited for: 14 -> 12; matrix products, arithmetic and copies ran while one was open for 6% -> 6% of each run, Pallas kernels for 8% -> 10%
where the time goes in v10:
time: 102 us; the launch traced here: 101 us
  Pallas kernels  37.3 us (37%)
  starting transfers between devices  31.7 us (31%)
  waiting for transfers between devices  23 us (23%)
  other arithmetic  4.64 us (5%)
  local copies, waits for them, and re-layouts  3.75 us (4%)
    ppermute x25, starting transfers between devices, permute(): return lax.ppermute(a, AXES, pairs)  31.7 us
    pallas_call x1, Pallas kernels, grads(): pl.pallas_call(grads_kernel, out_shape=dq + dkv, in_specs=[SM] + [VM] * 1...  23.1 us
    ppermute x25, waiting for transfers between devices, permute(): return lax.ppermute(a, AXES, pairs)  23 us
    pallas_call x2, Pallas kernels, stats(): pl.pallas_call(functools.partial(stats_kernel, which, n), out_shape=jax.S...  14.2 us
  transfers between devices with their start and end apart: 25, of which 12 were waited for; matrix products, arithmetic and copies ran while one was open for 6% of the time, Pallas kernels for 10%

profile of v10, /device:TPU:0, one launch (start us, length us, event | category | flops | bytes accessed | tf_op | source)
XLA Modules:
  0.0 101.3 jit_solution(785824792163550592)
XLA Ops:
  1.4 3.4 %collective-permute-start.2 = (bf16[1,128,256]{2,1,0:T(8,128)(2,1)S(1)}, bf16[1,128,256]{2,1,0:T(8,128)(2,1)S(1)}, u32[]{:S(2)}, u32[]{:S(2)}) collective-permute-start(bf16[1,128,256]{2,1,0:T(8,128)(2,1)S(1)} %maximum_bitcast_fusion), channel_id=1, source_target_pairs={{0,64},{1,65},{2,66},{3,67},{4,68},{5,69},{6,70},{7,71},{8,12},{9,... | collective-permute-start | bytes 196616 | tf_op jit(solution)/shard_map/ppermute | solution.py:289
  4.8 1.1 %collective-permute-start.1 = (bf16[1,128,256]{2,1,0:T(8,128)(2,1)S(1)}, bf16[1,128,256]{2,1,0:T(8,128)(2,1)S(1)}, u32[]{:S(2)}, u32[]{:S(2)}) collective-permute-start(bf16[1,128,256]{2,1,0:T(8,128)(2,1)S(1)} %maximum_bitcast_fusion), channel_id=1, source_target_pairs={{0,96},{1,97},{2,98},{3,99},{4,100},{5,101},{6,102},{7,103},{8,28}... | collective-permute-start | bytes 196616 | tf_op jit(solution)/shard_map/ppermute | solution.py:289
  7.8 2.8 %collective-permute-start.5 = (bf16[128,1536]{1,0:T(8,128)(2,1)S(1)}, bf16[128,1536]{1,0:T(8,128)(2,1)S(1)}, u32[]{:S(2)}, u32[]{:S(2)}) collective-permute-start(bf16[128,1536]{1,0:T(8,128)(2,1)S(1)} %constant_dynamic-update-slice_fusion.6.refs_0_), channel_id=1, source_target_pairs={{0,3},{1,0},{2,1},{3,2},{4,7},{5,4},{6,5},{7,6},{8,11},{9,8},{10,9... | collective-permute-start | bytes 1179656 | tf_op jit(solution)/shard_map/ppermute | solution.py:289
  11.3 2.0 %collective-permute-start.3 = (bf16[4,128,256]{2,1,0:T(8,128)(2,1)S(1)}, bf16[4,128,256]{2,1,0:T(8,128)(2,1)S(1)}, u32[]{:S(2)}, u32[]{:S(2)}) collective-permute-start(bf16[4,128,256]{2,1,0:T(8,128)(2,1)S(1)} %pad_maximum_fusion.refs_3_.refs_1_.refs_4_), channel_id=1, source_target_pairs={{0,16},{1,17},{2,18},{3,19},{4,20},{5,21},{6,22},{7,23},{8,40},{9,... | collective-permute-start | bytes 786440 | tf_op jit(solution)/shard_map/ppermute | solution.py:289
  13.6 3.7 %collective-permute-start.8 = (bf16[4,128,256]{2,1,0:T(8,128)(2,1)S(1)}, bf16[4,128,256]{2,1,0:T(8,128)(2,1)S(1)}, u32[]{:S(2)}, u32[]{:S(2)}) collective-permute-start(bf16[4,128,256]{2,1,0:T(8,128)(2,1)S(1)} %pad_maximum_fusion.refs_3_.refs_1_.refs_4_), channel_id=1, source_target_pairs={{0,4},{1,5},{2,6},{3,7},{4,0},{5,1},{6,2},{7,3},{8,72},{9,73},{10,... | collective-permute-start | bytes 786440 | tf_op jit(solution)/shard_map/ppermute | solution.py:289
  17.2 1.0 collective-permute-start.7
  18.2 1.6 %collective-permute-done.3.refs_4_.refs_2_.refs_5_ = bf16[4,128,256]{2,1,0:T(8,128)(2,1)S(1)} collective-permute-done((bf16[4,128,256]{2,1,0:T(8,128)(2,1)S(1)}, bf16[4,128,256]{2,1,0:T(8,128)(2,1)S(1)}, u32[]{:S(2)}, u32[]{:S(2)}) %collective-permute-start.3) | collective-permute-done | bytes 262176 | tf_op jit(solution)/shard_map/ppermute | solution.py:289
  24.7 3.4 %collective-permute-start.6 = (bf16[128,1536]{1,0:T(8,128)(2,1)S(1)}, bf16[128,1536]{1,0:T(8,128)(2,1)}, u32[]{:S(2)}, u32[]{:S(2)}) collective-permute-start(bf16[128,1536]{1,0:T(8,128)(2,1)S(1)} %constant_dynamic-update-slice_fusion.6.refs_0_), channel_id=1, source_target_pairs={{0,2},{1,3},{2,0},{3,1},{4,6},{5,7},{6,4},{7,5},{8,10},{9,11},{10,... | collective-permute-start | bytes 1179656 | tf_op jit(solution)/shard_map/ppermute | solution.py:289
  29.4 9.7 %stats_near.1.refs_9_ = f32[2,24,128]{2,1,0:T(8,128)S(1)} custom-call(s32[982]{0:T(1024)S(1)} %pad_add_fusion.2.meta, s32[3,16,256]{2,1,0:T(8,128)S(1)} %concatenate.34.lim, bf16[128,1536]{1,0:T(8,128)(2,1)S(1)} %constant_dynamic-update-slice_fusion.6.refs_0_, bf16[128,1536]{1,0:T(8,128)(2,1)S(1)} %collective-permute-done.4.refs_1_, ...), custom_call_target="tpu_custom_call" | custom-call | flops 3000000 | bytes 100000 | tf_op jit(solution)/shard_map/stats_near/pallas_call | solution.py:250
  39.1 4.5 %stats_far.1 = f32[2,24,128]{2,1,0:T(8,128)S(1)} custom-call(s32[982]{0:T(1024)S(1)} %pad_add_fusion.2.meta, s32[3,16,256]{2,1,0:T(8,128)S(1)} %concatenate.34.lim, bf16[128,1536]{1,0:T(8,128)(2,1)} %collective-permute-done.6.refs_0_.refs_3_, bf16[4,128,256]{2,1,0:T(8,128)(2,1)S(1)} %pad_maximum_fusion.refs_3_.refs_1_.refs_4_, ...), custom_call_target="tpu_custom_call" | custom-call | flops 1000000 | bytes 100000 | tf_op jit(solution)/shard_map/stats_far/pallas_call | solution.py:250
  44.4 3.3 %collective-permute-done.13 = f32[2,24,128]{2,1,0:T(8,128)S(1)} collective-permute-done((f32[2,24,128]{2,1,0:T(8,128)S(1)}, f32[2,24,128]{2,1,0:T(8,128)S(1)}, u32[]{:S(2)}, u32[]{:S(2)}) %collective-permute-start.13) | collective-permute-done | bytes 24608 | tf_op jit(solution)/shard_map/ppermute | solution.py:289
  47.7 2.2 %collective-permute-start.14 = (f32[2,24,128]{2,1,0:T(8,128)S(1)}, f32[2,24,128]{2,1,0:T(8,128)S(1)}, u32[]{:S(2)}, u32[]{:S(2)}) collective-permute-start(f32[2,24,128]{2,1,0:T(8,128)S(1)} %pad_maximum_fusion.1.st0), channel_id=1, source_target_pairs={{0,2},{1,3},{2,0},{3,1},{4,6},{5,7},{6,4},{7,5},{8,10},{9,11},{10,... | collective-permute-start | bytes 73736 | tf_op jit(solution)/shard_map/ppermute | solution.py:289
  49.9 3.3 %collective-permute-done.14.st1 = f32[2,24,128]{2,1,0:T(8,128)S(1)} collective-permute-done((f32[2,24,128]{2,1,0:T(8,128)S(1)}, f32[2,24,128]{2,1,0:T(8,128)S(1)}, u32[]{:S(2)}, u32[]{:S(2)}) %collective-permute-start.14) | collective-permute-done | bytes 24608 | tf_op jit(solution)/shard_map/ppermute | solution.py:289
  53.1 23.1 %grads.1 = (f32[128,768]{1,0:T(8,128)S(1)}, bf16[128,768]{1,0:T(8,128)(2,1)S(1)}, bf16[128,768]{1,0:T(8,128)(2,1)S(1)}, bf16[128,768]{1,0:T(8,128)(2,1)S(1)}, bf...) custom-call(s32[982]{0:T(1024)S(1)} %pad_add_fusion.2.meta, ...), custom_call_target="tpu_custom_call" | custom-call | tf_op jit(solution)/shard_map/grads/pallas_call | solution.py:266
  76.2 2.9 %collective-permute-done.18 = bf16[4,4,128,256]{3,2,1,0:T(8,128)(2,1)S(1)} collective-permute-done((bf16[4,4,128,256]{3,2,1,0:T(8,128)(2,1)}, bf16[4,4,128,256]{3,2,1,0:T(8,128)(2,1)S(1)}, u32[]{:S(2)}, u32[]{:S(2)}) %collective-permute-start.18) | collective-permute-done | bytes 1048608 | tf_op jit(solution)/shard_map/ppermute | solution.py:289
  79.3 3.5 %collective-permute-start.19 = (bf16[4,128,256]{2,1,0:T(8,128)(2,1)S(1)}, bf16[4,128,256]{2,1,0:T(8,128)(2,1)S(1)}, u32[]{:S(2)}, u32[]{:S(2)}) collective-permute-start(bf16[4,128,256]{2,1,0:T(8,128)(2,1)S(1)} %get-tuple-element.43), channel_id=1, source_target_pairs={{0,20},{1,21},{2,22},{3,23},{4,16},{5,17},{6,18},{7,19},{8,104},{9... | collective-permute-start | bytes 786440 | tf_op jit(solution)/shard_map/ppermute | solution.py:289
  83.8 1.8 %collective-permute-start.15 = (bf16[128,768]{1,0:T(8,128)(2,1)S(1)}, bf16[128,768]{1,0:T(8,128)(2,1)S(1)}, u32[]{:S(2)}, u32[]{:S(2)}) collective-permute-start(bf16[128,768]{1,0:T(8,128)(2,1)S(1)} %get-tuple-element.25), channel_id=1, source_target_pairs={{0,3},{1,0},{2,1},{3,2},{4,7},{5,4},{6,5},{7,6},{8,11},{9,8},{10,9... | collective-permute-start | bytes 589832 | tf_op jit(solution)/shard_map/ppermute | solution.py:289
  85.8 3.7 %collective-permute-done.19 = bf16[4,128,256]{2,1,0:T(8,128)(2,1)S(1)} collective-permute-done((bf16[4,128,256]{2,1,0:T(8,128)(2,1)S(1)}, bf16[4,128,256]{2,1,0:T(8,128)(2,1)S(1)}, u32[]{:S(2)}, u32[]{:S(2)}) %collective-permute-start.19) | collective-permute-done | bytes 262176 | tf_op jit(solution)/shard_map/ppermute | solution.py:289
  89.5 1.2 %collective-permute-start.17 = (bf16[128,768]{1,0:T(8,128)(2,1)S(1)}, bf16[128,768]{1,0:T(8,128)(2,1)S(1)}, u32[]{:S(2)}, u32[]{:S(2)}) collective-permute-start(bf16[128,768]{1,0:T(8,128)(2,1)S(1)} %get-tuple-element.27), channel_id=1, source_target_pairs={{0,2},{1,3},{2,0},{3,1},{4,6},{5,7},{6,4},{7,5},{8,10},{9,11},{10,... | collective-permute-start | bytes 589832 | tf_op jit(solution)/shard_map/ppermute | solution.py:289
  90.8 2.6 %collective-permute-done.20 = bf16[4,128,256]{2,1,0:T(8,128)(2,1)S(1)} collective-permute-done((bf16[4,128,256]{2,1,0:T(8,128)(2,1)S(1)}, bf16[4,128,256]{2,1,0:T(8,128)(2,1)S(1)}, u32[]{:S(2)}, u32[]{:S(2)}) %collective-permute-start.20) | collective-permute-done | bytes 262176 | tf_op jit(solution)/shard_map/ppermute | solution.py:289
  93.7 1.4 %collective-permute-start.24 = (bf16[128,256]{1,0:T(8,128)(2,1)S(1)}, bf16[128,256]{1,0:T(8,128)(2,1)S(1)}, u32[]{:S(2)}, u32[]{:S(2)}) collective-permute-start(bf16[128,256]{1,0:T(8,128)(2,1)S(1)} %get-tuple-element.47), channel_id=1, source_target_pairs={{0,64},{1,65},{2,66},{3,67},{4,68},{5,69},{6,70},{7,71},{8,12},{9,... | collective-permute-start | bytes 196616 | tf_op jit(solution)/shard_map/ppermute | solution.py:289
  95.7 1.3 %collective-permute-done.16 = bf16[128,768]{1,0:T(8,128)(2,1)S(1)} collective-permute-done((bf16[128,768]{1,0:T(8,128)(2,1)S(1)}, bf16[128,768]{1,0:T(8,128)(2,1)S(1)}, u32[]{:S(2)}, u32[]{:S(2)}) %collective-permute-start.16) | collective-permute-done | bytes 196640 | tf_op jit(solution)/shard_map/ppermute | solution.py:289
  98.0 1.6 %collective-permute-done.24 = bf16[128,256]{1,0:T(8,128)(2,1)S(1)} collective-permute-done((bf16[128,256]{1,0:T(8,128)(2,1)S(1)}, bf16[128,256]{1,0:T(8,128)(2,1)S(1)}, u32[]{:S(2)}, u32[]{:S(2)}) %collective-permute-start.24) | collective-permute-done | bytes 65568 | tf_op jit(solution)/shard_map/ppermute | solution.py:289
  99.6 1.1 %collective-permute-done.23 = bf16[128,256]{1,0:T(8,128)(2,1)S(1)} collective-permute-done((bf16[128,256]{1,0:T(8,128)(2,1)S(1)}, bf16[128,256]{1,0:T(8,128)(2,1)S(1)}, u32[]{:S(2)}, u32[]{:S(2)}) %collective-permute-start.23) | collective-permute-done | bytes 65568 | tf_op jit(solution)/shard_map/ppermute | solution.py:289
  (105 shorter events, 14.4 us)
Async XLA Ops:
  1.4 9.2 %collective-permute-start.2 = (bf16[1,128,256]{2,1,0:T(8,128)(2,1)S(1)}, bf16[1,128,256]{2,1,0:T(8,128)(2,1)S(1)}, u32[]{:S(2)}, u32[]{:S(2)}) collective-permute-start(bf16[1,128,256]{2,1,0:T(8,128)(2,1)S(1)} %maximum_bitcast_fusion), channel_id=1, source_target_pairs={{0,64},{1,65},{2,66},{3,67},{4,68},{5,69},{6,70},{7,71},{8,12},{9,... | collective-permute-start | bytes 196616 | tf_op jit(solution)/shard_map/ppermute | solution.py:289
  4.8 5.8 %collective-permute-start.1 = (bf16[1,128,256]{2,1,0:T(8,128)(2,1)S(1)}, bf16[1,128,256]{2,1,0:T(8,128)(2,1)S(1)}, u32[]{:S(2)}, u32[]{:S(2)}) collective-permute-start(bf16[1,128,256]{2,1,0:T(8,128)(2,1)S(1)} %maximum_bitcast_fusion), channel_id=1, source_target_pairs={{0,96},{1,97},{2,98},{3,99},{4,100},{5,101},{6,102},{7,103},{8,28}... | collective-permute-start | bytes 196616 | tf_op jit(solution)/shard_map/ppermute | solution.py:289
  5.8 5.5 %collective-permute-start = (bf16[1,128,256]{2,1,0:T(8,128)(2,1)S(1)}, bf16[1,128,256]{2,1,0:T(8,128)(2,1)S(1)}, u32[]{:S(2)}, u32[]{:S(2)}) collective-permute-start(bf16[1,128,256]{2,1,0:T(8,128)(2,1)S(1)} %maximum_bitcast_fusion), channel_id=1, source_target_pairs={{0,32},{1,33},{2,34},{3,35},{4,36},{5,37},{6,38},{7,39},{8,24},{9,... | collective-permute-start | bytes 196616 | tf_op jit(solution)/shard_map/ppermute | solution.py:289
  7.8 16.8 %collective-permute-start.5 = (bf16[128,1536]{1,0:T(8,128)(2,1)S(1)}, bf16[128,1536]{1,0:T(8,128)(2,1)S(1)}, u32[]{:S(2)}, u32[]{:S(2)}) collective-permute-start(bf16[128,1536]{1,0:T(8,128)(2,1)S(1)} %constant_dynamic-update-slice_fusion.6.refs_0_), channel_id=1, source_target_pairs={{0,3},{1,0},{2,1},{3,2},{4,7},{5,4},{6,5},{7,6},{8,11},{9,8},{10,9... | collective-permute-start | bytes 1179656 | tf_op jit(solution)/shard_map/ppermute | solution.py:289
  10.6 14.1 %collective-permute-start.4 = (bf16[128,1536]{1,0:T(8,128)(2,1)S(1)}, bf16[128,1536]{1,0:T(8,128)(2,1)S(1)}, u32[]{:S(2)}, u32[]{:S(2)}) collective-permute-start(bf16[128,1536]{1,0:T(8,128)(2,1)S(1)} %constant_dynamic-update-slice_fusion.6.refs_0_), channel_id=1, source_target_pairs={{0,1},{1,2},{2,3},{3,0},{4,5},{5,6},{6,7},{7,4},{8,9},{9,10},{10,1... | collective-permute-start | bytes 1179656 | tf_op jit(solution)/shard_map/ppermute | solution.py:289
  11.3 8.5 %collective-permute-start.3 = (bf16[4,128,256]{2,1,0:T(8,128)(2,1)S(1)}, bf16[4,128,256]{2,1,0:T(8,128)(2,1)S(1)}, u32[]{:S(2)}, u32[]{:S(2)}) collective-permute-start(bf16[4,128,256]{2,1,0:T(8,128)(2,1)S(1)} %pad_maximum_fusion.refs_3_.refs_1_.refs_4_), channel_id=1, source_target_pairs={{0,16},{1,17},{2,18},{3,19},{4,20},{5,21},{6,22},{7,23},{8,40},{9,... | collective-permute-start | bytes 786440 | tf_op jit(solution)/shard_map/ppermute | solution.py:289
  13.6 10.5 %collective-permute-start.8 = (bf16[4,128,256]{2,1,0:T(8,128)(2,1)S(1)}, bf16[4,128,256]{2,1,0:T(8,128)(2,1)S(1)}, u32[]{:S(2)}, u32[]{:S(2)}) collective-permute-start(bf16[4,128,256]{2,1,0:T(8,128)(2,1)S(1)} %pad_maximum_fusion.refs_3_.refs_1_.refs_4_), channel_id=1, source_target_pairs={{0,4},{1,5},{2,6},{3,7},{4,0},{5,1},{6,2},{7,3},{8,72},{9,73},{10,... | collective-permute-start | bytes 786440 | tf_op jit(solution)/shard_map/ppermute | solution.py:289
  17.2 6.9 %collective-permute-start.7 = (bf16[4,128,256]{2,1,0:T(8,128)(2,1)S(1)}, bf16[4,128,256]{2,1,0:T(8,128)(2,1)S(1)}, u32[]{:S(2)}, u32[]{:S(2)}) collective-permute-start(bf16[4,128,256]{2,1,0:T(8,128)(2,1)S(1)} %pad_maximum_fusion.refs_3_.refs_1_.refs_4_), channel_id=1, source_target_pairs={{0,20},{1,21},{2,22},{3,23},{4,16},{5,17},{6,18},{7,19},{8,104},{9... | collective-permute-start | bytes 786440 | tf_op jit(solution)/shard_map/ppermute | solution.py:289
  23.1 6.2 %collective-permute-start.9 = (bf16[4,128,256]{2,1,0:T(8,128)(2,1)S(1)}, bf16[4,128,256]{2,1,0:T(8,128)(2,1)S(1)}, u32[]{:S(2)}, u32[]{:S(2)}) collective-permute-start(bf16[4,128,256]{2,1,0:T(8,128)(2,1)S(1)} %pad_maximum_fusion.refs_3_.refs_1_.refs_4_), channel_id=1, source_target_pairs={{0,8},{1,9},{2,10},{3,11},{4,12},{5,13},{6,14},{7,15},{8,0},{9,1},... | collective-permute-start | bytes 786440 | tf_op jit(solution)/shard_map/ppermute | solution.py:289
  24.1 5.3 %collective-permute-start.10 = (bf16[4,128,256]{2,1,0:T(8,128)(2,1)S(1)}, bf16[4,128,256]{2,1,0:T(8,128)(2,1)S(1)}, u32[]{:S(2)}, u32[]{:S(2)}) collective-permute-start(bf16[4,128,256]{2,1,0:T(8,128)(2,1)S(1)} %collective-permute-done.3.refs_4_.refs_2_.refs_5_), channel_id=1, source_target_pairs={{0,8},{1,9},{2,10},{3,11},{4,12},{5,13},{6,14},{7,15},{8,0},{9,1},... | collective-permute-start | bytes 786440 | tf_op jit(solution)/shard_map/ppermute | solution.py:289
  24.1 5.2 %collective-permute-start.12 = (bf16[4,128,256]{2,1,0:T(8,128)(2,1)S(1)}, bf16[4,128,256]{2,1,0:T(8,128)(2,1)S(1)}, u32[]{:S(2)}, u32[]{:S(2)}) collective-permute-start(bf16[4,128,256]{2,1,0:T(8,128)(2,1)S(1)} %collective-permute-done.8.refs_6_.refs_4_.refs_7_), channel_id=1, source_target_pairs={{0,8},{1,9},{2,10},{3,11},{4,12},{5,13},{6,14},{7,15},{8,0},{9,1},... | collective-permute-start | bytes 786440 | tf_op jit(solution)/shard_map/ppermute | solution.py:289
  24.6 4.7 %collective-permute-start.11 = (bf16[4,128,256]{2,1,0:T(8,128)(2,1)S(1)}, bf16[4,128,256]{2,1,0:T(8,128)(2,1)S(1)}, u32[]{:S(2)}, u32[]{:S(2)}) collective-permute-start(bf16[4,128,256]{2,1,0:T(8,128)(2,1)S(1)} %collective-permute-done.7.refs_5_.refs_3_.refs_6_), channel_id=1, source_target_pairs={{0,8},{1,9},{2,10},{3,11},{4,12},{5,13},{6,14},{7,15},{8,0},{9,1},... | collective-permute-start | bytes 786440 | tf_op jit(solution)/shard_map/ppermute | solution.py:289
  24.7 14.4 %collective-permute-start.6 = (bf16[128,1536]{1,0:T(8,128)(2,1)S(1)}, bf16[128,1536]{1,0:T(8,128)(2,1)}, u32[]{:S(2)}, u32[]{:S(2)}) collective-permute-start(bf16[128,1536]{1,0:T(8,128)(2,1)S(1)} %constant_dynamic-update-slice_fusion.6.refs_0_), channel_id=1, source_target_pairs={{0,2},{1,3},{2,0},{3,1},{4,6},{5,7},{6,4},{7,5},{8,10},{9,11},{10,... | collective-permute-start | bytes 1179656 | tf_op jit(solution)/shard_map/ppermute | solution.py:289
  43.6 4.1 %collective-permute-start.13 = (f32[2,24,128]{2,1,0:T(8,128)S(1)}, f32[2,24,128]{2,1,0:T(8,128)S(1)}, u32[]{:S(2)}, u32[]{:S(2)}) collective-permute-start(f32[2,24,128]{2,1,0:T(8,128)S(1)} %stats_far.1), channel_id=1, source_target_pairs={{0,1},{1,0},{2,3},{3,2},{4,5},{5,4},{6,7},{7,6},{8,9},{9,8},{10,11... | collective-permute-start | bytes 73736 | tf_op jit(solution)/shard_map/ppermute | solution.py:289
  47.7 5.4 %collective-permute-start.14 = (f32[2,24,128]{2,1,0:T(8,128)S(1)}, f32[2,24,128]{2,1,0:T(8,128)S(1)}, u32[]{:S(2)}, u32[]{:S(2)}) collective-permute-start(f32[2,24,128]{2,1,0:T(8,128)S(1)} %pad_maximum_fusion.1.st0), channel_id=1, source_target_pairs={{0,2},{1,3},{2,0},{3,1},{4,6},{5,7},{6,4},{7,5},{8,10},{9,11},{10,... | collective-permute-start | bytes 73736 | tf_op jit(solution)/shard_map/ppermute | solution.py:289
  79.3 10.2 %collective-permute-start.19 = (bf16[4,128,256]{2,1,0:T(8,128)(2,1)S(1)}, bf16[4,128,256]{2,1,0:T(8,128)(2,1)S(1)}, u32[]{:S(2)}, u32[]{:S(2)}) collective-permute-start(bf16[4,128,256]{2,1,0:T(8,128)(2,1)S(1)} %get-tuple-element.43), channel_id=1, source_target_pairs={{0,20},{1,21},{2,22},{3,23},{4,16},{5,17},{6,18},{7,19},{8,104},{9... | collective-permute-start | bytes 786440 | tf_op jit(solution)/shard_map/ppermute | solution.py:289
  82.8 8.0 %collective-permute-start.21 = (bf16[4,128,256]{2,1,0:T(8,128)(2,1)S(1)}, bf16[4,128,256]{2,1,0:T(8,128)(2,1)S(1)}, u32[]{:S(2)}, u32[]{:S(2)}) collective-permute-start(bf16[4,128,256]{2,1,0:T(8,128)(2,1)S(1)} %get-tuple-element.44), channel_id=1, source_target_pairs={{0,4},{1,5},{2,6},{3,7},{4,0},{5,1},{6,2},{7,3},{8,72},{9,73},{10,... | collective-permute-start | bytes 786440 | tf_op jit(solution)/shard_map/ppermute | solution.py:289
  83.0 10.4 %collective-permute-start.20 = (bf16[4,128,256]{2,1,0:T(8,128)(2,1)S(1)}, bf16[4,128,256]{2,1,0:T(8,128)(2,1)S(1)}, u32[]{:S(2)}, u32[]{:S(2)}) collective-permute-start(bf16[4,128,256]{2,1,0:T(8,128)(2,1)S(1)} %get-tuple-element.45), channel_id=1, source_target_pairs={{0,16},{1,17},{2,18},{3,19},{4,20},{5,21},{6,22},{7,23},{8,40},{9,... | collective-permute-start | bytes 786440 | tf_op jit(solution)/shard_map/ppermute | solution.py:289
  83.8 11.3 %collective-permute-start.15 = (bf16[128,768]{1,0:T(8,128)(2,1)S(1)}, bf16[128,768]{1,0:T(8,128)(2,1)S(1)}, u32[]{:S(2)}, u32[]{:S(2)}) collective-permute-start(bf16[128,768]{1,0:T(8,128)(2,1)S(1)} %get-tuple-element.25), channel_id=1, source_target_pairs={{0,3},{1,0},{2,1},{3,2},{4,7},{5,4},{6,5},{7,6},{8,11},{9,8},{10,9... | collective-permute-start | bytes 589832 | tf_op jit(solution)/shard_map/ppermute | solution.py:289
  85.6 11.4 %collective-permute-start.16 = (bf16[128,768]{1,0:T(8,128)(2,1)S(1)}, bf16[128,768]{1,0:T(8,128)(2,1)S(1)}, u32[]{:S(2)}, u32[]{:S(2)}) collective-permute-start(bf16[128,768]{1,0:T(8,128)(2,1)S(1)} %get-tuple-element.26), channel_id=1, source_target_pairs={{0,1},{1,2},{2,3},{3,0},{4,5},{5,6},{6,7},{7,4},{8,9},{9,10},{10,1... | collective-permute-start | bytes 589832 | tf_op jit(solution)/shard_map/ppermute | solution.py:289
  89.5 7.5 %collective-permute-start.17 = (bf16[128,768]{1,0:T(8,128)(2,1)S(1)}, bf16[128,768]{1,0:T(8,128)(2,1)S(1)}, u32[]{:S(2)}, u32[]{:S(2)}) collective-permute-start(bf16[128,768]{1,0:T(8,128)(2,1)S(1)} %get-tuple-element.27), channel_id=1, source_target_pairs={{0,2},{1,3},{2,0},{3,1},{4,6},{5,7},{6,4},{7,5},{8,10},{9,11},{10,... | collective-permute-start | bytes 589832 | tf_op jit(solution)/shard_map/ppermute | solution.py:289
  93.6 4.3 %collective-permute-start.22 = (bf16[128,256]{1,0:T(8,128)(2,1)S(1)}, bf16[128,256]{1,0:T(8,128)(2,1)S(1)}, u32[]{:S(2)}, u32[]{:S(2)}) collective-permute-start(bf16[128,256]{1,0:T(8,128)(2,1)S(1)} %get-tuple-element.46), channel_id=1, source_target_pairs={{0,96},{1,97},{2,98},{3,99},{4,100},{5,101},{6,102},{7,103},{8,28}... | collective-permute-start | bytes 196616 | tf_op jit(solution)/shard_map/ppermute | solution.py:289
  93.7 5.8 %collective-permute-start.24 = (bf16[128,256]{1,0:T(8,128)(2,1)S(1)}, bf16[128,256]{1,0:T(8,128)(2,1)S(1)}, u32[]{:S(2)}, u32[]{:S(2)}) collective-permute-start(bf16[128,256]{1,0:T(8,128)(2,1)S(1)} %get-tuple-element.47), channel_id=1, source_target_pairs={{0,64},{1,65},{2,66},{3,67},{4,68},{5,69},{6,70},{7,71},{8,12},{9,... | collective-permute-start | bytes 196616 | tf_op jit(solution)/shard_map/ppermute | solution.py:289
  95.1 5.6 %collective-permute-start.23 = (bf16[128,256]{1,0:T(8,128)(2,1)S(1)}, bf16[128,256]{1,0:T(8,128)(2,1)S(1)}, u32[]{:S(2)}, u32[]{:S(2)}) collective-permute-start(bf16[128,256]{1,0:T(8,128)(2,1)S(1)} %get-tuple-element.48), channel_id=1, source_target_pairs={{0,32},{1,33},{2,34},{3,35},{4,36},{5,37},{6,38},{7,39},{8,24},{9,... | collective-permute-start | bytes 196616 | tf_op jit(solution)/shard_map/ppermute | solution.py:289
  (4 other events, 16.1 us)

commit v11 on v10

--- a/solution.py
+++ b/solution.py
@@ -355,7 +355,8 @@
     number = jnp.tile(jnp.arange(GROUPS, dtype=i32), 2)
     group = jnp.sum(inside * number, axis=2)
     block = jnp.sum(inside * (t[None, :, None] - (begin - first)[:, None, :]), axis=2)
-    group = jnp.where(t[None] < end[:, -1:], group, jnp.array([[12], [9], [3]], i32))
+    which = jnp.arange(3, dtype=i32)[:, None]
+    group = jnp.where(t[None] < end[:, -1:], group, jnp.where(which == ALL, 12, jnp.where(which == NEAR, 9, 3)))
     lists = jnp.concatenate([units, canon, end[:, GROUPS - 1 : GROUPS], end[:, -1:], group, block], axis=1)
     return jnp.concatenate([rank(arrived, arrived), lists.reshape(-1)]).astype(i32), lim
 

time: 102 us -> 101 us (level)
  waiting for transfers between devices: 23 us -> 21.6 us
  Pallas kernels: 37.3 us -> 38.6 us
    ppermute x25, waiting for transfers between devices: 23 us -> 21.6 us  [permute(): return lax.ppermute(a, AXES, pairs)]
where the time goes in v11:
time: 101 us
  Pallas kernels  38.6 us (38%)
  starting transfers between devices  32 us (32%)
  waiting for transfers between devices  21.6 us (21%)
  other arithmetic  4.65 us (5%)
  local copies, waits for them, and re-layouts  3.09 us (3%)
    ppermute x25, starting transfers between devices, permute(): return lax.ppermute(a, AXES, pairs)  32 us
    pallas_call x1, Pallas kernels, grads(): pl.pallas_call(grads_kernel, out_shape=dq + dkv, in_specs=[SM] + [VM] * 1...  23.8 us
    ppermute x25, waiting for transfers between devices, permute(): return lax.ppermute(a, AXES, pairs)  21.6 us
    pallas_call x2, Pallas kernels, stats(): pl.pallas_call(functools.partial(stats_kernel, which, n), out_shape=jax.S...  14.8 us
  transfers between devices with their start and end apart: 25, of which 12 were waited for; matrix products, arithmetic and copies ran while one was open for 6% of the time, Pallas kernels for 10%

profile of v11, /device:TPU:0, one launch (start us, length us, event | category | flops | bytes accessed | tf_op | source)
XLA Modules:
  0.0 100.8 jit_solution(17783339925615959405)
XLA Ops:
  1.4 3.4 %collective-permute-start.2 = (bf16[1,128,256]{2,1,0:T(8,128)(2,1)S(1)}, bf16[1,128,256]{2,1,0:T(8,128)(2,1)S(1)}, u32[]{:S(2)}, u32[]{:S(2)}) collective-permute-start(bf16[1,128,256]{2,1,0:T(8,128)(2,1)S(1)} %maximum_bitcast_fusion), channel_id=1, source_target_pairs={{0,64},{1,65},{2,66},{3,67},{4,68},{5,69},{6,70},{7,71},{8,12},{9,... | collective-permute-start | bytes 196616 | tf_op jit(solution)/shard_map/ppermute | solution.py:289
  4.8 1.1 %collective-permute-start.1 = (bf16[1,128,256]{2,1,0:T(8,128)(2,1)S(1)}, bf16[1,128,256]{2,1,0:T(8,128)(2,1)S(1)}, u32[]{:S(2)}, u32[]{:S(2)}) collective-permute-start(bf16[1,128,256]{2,1,0:T(8,128)(2,1)S(1)} %maximum_bitcast_fusion), channel_id=1, source_target_pairs={{0,96},{1,97},{2,98},{3,99},{4,100},{5,101},{6,102},{7,103},{8,28}... | collective-permute-start | bytes 196616 | tf_op jit(solution)/shard_map/ppermute | solution.py:289
  7.8 2.8 %collective-permute-start.5 = (bf16[128,1536]{1,0:T(8,128)(2,1)S(1)}, bf16[128,1536]{1,0:T(8,128)(2,1)S(1)}, u32[]{:S(2)}, u32[]{:S(2)}) collective-permute-start(bf16[128,1536]{1,0:T(8,128)(2,1)S(1)} %constant_dynamic-update-slice_fusion.6.refs_0_), channel_id=1, source_target_pairs={{0,3},{1,0},{2,1},{3,2},{4,7},{5,4},{6,5},{7,6},{8,11},{9,8},{10,9... | collective-permute-start | bytes 1179656 | tf_op jit(solution)/shard_map/ppermute | solution.py:289
  11.3 2.0 %collective-permute-start.3 = (bf16[4,128,256]{2,1,0:T(8,128)(2,1)S(1)}, bf16[4,128,256]{2,1,0:T(8,128)(2,1)S(1)}, u32[]{:S(2)}, u32[]{:S(2)}) collective-permute-start(bf16[4,128,256]{2,1,0:T(8,128)(2,1)S(1)} %pad_maximum_fusion.refs_3_.refs_1_.refs_4_), channel_id=1, source_target_pairs={{0,16},{1,17},{2,18},{3,19},{4,20},{5,21},{6,22},{7,23},{8,40},{9,... | collective-permute-start | bytes 786440 | tf_op jit(solution)/shard_map/ppermute | solution.py:289
  13.6 3.7 %collective-permute-start.8 = (bf16[4,128,256]{2,1,0:T(8,128)(2,1)S(1)}, bf16[4,128,256]{2,1,0:T(8,128)(2,1)S(1)}, u32[]{:S(2)}, u32[]{:S(2)}) collective-permute-start(bf16[4,128,256]{2,1,0:T(8,128)(2,1)S(1)} %pad_maximum_fusion.refs_3_.refs_1_.refs_4_), channel_id=1, source_target_pairs={{0,4},{1,5},{2,6},{3,7},{4,0},{5,1},{6,2},{7,3},{8,72},{9,73},{10,... | collective-permute-start | bytes 786440 | tf_op jit(solution)/shard_map/ppermute | solution.py:289
  17.2 1.0 %collective-permute-start.7 = (bf16[4,128,256]{2,1,0:T(8,128)(2,1)S(1)}, bf16[4,128,256]{2,1,0:T(8,128)(2,1)S(1)}, u32[]{:S(2)}, u32[]{:S(2)}) collective-permute-start(bf16[4,128,256]{2,1,0:T(8,128)(2,1)S(1)} %pad_maximum_fusion.refs_3_.refs_1_.refs_4_), channel_id=1, source_target_pairs={{0,20},{1,21},{2,22},{3,23},{4,16},{5,17},{6,18},{7,19},{8,104},{9... | collective-permute-start | bytes 786440 | tf_op jit(solution)/shard_map/ppermute | solution.py:289
  18.2 1.6 %collective-permute-done.3.refs_4_.refs_2_.refs_5_ = bf16[4,128,256]{2,1,0:T(8,128)(2,1)S(1)} collective-permute-done((bf16[4,128,256]{2,1,0:T(8,128)(2,1)S(1)}, bf16[4,128,256]{2,1,0:T(8,128)(2,1)S(1)}, u32[]{:S(2)}, u32[]{:S(2)}) %collective-permute-start.3) | collective-permute-done | bytes 262176 | tf_op jit(solution)/shard_map/ppermute | solution.py:289
  24.7 3.4 %collective-permute-start.6 = (bf16[128,1536]{1,0:T(8,128)(2,1)S(1)}, bf16[128,1536]{1,0:T(8,128)(2,1)}, u32[]{:S(2)}, u32[]{:S(2)}) collective-permute-start(bf16[128,1536]{1,0:T(8,128)(2,1)S(1)} %constant_dynamic-update-slice_fusion.6.refs_0_), channel_id=1, source_target_pairs={{0,2},{1,3},{2,0},{3,1},{4,6},{5,7},{6,4},{7,5},{8,10},{9,11},{10,... | collective-permute-start | bytes 1179656 | tf_op jit(solution)/shard_map/ppermute | solution.py:289
  28.7 9.7 %stats_near.1.refs_9_ = f32[2,24,128]{2,1,0:T(8,128)S(1)} custom-call(s32[982]{0:T(1024)S(1)} %pad_add_fusion.2.meta, s32[3,16,256]{2,1,0:T(8,128)S(1)} %concatenate.34.lim, bf16[128,1536]{1,0:T(8,128)(2,1)S(1)} %constant_dynamic-update-slice_fusion.6.refs_0_, bf16[128,1536]{1,0:T(8,128)(2,1)S(1)} %collective-permute-done.4.refs_1_, ...), custom_call_target="tpu_custom_call" | custom-call | flops 3000000 | bytes 100000 | tf_op jit(solution)/shard_map/stats_near/pallas_call | solution.py:250
  38.4 5.1 %stats_far.1 = f32[2,24,128]{2,1,0:T(8,128)S(1)} custom-call(s32[982]{0:T(1024)S(1)} %pad_add_fusion.2.meta, s32[3,16,256]{2,1,0:T(8,128)S(1)} %concatenate.34.lim, bf16[128,1536]{1,0:T(8,128)(2,1)} %collective-permute-done.6.refs_0_.refs_3_, bf16[4,128,256]{2,1,0:T(8,128)(2,1)S(1)} %pad_maximum_fusion.refs_3_.refs_1_.refs_4_, ...), custom_call_target="tpu_custom_call" | custom-call | flops 1000000 | bytes 100000 | tf_op jit(solution)/shard_map/stats_far/pallas_call | solution.py:250
  43.5 1.2 %collective-permute-start.13 = (f32[2,24,128]{2,1,0:T(8,128)S(1)}, f32[2,24,128]{2,1,0:T(8,128)S(1)}, u32[]{:S(2)}, u32[]{:S(2)}) collective-permute-start(f32[2,24,128]{2,1,0:T(8,128)S(1)} %stats_far.1), channel_id=1, source_target_pairs={{0,1},{1,0},{2,3},{3,2},{4,5},{5,4},{6,7},{7,6},{8,9},{9,8},{10,11... | collective-permute-start | bytes 73736 | tf_op jit(solution)/shard_map/ppermute | solution.py:289
  44.7 2.9 %collective-permute-done.13 = f32[2,24,128]{2,1,0:T(8,128)S(1)} collective-permute-done((f32[2,24,128]{2,1,0:T(8,128)S(1)}, f32[2,24,128]{2,1,0:T(8,128)S(1)}, u32[]{:S(2)}, u32[]{:S(2)}) %collective-permute-start.13) | collective-permute-done | bytes 24608 | tf_op jit(solution)/shard_map/ppermute | solution.py:289
  47.7 2.5 %collective-permute-start.14 = (f32[2,24,128]{2,1,0:T(8,128)S(1)}, f32[2,24,128]{2,1,0:T(8,128)S(1)}, u32[]{:S(2)}, u32[]{:S(2)}) collective-permute-start(f32[2,24,128]{2,1,0:T(8,128)S(1)} %pad_maximum_fusion.1.st0), channel_id=1, source_target_pairs={{0,2},{1,3},{2,0},{3,1},{4,6},{5,7},{6,4},{7,5},{8,10},{9,11},{10,... | collective-permute-start | bytes 73736 | tf_op jit(solution)/shard_map/ppermute | solution.py:289
  50.2 2.9 %collective-permute-done.14.st1 = f32[2,24,128]{2,1,0:T(8,128)S(1)} collective-permute-done((f32[2,24,128]{2,1,0:T(8,128)S(1)}, f32[2,24,128]{2,1,0:T(8,128)S(1)}, u32[]{:S(2)}, u32[]{:S(2)}) %collective-permute-start.14) | collective-permute-done | bytes 24608 | tf_op jit(solution)/shard_map/ppermute | solution.py:289
  53.1 23.8 %grads.1 = (f32[128,768]{1,0:T(8,128)S(1)}, bf16[128,768]{1,0:T(8,128)(2,1)S(1)}, bf16[128,768]{1,0:T(8,128)(2,1)S(1)}, bf16[128,768]{1,0:T(8,128)(2,1)S(1)}, bf...) custom-call(s32[982]{0:T(1024)S(1)} %pad_add_fusion.2.meta, ...), custom_call_target="tpu_custom_call" | custom-call | tf_op jit(solution)/shard_map/grads/pallas_call | solution.py:266
  76.9 2.9 %collective-permute-done.18 = bf16[4,4,128,256]{3,2,1,0:T(8,128)(2,1)S(1)} collective-permute-done((bf16[4,4,128,256]{3,2,1,0:T(8,128)(2,1)}, bf16[4,4,128,256]{3,2,1,0:T(8,128)(2,1)S(1)}, u32[]{:S(2)}, u32[]{:S(2)}) %collective-permute-start.18) | collective-permute-done | bytes 1048608 | tf_op jit(solution)/shard_map/ppermute | solution.py:289
  80.0 2.5 %collective-permute-start.19 = (bf16[4,128,256]{2,1,0:T(8,128)(2,1)S(1)}, bf16[4,128,256]{2,1,0:T(8,128)(2,1)S(1)}, u32[]{:S(2)}, u32[]{:S(2)}) collective-permute-start(bf16[4,128,256]{2,1,0:T(8,128)(2,1)S(1)} %get-tuple-element.43), channel_id=1, source_target_pairs={{0,20},{1,21},{2,22},{3,23},{4,16},{5,17},{6,18},{7,19},{8,104},{9... | collective-permute-start | bytes 786440 | tf_op jit(solution)/shard_map/ppermute | solution.py:289
  83.4 2.2 %collective-permute-start.15 = (bf16[128,768]{1,0:T(8,128)(2,1)S(1)}, bf16[128,768]{1,0:T(8,128)(2,1)S(1)}, u32[]{:S(2)}, u32[]{:S(2)}) collective-permute-start(bf16[128,768]{1,0:T(8,128)(2,1)S(1)} %get-tuple-element.25), channel_id=1, source_target_pairs={{0,3},{1,0},{2,1},{3,2},{4,7},{5,4},{6,5},{7,6},{8,11},{9,8},{10,9... | collective-permute-start | bytes 589832 | tf_op jit(solution)/shard_map/ppermute | solution.py:289
  85.6 3.6 %collective-permute-done.19 = bf16[4,128,256]{2,1,0:T(8,128)(2,1)S(1)} collective-permute-done((bf16[4,128,256]{2,1,0:T(8,128)(2,1)S(1)}, bf16[4,128,256]{2,1,0:T(8,128)(2,1)S(1)}, u32[]{:S(2)}, u32[]{:S(2)}) %collective-permute-start.19) | collective-permute-done | bytes 262176 | tf_op jit(solution)/shard_map/ppermute | solution.py:289
  89.2 1.5 %collective-permute-start.17 = (bf16[128,768]{1,0:T(8,128)(2,1)S(1)}, bf16[128,768]{1,0:T(8,128)(2,1)S(1)}, u32[]{:S(2)}, u32[]{:S(2)}) collective-permute-start(bf16[128,768]{1,0:T(8,128)(2,1)S(1)} %get-tuple-element.27), channel_id=1, source_target_pairs={{0,2},{1,3},{2,0},{3,1},{4,6},{5,7},{6,4},{7,5},{8,10},{9,11},{10,... | collective-permute-start | bytes 589832 | tf_op jit(solution)/shard_map/ppermute | solution.py:289
  90.7 2.2 %collective-permute-done.20 = bf16[4,128,256]{2,1,0:T(8,128)(2,1)S(1)} collective-permute-done((bf16[4,128,256]{2,1,0:T(8,128)(2,1)S(1)}, bf16[4,128,256]{2,1,0:T(8,128)(2,1)S(1)}, u32[]{:S(2)}, u32[]{:S(2)}) %collective-permute-start.20) | collective-permute-done | bytes 262176 | tf_op jit(solution)/shard_map/ppermute | solution.py:289
  93.5 1.7 %collective-permute-start.23 = (bf16[128,256]{1,0:T(8,128)(2,1)S(1)}, bf16[128,256]{1,0:T(8,128)(2,1)S(1)}, u32[]{:S(2)}, u32[]{:S(2)}) collective-permute-start(bf16[128,256]{1,0:T(8,128)(2,1)S(1)} %get-tuple-element.48), channel_id=1, source_target_pairs={{0,32},{1,33},{2,34},{3,35},{4,36},{5,37},{6,38},{7,39},{8,24},{9,... | collective-permute-start | bytes 196616 | tf_op jit(solution)/shard_map/ppermute | solution.py:289
  95.2 1.2 %collective-permute-done.17 = bf16[128,768]{1,0:T(8,128)(2,1)S(1)} collective-permute-done((bf16[128,768]{1,0:T(8,128)(2,1)S(1)}, bf16[128,768]{1,0:T(8,128)(2,1)S(1)}, u32[]{:S(2)}, u32[]{:S(2)}) %collective-permute-start.17) | collective-permute-done | bytes 196640 | tf_op jit(solution)/shard_map/ppermute | solution.py:289
  97.4 1.8 %collective-permute-done.24 = bf16[128,256]{1,0:T(8,128)(2,1)S(1)} collective-permute-done((bf16[128,256]{1,0:T(8,128)(2,1)S(1)}, bf16[128,256]{1,0:T(8,128)(2,1)S(1)}, u32[]{:S(2)}, u32[]{:S(2)}) %collective-permute-start.24) | collective-permute-done | bytes 65568 | tf_op jit(solution)/shard_map/ppermute | solution.py:289
  (104 shorter events, 13.3 us)
Async XLA Ops:
  1.4 9.2 %collective-permute-start.2 = (bf16[1,128,256]{2,1,0:T(8,128)(2,1)S(1)}, bf16[1,128,256]{2,1,0:T(8,128)(2,1)S(1)}, u32[]{:S(2)}, u32[]{:S(2)}) collective-permute-start(bf16[1,128,256]{2,1,0:T(8,128)(2,1)S(1)} %maximum_bitcast_fusion), channel_id=1, source_target_pairs={{0,64},{1,65},{2,66},{3,67},{4,68},{5,69},{6,70},{7,71},{8,12},{9,... | collective-permute-start | bytes 196616 | tf_op jit(solution)/shard_map/ppermute | solution.py:289
  4.8 5.9 %collective-permute-start.1 = (bf16[1,128,256]{2,1,0:T(8,128)(2,1)S(1)}, bf16[1,128,256]{2,1,0:T(8,128)(2,1)S(1)}, u32[]{:S(2)}, u32[]{:S(2)}) collective-permute-start(bf16[1,128,256]{2,1,0:T(8,128)(2,1)S(1)} %maximum_bitcast_fusion), channel_id=1, source_target_pairs={{0,96},{1,97},{2,98},{3,99},{4,100},{5,101},{6,102},{7,103},{8,28}... | collective-permute-start | bytes 196616 | tf_op jit(solution)/shard_map/ppermute | solution.py:289
  5.8 5.5 %collective-permute-start = (bf16[1,128,256]{2,1,0:T(8,128)(2,1)S(1)}, bf16[1,128,256]{2,1,0:T(8,128)(2,1)S(1)}, u32[]{:S(2)}, u32[]{:S(2)}) collective-permute-start(bf16[1,128,256]{2,1,0:T(8,128)(2,1)S(1)} %maximum_bitcast_fusion), channel_id=1, source_target_pairs={{0,32},{1,33},{2,34},{3,35},{4,36},{5,37},{6,38},{7,39},{8,24},{9,... | collective-permute-start | bytes 196616 | tf_op jit(solution)/shard_map/ppermute | solution.py:289
  7.8 16.8 %collective-permute-start.5 = (bf16[128,1536]{1,0:T(8,128)(2,1)S(1)}, bf16[128,1536]{1,0:T(8,128)(2,1)S(1)}, u32[]{:S(2)}, u32[]{:S(2)}) collective-permute-start(bf16[128,1536]{1,0:T(8,128)(2,1)S(1)} %constant_dynamic-update-slice_fusion.6.refs_0_), channel_id=1, source_target_pairs={{0,3},{1,0},{2,1},{3,2},{4,7},{5,4},{6,5},{7,6},{8,11},{9,8},{10,9... | collective-permute-start | bytes 1179656 | tf_op jit(solution)/shard_map/ppermute | solution.py:289
  10.6 14.1 %collective-permute-start.4 = (bf16[128,1536]{1,0:T(8,128)(2,1)S(1)}, bf16[128,1536]{1,0:T(8,128)(2,1)S(1)}, u32[]{:S(2)}, u32[]{:S(2)}) collective-permute-start(bf16[128,1536]{1,0:T(8,128)(2,1)S(1)} %constant_dynamic-update-slice_fusion.6.refs_0_), channel_id=1, source_target_pairs={{0,1},{1,2},{2,3},{3,0},{4,5},{5,6},{6,7},{7,4},{8,9},{9,10},{10,1... | collective-permute-start | bytes 1179656 | tf_op jit(solution)/shard_map/ppermute | solution.py:289
  11.3 8.5 %collective-permute-start.3 = (bf16[4,128,256]{2,1,0:T(8,128)(2,1)S(1)}, bf16[4,128,256]{2,1,0:T(8,128)(2,1)S(1)}, u32[]{:S(2)}, u32[]{:S(2)}) collective-permute-start(bf16[4,128,256]{2,1,0:T(8,128)(2,1)S(1)} %pad_maximum_fusion.refs_3_.refs_1_.refs_4_), channel_id=1, source_target_pairs={{0,16},{1,17},{2,18},{3,19},{4,20},{5,21},{6,22},{7,23},{8,40},{9,... | collective-permute-start | bytes 786440 | tf_op jit(solution)/shard_map/ppermute | solution.py:289
  13.6 10.5 %collective-permute-start.8 = (bf16[4,128,256]{2,1,0:T(8,128)(2,1)S(1)}, bf16[4,128,256]{2,1,0:T(8,128)(2,1)S(1)}, u32[]{:S(2)}, u32[]{:S(2)}) collective-permute-start(bf16[4,128,256]{2,1,0:T(8,128)(2,1)S(1)} %pad_maximum_fusion.refs_3_.refs_1_.refs_4_), channel_id=1, source_target_pairs={{0,4},{1,5},{2,6},{3,7},{4,0},{5,1},{6,2},{7,3},{8,72},{9,73},{10,... | collective-permute-start | bytes 786440 | tf_op jit(solution)/shard_map/ppermute | solution.py:289
  17.2 6.9 %collective-permute-start.7 = (bf16[4,128,256]{2,1,0:T(8,128)(2,1)S(1)}, bf16[4,128,256]{2,1,0:T(8,128)(2,1)S(1)}, u32[]{:S(2)}, u32[]{:S(2)}) collective-permute-start(bf16[4,128,256]{2,1,0:T(8,128)(2,1)S(1)} %pad_maximum_fusion.refs_3_.refs_1_.refs_4_), channel_id=1, source_target_pairs={{0,20},{1,21},{2,22},{3,23},{4,16},{5,17},{6,18},{7,19},{8,104},{9... | collective-permute-start | bytes 786440 | tf_op jit(solution)/shard_map/ppermute | solution.py:289
  23.1 5.6 %collective-permute-start.9 = (bf16[4,128,256]{2,1,0:T(8,128)(2,1)S(1)}, bf16[4,128,256]{2,1,0:T(8,128)(2,1)S(1)}, u32[]{:S(2)}, u32[]{:S(2)}) collective-permute-start(bf16[4,128,256]{2,1,0:T(8,128)(2,1)S(1)} %pad_maximum_fusion.refs_3_.refs_1_.refs_4_), channel_id=1, source_target_pairs={{0,8},{1,9},{2,10},{3,11},{4,12},{5,13},{6,14},{7,15},{8,0},{9,1},... | collective-permute-start | bytes 786440 | tf_op jit(solution)/shard_map/ppermute | solution.py:289
  24.1 4.6 %collective-permute-start.10 = (bf16[4,128,256]{2,1,0:T(8,128)(2,1)S(1)}, bf16[4,128,256]{2,1,0:T(8,128)(2,1)S(1)}, u32[]{:S(2)}, u32[]{:S(2)}) collective-permute-start(bf16[4,128,256]{2,1,0:T(8,128)(2,1)S(1)} %collective-permute-done.3.refs_4_.refs_2_.refs_5_), channel_id=1, source_target_pairs={{0,8},{1,9},{2,10},{3,11},{4,12},{5,13},{6,14},{7,15},{8,0},{9,1},... | collective-permute-start | bytes 786440 | tf_op jit(solution)/shard_map/ppermute | solution.py:289
  24.1 4.6 %collective-permute-start.12 = (bf16[4,128,256]{2,1,0:T(8,128)(2,1)S(1)}, bf16[4,128,256]{2,1,0:T(8,128)(2,1)S(1)}, u32[]{:S(2)}, u32[]{:S(2)}) collective-permute-start(bf16[4,128,256]{2,1,0:T(8,128)(2,1)S(1)} %collective-permute-done.8.refs_6_.refs_4_.refs_7_), channel_id=1, source_target_pairs={{0,8},{1,9},{2,10},{3,11},{4,12},{5,13},{6,14},{7,15},{8,0},{9,1},... | collective-permute-start | bytes 786440 | tf_op jit(solution)/shard_map/ppermute | solution.py:289
  24.6 4.1 %collective-permute-start.11 = (bf16[4,128,256]{2,1,0:T(8,128)(2,1)S(1)}, bf16[4,128,256]{2,1,0:T(8,128)(2,1)S(1)}, u32[]{:S(2)}, u32[]{:S(2)}) collective-permute-start(bf16[4,128,256]{2,1,0:T(8,128)(2,1)S(1)} %collective-permute-done.7.refs_5_.refs_3_.refs_6_), channel_id=1, source_target_pairs={{0,8},{1,9},{2,10},{3,11},{4,12},{5,13},{6,14},{7,15},{8,0},{9,1},... | collective-permute-start | bytes 786440 | tf_op jit(solution)/shard_map/ppermute | solution.py:289
  24.7 13.7 %collective-permute-start.6 = (bf16[128,1536]{1,0:T(8,128)(2,1)S(1)}, bf16[128,1536]{1,0:T(8,128)(2,1)}, u32[]{:S(2)}, u32[]{:S(2)}) collective-permute-start(bf16[128,1536]{1,0:T(8,128)(2,1)S(1)} %constant_dynamic-update-slice_fusion.6.refs_0_), channel_id=1, source_target_pairs={{0,2},{1,3},{2,0},{3,1},{4,6},{5,7},{6,4},{7,5},{8,10},{9,11},{10,... | collective-permute-start | bytes 1179656 | tf_op jit(solution)/shard_map/ppermute | solution.py:289
  43.5 4.1 %collective-permute-start.13 = (f32[2,24,128]{2,1,0:T(8,128)S(1)}, f32[2,24,128]{2,1,0:T(8,128)S(1)}, u32[]{:S(2)}, u32[]{:S(2)}) collective-permute-start(f32[2,24,128]{2,1,0:T(8,128)S(1)} %stats_far.1), channel_id=1, source_target_pairs={{0,1},{1,0},{2,3},{3,2},{4,5},{5,4},{6,7},{7,6},{8,9},{9,8},{10,11... | collective-permute-start | bytes 73736 | tf_op jit(solution)/shard_map/ppermute | solution.py:289
  47.7 5.4 %collective-permute-start.14 = (f32[2,24,128]{2,1,0:T(8,128)S(1)}, f32[2,24,128]{2,1,0:T(8,128)S(1)}, u32[]{:S(2)}, u32[]{:S(2)}) collective-permute-start(f32[2,24,128]{2,1,0:T(8,128)S(1)} %pad_maximum_fusion.1.st0), channel_id=1, source_target_pairs={{0,2},{1,3},{2,0},{3,1},{4,6},{5,7},{6,4},{7,5},{8,10},{9,11},{10,... | collective-permute-start | bytes 73736 | tf_op jit(solution)/shard_map/ppermute | solution.py:289
  80.0 9.3 %collective-permute-start.19 = (bf16[4,128,256]{2,1,0:T(8,128)(2,1)S(1)}, bf16[4,128,256]{2,1,0:T(8,128)(2,1)S(1)}, u32[]{:S(2)}, u32[]{:S(2)}) collective-permute-start(bf16[4,128,256]{2,1,0:T(8,128)(2,1)S(1)} %get-tuple-element.43), channel_id=1, source_target_pairs={{0,20},{1,21},{2,22},{3,23},{4,16},{5,17},{6,18},{7,19},{8,104},{9... | collective-permute-start | bytes 786440 | tf_op jit(solution)/shard_map/ppermute | solution.py:289
  82.5 8.2 %collective-permute-start.21 = (bf16[4,128,256]{2,1,0:T(8,128)(2,1)S(1)}, bf16[4,128,256]{2,1,0:T(8,128)(2,1)S(1)}, u32[]{:S(2)}, u32[]{:S(2)}) collective-permute-start(bf16[4,128,256]{2,1,0:T(8,128)(2,1)S(1)} %get-tuple-element.44), channel_id=1, source_target_pairs={{0,4},{1,5},{2,6},{3,7},{4,0},{5,1},{6,2},{7,3},{8,72},{9,73},{10,... | collective-permute-start | bytes 786440 | tf_op jit(solution)/shard_map/ppermute | solution.py:289
  82.5 10.4 %collective-permute-start.20 = (bf16[4,128,256]{2,1,0:T(8,128)(2,1)S(1)}, bf16[4,128,256]{2,1,0:T(8,128)(2,1)S(1)}, u32[]{:S(2)}, u32[]{:S(2)}) collective-permute-start(bf16[4,128,256]{2,1,0:T(8,128)(2,1)S(1)} %get-tuple-element.45), channel_id=1, source_target_pairs={{0,16},{1,17},{2,18},{3,19},{4,20},{5,21},{6,22},{7,23},{8,40},{9,... | collective-permute-start | bytes 786440 | tf_op jit(solution)/shard_map/ppermute | solution.py:289
  83.4 10.1 %collective-permute-start.15 = (bf16[128,768]{1,0:T(8,128)(2,1)S(1)}, bf16[128,768]{1,0:T(8,128)(2,1)S(1)}, u32[]{:S(2)}, u32[]{:S(2)}) collective-permute-start(bf16[128,768]{1,0:T(8,128)(2,1)S(1)} %get-tuple-element.25), channel_id=1, source_target_pairs={{0,3},{1,0},{2,1},{3,2},{4,7},{5,4},{6,5},{7,6},{8,11},{9,8},{10,9... | collective-permute-start | bytes 589832 | tf_op jit(solution)/shard_map/ppermute | solution.py:289
  85.6 9.5 %collective-permute-start.16 = (bf16[128,768]{1,0:T(8,128)(2,1)S(1)}, bf16[128,768]{1,0:T(8,128)(2,1)S(1)}, u32[]{:S(2)}, u32[]{:S(2)}) collective-permute-start(bf16[128,768]{1,0:T(8,128)(2,1)S(1)} %get-tuple-element.26), channel_id=1, source_target_pairs={{0,1},{1,2},{2,3},{3,0},{4,5},{5,6},{6,7},{7,4},{8,9},{9,10},{10,1... | collective-permute-start | bytes 589832 | tf_op jit(solution)/shard_map/ppermute | solution.py:289
  89.2 7.2 %collective-permute-start.17 = (bf16[128,768]{1,0:T(8,128)(2,1)S(1)}, bf16[128,768]{1,0:T(8,128)(2,1)S(1)}, u32[]{:S(2)}, u32[]{:S(2)}) collective-permute-start(bf16[128,768]{1,0:T(8,128)(2,1)S(1)} %get-tuple-element.27), channel_id=1, source_target_pairs={{0,2},{1,3},{2,0},{3,1},{4,6},{5,7},{6,4},{7,5},{8,10},{9,11},{10,... | collective-permute-start | bytes 589832 | tf_op jit(solution)/shard_map/ppermute | solution.py:289
  93.1 4.3 %collective-permute-start.22 = (bf16[128,256]{1,0:T(8,128)(2,1)S(1)}, bf16[128,256]{1,0:T(8,128)(2,1)S(1)}, u32[]{:S(2)}, u32[]{:S(2)}) collective-permute-start(bf16[128,256]{1,0:T(8,128)(2,1)S(1)} %get-tuple-element.46), channel_id=1, source_target_pairs={{0,96},{1,97},{2,98},{3,99},{4,100},{5,101},{6,102},{7,103},{8,28}... | collective-permute-start | bytes 196616 | tf_op jit(solution)/shard_map/ppermute | solution.py:289
  93.5 5.8 %collective-permute-start.24 = (bf16[128,256]{1,0:T(8,128)(2,1)S(1)}, bf16[128,256]{1,0:T(8,128)(2,1)S(1)}, u32[]{:S(2)}, u32[]{:S(2)}) collective-permute-start(bf16[128,256]{1,0:T(8,128)(2,1)S(1)} %get-tuple-element.47), channel_id=1, source_target_pairs={{0,64},{1,65},{2,66},{3,67},{4,68},{5,69},{6,70},{7,71},{8,12},{9,... | collective-permute-start | bytes 196616 | tf_op jit(solution)/shard_map/ppermute | solution.py:289
  93.5 6.6 %collective-permute-start.23 = (bf16[128,256]{1,0:T(8,128)(2,1)S(1)}, bf16[128,256]{1,0:T(8,128)(2,1)S(1)}, u32[]{:S(2)}, u32[]{:S(2)}) collective-permute-start(bf16[128,256]{1,0:T(8,128)(2,1)S(1)} %get-tuple-element.48), channel_id=1, source_target_pairs={{0,32},{1,33},{2,34},{3,35},{4,36},{5,37},{6,38},{7,39},{8,24},{9,... | collective-permute-start | bytes 196616 | tf_op jit(solution)/shard_map/ppermute | solution.py:289
  (3 other events, 15.5 us)

commit v12 on v11

--- a/solution.py
+++ b/solution.py
@@ -169,7 +169,7 @@
             out[1, pl.ds(row, 1), :] = (dd / safe)[:, at]
 
 
-def grads_kernel(meta, lim, st0, st1, *refs):
+def grads_kernel(meta, lim, st0, st1, st2, st3, *refs):
     qds, kvs = refs[:4], refs[4:12]
     dqs, dkvs, dkv_other = refs[12:16], refs[16:20], refs[20]
     q_s, do_s, kv_s, s0, s1, dp0, dp1, acc, dq_s, p0, p1, ds0, ds1, lse, delta = refs[21:]
@@ -178,7 +178,8 @@
     load_rows(meta, base, qds, q_s, do_s)
     acc[...] = jnp.zeros_like(acc)
     dq_s[...] = jnp.zeros_like(dq_s)
-    all_lse, all_delta = merged(st0[0], st0[1], st1[0], st1[1])
+    left, right = merged(st0[0], st0[1], st1[0], st1[1]), merged(st2[0], st2[1], st3[0], st3[1])
+    all_lse, all_delta = merged(*left, *right)
     lse[...] = jnp.zeros_like(lse)
     delta[...] = jnp.zeros_like(delta)
     for g in range(GROUPS):
@@ -266,7 +267,7 @@
     return pl.pallas_call(
         grads_kernel,
         out_shape=dq + dkv,
-        in_specs=[SM] + [VM] * 15,
+        in_specs=[SM] + [VM] * 17,
         out_specs=[VM] * 9,
         scratch_shapes=COPIES
         + [
@@ -376,10 +377,8 @@
 
     part = stats(NEAR, meta, lim, near, kvs)
     part = stats(FAR, meta, lim, [far], kvs, part)
-    got = permute(part, lambda y, z, core, x: (y, z, core, x ^ 1))
-    part = jnp.stack(merged(part[0], part[1], got[0], got[1]))
-    got = permute(part, lambda y, z, core, x: (y, z, core, x ^ 2))
-    results = grads(meta, lim, (part, got), arrays)
+    sts = [part] + [x_shift(part, r) for r in STEPS[1:]]
+    results = grads(meta, lim, sts, arrays)
     dqs, dkv, dkv_other = results[:4], results[4:8], results[8]
 
     def total(*parts):

time: 101 us -> 101 us (level)
  Pallas kernels: 38.6 us -> 37.5 us
    ppermute x25 -> x26, starting transfers between devices: 32 us -> 32.4 us  [permute(): return lax.ppermute(a, AXES, pairs)]
    ppermute x25 -> x26, waiting for transfers between devices: 21.6 us -> 21.4 us  [permute(): return lax.ppermute(a, AXES, pairs)]
  transfers between devices with their start and end apart: 25 -> 26, of which waited for: 12 -> 14; matrix products, arithmetic and copies ran while one was open for 6% -> 6% of each run, Pallas kernels for 10% -> 10%
where the time goes in v12:
time: 101 us; the launch traced here: 99.9 us
  Pallas kernels  37.5 us (37%)
  starting transfers between devices  32.4 us (32%)
  waiting for transfers between devices  21.4 us (21%)
  other arithmetic  4.62 us (5%)
  local copies, waits for them, and re-layouts  3.09 us (3%)
    ppermute x26, starting transfers between devices, permute(): return lax.ppermute(a, AXES, pairs)  32.4 us
    pallas_call x1, Pallas kernels, grads(): pl.pallas_call(grads_kernel, out_shape=dq + dkv, in_specs=[SM] + [VM] * 1...  23.6 us
    ppermute x26, waiting for transfers between devices, permute(): return lax.ppermute(a, AXES, pairs)  21.4 us
    pallas_call x2, Pallas kernels, stats(): pl.pallas_call(functools.partial(stats_kernel, which, n), out_shape=jax.S...  13.9 us
  transfers between devices with their start and end apart: 26, of which 14 were waited for; matrix products, arithmetic and copies ran while one was open for 6% of the time, Pallas kernels for 10%

profile of v12, /device:TPU:0, one launch (start us, length us, event | category | flops | bytes accessed | tf_op | source)
XLA Modules:
  0.0 99.9 jit_solution(15540244300773540077)
XLA Ops:
  1.4 3.4 %collective-permute-start.2 = (bf16[1,128,256]{2,1,0:T(8,128)(2,1)S(1)}, bf16[1,128,256]{2,1,0:T(8,128)(2,1)S(1)}, u32[]{:S(2)}, u32[]{:S(2)}) collective-permute-start(bf16[1,128,256]{2,1,0:T(8,128)(2,1)S(1)} %maximum_bitcast_fusion), channel_id=1, source_target_pairs={{0,64},{1,65},{2,66},{3,67},{4,68},{5,69},{6,70},{7,71},{8,12},{9,... | collective-permute-start | bytes 196616 | tf_op jit(solution)/shard_map/ppermute | solution.py:290
  4.8 1.1 %collective-permute-start.1 = (bf16[1,128,256]{2,1,0:T(8,128)(2,1)S(1)}, bf16[1,128,256]{2,1,0:T(8,128)(2,1)S(1)}, u32[]{:S(2)}, u32[]{:S(2)}) collective-permute-start(bf16[1,128,256]{2,1,0:T(8,128)(2,1)S(1)} %maximum_bitcast_fusion), channel_id=1, source_target_pairs={{0,96},{1,97},{2,98},{3,99},{4,100},{5,101},{6,102},{7,103},{8,28}... | collective-permute-start | bytes 196616 | tf_op jit(solution)/shard_map/ppermute | solution.py:290
  7.8 2.8 %collective-permute-start.5 = (bf16[128,1536]{1,0:T(8,128)(2,1)S(1)}, bf16[128,1536]{1,0:T(8,128)(2,1)S(1)}, u32[]{:S(2)}, u32[]{:S(2)}) collective-permute-start(bf16[128,1536]{1,0:T(8,128)(2,1)S(1)} %constant_dynamic-update-slice_fusion.6.refs_0_), channel_id=1, source_target_pairs={{0,3},{1,0},{2,1},{3,2},{4,7},{5,4},{6,5},{7,6},{8,11},{9,8},{10,9... | collective-permute-start | bytes 1179656 | tf_op jit(solution)/shard_map/ppermute | solution.py:290
  11.3 2.0 %collective-permute-start.3 = (bf16[4,128,256]{2,1,0:T(8,128)(2,1)S(1)}, bf16[4,128,256]{2,1,0:T(8,128)(2,1)S(1)}, u32[]{:S(2)}, u32[]{:S(2)}) collective-permute-start(bf16[4,128,256]{2,1,0:T(8,128)(2,1)S(1)} %pad_maximum_fusion.refs_3_.refs_1_.refs_4_), channel_id=1, source_target_pairs={{0,16},{1,17},{2,18},{3,19},{4,20},{5,21},{6,22},{7,23},{8,40},{9,... | collective-permute-start | bytes 786440 | tf_op jit(solution)/shard_map/ppermute | solution.py:290
  13.6 3.7 %collective-permute-start.8 = (bf16[4,128,256]{2,1,0:T(8,128)(2,1)S(1)}, bf16[4,128,256]{2,1,0:T(8,128)(2,1)S(1)}, u32[]{:S(2)}, u32[]{:S(2)}) collective-permute-start(bf16[4,128,256]{2,1,0:T(8,128)(2,1)S(1)} %pad_maximum_fusion.refs_3_.refs_1_.refs_4_), channel_id=1, source_target_pairs={{0,4},{1,5},{2,6},{3,7},{4,0},{5,1},{6,2},{7,3},{8,72},{9,73},{10,... | collective-permute-start | bytes 786440 | tf_op jit(solution)/shard_map/ppermute | solution.py:290
  17.2 1.0 %collective-permute-start.7 = (bf16[4,128,256]{2,1,0:T(8,128)(2,1)S(1)}, bf16[4,128,256]{2,1,0:T(8,128)(2,1)S(1)}, u32[]{:S(2)}, u32[]{:S(2)}) collective-permute-start(bf16[4,128,256]{2,1,0:T(8,128)(2,1)S(1)} %pad_maximum_fusion.refs_3_.refs_1_.refs_4_), channel_id=1, source_target_pairs={{0,20},{1,21},{2,22},{3,23},{4,16},{5,17},{6,18},{7,19},{8,104},{9... | collective-permute-start | bytes 786440 | tf_op jit(solution)/shard_map/ppermute | solution.py:290
  18.2 1.6 %collective-permute-done.3.refs_4_.refs_2_.refs_5_ = bf16[4,128,256]{2,1,0:T(8,128)(2,1)S(1)} collective-permute-done((bf16[4,128,256]{2,1,0:T(8,128)(2,1)S(1)}, bf16[4,128,256]{2,1,0:T(8,128)(2,1)S(1)}, u32[]{:S(2)}, u32[]{:S(2)}) %collective-permute-start.3) | collective-permute-done | bytes 262176 | tf_op jit(solution)/shard_map/ppermute | solution.py:290
  24.7 3.4 %collective-permute-start.6 = (bf16[128,1536]{1,0:T(8,128)(2,1)S(1)}, bf16[128,1536]{1,0:T(8,128)(2,1)}, u32[]{:S(2)}, u32[]{:S(2)}) collective-permute-start(bf16[128,1536]{1,0:T(8,128)(2,1)S(1)} %constant_dynamic-update-slice_fusion.6.refs_0_), channel_id=1, source_target_pairs={{0,2},{1,3},{2,0},{3,1},{4,6},{5,7},{6,4},{7,5},{8,10},{9,11},{10,... | collective-permute-start | bytes 1179656 | tf_op jit(solution)/shard_map/ppermute | solution.py:290
  28.7 9.7 %stats_near.1.refs_9_ = f32[2,24,128]{2,1,0:T(8,128)S(1)} custom-call(s32[982]{0:T(1024)S(1)} %pad_add_fusion.2.meta, s32[3,16,256]{2,1,0:T(8,128)S(1)} %concatenate.34.lim, bf16[128,1536]{1,0:T(8,128)(2,1)S(1)} %constant_dynamic-update-slice_fusion.6.refs_0_, bf16[128,1536]{1,0:T(8,128)(2,1)S(1)} %collective-permute-done.4.refs_1_, ...), custom_call_target="tpu_custom_call" | custom-call | flops 3000000 | bytes 100000 | tf_op jit(solution)/shard_map/stats_near/pallas_call | solution.py:251
  38.4 4.2 %stats_far.1.st0 = f32[2,24,128]{2,1,0:T(8,128)S(1)} custom-call(s32[982]{0:T(1024)S(1)} %pad_add_fusion.2.meta, s32[3,16,256]{2,1,0:T(8,128)S(1)} %concatenate.34.lim, bf16[128,1536]{1,0:T(8,128)(2,1)} %collective-permute-done.6.refs_0_.refs_3_, bf16[4,128,256]{2,1,0:T(8,128)(2,1)S(1)} %pad_maximum_fusion.refs_3_.refs_1_.refs_4_, ...), custom_call_target="tpu_custom_call" | custom-call | flops 1000000 | bytes 100000 | tf_op jit(solution)/shard_map/stats_far/pallas_call | solution.py:251
  42.6 3.3 %collective-permute-start.15 = (f32[2,24,128]{2,1,0:T(8,128)S(1)}, f32[2,24,128]{2,1,0:T(8,128)S(1)}, u32[]{:S(2)}, u32[]{:S(2)}) collective-permute-start(f32[2,24,128]{2,1,0:T(8,128)S(1)} %stats_far.1.st0), channel_id=1, source_target_pairs={{0,2},{1,3},{2,0},{3,1},{4,6},{5,7},{6,4},{7,5},{8,10},{9,11},{10,... | collective-permute-start | bytes 73736 | tf_op jit(solution)/shard_map/ppermute | solution.py:290
  45.9 1.1 %collective-permute-start.14 = (f32[2,24,128]{2,1,0:T(8,128)S(1)}, f32[2,24,128]{2,1,0:T(8,128)S(1)}, u32[]{:S(2)}, u32[]{:S(2)}) collective-permute-start(f32[2,24,128]{2,1,0:T(8,128)S(1)} %stats_far.1.st0), channel_id=1, source_target_pairs={{0,3},{1,0},{2,1},{3,2},{4,7},{5,4},{6,5},{7,6},{8,11},{9,8},{10,9... | collective-permute-start | bytes 73736 | tf_op jit(solution)/shard_map/ppermute | solution.py:290
  48.2 1.6 %collective-permute-done.14.st2 = f32[2,24,128]{2,1,0:T(8,128)S(1)} collective-permute-done((f32[2,24,128]{2,1,0:T(8,128)S(1)}, f32[2,24,128]{2,1,0:T(8,128)S(1)}, u32[]{:S(2)}, u32[]{:S(2)}) %collective-permute-start.14) | collective-permute-done | bytes 24608 | tf_op jit(solution)/shard_map/ppermute | solution.py:290
  49.8 2.3 %collective-permute-done.13.st1 = f32[2,24,128]{2,1,0:T(8,128)S(1)} collective-permute-done((f32[2,24,128]{2,1,0:T(8,128)S(1)}, f32[2,24,128]{2,1,0:T(8,128)S(1)}, u32[]{:S(2)}, u32[]{:S(2)}) %collective-permute-start.13) | collective-permute-done | bytes 24608 | tf_op jit(solution)/shard_map/ppermute | solution.py:290
  52.1 23.6 %grads.1 = (f32[128,768]{1,0:T(8,128)S(1)}, bf16[128,768]{1,0:T(8,128)(2,1)S(1)}, bf16[128,768]{1,0:T(8,128)(2,1)S(1)}, bf16[128,768]{1,0:T(8,128)(2,1)S(1)}, bf...) custom-call(s32[982]{0:T(1024)S(1)} %pad_add_fusion.2.meta, ...), custom_call_target="tpu_custom_call" | custom-call | tf_op jit(solution)/shard_map/grads/pallas_call | solution.py:267
  75.8 2.9 %collective-permute-done.19 = bf16[4,4,128,256]{3,2,1,0:T(8,128)(2,1)S(1)} collective-permute-done((bf16[4,4,128,256]{3,2,1,0:T(8,128)(2,1)}, bf16[4,4,128,256]{3,2,1,0:T(8,128)(2,1)S(1)}, u32[]{:S(2)}, u32[]{:S(2)}) %collective-permute-start.19) | collective-permute-done | bytes 1048608 | tf_op jit(solution)/shard_map/ppermute | solution.py:290
  78.9 2.1 %collective-permute-start.20 = (bf16[4,128,256]{2,1,0:T(8,128)(2,1)S(1)}, bf16[4,128,256]{2,1,0:T(8,128)(2,1)S(1)}, u32[]{:S(2)}, u32[]{:S(2)}) collective-permute-start(bf16[4,128,256]{2,1,0:T(8,128)(2,1)S(1)} %get-tuple-element.43), channel_id=1, source_target_pairs={{0,20},{1,21},{2,22},{3,23},{4,16},{5,17},{6,18},{7,19},{8,104},{9... | collective-permute-start | bytes 786440 | tf_op jit(solution)/shard_map/ppermute | solution.py:290
  80.9 1.9 %collective-permute-start.22 = (bf16[4,128,256]{2,1,0:T(8,128)(2,1)S(1)}, bf16[4,128,256]{2,1,0:T(8,128)(2,1)S(1)}, u32[]{:S(2)}, u32[]{:S(2)}) collective-permute-start(bf16[4,128,256]{2,1,0:T(8,128)(2,1)S(1)} %get-tuple-element.44), channel_id=1, source_target_pairs={{0,4},{1,5},{2,6},{3,7},{4,0},{5,1},{6,2},{7,3},{8,72},{9,73},{10,... | collective-permute-start | bytes 786440 | tf_op jit(solution)/shard_map/ppermute | solution.py:290
  83.1 1.7 %collective-permute-start.17 = (bf16[128,768]{1,0:T(8,128)(2,1)S(1)}, bf16[128,768]{1,0:T(8,128)(2,1)S(1)}, u32[]{:S(2)}, u32[]{:S(2)}) collective-permute-start(bf16[128,768]{1,0:T(8,128)(2,1)S(1)} %get-tuple-element.26), channel_id=1, source_target_pairs={{0,1},{1,2},{2,3},{3,0},{4,5},{5,6},{6,7},{7,4},{8,9},{9,10},{10,1... | collective-permute-start | bytes 589832 | tf_op jit(solution)/shard_map/ppermute | solution.py:290
  84.8 2.8 %collective-permute-done.20 = bf16[4,128,256]{2,1,0:T(8,128)(2,1)S(1)} collective-permute-done((bf16[4,128,256]{2,1,0:T(8,128)(2,1)S(1)}, bf16[4,128,256]{2,1,0:T(8,128)(2,1)S(1)}, u32[]{:S(2)}, u32[]{:S(2)}) %collective-permute-start.20) | collective-permute-done | bytes 262176 | tf_op jit(solution)/shard_map/ppermute | solution.py:290
  87.6 1.2 %collective-permute-done.22 = bf16[4,128,256]{2,1,0:T(8,128)(2,1)S(1)} collective-permute-done((bf16[4,128,256]{2,1,0:T(8,128)(2,1)S(1)}, bf16[4,128,256]{2,1,0:T(8,128)(2,1)S(1)}, u32[]{:S(2)}, u32[]{:S(2)}) %collective-permute-start.22) | collective-permute-done | bytes 262176 | tf_op jit(solution)/shard_map/ppermute | solution.py:290
  88.9 2.7 %collective-permute-done.21 = bf16[4,128,256]{2,1,0:T(8,128)(2,1)S(1)} collective-permute-done((bf16[4,128,256]{2,1,0:T(8,128)(2,1)S(1)}, bf16[4,128,256]{2,1,0:T(8,128)(2,1)S(1)}, u32[]{:S(2)}, u32[]{:S(2)}) %collective-permute-start.21) | collective-permute-done | bytes 262176 | tf_op jit(solution)/shard_map/ppermute | solution.py:290
  91.8 1.0 %collective-permute-start.23 = (bf16[128,256]{1,0:T(8,128)(2,1)S(1)}, bf16[128,256]{1,0:T(8,128)(2,1)S(1)}, u32[]{:S(2)}, u32[]{:S(2)}) collective-permute-start(bf16[128,256]{1,0:T(8,128)(2,1)S(1)} %get-tuple-element.46), channel_id=1, source_target_pairs={{0,96},{1,97},{2,98},{3,99},{4,100},{5,101},{6,102},{7,103},{8,28}... | collective-permute-start | bytes 196616 | tf_op jit(solution)/shard_map/ppermute | solution.py:290
  96.1 2.5 %collective-permute-done.25 = bf16[128,256]{1,0:T(8,128)(2,1)S(1)} collective-permute-done((bf16[128,256]{1,0:T(8,128)(2,1)S(1)}, bf16[128,256]{1,0:T(8,128)(2,1)S(1)}, u32[]{:S(2)}, u32[]{:S(2)}) %collective-permute-start.25) | collective-permute-done | bytes 65568 | tf_op jit(solution)/shard_map/ppermute | solution.py:290
  (104 shorter events, 15.5 us)
Async XLA Ops:
  1.4 9.2 %collective-permute-start.2 = (bf16[1,128,256]{2,1,0:T(8,128)(2,1)S(1)}, bf16[1,128,256]{2,1,0:T(8,128)(2,1)S(1)}, u32[]{:S(2)}, u32[]{:S(2)}) collective-permute-start(bf16[1,128,256]{2,1,0:T(8,128)(2,1)S(1)} %maximum_bitcast_fusion), channel_id=1, source_target_pairs={{0,64},{1,65},{2,66},{3,67},{4,68},{5,69},{6,70},{7,71},{8,12},{9,... | collective-permute-start | bytes 196616 | tf_op jit(solution)/shard_map/ppermute | solution.py:290
  4.8 5.9 %collective-permute-start.1 = (bf16[1,128,256]{2,1,0:T(8,128)(2,1)S(1)}, bf16[1,128,256]{2,1,0:T(8,128)(2,1)S(1)}, u32[]{:S(2)}, u32[]{:S(2)}) collective-permute-start(bf16[1,128,256]{2,1,0:T(8,128)(2,1)S(1)} %maximum_bitcast_fusion), channel_id=1, source_target_pairs={{0,96},{1,97},{2,98},{3,99},{4,100},{5,101},{6,102},{7,103},{8,28}... | collective-permute-start | bytes 196616 | tf_op jit(solution)/shard_map/ppermute | solution.py:290
  5.8 5.5 %collective-permute-start = (bf16[1,128,256]{2,1,0:T(8,128)(2,1)S(1)}, bf16[1,128,256]{2,1,0:T(8,128)(2,1)S(1)}, u32[]{:S(2)}, u32[]{:S(2)}) collective-permute-start(bf16[1,128,256]{2,1,0:T(8,128)(2,1)S(1)} %maximum_bitcast_fusion), channel_id=1, source_target_pairs={{0,32},{1,33},{2,34},{3,35},{4,36},{5,37},{6,38},{7,39},{8,24},{9,... | collective-permute-start | bytes 196616 | tf_op jit(solution)/shard_map/ppermute | solution.py:290
  7.8 16.8 %collective-permute-start.5 = (bf16[128,1536]{1,0:T(8,128)(2,1)S(1)}, bf16[128,1536]{1,0:T(8,128)(2,1)S(1)}, u32[]{:S(2)}, u32[]{:S(2)}) collective-permute-start(bf16[128,1536]{1,0:T(8,128)(2,1)S(1)} %constant_dynamic-update-slice_fusion.6.refs_0_), channel_id=1, source_target_pairs={{0,3},{1,0},{2,1},{3,2},{4,7},{5,4},{6,5},{7,6},{8,11},{9,8},{10,9... | collective-permute-start | bytes 1179656 | tf_op jit(solution)/shard_map/ppermute | solution.py:290
  10.6 14.1 %collective-permute-start.4 = (bf16[128,1536]{1,0:T(8,128)(2,1)S(1)}, bf16[128,1536]{1,0:T(8,128)(2,1)S(1)}, u32[]{:S(2)}, u32[]{:S(2)}) collective-permute-start(bf16[128,1536]{1,0:T(8,128)(2,1)S(1)} %constant_dynamic-update-slice_fusion.6.refs_0_), channel_id=1, source_target_pairs={{0,1},{1,2},{2,3},{3,0},{4,5},{5,6},{6,7},{7,4},{8,9},{9,10},{10,1... | collective-permute-start | bytes 1179656 | tf_op jit(solution)/shard_map/ppermute | solution.py:290
  11.3 8.5 %collective-permute-start.3 = (bf16[4,128,256]{2,1,0:T(8,128)(2,1)S(1)}, bf16[4,128,256]{2,1,0:T(8,128)(2,1)S(1)}, u32[]{:S(2)}, u32[]{:S(2)}) collective-permute-start(bf16[4,128,256]{2,1,0:T(8,128)(2,1)S(1)} %pad_maximum_fusion.refs_3_.refs_1_.refs_4_), channel_id=1, source_target_pairs={{0,16},{1,17},{2,18},{3,19},{4,20},{5,21},{6,22},{7,23},{8,40},{9,... | collective-permute-start | bytes 786440 | tf_op jit(solution)/shard_map/ppermute | solution.py:290
  13.6 10.5 %collective-permute-start.8 = (bf16[4,128,256]{2,1,0:T(8,128)(2,1)S(1)}, bf16[4,128,256]{2,1,0:T(8,128)(2,1)S(1)}, u32[]{:S(2)}, u32[]{:S(2)}) collective-permute-start(bf16[4,128,256]{2,1,0:T(8,128)(2,1)S(1)} %pad_maximum_fusion.refs_3_.refs_1_.refs_4_), channel_id=1, source_target_pairs={{0,4},{1,5},{2,6},{3,7},{4,0},{5,1},{6,2},{7,3},{8,72},{9,73},{10,... | collective-permute-start | bytes 786440 | tf_op jit(solution)/shard_map/ppermute | solution.py:290
  17.2 6.9 %collective-permute-start.7 = (bf16[4,128,256]{2,1,0:T(8,128)(2,1)S(1)}, bf16[4,128,256]{2,1,0:T(8,128)(2,1)S(1)}, u32[]{:S(2)}, u32[]{:S(2)}) collective-permute-start(bf16[4,128,256]{2,1,0:T(8,128)(2,1)S(1)} %pad_maximum_fusion.refs_3_.refs_1_.refs_4_), channel_id=1, source_target_pairs={{0,20},{1,21},{2,22},{3,23},{4,16},{5,17},{6,18},{7,19},{8,104},{9... | collective-permute-start | bytes 786440 | tf_op jit(solution)/shard_map/ppermute | solution.py:290
  23.1 5.6 %collective-permute-start.9 = (bf16[4,128,256]{2,1,0:T(8,128)(2,1)S(1)}, bf16[4,128,256]{2,1,0:T(8,128)(2,1)S(1)}, u32[]{:S(2)}, u32[]{:S(2)}) collective-permute-start(bf16[4,128,256]{2,1,0:T(8,128)(2,1)S(1)} %pad_maximum_fusion.refs_3_.refs_1_.refs_4_), channel_id=1, source_target_pairs={{0,8},{1,9},{2,10},{3,11},{4,12},{5,13},{6,14},{7,15},{8,0},{9,1},... | collective-permute-start | bytes 786440 | tf_op jit(solution)/shard_map/ppermute | solution.py:290
  24.1 4.6 %collective-permute-start.10 = (bf16[4,128,256]{2,1,0:T(8,128)(2,1)S(1)}, bf16[4,128,256]{2,1,0:T(8,128)(2,1)S(1)}, u32[]{:S(2)}, u32[]{:S(2)}) collective-permute-start(bf16[4,128,256]{2,1,0:T(8,128)(2,1)S(1)} %collective-permute-done.3.refs_4_.refs_2_.refs_5_), channel_id=1, source_target_pairs={{0,8},{1,9},{2,10},{3,11},{4,12},{5,13},{6,14},{7,15},{8,0},{9,1},... | collective-permute-start | bytes 786440 | tf_op jit(solution)/shard_map/ppermute | solution.py:290
  24.1 4.6 %collective-permute-start.12 = (bf16[4,128,256]{2,1,0:T(8,128)(2,1)S(1)}, bf16[4,128,256]{2,1,0:T(8,128)(2,1)S(1)}, u32[]{:S(2)}, u32[]{:S(2)}) collective-permute-start(bf16[4,128,256]{2,1,0:T(8,128)(2,1)S(1)} %collective-permute-done.8.refs_6_.refs_4_.refs_7_), channel_id=1, source_target_pairs={{0,8},{1,9},{2,10},{3,11},{4,12},{5,13},{6,14},{7,15},{8,0},{9,1},... | collective-permute-start | bytes 786440 | tf_op jit(solution)/shard_map/ppermute | solution.py:290
  24.6 4.1 %collective-permute-start.11 = (bf16[4,128,256]{2,1,0:T(8,128)(2,1)S(1)}, bf16[4,128,256]{2,1,0:T(8,128)(2,1)S(1)}, u32[]{:S(2)}, u32[]{:S(2)}) collective-permute-start(bf16[4,128,256]{2,1,0:T(8,128)(2,1)S(1)} %collective-permute-done.7.refs_5_.refs_3_.refs_6_), channel_id=1, source_target_pairs={{0,8},{1,9},{2,10},{3,11},{4,12},{5,13},{6,14},{7,15},{8,0},{9,1},... | collective-permute-start | bytes 786440 | tf_op jit(solution)/shard_map/ppermute | solution.py:290
  24.7 13.7 %collective-permute-start.6 = (bf16[128,1536]{1,0:T(8,128)(2,1)S(1)}, bf16[128,1536]{1,0:T(8,128)(2,1)}, u32[]{:S(2)}, u32[]{:S(2)}) collective-permute-start(bf16[128,1536]{1,0:T(8,128)(2,1)S(1)} %constant_dynamic-update-slice_fusion.6.refs_0_), channel_id=1, source_target_pairs={{0,2},{1,3},{2,0},{3,1},{4,6},{5,7},{6,4},{7,5},{8,10},{9,11},{10,... | collective-permute-start | bytes 1179656 | tf_op jit(solution)/shard_map/ppermute | solution.py:290
  42.6 5.6 %collective-permute-start.15 = (f32[2,24,128]{2,1,0:T(8,128)S(1)}, f32[2,24,128]{2,1,0:T(8,128)S(1)}, u32[]{:S(2)}, u32[]{:S(2)}) collective-permute-start(f32[2,24,128]{2,1,0:T(8,128)S(1)} %stats_far.1.st0), channel_id=1, source_target_pairs={{0,2},{1,3},{2,0},{3,1},{4,6},{5,7},{6,4},{7,5},{8,10},{9,11},{10,... | collective-permute-start | bytes 73736 | tf_op jit(solution)/shard_map/ppermute | solution.py:290
  47.1 5.0 %collective-permute-start.13 = (f32[2,24,128]{2,1,0:T(8,128)S(1)}, f32[2,24,128]{2,1,0:T(8,128)S(1)}, u32[]{:S(2)}, u32[]{:S(2)}) collective-permute-start(f32[2,24,128]{2,1,0:T(8,128)S(1)} %stats_far.1.st0), channel_id=1, source_target_pairs={{0,1},{1,2},{2,3},{3,0},{4,5},{5,6},{6,7},{7,4},{8,9},{9,10},{10,1... | collective-permute-start | bytes 73736 | tf_op jit(solution)/shard_map/ppermute | solution.py:290
  78.9 8.8 %collective-permute-start.20 = (bf16[4,128,256]{2,1,0:T(8,128)(2,1)S(1)}, bf16[4,128,256]{2,1,0:T(8,128)(2,1)S(1)}, u32[]{:S(2)}, u32[]{:S(2)}) collective-permute-start(bf16[4,128,256]{2,1,0:T(8,128)(2,1)S(1)} %get-tuple-element.43), channel_id=1, source_target_pairs={{0,20},{1,21},{2,22},{3,23},{4,16},{5,17},{6,18},{7,19},{8,104},{9... | collective-permute-start | bytes 786440 | tf_op jit(solution)/shard_map/ppermute | solution.py:290
  80.9 8.0 %collective-permute-start.22 = (bf16[4,128,256]{2,1,0:T(8,128)(2,1)S(1)}, bf16[4,128,256]{2,1,0:T(8,128)(2,1)S(1)}, u32[]{:S(2)}, u32[]{:S(2)}) collective-permute-start(bf16[4,128,256]{2,1,0:T(8,128)(2,1)S(1)} %get-tuple-element.44), channel_id=1, source_target_pairs={{0,4},{1,5},{2,6},{3,7},{4,0},{5,1},{6,2},{7,3},{8,72},{9,73},{10,... | collective-permute-start | bytes 786440 | tf_op jit(solution)/shard_map/ppermute | solution.py:290
  82.8 8.8 %collective-permute-start.21 = (bf16[4,128,256]{2,1,0:T(8,128)(2,1)S(1)}, bf16[4,128,256]{2,1,0:T(8,128)(2,1)S(1)}, u32[]{:S(2)}, u32[]{:S(2)}) collective-permute-start(bf16[4,128,256]{2,1,0:T(8,128)(2,1)S(1)} %get-tuple-element.45), channel_id=1, source_target_pairs={{0,16},{1,17},{2,18},{3,19},{4,20},{5,21},{6,22},{7,23},{8,40},{9,... | collective-permute-start | bytes 786440 | tf_op jit(solution)/shard_map/ppermute | solution.py:290
  82.8 10.8 %collective-permute-start.16 = (bf16[128,768]{1,0:T(8,128)(2,1)S(1)}, bf16[128,768]{1,0:T(8,128)(2,1)S(1)}, u32[]{:S(2)}, u32[]{:S(2)}) collective-permute-start(bf16[128,768]{1,0:T(8,128)(2,1)S(1)} %get-tuple-element.25), channel_id=1, source_target_pairs={{0,3},{1,0},{2,1},{3,2},{4,7},{5,4},{6,5},{7,6},{8,11},{9,8},{10,9... | collective-permute-start | bytes 589832 | tf_op jit(solution)/shard_map/ppermute | solution.py:290
  83.1 10.8 %collective-permute-start.17 = (bf16[128,768]{1,0:T(8,128)(2,1)S(1)}, bf16[128,768]{1,0:T(8,128)(2,1)S(1)}, u32[]{:S(2)}, u32[]{:S(2)}) collective-permute-start(bf16[128,768]{1,0:T(8,128)(2,1)S(1)} %get-tuple-element.26), channel_id=1, source_target_pairs={{0,1},{1,2},{2,3},{3,0},{4,5},{5,6},{6,7},{7,4},{8,9},{9,10},{10,1... | collective-permute-start | bytes 589832 | tf_op jit(solution)/shard_map/ppermute | solution.py:290
  87.6 7.2 %collective-permute-start.18 = (bf16[128,768]{1,0:T(8,128)(2,1)S(1)}, bf16[128,768]{1,0:T(8,128)(2,1)S(1)}, u32[]{:S(2)}, u32[]{:S(2)}) collective-permute-start(bf16[128,768]{1,0:T(8,128)(2,1)S(1)} %get-tuple-element.27), channel_id=1, source_target_pairs={{0,2},{1,3},{2,0},{3,1},{4,6},{5,7},{6,4},{7,5},{8,10},{9,11},{10,... | collective-permute-start | bytes 589832 | tf_op jit(solution)/shard_map/ppermute | solution.py:290
  91.8 4.3 %collective-permute-start.23 = (bf16[128,256]{1,0:T(8,128)(2,1)S(1)}, bf16[128,256]{1,0:T(8,128)(2,1)S(1)}, u32[]{:S(2)}, u32[]{:S(2)}) collective-permute-start(bf16[128,256]{1,0:T(8,128)(2,1)S(1)} %get-tuple-element.46), channel_id=1, source_target_pairs={{0,96},{1,97},{2,98},{3,99},{4,100},{5,101},{6,102},{7,103},{8,28}... | collective-permute-start | bytes 196616 | tf_op jit(solution)/shard_map/ppermute | solution.py:290
  92.8 5.8 %collective-permute-start.25 = (bf16[128,256]{1,0:T(8,128)(2,1)S(1)}, bf16[128,256]{1,0:T(8,128)(2,1)S(1)}, u32[]{:S(2)}, u32[]{:S(2)}) collective-permute-start(bf16[128,256]{1,0:T(8,128)(2,1)S(1)} %get-tuple-element.47), channel_id=1, source_target_pairs={{0,64},{1,65},{2,66},{3,67},{4,68},{5,69},{6,70},{7,71},{8,12},{9,... | collective-permute-start | bytes 196616 | tf_op jit(solution)/shard_map/ppermute | solution.py:290
  93.6 5.7 %collective-permute-start.24 = (bf16[128,256]{1,0:T(8,128)(2,1)S(1)}, bf16[128,256]{1,0:T(8,128)(2,1)S(1)}, u32[]{:S(2)}, u32[]{:S(2)}) collective-permute-start(bf16[128,256]{1,0:T(8,128)(2,1)S(1)} %get-tuple-element.48), channel_id=1, source_target_pairs={{0,32},{1,33},{2,34},{3,35},{4,36},{5,37},{6,38},{7,39},{8,24},{9,... | collective-permute-start | bytes 196616 | tf_op jit(solution)/shard_map/ppermute | solution.py:290
  (4 other events, 19.3 us)
